TPU v7x, 256 devices: a whole 4x4x8 slice. The times are simulated.
256 devices in a mesh: section: 4 (over y), peer: 64 (over x, z, core).
Axes of the slice: x: 4, y: 4, z: 8, core: 2. Of those that a mesh axis runs over, the one named last changes fastest.
Arguments:
- carried: bfloat16 [4, 512, 5120], P('section', 'peer'), may hold values from -6 to 6
- destination: int32 [4, 512, 1], P('section', 'peer'), may hold values from 0 to 63; in each aligned block of 512 rows (0 to 511, 512 to 1023, ..., all dimensions but the last counted through in order) at most 16 rows name the same one
- norm_gain: bfloat16 [4, 5120], P('section'), may hold values from 0.099609375 to 1.8984375
- w_gate: bfloat16 [4, 13824, 5120], P('section', 'peer'), may hold values from -0.078125 to 0.078125
- w_up: bfloat16 [4, 13824, 5120], P('section', 'peer'), may hold values from -0.078125 to 0.078125
- w_down: bfloat16 [4, 13824, 5120], P('section', 'peer'), may hold values from -0.0546875 to 0.0546875
Outputs:
- layer_out: bfloat16 [4, 1024, 5120], P('section', 'peer')
Inputs may be any that keep to these rules, and one draw needn't show every extreme that they name: `destination`: in each section at most 16 rows name the same peer, and in some section some peer is named by exactly 16 rows.
All inputs are finite; a program needn't handle non-finite values.
Results may differ from a plain program's by a relative error of at most 0.0048.
Values may be sent and summed in bfloat16 or wider, within the bound.
No kernel may reach another device: no remote copies, remote signals or barrier semaphores. Data moves between devices by JAX's collectives and lax.ppermute only.
A program may use at most 128 MiB of HBM per device.

v0:
```python
import jax
import jax.numpy as jnp
from jax import lax
from jax.sharding import PartitionSpec as P

SLOTS = 16


epsilon = 1e-05


def from_behind(array, axis, by):
    peers = lax.axis_size(axis)
    return lax.ppermute(array, axis, [(i, (i + by) % peers) for i in range(peers)])


def apply_layer(rows_in, gain_row, gate_mat, up_mat):
    floated = rows_in.astype(jnp.float32)
    scale = lax.rsqrt(jnp.mean(floated * floated, axis=-1, keepdims=True) + epsilon)
    normed = (floated * scale * gain_row.astype(jnp.float32)).astype(jnp.bfloat16)
    contract = (((1,), (1,)), ((), ()))
    gate_value = lax.dot_general(normed, gate_mat, contract, preferred_element_type=jnp.float32)
    up_value = lax.dot_general(normed, up_mat, contract, preferred_element_type=jnp.float32)
    return (jax.nn.silu(gate_value) * up_value).astype(jnp.bfloat16)


def body(carried, destination, norm_gain, w_gate, w_up, w_down):
    arriving = from_behind(carried[0], "section", 1)
    rows_all = lax.all_gather(arriving, "peer", axis=0, tiled=True)
    dest_all = lax.all_gather(destination[0, :, 0], "peer", axis=0, tiled=True)
    peer_count = lax.axis_size("peer")
    my_index = lax.axis_index("peer")
    total_rows = rows_all.shape[0]
    width = rows_all.shape[1]
    onehot = (dest_all[:, None] == jnp.arange(peer_count, dtype=jnp.int32)[None, :]).astype(
        jnp.int32
    )
    rank_row = jnp.sum((jnp.cumsum(onehot, axis=0) - onehot) * onehot, axis=1)
    position = dest_all * SLOTS + rank_row
    source_of = (
        jnp.full((peer_count * SLOTS,), total_rows, jnp.int32)
        .at[position]
        .set(jnp.arange(total_rows, dtype=jnp.int32))
    )
    zero_row = jnp.zeros((1, width), jnp.bfloat16)
    gain_row = norm_gain[0]
    gate_mat = w_gate[0]
    up_mat = w_up[0]
    down_mat = w_down[0]
    slot_rows = jnp.take(jnp.concatenate([rows_all, zero_row], axis=0), source_of, axis=0)
    hidden = apply_layer(slot_rows, gain_row, gate_mat, up_mat)
    summed = lax.psum_scatter(
        jnp.dot(hidden, down_mat, preferred_element_type=jnp.float32),
        "peer",
        scatter_dimension=0,
        tiled=True,
    )
    own_rows = lax.dynamic_slice_in_dim(slot_rows, my_index * SLOTS, SLOTS, 0)
    mixed = (own_rows.astype(jnp.float32) + summed).astype(jnp.bfloat16)
    return mixed[None]


def solution(mesh):
    return jax.shard_map(
        body,
        mesh=mesh,
        in_specs=(
            P("section", "peer", None),
            P("section", "peer", None),
            P("section", None),
            P("section", "peer", None),
            P("section", "peer", None),
            P("section", "peer", None),
        ),
        out_specs=P("section", "peer", None),
        check_vma=False,
    )
```

profile of v0, /device:TPU:1, one launch (start us, length us, event | category | flops | bytes accessed | tf_op | source)
XLA Modules:
  0.0 357.3 jit_solution(7558241888951947654)
XLA Ops:
  6.5 0.0 copy-start
  6.5 0.0 all-gather.3.cloned.1.call-start
  6.5 2.1 collective-permute-start
  8.7 3.5 collective-permute-done
  12.1 0.0 copy-start.2
  12.1 0.6 copy-done.2
  12.8 0.0 all-gather.3.cloned.1.call-update
  12.8 0.0 reduce-scatter.2.cloned.1.call-start
  12.9 0.8 mul.56
  13.6 1.3 dynamic-slice
  15.6 0.8 bitcast_dynamic-update-slice_fusion
  16.3 21.1 %all-reduce.1 = s32[512]{0:T(512)S(1)} all-reduce(s32[512]{0:T(512)S(1)} %bitcast_dynamic-update-slice_fusion), channel_id=2, replica_groups=mesh['section'=4,'peer'=64] {'peer'}, use_global_device_ids=true, to_apply=%add.1 | all-reduce | flops 512 | bytes 4096 | tf_op jit(solution)/shard_map/all_gather | solution.py:30
  37.4 1.2 reduce-window.6
  38.6 0.2 slice_reduce_fusion
  38.9 0.1 fusion.34
  39.0 2.6 scatter_custom_fusion
  41.7 54.5 %all-gather.3.cloned.1.call-done = bf16[512,5120]{1,0:T(8,128)(2,1)} async-done(((bf16[8,5120]{1,0:T(8,128)(2,1)}), bf16[512,5120]{1,0:T(8,128)(2,1)}) %all-gather.3.cloned.1.call-update) | async-done | bytes 5242896 | tf_op jit(solution)/shard_map/all_gather | solution.py:29
  96.2 5.4 %concatenate.3 = bf16[513,5120]{1,0:T(8,128)(2,1)} pad(bf16[512,5120]{1,0:T(8,128)(2,1)} %all-gather.3.cloned.1.call-done, bf16[]{:T(256)} %constant.18.clone.1), padding=0_1x0_0 | pad | bytes 10496002 | tf_op jit(solution)/shard_map/concatenate | solution.py:50
  101.5 21.7 %gather_fusion = bf16[1024,5120]{1,0:T(8,128)(2,1)} fusion(bf16[513,5120]{1,0:T(8,128)(2,1)} %concatenate.3, s32[1024]{0:T(1024)S(1)} %fusion.36), kind=kCustom, calls=%fused_computation | custom fusion | bytes 20975616 | tf_op jit(solution)/shard_map/jit(_take)/gather | solution.py:50
  123.3 0.0 copy-start.3
  123.3 7.5 %fusion = (f32[1024]{0:T(1024)S(1)}, bf16[1024,5120]{1,0:T(8,128)(2,1)S(1)}) fusion(bf16[1024,5120]{1,0:T(8,128)(2,1)} %gather_fusion, pred[1024]{0:T(1024)(128)(4,1)S(1)} %compare_and_fusion), kind=kLoop, calls=%fused_computation.4 | loop fusion | flops 20970496 | bytes 20976640 | tf_op jit(solution)/shard_map/reduce_sum | solution.py:19
  130.8 0.0 copy-start.1
  130.9 3.9 %copy-done.1 = bf16[1024,5120]{1,0:T(8,128)(2,1)} copy-done((bf16[1024,5120]{1,0:T(8,128)(2,1)}, bf16[1024,5120]{1,0:T(8,128)(2,1)S(1)}, u32[]{:S(2)}) %copy-start.1) | copy-done | bytes 10485784
  134.8 0.0 copy-done.3
  134.8 3.6 %fusion.5 = f32[1024,216]{0,1:T(8,128)S(1)} fusion(bf16[1024,5120]{1,0:T(8,128)(2,1)S(1)} %get-tuple-element.6, f32[5120]{0:T(1024)S(1)} %bitcast.43, f32[1024]{0:T(1024)S(1)} %add_rsqrt_fusion, bf16[1,216,5120]{2,1,0:T(8,128)(2,1)S(1)} %copy-done.3), kind=kOutput, calls=%fused_computation.9 | convolution fusion | flops 2285895680 | bytes 13606912 | tf_op jit(solution)/shard_map/dot_general | solution.py:22
  138.4 0.0 copy-done
  138.5 13.6 %fusion.7 = f32[1024,5120]{1,0:T(8,128)} fusion(bf16[1,216,5120]{2,1,0:T(8,128)(2,1)S(1)} %copy-done, bf16[1,216,5120]{2,1,0:T(8,128)(2,1)} %param.10, bf16[1024,5120]{1,0:T(8,128)(2,1)} %copy-done.1, f32[5120]{0:T(1024)S(1)} %bitcast.44, f32[1024]{0:T(1024)S(1)} %add_rsqrt_fusion, f32[1024,216]{0,1:T(8,128)S(1)} %fusion.5), kind=kOutput, calls=%fused_computation.10 | convolution fusion | flops 4552146944 | bytes 36790272 | tf_op jit(solution)/shard_map/dot_general | solution.py:53
  152.1 0.0 reduce-scatter.2.cloned.1.call-update
  152.1 196.7 %reduce-scatter.2.cloned.1.call-done = f32[16,5120]{1,0:T(8,128)} async-done(((f32[1024,5120]{1,0:T(8,128)}), f32[16,5120]{1,0:T(8,128)}) %reduce-scatter.2.cloned.1.call-update) | async-done | bytes 327696 | tf_op jit(solution)/shard_map/reduce_scatter | solution.py:52
  348.8 1.7 fusion.31
  (9 shorter events, 0.1 us)
Async XLA Ops:
  6.5 131.9 %copy-start = (bf16[1,216,5120]{2,1,0:T(8,128)(2,1)S(1)}, bf16[1,216,5120]{2,1,0:T(8,128)(2,1)}, u32[]{:S(2)}) copy-start(bf16[1,216,5120]{2,1,0:T(8,128)(2,1)} %param.11) | copy-start | bytes 6635524
  6.5 89.6 %all-gather.3.cloned.1.call-start = ((), (), s32[]{:S(2)}) async-start(), calls=%async_computation.1 | async-start | bytes 5324800 | tf_op jit(solution)/shard_map/all_gather | solution.py:29
  6.5 5.6 %collective-permute-start = (bf16[8,5120]{1,0:T(8,128)(2,1)}, bf16[8,5120]{1,0:T(8,128)(2,1)S(1)}, u32[]{:S(2)}, u32[]{:S(2)}) collective-permute-start(bf16[8,5120]{1,0:T(8,128)(2,1)} %bitcast.46), channel_id=1, source_target_pairs={{0,64},{64,128},{128,192},{192,0},{1,65},{65,129},{129,193},{193,1... | collective-permute-start | bytes 245768 | tf_op jit(solution)/shard_map/ppermute | solution.py:14
  12.1 0.6 copy-start.2
  12.8 336.0 %reduce-scatter.2.cloned.1.call-start = ((), (), s32[]{:S(2)}) async-start(), calls=%async_computation.2 | async-start | bytes 21299200 | tf_op jit(solution)/shard_map/reduce_scatter | solution.py:52
  123.3 11.5 %copy-start.3 = (bf16[1,216,5120]{2,1,0:T(8,128)(2,1)S(1)}, bf16[1,216,5120]{2,1,0:T(8,128)(2,1)}, u32[]{:S(2)}) copy-start(bf16[1,216,5120]{2,1,0:T(8,128)(2,1)} %param.9) | copy-start | bytes 6635524
  130.8 4.0 %copy-start.1 = (bf16[1024,5120]{1,0:T(8,128)(2,1)}, bf16[1024,5120]{1,0:T(8,128)(2,1)S(1)}, u32[]{:S(2)}) copy-start(bf16[1024,5120]{1,0:T(8,128)(2,1)S(1)} %get-tuple-element.6) | copy-start | bytes 31457284
Sparse Core Ops, SparseCore 0:
  12.9 83.2 all-gather.2
  152.2 196.5 reduce-scatter.1
where the time goes:
time: 361 us; the launch traced here: 357 us
  waiting for transfers between devices  255 us (71%)
  local copies, waits for them, and re-layouts  36.6 us (10%)
  blocking collectives  21.1 us (6%)
  matrix products  17.2 us (5%)
  between operations  14.2 us (4%)
  other arithmetic  11.4 us (3%)
    reduce_scatter x1, waiting for transfers between devices, body(): lax.psum_scatter(jnp.dot(hidden, down_mat, preferred_element_type=jnp.flo...  197 us
    all_gather x1, waiting for transfers between devices, body(): rows_all = lax.all_gather(arriving, 'peer', axis=0, tiled=True)  54.5 us
    gather x1, local copies, waits for them, and re-layouts, body(): jnp.take(jnp.concatenate([rows_all, zero_row], axis=0), source_of, axis=0)  21.7 us
    all_gather x1, blocking collectives, body(): dest_all = lax.all_gather(destination[0, :, 0], 'peer', axis=0, tiled=True)  21.1 us
    dot_general x1, matrix products, body(): jnp.dot(hidden, down_mat, preferred_element_type=jnp.float32)  13.6 us
    reduce_sum x1, other arithmetic, apply_layer(): jnp.mean(floated * floated, axis=-1, keepdims=True) + epsilon  7.55 us
  transfers between devices with their start and end apart: 3, of which 3 were waited for; matrix products, arithmetic and copies ran while one was open for 2% of the time, Pallas kernels for 0%

commit v1 on v0

v1 whole, which is shorter than its diff:
```python
import jax
import jax.numpy as jnp
from jax import lax
from jax.sharding import Mesh
from jax.sharding import PartitionSpec as P

SLOTS = 16
X, Z, CORES, SECTIONS = 4, 8, 2, 4
EPSILON = 1e-05
BF, F32 = jnp.bfloat16, jnp.float32


def shift(array, axis, by):
    n = lax.axis_size(axis)
    return lax.ppermute(array, axis, [(i, (i + by) % n) for i in range(n)])


def handoff(rows, by):
    pairs = [
        (s * X + x, ((s + 1) % SECTIONS) * X + (x + by) % X)
        for s in range(SECTIONS)
        for x in range(X)
    ]
    return lax.ppermute(rows, ("section", "x"), pairs)


def gather_z(block):
    up = down = block
    held = {0: block}
    for step in range(1, Z // 2 + 1):
        up = shift(up, "z", 1)
        held[step] = up
        if step < Z // 2:
            down = shift(down, "z", -1)
            held[Z - step] = down
    return [held[k] for k in range(Z)]


def add(a, b):
    return a.astype(F32) + b.astype(F32)


def in_order(array, axis, here):
    n = array.shape[axis]
    flipped = jnp.flip(array, axis)
    doubled = jnp.concatenate([flipped, flipped], axis)
    return lax.dynamic_slice_in_dim(doubled, n - 1 - here, n, axis)


def body(carried, destination, norm_gain, w_gate, w_up, w_down):
    width = carried.shape[2]
    x, z, core = lax.axis_index("x"), lax.axis_index("z"), lax.axis_index("core")
    rows_each = carried.shape[1]
    total = rows_each * X * Z * CORES
    quarter, eighth = width // X, width // (X * CORES)

    own = [w_gate[0], w_up[0], w_down[0]]
    other = [shift(w, "core", 1) for w in own]

    dest = lax.optimization_barrier(jnp.broadcast_to(destination[0], (rows_each, 128)))
    dest_all = lax.all_gather(dest, ("x", "z", "core"), axis=0, tiled=True)
    dest_all = lax.optimization_barrier(dest_all)[:, 0]
    row = jnp.arange(total, dtype=jnp.int32)
    earlier = (dest_all[:, None] == dest_all[None, :]) & (row[None, :] < row[:, None])
    rank = jnp.sum(earlier.astype(jnp.int32), axis=1)

    line = jnp.concatenate([handoff(carried[0], k) for k in range(X)], axis=0)
    rows = jnp.concatenate(gather_z(line), axis=0)

    floated = rows.astype(F32)
    scale = lax.rsqrt(jnp.mean(floated * floated, axis=-1, keepdims=True) + EPSILON)
    normed = (floated * scale * norm_gain[0].astype(F32)).astype(BF)
    contract = (((1,), (1,)), ((), ()))

    def absolute(array):
        shaped = array.reshape(Z, X, rows_each, array.shape[-1])
        shaped = in_order(in_order(shaped, 0, z), 1, x)
        return shaped.reshape(array.shape)

    def hidden_of(gate_mat, up_mat):
        gate = lax.dot_general(normed, gate_mat, contract, preferred_element_type=F32)
        up = lax.dot_general(normed, up_mat, contract, preferred_element_type=F32)
        return absolute((jax.nn.silu(gate) * up).astype(BF))

    hidden = [hidden_of(own[0], own[1]), hidden_of(other[0], other[1])]
    partial = jnp.dot(hidden[0], own[2], preferred_element_type=F32) + jnp.dot(
        hidden[1], other[2], preferred_element_type=F32
    )

    def part(k):
        return lax.dynamic_slice_in_dim(partial, lax.rem(x + k, X) * quarter, quarter, 1)

    half = quarter // 2
    far = part(2).astype(BF)
    up = shift(far[:, :half], "x", 1)
    down = shift(far[:, half:], "x", -1)
    near = part(1)
    up = jnp.concatenate([add(near[:, :half], up), near[:, half:]], 1).astype(BF)
    up = shift(up, "x", 1)
    near = part(3)
    down = jnp.concatenate([near[:, :half], add(near[:, half:], down)], 1).astype(BF)
    down = shift(down, "x", -1)
    summed = part(0) + up.astype(F32) + down.astype(F32)

    def swap(array):
        mine = lax.dynamic_slice_in_dim(array, core * eighth, eighth, 1)
        theirs = lax.dynamic_slice_in_dim(array, (1 - core) * eighth, eighth, 1)
        theirs = shift(theirs, "core", 1)
        first = jnp.where(core == 0, mine, theirs)
        second = jnp.where(core == 0, theirs, mine)
        return jnp.concatenate([first, second], 0)

    summed = swap(summed).astype(BF)
    residual = swap(absolute(lax.dynamic_slice_in_dim(rows, x * quarter, quarter, 1)))

    def by_core(per_row):
        return per_row.reshape(X, Z, CORES, rows_each).transpose(2, 1, 0, 3).reshape(total)

    dest_of, rank_of = by_core(dest_all), by_core(rank)
    slots = X * CORES * SLOTS
    dest_z = (dest_of // CORES) % Z
    slot_of = ((dest_of // (CORES * Z)) * CORES + dest_of % CORES) * SLOTS + rank_of
    slot = jnp.arange(slots, dtype=jnp.int32)

    def pick(k):
        at = lax.rem(z + k, Z)
        return ((slot_of[None, :] == slot[:, None]) & (dest_z == at)[None, :]).astype(BF)

    def slotted(k):
        return jnp.dot(pick(k), summed, preferred_element_type=F32)

    up = slotted(Z // 2)
    for k in range(Z // 2 - 1, -1, -1):
        up = shift(up.astype(BF), "z", 1)
        if k:
            up = add(slotted(k), up)
    down = slotted(Z // 2 + 1)
    for k in range(Z // 2 + 2, Z + 1):
        down = shift(down.astype(BF), "z", -1)
        if k < Z:
            down = add(slotted(k), down)
    mine = slotted(0) + jnp.dot(pick(0), residual, preferred_element_type=F32)
    mixed = (mine + up.astype(F32) + down.astype(F32)).astype(BF)

    pieces = lax.all_to_all(
        mixed.reshape(X * CORES, SLOTS, eighth), ("x", "core"), 0, 0, tiled=True
    )
    return pieces.transpose(1, 0, 2).reshape(1, SLOTS, width)


def solution(mesh):
    split = Mesh(
        mesh.devices.reshape(SECTIONS, X, Z, CORES), ("section", "x", "z", "core")
    )
    peers = ("x", "z", "core")
    return jax.shard_map(
        body,
        mesh=split,
        in_specs=(
            P("section", peers, None),
            P("section", peers, None),
            P("section", None),
            P("section", peers, None),
            P("section", peers, None),
            P("section", peers, None),
        ),
        out_specs=P("section", peers, None),
        check_vma=False,
    )
```

time: 361 us -> 185 us (0.51)
  waiting for transfers between devices: 255 us -> 51.7 us
  starting transfers between devices: 2.17 us -> 44.9 us
  blocking collectives: 21.1 us -> 58.9 us
  local copies, waits for them, and re-layouts: 36.6 us -> 5.91 us
  between operations: 14.2 us -> 0.57 us
  other arithmetic: 11.4 us -> 6.68 us
    reduce_scatter x1 -> x0, waiting for transfers between devices: 197 us -> none  [body(): lax.psum_scatter(jnp.dot(hidden, down_mat, preferred_element_type=jnp.flo...]
    all_gather x1 -> x0, waiting for transfers between devices: 54.5 us -> none  [body(): rows_all = lax.all_gather(arriving, 'peer', axis=0, tiled=True)]
    ppermute x1 -> x27, waiting for transfers between devices: 3.48 us -> 51.7 us  [the longest x23 51.7 us: shift(): return lax.ppermute(array, axis, [(i, (i + by) % n) for i in range(n)])]
    ppermute x1 -> x27, starting transfers between devices: 2.13 us -> 44.9 us  [the longest x23 36.5 us: shift(): return lax.ppermute(array, axis, [(i, (i + by) % n) for i in range(n)])]
    all_gather x1, blocking collectives: 21.1 us -> 46.6 us  [body(): dest_all = lax.all_gather(dest, ('x', 'z', 'core'), axis=0, tiled=True)]
    gather x1 -> x0, local copies, waits for them, and re-layouts: 21.7 us -> none  [body(): jnp.take(jnp.concatenate([rows_all, zero_row], axis=0), source_of, axis=0)]
    all_to_all x0 -> x1, blocking collectives: none -> 12.4 us  [body(): lax.all_to_all(mixed.reshape(X * CORES, SLOTS, eighth), ('x', 'core'), 0,...]
    reduce_sum x2, other arithmetic: 7.67 us -> 0.85 us  [the longest x1 0.6 us: body(): jnp.mean(floated * floated, axis=-1, keepdims=True) + EPSILON]
  transfers between devices with their start and end apart: 3 -> 27, of which waited for: 3 -> 12; matrix products, arithmetic and copies ran while one was open for 2% -> 12% of each run, Pallas kernels for 0% -> 0%
where the time goes in v1:
time: 185 us; the launch traced here: 184 us
  blocking collectives  58.9 us (32%)
  waiting for transfers between devices  51.7 us (28%)
  starting transfers between devices  44.9 us (24%)
  matrix products  15.6 us (8%)
  other arithmetic  6.68 us (4%)
  local copies, waits for them, and re-layouts  5.91 us (3%)
    ppermute x23, waiting for transfers between devices, shift(): return lax.ppermute(array, axis, [(i, (i + by) % n) for i in range(n)])  51.7 us
    all_gather x1, blocking collectives, body(): dest_all = lax.all_gather(dest, ('x', 'z', 'core'), axis=0, tiled=True)  46.6 us
    ppermute x23, starting transfers between devices, shift(): return lax.ppermute(array, axis, [(i, (i + by) % n) for i in range(n)])  36.5 us
    all_to_all x1, blocking collectives, body(): lax.all_to_all(mixed.reshape(X * CORES, SLOTS, eighth), ('x', 'core'), 0,...  12.4 us
    ppermute x4, starting transfers between devices, handoff(): return lax.ppermute(rows, ('section', 'x'), pairs)  8.39 us
    dot_general x2, matrix products, hidden_of(): up = lax.dot_general(normed, up_mat, contract, preferred_element_type=F32)  4.02 us
    dot_general x2, matrix products, hidden_of(): lax.dot_general(normed, gate_mat, contract, preferred_element_type=F32)  4.01 us
  transfers between devices with their start and end apart: 27, of which 12 were waited for; matrix products, arithmetic and copies ran while one was open for 12% of the time, Pallas kernels for 0%

profile of v1, /device:TPU:1, one launch (start us, length us, event | category | flops | bytes accessed | tf_op | source)
XLA Modules:
  0.0 184.3 jit_solution(15952883772967988268)
XLA Ops:
  0.0 2.1 %collective-permute-start = (bf16[8,5120]{1,0:T(8,128)(2,1)}, bf16[8,5120]{1,0:T(8,128)(2,1)S(1)}, u32[]{:S(2)}, u32[]{:S(2)}) collective-permute-start(bf16[8,5120]{1,0:T(8,128)(2,1)} %bitcast.48), channel_id=1, source_target_pairs={{0,64},{16,80},{32,96},{48,112},{64,128},{80,144},{96,160},{112,17... | collective-permute-start | bytes 245768 | tf_op jit(solution)/shard_map/ppermute | solution.py:24
  2.1 2.2 %collective-permute-start.1 = (bf16[8,5120]{1,0:T(8,128)(2,1)}, bf16[8,5120]{1,0:T(8,128)(2,1)S(1)}, u32[]{:S(2)}, u32[]{:S(2)}) collective-permute-start(bf16[8,5120]{1,0:T(8,128)(2,1)} %bitcast.49), channel_id=1, source_target_pairs={{0,80},{16,96},{32,112},{48,64},{64,144},{80,160},{96,176},{112,12... | collective-permute-start | bytes 245768 | tf_op jit(solution)/shard_map/ppermute | solution.py:24
  4.4 3.2 %collective-permute-start.2 = (bf16[8,5120]{1,0:T(8,128)(2,1)}, bf16[8,5120]{1,0:T(8,128)(2,1)S(1)}, u32[]{:S(2)}, u32[]{:S(2)}) collective-permute-start(bf16[8,5120]{1,0:T(8,128)(2,1)} %bitcast.50), channel_id=1, source_target_pairs={{0,96},{16,112},{32,64},{48,80},{64,160},{80,176},{96,128},{112,14... | collective-permute-start | bytes 245768 | tf_op jit(solution)/shard_map/ppermute | solution.py:24
  7.5 0.9 collective-permute-start.3
  8.4 1.7 collective-permute-start.11
  10.1 0.7 broadcast_in_dim.5
  10.9 46.6 %all_gather.3 = s32[512,128]{1,0:T(8,128)S(1)} all-gather(s32[8,128]{1,0:T(8,128)S(1)} %broadcast_in_dim.5), channel_id=1, replica_groups=mesh['section'=4,'x'=4,'z'=8,'core'=2] {'x','z','core'}, dimensions={0}, use_global_device_ids=true | all-gather | bytes 266240 | tf_op jit(solution)/shard_map/all_gather | solution.py:61
  57.9 0.6 constant_dynamic-update-slice_fusion.3
  58.6 0.3 collective-permute-start.13
  58.9 0.6 constant_dynamic-update-slice_fusion.2
  59.6 0.6 constant_dynamic-update-slice_fusion.1
  60.2 0.6 constant_dynamic-update-slice_fusion
  60.9 2.7 %collective-permute-start.8 = (bf16[32,5120]{1,0:T(8,128)(2,1)}, bf16[32,5120]{1,0:T(8,128)(2,1)S(1)}, u32[]{:S(2)}, u32[]{:S(2)}) collective-permute-start(bf16[32,5120]{1,0:T(8,128)(2,1)} %get-tuple-element.17), channel_id=1, source_target_pairs={{0,14},{2,0},{4,2},{6,4},{8,6},{10,8},{12,10},{14,12},{1,15},{3,1}... | collective-permute-start | bytes 983048 | tf_op jit(solution)/shard_map/ppermute | solution.py:15
  64.2 0.8 mul.99
  65.0 6.5 %collective-permute-done.4 = bf16[32,5120]{1,0:T(8,128)(2,1)S(1)} collective-permute-done((bf16[32,5120]{1,0:T(8,128)(2,1)}, bf16[32,5120]{1,0:T(8,128)(2,1)S(1)}, u32[]{:S(2)}, u32[]{:S(2)}) %collective-permute-start.4) | collective-permute-done | bytes 327712 | tf_op jit(solution)/shard_map/ppermute | solution.py:15
  71.4 2.7 %collective-permute-start.9 = (bf16[32,5120]{1,0:T(8,128)(2,1)S(1)}, bf16[32,5120]{1,0:T(8,128)(2,1)S(1)}, u32[]{:S(2)}, u32[]{:S(2)}) collective-permute-start(bf16[32,5120]{1,0:T(8,128)(2,1)S(1)} %collective-permute-done.8), channel_id=1, source_target_pairs={{0,14},{2,0},{4,2},{6,4},{8,6},{10,8},{12,10},{14,12},{1,15},{3,1}... | collective-permute-start | bytes 983048 | tf_op jit(solution)/shard_map/ppermute | solution.py:15
  74.1 6.7 %collective-permute-done.5 = bf16[32,5120]{1,0:T(8,128)(2,1)S(1)} collective-permute-done((bf16[32,5120]{1,0:T(8,128)(2,1)S(1)}, bf16[32,5120]{1,0:T(8,128)(2,1)S(1)}, u32[]{:S(2)}, u32[]{:S(2)}) %collective-permute-start.5) | collective-permute-done | bytes 327712 | tf_op jit(solution)/shard_map/ppermute | solution.py:15
  80.9 2.7 %collective-permute-start.10 = (bf16[32,5120]{1,0:T(8,128)(2,1)S(1)}, bf16[32,5120]{1,0:T(8,128)(2,1)S(1)}, u32[]{:S(2)}, u32[]{:S(2)}) collective-permute-start(bf16[32,5120]{1,0:T(8,128)(2,1)S(1)} %collective-permute-done.9), channel_id=1, source_target_pairs={{0,14},{2,0},{4,2},{6,4},{8,6},{10,8},{12,10},{14,12},{1,15},{3,1}... | collective-permute-start | bytes 983048 | tf_op jit(solution)/shard_map/ppermute | solution.py:15
  83.6 5.8 %collective-permute-done.6 = bf16[32,5120]{1,0:T(8,128)(2,1)S(1)} collective-permute-done((bf16[32,5120]{1,0:T(8,128)(2,1)S(1)}, bf16[32,5120]{1,0:T(8,128)(2,1)S(1)}, u32[]{:S(2)}, u32[]{:S(2)}) %collective-permute-start.6) | collective-permute-done | bytes 327712 | tf_op jit(solution)/shard_map/ppermute | solution.py:15
  89.4 7.6 %collective-permute-done.7 = bf16[32,5120]{1,0:T(8,128)(2,1)S(1)} collective-permute-done((bf16[32,5120]{1,0:T(8,128)(2,1)S(1)}, bf16[32,5120]{1,0:T(8,128)(2,1)S(1)}, u32[]{:S(2)}, u32[]{:S(2)}) %collective-permute-start.7) | collective-permute-done | bytes 327712 | tf_op jit(solution)/shard_map/ppermute | solution.py:15
  97.1 0.6 fusion
  97.8 1.2 fusion.73
  99.0 0.4 copy-done.2
  99.4 1.2 multiply_convert_fusion.1
  100.8 2.8 %fusion.77 = f32[256,216]{0,1:T(8,128)S(1)} fusion(bf16[216,5120]{1,0:T(8,128)(2,1)} %collective-permute-done.11, bf16[256,5120]{1,0:T(8,128)(2,1)S(1)} %constant_dynamic-update-slice_fusion.4, f32[5120]{0:T(1024)S(1)} %bitcast.43, f32[256]{0:T(256)S(1)} %add_rsqrt_fusion), kind=kOutput, calls=%fused_computation.146 | convolution fusion | flops 571473920 | bytes 5075968 | tf_op jit(solution)/shard_map/dot_general | solution.py:81
  103.6 2.8 %multiply_convert_fusion = bf16[256,216]{0,1:T(8,128)(2,1)S(1)} fusion(f32[256,216]{0,1:T(8,128)S(1)} %fusion.77, bf16[216,5120]{1,0:T(8,128)(2,1)} %collective-permute-done.12, bf16[256,5120]{1,0:T(8,128)(2,1)S(1)} %constant_dynamic-update-slice_fusion.4, f32[5120]{0:T(1024)S(1)} %bitcast.44, f32[256]{0:T(256)S(1)} %add_rsqrt_fusion), kind=kOutput, calls=%fused_computation.68 | convolution fusion | flops 571805696 | bytes 5186560 | tf_op jit(solution)/shard_map/dot_general | solution.py:82
  106.8 2.5 %fusion.67 = f32[256,5120]{1,0:T(8,128)S(1)} fusion(bf16[256,216]{1,0:T(8,128)(2,1)S(1)} %bitcast.37, bf16[1,216,5120]{2,1,0:T(8,128)(2,1)} %param.11), kind=kOutput, calls=%fused_computation.139 | convolution fusion | flops 566231040 | bytes 7565312 | tf_op jit(solution)/shard_map/dot_general | solution.py:86
  109.3 2.6 %convolution_add_fusion = f32[256,5120]{1,0:T(8,128)S(1)} fusion(f32[256,5120]{1,0:T(8,128)S(1)} %fusion.67, bf16[256,216]{1,0:T(8,128)(2,1)S(1)} %bitcast.34, bf16[216,5120]{1,0:T(8,128)(2,1)} %collective-permute-done.13), kind=kOutput, calls=%fused_computation | convolution fusion | flops 567541760 | bytes 12808192 | tf_op jit(solution)/shard_map/dot_general | solution.py:86
  112.2 2.7 %collective-permute-start.16 = (bf16[256,640]{1,0:T(8,128)(2,1)S(1)}, bf16[256,640]{1,0:T(8,128)(2,1)S(1)}, u32[]{:S(2)}, u32[]{:S(2)}) collective-permute-start(bf16[256,640]{1,0:T(8,128)(2,1)S(1)} %get-tuple-element.16), channel_id=1, source_target_pairs={{0,48},{16,0},{32,16},{48,32},{1,49},{17,1},{33,17},{49,33},{2,50}... | collective-permute-start | bytes 983048 | tf_op jit(solution)/shard_map/ppermute | solution.py:15
  115.0 4.3 %collective-permute-done.14 = bf16[256,640]{1,0:T(8,128)(2,1)S(1)} collective-permute-done((bf16[256,640]{1,0:T(8,128)(2,1)S(1)}, bf16[256,640]{1,0:T(8,128)(2,1)S(1)}, u32[]{:S(2)}, u32[]{:S(2)}) %collective-permute-start.14) | collective-permute-done | bytes 327712 | tf_op jit(solution)/shard_map/ppermute | solution.py:15
  119.5 0.9 pad_maximum_fusion.1
  120.4 2.7 %collective-permute-start.17 = (bf16[256,1280]{1,0:T(8,128)(2,1)}, bf16[256,1280]{1,0:T(8,128)(2,1)}, u32[]{:S(2)}, u32[]{:S(2)}) collective-permute-start(bf16[256,1280]{1,0:T(8,128)(2,1)} %pad_maximum_fusion.1), channel_id=1, source_target_pairs={{0,48},{16,0},{32,16},{48,32},{1,49},{17,1},{33,17},{49,33},{2,50}... | collective-permute-start | bytes 1966088 | tf_op jit(solution)/shard_map/ppermute | solution.py:15
  123.1 0.9 pad_maximum_fusion
  124.7 5.5 %collective-permute-start.19 = (bf16[256,640]{1,0:T(8,128)(2,1)S(1)}, bf16[256,640]{1,0:T(8,128)(2,1)S(1)}, u32[]{:S(2)}, u32[]{:S(2)}) collective-permute-start(bf16[256,640]{1,0:T(8,128)(2,1)S(1)} %constant_dynamic-slice_fusion), channel_id=1, source_target_pairs={{0,1},{1,0},{2,3},{3,2},{4,5},{5,4},{6,7},{7,6},{8,9},{9,8},{10,11... | collective-permute-start | bytes 983048 | tf_op jit(solution)/shard_map/ppermute | solution.py:15
  130.2 2.0 %collective-permute-done.17 = bf16[256,1280]{1,0:T(8,128)(2,1)} collective-permute-done((bf16[256,1280]{1,0:T(8,128)(2,1)}, bf16[256,1280]{1,0:T(8,128)(2,1)}, u32[]{:S(2)}, u32[]{:S(2)}) %collective-permute-start.17) | collective-permute-done | bytes 655392 | tf_op jit(solution)/shard_map/ppermute | solution.py:15
  132.2 4.0 %collective-permute-done.15 = bf16[256,1280]{1,0:T(8,128)(2,1)} collective-permute-done((bf16[256,1280]{1,0:T(8,128)(2,1)}, bf16[256,1280]{1,0:T(8,128)(2,1)}, u32[]{:S(2)}, u32[]{:S(2)}) %collective-permute-start.15) | collective-permute-done | bytes 655392 | tf_op jit(solution)/shard_map/ppermute | solution.py:15
  136.3 1.9 %convert_add_fusion = bf16[256,1280]{1,0:T(8,128)(2,1)S(1)} fusion(bf16[256,1280]{1,0:T(8,128)(2,1)} %collective-permute-done.17, bf16[256,1280]{1,0:T(8,128)(2,1)} %collective-permute-done.15, f32[256,5120]{1,0:T(8,128)} %copy-done, s32[]{:T(128)S(6)} %select_n.139), kind=kLoop, calls=%fused_computation.10 | loop fusion | flops 1638400 | bytes 3276804 | tf_op jit(solution)/shard_map/add | solution.py:103
  138.2 6.7 %collective-permute-start.18 = (bf16[256,640]{1,0:T(8,128)(2,1)S(1)}, bf16[256,640]{1,0:T(8,128)(2,1)S(1)}, u32[]{:S(2)}, u32[]{:S(2)}) collective-permute-start(bf16[256,640]{1,0:T(8,128)(2,1)S(1)} %constant_dynamic-slice_fusion.2), channel_id=1, source_target_pairs={{0,1},{1,0},{2,3},{3,2},{4,5},{5,4},{6,7},{7,6},{8,9},{9,8},{10,11... | collective-permute-start | bytes 983048 | tf_op jit(solution)/shard_map/ppermute | solution.py:15
  145.1 1.1 collective-permute-done.18
  147.0 2.7 %collective-permute-start.24 = (bf16[128,640]{1,0:T(8,128)(2,1)S(1)}, bf16[128,640]{1,0:T(8,128)(2,1)S(1)}, u32[]{:S(2)}, u32[]{:S(2)}) collective-permute-start(bf16[128,640]{1,0:T(8,128)(2,1)S(1)} %convolution_convert_fusion), channel_id=1, source_target_pairs={{0,14},{2,0},{4,2},{6,4},{8,6},{10,8},{12,10},{14,12},{1,15},{3,1}... | collective-permute-start | bytes 491528 | tf_op jit(solution)/shard_map/ppermute | solution.py:15
  149.7 3.6 %collective-permute-done.20 = bf16[128,640]{1,0:T(8,128)(2,1)S(1)} collective-permute-done((bf16[128,640]{1,0:T(8,128)(2,1)S(1)}, bf16[128,640]{1,0:T(8,128)(2,1)S(1)}, u32[]{:S(2)}, u32[]{:S(2)}) %collective-permute-start.20) | collective-permute-done | bytes 163872 | tf_op jit(solution)/shard_map/ppermute | solution.py:15
  154.0 2.7 %collective-permute-start.25 = (bf16[128,640]{1,0:T(8,128)(2,1)S(1)}, bf16[128,640]{1,0:T(8,128)(2,1)S(1)}, u32[]{:S(2)}, u32[]{:S(2)}) collective-permute-start(bf16[128,640]{1,0:T(8,128)(2,1)S(1)} %fusion.9), channel_id=1, source_target_pairs={{0,14},{2,0},{4,2},{6,4},{8,6},{10,8},{12,10},{14,12},{1,15},{3,1}... | collective-permute-start | bytes 491528 | tf_op jit(solution)/shard_map/ppermute | solution.py:15
  156.7 2.7 %collective-permute-done.21 = bf16[128,640]{1,0:T(8,128)(2,1)S(1)} collective-permute-done((bf16[128,640]{1,0:T(8,128)(2,1)S(1)}, bf16[128,640]{1,0:T(8,128)(2,1)S(1)}, u32[]{:S(2)}, u32[]{:S(2)}) %collective-permute-start.21) | collective-permute-done | bytes 163872 | tf_op jit(solution)/shard_map/ppermute | solution.py:15
  160.1 2.7 %collective-permute-start.26 = (bf16[128,640]{1,0:T(8,128)(2,1)S(1)}, bf16[128,640]{1,0:T(8,128)(2,1)S(1)}, u32[]{:S(2)}, u32[]{:S(2)}) collective-permute-start(bf16[128,640]{1,0:T(8,128)(2,1)S(1)} %fusion.8), channel_id=1, source_target_pairs={{0,14},{2,0},{4,2},{6,4},{8,6},{10,8},{12,10},{14,12},{1,15},{3,1}... | collective-permute-start | bytes 491528 | tf_op jit(solution)/shard_map/ppermute | solution.py:15
  162.8 2.3 %collective-permute-done.22 = bf16[128,640]{1,0:T(8,128)(2,1)S(1)} collective-permute-done((bf16[128,640]{1,0:T(8,128)(2,1)S(1)}, bf16[128,640]{1,0:T(8,128)(2,1)S(1)}, u32[]{:S(2)}, u32[]{:S(2)}) %collective-permute-start.22) | collective-permute-done | bytes 163872 | tf_op jit(solution)/shard_map/ppermute | solution.py:15
  165.8 5.1 %collective-permute-done.23 = bf16[128,640]{1,0:T(8,128)(2,1)S(1)} collective-permute-done((bf16[128,640]{1,0:T(8,128)(2,1)S(1)}, bf16[128,640]{1,0:T(8,128)(2,1)S(1)}, u32[]{:S(2)}, u32[]{:S(2)}) %collective-permute-start.23) | collective-permute-done | bytes 163872 | tf_op jit(solution)/shard_map/ppermute | solution.py:15
  171.2 12.4 %all_to_all.5 = bf16[8,16,640]{2,1,0:T(8,128)(2,1)S(1)} all-to-all(bf16[8,16,640]{2,1,0:T(8,128)(2,1)S(1)} %bitcast.38), channel_id=1, replica_groups=mesh['section'=4,'x'=4,'z'=8,'core'=2] {'x','core'}, dimensions={0} | all-to-all | bytes 327680 | tf_op jit(solution)/shard_map/all_to_all | solution.py:145
  183.6 0.7 reshape.210
  (82 shorter events, 6.3 us)
Async XLA Ops:
  0.0 57.7 %collective-permute-start = (bf16[8,5120]{1,0:T(8,128)(2,1)}, bf16[8,5120]{1,0:T(8,128)(2,1)S(1)}, u32[]{:S(2)}, u32[]{:S(2)}) collective-permute-start(bf16[8,5120]{1,0:T(8,128)(2,1)} %bitcast.48), channel_id=1, source_target_pairs={{0,64},{16,80},{32,96},{48,112},{64,128},{80,144},{96,160},{112,17... | collective-permute-start | bytes 245768 | tf_op jit(solution)/shard_map/ppermute | solution.py:24
  2.1 56.5 %collective-permute-start.1 = (bf16[8,5120]{1,0:T(8,128)(2,1)}, bf16[8,5120]{1,0:T(8,128)(2,1)S(1)}, u32[]{:S(2)}, u32[]{:S(2)}) collective-permute-start(bf16[8,5120]{1,0:T(8,128)(2,1)} %bitcast.49), channel_id=1, source_target_pairs={{0,80},{16,96},{32,112},{48,64},{64,144},{80,160},{96,176},{112,12... | collective-permute-start | bytes 245768 | tf_op jit(solution)/shard_map/ppermute | solution.py:24
  4.4 55.2 %collective-permute-start.2 = (bf16[8,5120]{1,0:T(8,128)(2,1)}, bf16[8,5120]{1,0:T(8,128)(2,1)S(1)}, u32[]{:S(2)}, u32[]{:S(2)}) collective-permute-start(bf16[8,5120]{1,0:T(8,128)(2,1)} %bitcast.50), channel_id=1, source_target_pairs={{0,96},{16,112},{32,64},{48,80},{64,160},{80,176},{96,128},{112,14... | collective-permute-start | bytes 245768 | tf_op jit(solution)/shard_map/ppermute | solution.py:24
  7.5 52.7 %collective-permute-start.3 = (bf16[8,5120]{1,0:T(8,128)(2,1)}, bf16[8,5120]{1,0:T(8,128)(2,1)S(1)}, u32[]{:S(2)}, u32[]{:S(2)}) collective-permute-start(bf16[8,5120]{1,0:T(8,128)(2,1)} %bitcast.51), channel_id=1, source_target_pairs={{0,112},{16,64},{32,80},{48,96},{64,176},{80,128},{96,144},{112,16... | collective-permute-start | bytes 245768 | tf_op jit(solution)/shard_map/ppermute | solution.py:24
  8.4 92.4 %collective-permute-start.11 = (bf16[216,5120]{1,0:T(8,128)(2,1)}, bf16[216,5120]{1,0:T(8,128)(2,1)}, u32[]{:S(2)}, u32[]{:S(2)}) collective-permute-start(bf16[216,5120]{1,0:T(8,128)(2,1)} %bitcast.46), channel_id=1, source_target_pairs={{0,1},{1,0},{2,3},{3,2},{4,5},{5,4},{6,7},{7,6},{8,9},{9,8},{10,11... | collective-permute-start | bytes 6635528 | tf_op jit(solution)/shard_map/ppermute | solution.py:15
  57.7 45.9 %collective-permute-start.12 = (bf16[216,5120]{1,0:T(8,128)(2,1)}, bf16[216,5120]{1,0:T(8,128)(2,1)}, u32[]{:S(2)}, u32[]{:S(2)}) collective-permute-start(bf16[216,5120]{1,0:T(8,128)(2,1)} %bitcast.47), channel_id=1, source_target_pairs={{0,1},{1,0},{2,3},{3,2},{4,5},{5,4},{6,7},{7,6},{8,9},{9,8},{10,11... | collective-permute-start | bytes 6635528 | tf_op jit(solution)/shard_map/ppermute | solution.py:15
  58.6 50.7 %collective-permute-start.13 = (bf16[216,5120]{1,0:T(8,128)(2,1)}, bf16[216,5120]{1,0:T(8,128)(2,1)}, u32[]{:S(2)}, u32[]{:S(2)}) collective-permute-start(bf16[216,5120]{1,0:T(8,128)(2,1)} %bitcast.32), channel_id=1, source_target_pairs={{0,1},{1,0},{2,3},{3,2},{4,5},{5,4},{6,7},{7,6},{8,9},{9,8},{10,11... | collective-permute-start | bytes 6635528 | tf_op jit(solution)/shard_map/ppermute | solution.py:15
  60.9 10.6 %collective-permute-start.4 = (bf16[32,5120]{1,0:T(8,128)(2,1)}, bf16[32,5120]{1,0:T(8,128)(2,1)S(1)}, u32[]{:S(2)}, u32[]{:S(2)}) collective-permute-start(bf16[32,5120]{1,0:T(8,128)(2,1)} %get-tuple-element.17), channel_id=1, source_target_pairs={{0,2},{2,4},{4,6},{6,8},{8,10},{10,12},{12,14},{14,0},{1,3},{3,5},... | collective-permute-start | bytes 983048 | tf_op jit(solution)/shard_map/ppermute | solution.py:15
  60.9 10.6 %collective-permute-start.8 = (bf16[32,5120]{1,0:T(8,128)(2,1)}, bf16[32,5120]{1,0:T(8,128)(2,1)S(1)}, u32[]{:S(2)}, u32[]{:S(2)}) collective-permute-start(bf16[32,5120]{1,0:T(8,128)(2,1)} %get-tuple-element.17), channel_id=1, source_target_pairs={{0,14},{2,0},{4,2},{6,4},{8,6},{10,8},{12,10},{14,12},{1,15},{3,1}... | collective-permute-start | bytes 983048 | tf_op jit(solution)/shard_map/ppermute | solution.py:15
  71.4 9.4 %collective-permute-start.5 = (bf16[32,5120]{1,0:T(8,128)(2,1)S(1)}, bf16[32,5120]{1,0:T(8,128)(2,1)S(1)}, u32[]{:S(2)}, u32[]{:S(2)}) collective-permute-start(bf16[32,5120]{1,0:T(8,128)(2,1)S(1)} %collective-permute-done.4), channel_id=1, source_target_pairs={{0,2},{2,4},{4,6},{6,8},{8,10},{10,12},{12,14},{14,0},{1,3},{3,5},... | collective-permute-start | bytes 983048 | tf_op jit(solution)/shard_map/ppermute | solution.py:15
  71.4 9.4 %collective-permute-start.9 = (bf16[32,5120]{1,0:T(8,128)(2,1)S(1)}, bf16[32,5120]{1,0:T(8,128)(2,1)S(1)}, u32[]{:S(2)}, u32[]{:S(2)}) collective-permute-start(bf16[32,5120]{1,0:T(8,128)(2,1)S(1)} %collective-permute-done.8), channel_id=1, source_target_pairs={{0,14},{2,0},{4,2},{6,4},{8,6},{10,8},{12,10},{14,12},{1,15},{3,1}... | collective-permute-start | bytes 983048 | tf_op jit(solution)/shard_map/ppermute | solution.py:15
  80.9 8.5 %collective-permute-start.6 = (bf16[32,5120]{1,0:T(8,128)(2,1)S(1)}, bf16[32,5120]{1,0:T(8,128)(2,1)S(1)}, u32[]{:S(2)}, u32[]{:S(2)}) collective-permute-start(bf16[32,5120]{1,0:T(8,128)(2,1)S(1)} %collective-permute-done.5), channel_id=1, source_target_pairs={{0,2},{2,4},{4,6},{6,8},{8,10},{10,12},{12,14},{14,0},{1,3},{3,5},... | collective-permute-start | bytes 983048 | tf_op jit(solution)/shard_map/ppermute | solution.py:15
  80.9 16.1 %collective-permute-start.10 = (bf16[32,5120]{1,0:T(8,128)(2,1)S(1)}, bf16[32,5120]{1,0:T(8,128)(2,1)S(1)}, u32[]{:S(2)}, u32[]{:S(2)}) collective-permute-start(bf16[32,5120]{1,0:T(8,128)(2,1)S(1)} %collective-permute-done.9), channel_id=1, source_target_pairs={{0,14},{2,0},{4,2},{6,4},{8,6},{10,8},{12,10},{14,12},{1,15},{3,1}... | collective-permute-start | bytes 983048 | tf_op jit(solution)/shard_map/ppermute | solution.py:15
  89.4 7.6 %collective-permute-start.7 = (bf16[32,5120]{1,0:T(8,128)(2,1)S(1)}, bf16[32,5120]{1,0:T(8,128)(2,1)S(1)}, u32[]{:S(2)}, u32[]{:S(2)}) collective-permute-start(bf16[32,5120]{1,0:T(8,128)(2,1)S(1)} %collective-permute-done.6), channel_id=1, source_target_pairs={{0,2},{2,4},{4,6},{6,8},{8,10},{10,12},{12,14},{14,0},{1,3},{3,5},... | collective-permute-start | bytes 983048 | tf_op jit(solution)/shard_map/ppermute | solution.py:15
  89.4 8.3 %copy-start.1 = (bf16[1,216,5120]{2,1,0:T(8,128)(2,1)S(1)}, bf16[1,216,5120]{2,1,0:T(8,128)(2,1)}, u32[]{:S(2)}) copy-start(bf16[1,216,5120]{2,1,0:T(8,128)(2,1)} %param.9) | copy-start | bytes 6635524
  97.8 1.6 copy-start.2
  111.9 7.6 %copy-start = (f32[256,5120]{1,0:T(8,128)}, f32[256,5120]{1,0:T(8,128)S(1)}, u32[]{:S(2)}) copy-start(f32[256,5120]{1,0:T(8,128)S(1)} %convolution_add_fusion) | copy-start | bytes 15728644
  112.1 7.2 %collective-permute-start.14 = (bf16[256,640]{1,0:T(8,128)(2,1)S(1)}, bf16[256,640]{1,0:T(8,128)(2,1)S(1)}, u32[]{:S(2)}, u32[]{:S(2)}) collective-permute-start(bf16[256,640]{1,0:T(8,128)(2,1)S(1)} %get-tuple-element.15), channel_id=1, source_target_pairs={{0,16},{16,32},{32,48},{48,0},{1,17},{17,33},{33,49},{49,1},{2,18}... | collective-permute-start | bytes 983048 | tf_op jit(solution)/shard_map/ppermute | solution.py:15
  112.2 7.1 %collective-permute-start.16 = (bf16[256,640]{1,0:T(8,128)(2,1)S(1)}, bf16[256,640]{1,0:T(8,128)(2,1)S(1)}, u32[]{:S(2)}, u32[]{:S(2)}) collective-permute-start(bf16[256,640]{1,0:T(8,128)(2,1)S(1)} %get-tuple-element.16), channel_id=1, source_target_pairs={{0,48},{16,0},{32,16},{48,32},{1,49},{17,1},{33,17},{49,33},{2,50}... | collective-permute-start | bytes 983048 | tf_op jit(solution)/shard_map/ppermute | solution.py:15
  120.4 11.9 %collective-permute-start.17 = (bf16[256,1280]{1,0:T(8,128)(2,1)}, bf16[256,1280]{1,0:T(8,128)(2,1)}, u32[]{:S(2)}, u32[]{:S(2)}) collective-permute-start(bf16[256,1280]{1,0:T(8,128)(2,1)} %pad_maximum_fusion.1), channel_id=1, source_target_pairs={{0,48},{16,0},{32,16},{48,32},{1,49},{17,1},{33,17},{49,33},{2,50}... | collective-permute-start | bytes 1966088 | tf_op jit(solution)/shard_map/ppermute | solution.py:15
  124.0 12.3 %collective-permute-start.15 = (bf16[256,1280]{1,0:T(8,128)(2,1)}, bf16[256,1280]{1,0:T(8,128)(2,1)}, u32[]{:S(2)}, u32[]{:S(2)}) collective-permute-start(bf16[256,1280]{1,0:T(8,128)(2,1)} %pad_maximum_fusion), channel_id=1, source_target_pairs={{0,16},{16,32},{32,48},{48,0},{1,17},{17,33},{33,49},{49,1},{2,18}... | collective-permute-start | bytes 1966088 | tf_op jit(solution)/shard_map/ppermute | solution.py:15
  124.7 20.2 %collective-permute-start.19 = (bf16[256,640]{1,0:T(8,128)(2,1)S(1)}, bf16[256,640]{1,0:T(8,128)(2,1)S(1)}, u32[]{:S(2)}, u32[]{:S(2)}) collective-permute-start(bf16[256,640]{1,0:T(8,128)(2,1)S(1)} %constant_dynamic-slice_fusion), channel_id=1, source_target_pairs={{0,1},{1,0},{2,3},{3,2},{4,5},{5,4},{6,7},{7,6},{8,9},{9,8},{10,11... | collective-permute-start | bytes 983048 | tf_op jit(solution)/shard_map/ppermute | solution.py:15
  138.2 7.9 %collective-permute-start.18 = (bf16[256,640]{1,0:T(8,128)(2,1)S(1)}, bf16[256,640]{1,0:T(8,128)(2,1)S(1)}, u32[]{:S(2)}, u32[]{:S(2)}) collective-permute-start(bf16[256,640]{1,0:T(8,128)(2,1)S(1)} %constant_dynamic-slice_fusion.2), channel_id=1, source_target_pairs={{0,1},{1,0},{2,3},{3,2},{4,5},{5,4},{6,7},{7,6},{8,9},{9,8},{10,11... | collective-permute-start | bytes 983048 | tf_op jit(solution)/shard_map/ppermute | solution.py:15
  146.6 6.7 %collective-permute-start.20 = (bf16[128,640]{1,0:T(8,128)(2,1)S(1)}, bf16[128,640]{1,0:T(8,128)(2,1)S(1)}, u32[]{:S(2)}, u32[]{:S(2)}) collective-permute-start(bf16[128,640]{1,0:T(8,128)(2,1)S(1)} %convolution_convert_fusion.1), channel_id=1, source_target_pairs={{0,2},{2,4},{4,6},{6,8},{8,10},{10,12},{12,14},{14,0},{1,3},{3,5},... | collective-permute-start | bytes 491528 | tf_op jit(solution)/shard_map/ppermute | solution.py:15
  147.0 6.7 %collective-permute-start.24 = (bf16[128,640]{1,0:T(8,128)(2,1)S(1)}, bf16[128,640]{1,0:T(8,128)(2,1)S(1)}, u32[]{:S(2)}, u32[]{:S(2)}) collective-permute-start(bf16[128,640]{1,0:T(8,128)(2,1)S(1)} %convolution_convert_fusion), channel_id=1, source_target_pairs={{0,14},{2,0},{4,2},{6,4},{8,6},{10,8},{12,10},{14,12},{1,15},{3,1}... | collective-permute-start | bytes 491528 | tf_op jit(solution)/shard_map/ppermute | solution.py:15
  153.6 5.8 %collective-permute-start.21 = (bf16[128,640]{1,0:T(8,128)(2,1)S(1)}, bf16[128,640]{1,0:T(8,128)(2,1)S(1)}, u32[]{:S(2)}, u32[]{:S(2)}) collective-permute-start(bf16[128,640]{1,0:T(8,128)(2,1)S(1)} %fusion.7), channel_id=1, source_target_pairs={{0,2},{2,4},{4,6},{6,8},{8,10},{10,12},{12,14},{14,0},{1,3},{3,5},... | collective-permute-start | bytes 491528 | tf_op jit(solution)/shard_map/ppermute | solution.py:15
  154.0 5.8 %collective-permute-start.25 = (bf16[128,640]{1,0:T(8,128)(2,1)S(1)}, bf16[128,640]{1,0:T(8,128)(2,1)S(1)}, u32[]{:S(2)}, u32[]{:S(2)}) collective-permute-start(bf16[128,640]{1,0:T(8,128)(2,1)S(1)} %fusion.9), channel_id=1, source_target_pairs={{0,14},{2,0},{4,2},{6,4},{8,6},{10,8},{12,10},{14,12},{1,15},{3,1}... | collective-permute-start | bytes 491528 | tf_op jit(solution)/shard_map/ppermute | solution.py:15
  159.7 5.5 %collective-permute-start.22 = (bf16[128,640]{1,0:T(8,128)(2,1)S(1)}, bf16[128,640]{1,0:T(8,128)(2,1)S(1)}, u32[]{:S(2)}, u32[]{:S(2)}) collective-permute-start(bf16[128,640]{1,0:T(8,128)(2,1)S(1)} %fusion.6), channel_id=1, source_target_pairs={{0,2},{2,4},{4,6},{6,8},{8,10},{10,12},{12,14},{14,0},{1,3},{3,5},... | collective-permute-start | bytes 491528 | tf_op jit(solution)/shard_map/ppermute | solution.py:15
  160.1 5.7 %collective-permute-start.26 = (bf16[128,640]{1,0:T(8,128)(2,1)S(1)}, bf16[128,640]{1,0:T(8,128)(2,1)S(1)}, u32[]{:S(2)}, u32[]{:S(2)}) collective-permute-start(bf16[128,640]{1,0:T(8,128)(2,1)S(1)} %fusion.8), channel_id=1, source_target_pairs={{0,14},{2,0},{4,2},{6,4},{8,6},{10,8},{12,10},{14,12},{1,15},{3,1}... | collective-permute-start | bytes 491528 | tf_op jit(solution)/shard_map/ppermute | solution.py:15
  165.4 5.5 %collective-permute-start.23 = (bf16[128,640]{1,0:T(8,128)(2,1)S(1)}, bf16[128,640]{1,0:T(8,128)(2,1)S(1)}, u32[]{:S(2)}, u32[]{:S(2)}) collective-permute-start(bf16[128,640]{1,0:T(8,128)(2,1)S(1)} %fusion.5), channel_id=1, source_target_pairs={{0,2},{2,4},{4,6},{6,8},{8,10},{10,12},{12,14},{14,0},{1,3},{3,5},... | collective-permute-start | bytes 491528 | tf_op jit(solution)/shard_map/ppermute | solution.py:15

commit v2 on v1

--- a/solution.py
+++ b/solution.py
@@ -6,8 +6,10 @@
 
 SLOTS = 16
 X, Z, CORES, SECTIONS = 4, 8, 2, 4
+LANES = 128
 EPSILON = 1e-05
 BF, F32 = jnp.bfloat16, jnp.float32
+FIRST, LAST = (0, 1, 7, 2, 6), (3, 5, 4)
 
 
 def shift(array, axis, by):
@@ -33,18 +35,11 @@
         if step < Z // 2:
             down = shift(down, "z", -1)
             held[Z - step] = down
-    return [held[k] for k in range(Z)]
+    return held
 
 
 def add(a, b):
     return a.astype(F32) + b.astype(F32)
-
-
-def in_order(array, axis, here):
-    n = array.shape[axis]
-    flipped = jnp.flip(array, axis)
-    doubled = jnp.concatenate([flipped, flipped], axis)
-    return lax.dynamic_slice_in_dim(doubled, n - 1 - here, n, axis)
 
 
 def body(carried, destination, norm_gain, w_gate, w_up, w_down):
@@ -54,41 +49,40 @@
     total = rows_each * X * Z * CORES
     quarter, eighth = width // X, width // (X * CORES)
 
-    own = [w_gate[0], w_up[0], w_down[0]]
-    other = [shift(w, "core", 1) for w in own]
+    def pair(own):
+        return jnp.concatenate([own, shift(own, "core", 1)], 0)
 
-    dest = lax.optimization_barrier(jnp.broadcast_to(destination[0], (rows_each, 128)))
-    dest_all = lax.all_gather(dest, ("x", "z", "core"), axis=0, tiled=True)
-    dest_all = lax.optimization_barrier(dest_all)[:, 0]
-    row = jnp.arange(total, dtype=jnp.int32)
-    earlier = (dest_all[:, None] == dest_all[None, :]) & (row[None, :] < row[:, None])
-    rank = jnp.sum(earlier.astype(jnp.int32), axis=1)
+    gate_mat, up_mat, down_mat = pair(w_gate[0]), pair(w_up[0]), pair(w_down[0])
+    down_part = [
+        lax.dynamic_slice_in_dim(down_mat, lax.rem(x + k, X) * quarter, quarter, 1)
+        for k in range(X)
+    ]
 
-    line = jnp.concatenate([handoff(carried[0], k) for k in range(X)], axis=0)
-    rows = jnp.concatenate(gather_z(line), axis=0)
+    line = jnp.zeros((X * rows_each, width + LANES), BF)
+    for k in range(X):
+        line = lax.dynamic_update_slice(
+            line, handoff(carried[0], k), (lax.rem(x + X - k, X) * rows_each, 0)
+        )
+    dest = jnp.broadcast_to(destination[0].astype(BF), (rows_each, LANES))
+    line = lax.dynamic_update_slice(line, dest, (0, width))
+    held = gather_z(line)
 
-    floated = rows.astype(F32)
-    scale = lax.rsqrt(jnp.mean(floated * floated, axis=-1, keepdims=True) + EPSILON)
-    normed = (floated * scale * norm_gain[0].astype(F32)).astype(BF)
+    gain = norm_gain[0].astype(F32)
     contract = (((1,), (1,)), ((), ()))
 
-    def absolute(array):
-        shaped = array.reshape(Z, X, rows_each, array.shape[-1])
-        shaped = in_order(in_order(shaped, 0, z), 1, x)
-        return shaped.reshape(array.shape)
-
-    def hidden_of(gate_mat, up_mat):
+    def hidden_of(order):
+        floated = jnp.concatenate([held[k] for k in order], 0)[:, :width].astype(F32)
+        scale = lax.rsqrt(jnp.mean(floated * floated, axis=-1, keepdims=True) + EPSILON)
+        normed = (floated * scale * gain).astype(BF)
         gate = lax.dot_general(normed, gate_mat, contract, preferred_element_type=F32)
         up = lax.dot_general(normed, up_mat, contract, preferred_element_type=F32)
-        return absolute((jax.nn.silu(gate) * up).astype(BF))
+        return (jax.nn.silu(gate) * up).astype(BF)
 
-    hidden = [hidden_of(own[0], own[1]), hidden_of(other[0], other[1])]
-    partial = jnp.dot(hidden[0], own[2], preferred_element_type=F32) + jnp.dot(
-        hidden[1], other[2], preferred_element_type=F32
-    )
+    hidden = jnp.concatenate([hidden_of(FIRST), hidden_of(LAST)], 0)
+    order = FIRST + LAST
 
     def part(k):
-        return lax.dynamic_slice_in_dim(partial, lax.rem(x + k, X) * quarter, quarter, 1)
+        return jnp.dot(hidden, down_part[k], preferred_element_type=F32)
 
     half = quarter // 2
     far = part(2).astype(BF)
@@ -105,21 +99,35 @@
     def swap(array):
         mine = lax.dynamic_slice_in_dim(array, core * eighth, eighth, 1)
         theirs = lax.dynamic_slice_in_dim(array, (1 - core) * eighth, eighth, 1)
-        theirs = shift(theirs, "core", 1)
-        first = jnp.where(core == 0, mine, theirs)
-        second = jnp.where(core == 0, theirs, mine)
-        return jnp.concatenate([first, second], 0)
+        return jnp.concatenate([mine, shift(theirs, "core", 1)], 0)
+
+    kept = jnp.concatenate([held[k][:, :width] for k in order], 0)
+    residual = swap(lax.dynamic_slice_in_dim(kept, x * quarter, quarter, 1))
+
+    dest = jnp.concatenate([held[k][:rows_each, width:] for k in order], 0)
+    dests = jnp.zeros((X,) + dest.shape, BF)
+    for k in range(X):
+        there = shift(dest, "x", k) if k else dest
+        dests = lax.dynamic_update_slice(dests, there[None], (lax.rem(x + X - k, X), 0, 0))
+    dests = dests.reshape(X, Z, rows_each, LANES).transpose(1, 0, 2, 3)
+    dests = dests.reshape(total // CORES, LANES)
+    dest = jnp.concatenate([dests, shift(dests, "core", 1)], 0)[:, 0].astype(jnp.int32)
+    index = jnp.arange(total, dtype=jnp.int32)
+    block = (index // (X * rows_each)) % Z
+    behind = jnp.zeros_like(block)
+    for i, k in enumerate(order):
+        behind = jnp.where(block == i, k, behind)
+    source_core = jnp.where(index < total // CORES, core, 1 - core)
+    source = ((index // rows_each) % X) * Z + lax.rem(z + Z - behind, Z)
+    key = (source * CORES + source_core) * rows_each + index % rows_each
+    earlier = (dest[:, None] == dest[None, :]) & (key[None, :] < key[:, None])
+    rank = jnp.sum(earlier.astype(jnp.int32), axis=1)
 
     summed = swap(summed).astype(BF)
-    residual = swap(absolute(lax.dynamic_slice_in_dim(rows, x * quarter, quarter, 1)))
 
-    def by_core(per_row):
-        return per_row.reshape(X, Z, CORES, rows_each).transpose(2, 1, 0, 3).reshape(total)
-
-    dest_of, rank_of = by_core(dest_all), by_core(rank)
     slots = X * CORES * SLOTS
-    dest_z = (dest_of // CORES) % Z
-    slot_of = ((dest_of // (CORES * Z)) * CORES + dest_of % CORES) * SLOTS + rank_of
+    dest_z = (dest // CORES) % Z
+    slot_of = ((dest // (CORES * Z)) * CORES + dest % CORES) * SLOTS + rank
     slot = jnp.arange(slots, dtype=jnp.int32)
 
     def pick(k):

time: 185 us -> 140 us (0.76)
  blocking collectives: 58.9 us -> 14.3 us
  starting transfers between devices: 44.9 us -> 54 us
  matrix products: 15.6 us -> 10.4 us
  other arithmetic: 6.68 us -> 2.94 us
  local copies, waits for them, and re-layouts: 5.91 us -> 2.3 us
  waiting for transfers between devices: 51.7 us -> 55.3 us
    all_gather x1 -> x0, blocking collectives: 46.6 us -> none  [body(): dest_all = lax.all_gather(dest, ('x', 'z', 'core'), axis=0, tiled=True)]
    ppermute x23 -> x27, starting transfers between devices: 36.5 us -> 46.9 us  [shift(): return lax.ppermute(array, axis, [(i, (i + by) % n) for i in range(n)])]
    ppermute x4, waiting for transfers between devices: 0.01 us -> 5.22 us  [handoff(): return lax.ppermute(rows, ('section', 'x'), pairs)]
    dot_general x2 -> x4, matrix products: 5.08 us -> 2.07 us  [part(): return jnp.dot(hidden, down_part[k], preferred_element_type=F32)]
    all_to_all x1, blocking collectives: 12.4 us -> 14.3 us  [body(): lax.all_to_all(mixed.reshape(X * CORES, SLOTS, eighth), ('x', 'core'), 0,...]
    add x2, other arithmetic: 1.93 us -> 0.04 us  [the longest x1 0.02 us: body(): key = (source * CORES + source_core) * rows_each + index % rows_each]
    ppermute x23 -> x27, waiting for transfers between devices: 51.7 us -> 50.1 us  [shift(): return lax.ppermute(array, axis, [(i, (i + by) % n) for i in range(n)])]
  transfers between devices with their start and end apart: 27 -> 31, of which waited for: 12 -> 13; matrix products, arithmetic and copies ran while one was open for 12% -> 10% of each run, Pallas kernels for 0% -> 0%
where the time goes in v2:
time: 140 us
  waiting for transfers between devices  55.3 us (40%)
  starting transfers between devices  54 us (39%)
  blocking collectives  14.3 us (10%)
  matrix products  10.4 us (7%)
  other arithmetic  2.94 us (2%)
  local copies, waits for them, and re-layouts  2.3 us (2%)
    ppermute x27, waiting for transfers between devices, shift(): return lax.ppermute(array, axis, [(i, (i + by) % n) for i in range(n)])  50.1 us
    ppermute x27, starting transfers between devices, shift(): return lax.ppermute(array, axis, [(i, (i + by) % n) for i in range(n)])  46.9 us
    all_to_all x1, blocking collectives, body(): lax.all_to_all(mixed.reshape(X * CORES, SLOTS, eighth), ('x', 'core'), 0,...  14.3 us
    ppermute x4, starting transfers between devices, handoff(): return lax.ppermute(rows, ('section', 'x'), pairs)  7.18 us
    ppermute x4, waiting for transfers between devices, handoff(): return lax.ppermute(rows, ('section', 'x'), pairs)  5.22 us
    dot_general x2, matrix products, hidden_of(): lax.dot_general(normed, gate_mat, contract, preferred_element_type=F32)  2.96 us
    dot_general x2, matrix products, hidden_of(): up = lax.dot_general(normed, up_mat, contract, preferred_element_type=F32)  2.93 us
  transfers between devices with their start and end apart: 31, of which 13 were waited for; matrix products, arithmetic and copies ran while one was open for 10% of the time, Pallas kernels for 0%

profile of v2, /device:TPU:1, one launch (start us, length us, event | category | flops | bytes accessed | tf_op | source)
XLA Modules:
  0.0 140.0 jit_solution(13372509882183956228)
XLA Ops:
  0.0 4.3 %collective-permute-start.3 = (bf16[8,5120]{1,0:T(8,128)(2,1)}, bf16[8,5120]{1,0:T(8,128)(2,1)S(1)}, u32[]{:S(2)}, u32[]{:S(2)}) collective-permute-start(bf16[8,5120]{1,0:T(8,128)(2,1)} %bitcast.41), channel_id=1, source_target_pairs={{0,112},{16,64},{32,80},{48,96},{64,176},{80,128},{96,144},{112,16... | collective-permute-start | bytes 245768 | tf_op jit(solution)/shard_map/ppermute | solution.py:26
  4.3 1.5 %collective-permute-start.2 = (bf16[8,5120]{1,0:T(8,128)(2,1)}, bf16[8,5120]{1,0:T(8,128)(2,1)S(1)}, u32[]{:S(2)}, u32[]{:S(2)}) collective-permute-start(bf16[8,5120]{1,0:T(8,128)(2,1)} %bitcast.42), channel_id=1, source_target_pairs={{0,96},{16,112},{32,64},{48,80},{64,160},{80,176},{96,128},{112,14... | collective-permute-start | bytes 245768 | tf_op jit(solution)/shard_map/ppermute | solution.py:26
  5.9 1.3 collective-permute-start.1
  7.2 1.7 %collective-permute-start.15 = (bf16[216,5120]{1,0:T(8,128)(2,1)}, bf16[216,5120]{1,0:T(8,128)(2,1)S(1)}, u32[]{:S(2)}, u32[]{:S(2)}) collective-permute-start(bf16[216,5120]{1,0:T(8,128)(2,1)} %bitcast.35), channel_id=1, source_target_pairs={{0,1},{1,0},{2,3},{3,2},{4,5},{5,4},{6,7},{7,6},{8,9},{9,8},{10,11... | collective-permute-start | bytes 6635528 | tf_op jit(solution)/shard_map/ppermute | solution.py:17
  8.9 0.7 convert_bitcast_fusion
  9.6 0.7 mul.172
  10.4 5.2 %collective-permute-done = bf16[8,5120]{1,0:T(8,128)(2,1)S(1)} collective-permute-done((bf16[8,5120]{1,0:T(8,128)(2,1)}, bf16[8,5120]{1,0:T(8,128)(2,1)S(1)}, u32[]{:S(2)}, u32[]{:S(2)}) %collective-permute-start) | collective-permute-done | bytes 81952 | tf_op jit(solution)/shard_map/ppermute | solution.py:26
  15.6 0.9 collective-permute-start.16
  16.8 5.6 %collective-permute-start.5 = (bf16[32,5248]{1,0:T(8,128)(2,1)S(1)}, bf16[32,5248]{1,0:T(8,128)(2,1)S(1)}, u32[]{:S(2)}, u32[]{:S(2)}) collective-permute-start(bf16[32,5248]{1,0:T(8,128)(2,1)S(1)} %get-tuple-element.21), channel_id=1, source_target_pairs={{0,14},{2,0},{4,2},{6,4},{8,6},{10,8},{12,10},{14,12},{1,15},{3,1}... | collective-permute-start | bytes 1007624 | tf_op jit(solution)/shard_map/ppermute | solution.py:17
  22.5 6.7 %collective-permute-done.5 = bf16[32,5248]{1,0:T(8,128)(2,1)S(1)} collective-permute-done((bf16[32,5248]{1,0:T(8,128)(2,1)S(1)}, bf16[32,5248]{1,0:T(8,128)(2,1)S(1)}, u32[]{:S(2)}, u32[]{:S(2)}) %collective-permute-start.5) | collective-permute-done | bytes 335904 | tf_op jit(solution)/shard_map/ppermute | solution.py:17
  29.2 3.4 %collective-permute-start.7 = (bf16[32,5248]{1,0:T(8,128)(2,1)S(1)}, bf16[32,5248]{1,0:T(8,128)(2,1)S(1)}, u32[]{:S(2)}, u32[]{:S(2)}) collective-permute-start(bf16[32,5248]{1,0:T(8,128)(2,1)S(1)} %collective-permute-done.5), channel_id=1, source_target_pairs={{0,14},{2,0},{4,2},{6,4},{8,6},{10,8},{12,10},{14,12},{1,15},{3,1}... | collective-permute-start | bytes 1007624 | tf_op jit(solution)/shard_map/ppermute | solution.py:17
  32.8 8.8 %collective-permute-done.6 = bf16[32,5248]{1,0:T(8,128)(2,1)S(1)} collective-permute-done((bf16[32,5248]{1,0:T(8,128)(2,1)S(1)}, bf16[32,5248]{1,0:T(8,128)(2,1)S(1)}, u32[]{:S(2)}, u32[]{:S(2)}) %collective-permute-start.6) | collective-permute-done | bytes 335904 | tf_op jit(solution)/shard_map/ppermute | solution.py:17
  41.7 0.4 fusion
  42.1 0.3 collective-permute-start.9
  42.4 1.2 collective-permute-start.8
  43.7 6.7 %collective-permute-done.8 = bf16[32,5248]{1,0:T(8,128)(2,1)S(1)} collective-permute-done((bf16[32,5248]{1,0:T(8,128)(2,1)S(1)}, bf16[32,5248]{1,0:T(8,128)(2,1)S(1)}, u32[]{:S(2)}, u32[]{:S(2)}) %collective-permute-start.8) | collective-permute-done | bytes 335904 | tf_op jit(solution)/shard_map/ppermute | solution.py:17
  50.6 7.1 %collective-permute-done.10 = bf16[32,5248]{1,0:T(8,128)(2,1)S(1)} collective-permute-done((bf16[32,5248]{1,0:T(8,128)(2,1)S(1)}, bf16[32,5248]{1,0:T(8,128)(2,1)S(1)}, u32[]{:S(2)}, u32[]{:S(2)}) %collective-permute-start.10) | collective-permute-done | bytes 335904 | tf_op jit(solution)/shard_map/ppermute | solution.py:17
  57.7 0.7 collective-permute-start.13
  58.4 0.8 collective-permute-start.11
  59.2 0.3 fusion.8
  59.5 2.7 %collective-permute-done.11 = bf16[64,128]{1,0:T(8,128)(2,1)S(1)} collective-permute-done((bf16[64,128]{1,0:T(8,128)(2,1)S(1)}, bf16[64,128]{1,0:T(8,128)(2,1)S(1)}, u32[]{:S(2)}, u32[]{:S(2)}) %collective-permute-start.11) | collective-permute-done | bytes 16416 | tf_op jit(solution)/shard_map/ppermute | solution.py:17
  62.4 1.5 %fusion.5 = f32[96,432]{1,0:T(8,128)S(1)} fusion(bf16[216,5120]{1,0:T(8,128)(2,1)S(1)} %collective-permute-done.15, bf16[216,5120]{1,0:T(8,128)(2,1)S(1)} %bitcast.36, f32[5120]{0:T(1024)S(1)} %bitcast.31, f32[96]{0:T(128)S(1)} %add_rsqrt_fusion.1, bf16[32,5248]{1,0:T(8,128)(2,1)S(1)} %collective-permute-done.10, ...), kind=kOutput, calls=%fused_computation.17 | convolution fusion | flops 437944320 | bytes 5618048 | tf_op jit(solution)/shard_map/dot_general | solution.py:77
  64.0 1.5 %multiply_convert_fusion.1 = bf16[96,432]{1,0:T(8,128)(2,1)S(1)} fusion(f32[96,432]{1,0:T(8,128)S(1)} %fusion.5, bf16[216,5120]{1,0:T(8,128)(2,1)S(1)} %collective-permute-done.16, bf16[216,5120]{1,0:T(8,128)(2,1)S(1)} %bitcast.39, f32[5120]{0:T(1024)S(1)} %bitcast.32, f32[96]{0:T(128)S(1)} %add_rsqrt_fusion.1, ...), kind=kOutput, calls=%fused_computation.86 | convolution fusion | flops 438193152 | bytes 5700992 | tf_op jit(solution)/shard_map/dot_general | solution.py:78
  65.5 1.5 %fusion.6 = f32[160,432]{1,0:T(8,128)S(1)} fusion(bf16[216,5120]{1,0:T(8,128)(2,1)S(1)} %collective-permute-done.15, bf16[216,5120]{1,0:T(8,128)(2,1)S(1)} %bitcast.37, f32[5120]{0:T(1024)S(1)} %bitcast.33, f32[160]{0:T(256)S(1)} %add_rsqrt_fusion, bf16[160,5248]{1,0:T(8,128)(2,1)S(1)} %constant_dynamic-update-slice_fusion.8), kind=kOutput, calls=%fused_computation.18 | convolution fusion | flops 719912960 | bytes 6360064 | tf_op jit(solution)/shard_map/dot_general | solution.py:77
  67.0 1.5 %multiply_convert_fusion = bf16[160,432]{1,0:T(8,128)(2,1)S(1)} fusion(f32[160,432]{1,0:T(8,128)S(1)} %fusion.6, bf16[216,5120]{1,0:T(8,128)(2,1)S(1)} %collective-permute-done.16, bf16[216,5120]{1,0:T(8,128)(2,1)S(1)} %bitcast.40, f32[5120]{0:T(1024)S(1)} %bitcast.34, f32[160]{0:T(256)S(1)} %add_rsqrt_fusion, ...), kind=kOutput, calls=%fused_computation.74 | convolution fusion | flops 720327680 | bytes 6549504 | tf_op jit(solution)/shard_map/dot_general | solution.py:78
  68.6 0.5 convolution_convert_fusion
  69.4 2.5 %collective-permute-start.20 = (bf16[256,640]{1,0:T(8,128)(2,1)S(1)}, bf16[256,640]{1,0:T(8,128)(2,1)S(1)}, u32[]{:S(2)}, u32[]{:S(2)}) collective-permute-start(bf16[256,640]{1,0:T(8,128)(2,1)S(1)} %get-tuple-element.12), channel_id=1, source_target_pairs={{0,48},{16,0},{32,16},{48,32},{1,49},{17,1},{33,17},{49,33},{2,50}... | collective-permute-start | bytes 983048 | tf_op jit(solution)/shard_map/ppermute | solution.py:17
  72.0 0.5 fusion.25
  72.5 0.5 fusion.20
  73.1 3.3 %collective-permute-done.18 = bf16[256,640]{1,0:T(8,128)(2,1)S(1)} collective-permute-done((bf16[256,640]{1,0:T(8,128)(2,1)S(1)}, bf16[256,640]{1,0:T(8,128)(2,1)S(1)}, u32[]{:S(2)}, u32[]{:S(2)}) %collective-permute-start.18) | collective-permute-done | bytes 327712 | tf_op jit(solution)/shard_map/ppermute | solution.py:17
  76.8 2.7 %collective-permute-start.21 = (bf16[256,1280]{1,0:T(8,128)(2,1)S(1)}, bf16[256,1280]{1,0:T(8,128)(2,1)S(1)}, u32[]{:S(2)}, u32[]{:S(2)}) collective-permute-start(bf16[256,1280]{1,0:T(8,128)(2,1)S(1)} %pad_maximum_fusion.9), channel_id=1, source_target_pairs={{0,48},{16,0},{32,16},{48,32},{1,49},{17,1},{33,17},{49,33},{2,50}... | collective-permute-start | bytes 1966088 | tf_op jit(solution)/shard_map/ppermute | solution.py:17
  79.5 10.2 %collective-permute-start.14 = (bf16[256,128]{1,0:T(8,128)(2,1)S(1)}, bf16[256,128]{1,0:T(8,128)(2,1)S(1)}, u32[]{:S(2)}, u32[]{:S(2)}) collective-permute-start(bf16[256,128]{1,0:T(8,128)(2,1)S(1)} %bitcast.27), channel_id=1, source_target_pairs={{0,1},{1,0},{2,3},{3,2},{4,5},{5,4},{6,7},{7,6},{8,9},{9,8},{10,11... | collective-permute-start | bytes 196616 | tf_op jit(solution)/shard_map/ppermute | solution.py:17
  89.7 0.4 constant_dynamic-slice_fusion.1
  90.1 0.3 collective-permute-start.23
  90.8 0.5 fusion.7
  91.5 7.4 %collective-permute-start.22 = (bf16[256,640]{1,0:T(8,128)(2,1)S(1)}, bf16[256,640]{1,0:T(8,128)(2,1)S(1)}, u32[]{:S(2)}, u32[]{:S(2)}) collective-permute-start(bf16[256,640]{1,0:T(8,128)(2,1)S(1)} %get-tuple-element.10), channel_id=1, source_target_pairs={{0,1},{1,0},{2,3},{3,2},{4,5},{5,4},{6,7},{7,6},{8,9},{9,8},{10,11... | collective-permute-start | bytes 983048 | tf_op jit(solution)/shard_map/ppermute | solution.py:17
  98.8 0.3 convert_reduce_fusion
  99.2 0.9 collective-permute-done.22
  100.8 2.7 %collective-permute-start.28 = (bf16[128,640]{1,0:T(8,128)(2,1)S(1)}, bf16[128,640]{1,0:T(8,128)(2,1)S(1)}, u32[]{:S(2)}, u32[]{:S(2)}) collective-permute-start(bf16[128,640]{1,0:T(8,128)(2,1)S(1)} %convolution_convert_fusion.1), channel_id=1, source_target_pairs={{0,14},{2,0},{4,2},{6,4},{8,6},{10,8},{12,10},{14,12},{1,15},{3,1}... | collective-permute-start | bytes 491528 | tf_op jit(solution)/shard_map/ppermute | solution.py:17
  103.5 3.6 %collective-permute-done.24 = bf16[128,640]{1,0:T(8,128)(2,1)S(1)} collective-permute-done((bf16[128,640]{1,0:T(8,128)(2,1)S(1)}, bf16[128,640]{1,0:T(8,128)(2,1)S(1)}, u32[]{:S(2)}, u32[]{:S(2)}) %collective-permute-start.24) | collective-permute-done | bytes 163872 | tf_op jit(solution)/shard_map/ppermute | solution.py:17
  107.7 2.7 %collective-permute-start.29 = (bf16[128,640]{1,0:T(8,128)(2,1)S(1)}, bf16[128,640]{1,0:T(8,128)(2,1)S(1)}, u32[]{:S(2)}, u32[]{:S(2)}) collective-permute-start(bf16[128,640]{1,0:T(8,128)(2,1)S(1)} %fusion.17), channel_id=1, source_target_pairs={{0,14},{2,0},{4,2},{6,4},{8,6},{10,8},{12,10},{14,12},{1,15},{3,1}... | collective-permute-start | bytes 491528 | tf_op jit(solution)/shard_map/ppermute | solution.py:17
  110.5 2.7 %collective-permute-done.25 = bf16[128,640]{1,0:T(8,128)(2,1)S(1)} collective-permute-done((bf16[128,640]{1,0:T(8,128)(2,1)S(1)}, bf16[128,640]{1,0:T(8,128)(2,1)S(1)}, u32[]{:S(2)}, u32[]{:S(2)}) %collective-permute-start.25) | collective-permute-done | bytes 163872 | tf_op jit(solution)/shard_map/ppermute | solution.py:17
  113.8 2.7 %collective-permute-start.30 = (bf16[128,640]{1,0:T(8,128)(2,1)S(1)}, bf16[128,640]{1,0:T(8,128)(2,1)S(1)}, u32[]{:S(2)}, u32[]{:S(2)}) collective-permute-start(bf16[128,640]{1,0:T(8,128)(2,1)S(1)} %fusion.16), channel_id=1, source_target_pairs={{0,14},{2,0},{4,2},{6,4},{8,6},{10,8},{12,10},{14,12},{1,15},{3,1}... | collective-permute-start | bytes 491528 | tf_op jit(solution)/shard_map/ppermute | solution.py:17
  116.5 2.3 %collective-permute-done.26 = bf16[128,640]{1,0:T(8,128)(2,1)S(1)} collective-permute-done((bf16[128,640]{1,0:T(8,128)(2,1)S(1)}, bf16[128,640]{1,0:T(8,128)(2,1)S(1)}, u32[]{:S(2)}, u32[]{:S(2)}) %collective-permute-start.26) | collective-permute-done | bytes 163872 | tf_op jit(solution)/shard_map/ppermute | solution.py:17
  119.5 5.1 %collective-permute-done.27 = bf16[128,640]{1,0:T(8,128)(2,1)S(1)} collective-permute-done((bf16[128,640]{1,0:T(8,128)(2,1)S(1)}, bf16[128,640]{1,0:T(8,128)(2,1)S(1)}, u32[]{:S(2)}, u32[]{:S(2)}) %collective-permute-start.27) | collective-permute-done | bytes 163872 | tf_op jit(solution)/shard_map/ppermute | solution.py:17
  124.6 0.3 fusion.18
  124.9 14.3 %all_to_all.5 = bf16[8,16,640]{2,1,0:T(8,128)(2,1)S(1)} all-to-all(bf16[8,16,640]{2,1,0:T(8,128)(2,1)S(1)} %bitcast.30), channel_id=1, replica_groups=mesh['section'=4,'x'=4,'z'=8,'core'=2] {'x','core'}, dimensions={0} | all-to-all | bytes 327680 | tf_op jit(solution)/shard_map/all_to_all | solution.py:153
  139.3 0.7 reshape.294
  (93 shorter events, 4.9 us)
Async XLA Ops:
  0.0 16.7 %collective-permute-start.3 = (bf16[8,5120]{1,0:T(8,128)(2,1)}, bf16[8,5120]{1,0:T(8,128)(2,1)S(1)}, u32[]{:S(2)}, u32[]{:S(2)}) collective-permute-start(bf16[8,5120]{1,0:T(8,128)(2,1)} %bitcast.41), channel_id=1, source_target_pairs={{0,112},{16,64},{32,80},{48,96},{64,176},{80,128},{96,144},{112,16... | collective-permute-start | bytes 245768 | tf_op jit(solution)/shard_map/ppermute | solution.py:26
  4.3 12.4 %collective-permute-start.2 = (bf16[8,5120]{1,0:T(8,128)(2,1)}, bf16[8,5120]{1,0:T(8,128)(2,1)S(1)}, u32[]{:S(2)}, u32[]{:S(2)}) collective-permute-start(bf16[8,5120]{1,0:T(8,128)(2,1)} %bitcast.42), channel_id=1, source_target_pairs={{0,96},{16,112},{32,64},{48,80},{64,160},{80,176},{96,128},{112,14... | collective-permute-start | bytes 245768 | tf_op jit(solution)/shard_map/ppermute | solution.py:26
  5.9 10.7 %collective-permute-start.1 = (bf16[8,5120]{1,0:T(8,128)(2,1)}, bf16[8,5120]{1,0:T(8,128)(2,1)S(1)}, u32[]{:S(2)}, u32[]{:S(2)}) collective-permute-start(bf16[8,5120]{1,0:T(8,128)(2,1)} %bitcast.43), channel_id=1, source_target_pairs={{0,80},{16,96},{32,112},{48,64},{64,144},{80,160},{96,176},{112,12... | collective-permute-start | bytes 245768 | tf_op jit(solution)/shard_map/ppermute | solution.py:26
  7.2 8.5 %collective-permute-start = (bf16[8,5120]{1,0:T(8,128)(2,1)}, bf16[8,5120]{1,0:T(8,128)(2,1)S(1)}, u32[]{:S(2)}, u32[]{:S(2)}) collective-permute-start(bf16[8,5120]{1,0:T(8,128)(2,1)} %bitcast.44), channel_id=1, source_target_pairs={{0,64},{16,80},{32,96},{48,112},{64,128},{80,144},{96,160},{112,17... | collective-permute-start | bytes 245768 | tf_op jit(solution)/shard_map/ppermute | solution.py:26
  7.2 55.2 %collective-permute-start.15 = (bf16[216,5120]{1,0:T(8,128)(2,1)}, bf16[216,5120]{1,0:T(8,128)(2,1)S(1)}, u32[]{:S(2)}, u32[]{:S(2)}) collective-permute-start(bf16[216,5120]{1,0:T(8,128)(2,1)} %bitcast.35), channel_id=1, source_target_pairs={{0,1},{1,0},{2,3},{3,2},{4,5},{5,4},{6,7},{7,6},{8,9},{9,8},{10,11... | collective-permute-start | bytes 6635528 | tf_op jit(solution)/shard_map/ppermute | solution.py:17
  15.6 48.2 %collective-permute-start.16 = (bf16[216,5120]{1,0:T(8,128)(2,1)}, bf16[216,5120]{1,0:T(8,128)(2,1)S(1)}, u32[]{:S(2)}, u32[]{:S(2)}) collective-permute-start(bf16[216,5120]{1,0:T(8,128)(2,1)} %bitcast.38), channel_id=1, source_target_pairs={{0,1},{1,0},{2,3},{3,2},{4,5},{5,4},{6,7},{7,6},{8,9},{9,8},{10,11... | collective-permute-start | bytes 6635528 | tf_op jit(solution)/shard_map/ppermute | solution.py:17
  16.6 51.9 %collective-permute-start.17 = (bf16[216,5120]{1,0:T(8,128)(2,1)}, bf16[216,5120]{1,0:T(8,128)(2,1)S(1)}, u32[]{:S(2)}, u32[]{:S(2)}) collective-permute-start(bf16[216,5120]{1,0:T(8,128)(2,1)} %bitcast.21), channel_id=1, source_target_pairs={{0,1},{1,0},{2,3},{3,2},{4,5},{5,4},{6,7},{7,6},{8,9},{9,8},{10,11... | collective-permute-start | bytes 6635528 | tf_op jit(solution)/shard_map/ppermute | solution.py:17
  16.8 12.4 %collective-permute-start.5 = (bf16[32,5248]{1,0:T(8,128)(2,1)S(1)}, bf16[32,5248]{1,0:T(8,128)(2,1)S(1)}, u32[]{:S(2)}, u32[]{:S(2)}) collective-permute-start(bf16[32,5248]{1,0:T(8,128)(2,1)S(1)} %get-tuple-element.21), channel_id=1, source_target_pairs={{0,14},{2,0},{4,2},{6,4},{8,6},{10,8},{12,10},{14,12},{1,15},{3,1}... | collective-permute-start | bytes 1007624 | tf_op jit(solution)/shard_map/ppermute | solution.py:17
  22.4 10.2 %collective-permute-start.4 = (bf16[32,5248]{1,0:T(8,128)(2,1)S(1)}, bf16[32,5248]{1,0:T(8,128)(2,1)S(1)}, u32[]{:S(2)}, u32[]{:S(2)}) collective-permute-start(bf16[32,5248]{1,0:T(8,128)(2,1)S(1)} %get-tuple-element.21), channel_id=1, source_target_pairs={{0,2},{2,4},{4,6},{6,8},{8,10},{10,12},{12,14},{14,0},{1,3},{3,5},... | collective-permute-start | bytes 1007624 | tf_op jit(solution)/shard_map/ppermute | solution.py:17
  29.2 12.4 %collective-permute-start.7 = (bf16[32,5248]{1,0:T(8,128)(2,1)S(1)}, bf16[32,5248]{1,0:T(8,128)(2,1)S(1)}, u32[]{:S(2)}, u32[]{:S(2)}) collective-permute-start(bf16[32,5248]{1,0:T(8,128)(2,1)S(1)} %collective-permute-done.5), channel_id=1, source_target_pairs={{0,14},{2,0},{4,2},{6,4},{8,6},{10,8},{12,10},{14,12},{1,15},{3,1}... | collective-permute-start | bytes 1007624 | tf_op jit(solution)/shard_map/ppermute | solution.py:17
  32.6 9.0 %collective-permute-start.6 = (bf16[32,5248]{1,0:T(8,128)(2,1)S(1)}, bf16[32,5248]{1,0:T(8,128)(2,1)S(1)}, u32[]{:S(2)}, u32[]{:S(2)}) collective-permute-start(bf16[32,5248]{1,0:T(8,128)(2,1)S(1)} %collective-permute-done.4), channel_id=1, source_target_pairs={{0,2},{2,4},{4,6},{6,8},{8,10},{10,12},{12,14},{14,0},{1,3},{3,5},... | collective-permute-start | bytes 1007624 | tf_op jit(solution)/shard_map/ppermute | solution.py:17
  42.1 20.3 %copy-start.1 = (bf16[1,216,5120]{2,1,0:T(8,128)(2,1)S(1)}, bf16[1,216,5120]{2,1,0:T(8,128)(2,1)}, u32[]{:S(2)}) copy-start(bf16[1,216,5120]{2,1,0:T(8,128)(2,1)} %param.9) | copy-start | bytes 6635524
  42.1 8.4 %collective-permute-start.9 = (bf16[32,5248]{1,0:T(8,128)(2,1)S(1)}, bf16[32,5248]{1,0:T(8,128)(2,1)S(1)}, u32[]{:S(2)}, u32[]{:S(2)}) collective-permute-start(bf16[32,5248]{1,0:T(8,128)(2,1)S(1)} %collective-permute-done.7), channel_id=1, source_target_pairs={{0,14},{2,0},{4,2},{6,4},{8,6},{10,8},{12,10},{14,12},{1,15},{3,1}... | collective-permute-start | bytes 1007624 | tf_op jit(solution)/shard_map/ppermute | solution.py:17
  42.4 8.1 %collective-permute-start.8 = (bf16[32,5248]{1,0:T(8,128)(2,1)S(1)}, bf16[32,5248]{1,0:T(8,128)(2,1)S(1)}, u32[]{:S(2)}, u32[]{:S(2)}) collective-permute-start(bf16[32,5248]{1,0:T(8,128)(2,1)S(1)} %collective-permute-done.6), channel_id=1, source_target_pairs={{0,2},{2,4},{4,6},{6,8},{8,10},{10,12},{12,14},{14,0},{1,3},{3,5},... | collective-permute-start | bytes 1007624 | tf_op jit(solution)/shard_map/ppermute | solution.py:17
  50.5 7.2 %collective-permute-start.10 = (bf16[32,5248]{1,0:T(8,128)(2,1)S(1)}, bf16[32,5248]{1,0:T(8,128)(2,1)S(1)}, u32[]{:S(2)}, u32[]{:S(2)}) collective-permute-start(bf16[32,5248]{1,0:T(8,128)(2,1)S(1)} %collective-permute-done.8), channel_id=1, source_target_pairs={{0,2},{2,4},{4,6},{6,8},{8,10},{10,12},{12,14},{14,0},{1,3},{3,5},... | collective-permute-start | bytes 1007624 | tf_op jit(solution)/shard_map/ppermute | solution.py:17
  57.7 21.8 %collective-permute-start.13 = (bf16[64,128]{1,0:T(8,128)(2,1)S(1)}, bf16[64,128]{1,0:T(8,128)(2,1)S(1)}, u32[]{:S(2)}, u32[]{:S(2)}) collective-permute-start(bf16[64,128]{1,0:T(8,128)(2,1)S(1)} %constant_dynamic-update-slice_fusion), channel_id=1, source_target_pairs={{0,48},{16,0},{32,16},{48,32},{1,49},{17,1},{33,17},{49,33},{2,50}... | collective-permute-start | bytes 49160 | tf_op jit(solution)/shard_map/ppermute | solution.py:17
  58.4 3.8 %collective-permute-start.11 = (bf16[64,128]{1,0:T(8,128)(2,1)S(1)}, bf16[64,128]{1,0:T(8,128)(2,1)S(1)}, u32[]{:S(2)}, u32[]{:S(2)}) collective-permute-start(bf16[64,128]{1,0:T(8,128)(2,1)S(1)} %constant_dynamic-update-slice_fusion), channel_id=1, source_target_pairs={{0,16},{16,32},{32,48},{48,0},{1,17},{17,33},{33,49},{49,1},{2,18}... | collective-permute-start | bytes 49160 | tf_op jit(solution)/shard_map/ppermute | solution.py:17
  62.2 7.2 %collective-permute-start.12 = (bf16[64,128]{1,0:T(8,128)(2,1)S(1)}, bf16[64,128]{1,0:T(8,128)(2,1)S(1)}, u32[]{:S(2)}, u32[]{:S(2)}) collective-permute-start(bf16[64,128]{1,0:T(8,128)(2,1)S(1)} %constant_dynamic-update-slice_fusion), channel_id=1, source_target_pairs={{0,32},{16,48},{32,0},{48,16},{1,33},{17,49},{33,1},{49,17},{2,34}... | collective-permute-start | bytes 49160 | tf_op jit(solution)/shard_map/ppermute | solution.py:17
  62.4 1.6 %copy-start.2 = (bf16[1,216,5120]{2,1,0:T(8,128)(2,1)S(1)}, bf16[1,216,5120]{2,1,0:T(8,128)(2,1)}, u32[]{:S(2)}) copy-start(bf16[1,216,5120]{2,1,0:T(8,128)(2,1)} %param.10) | copy-start | bytes 6635524
  67.0 1.6 %copy-start = (bf16[1,216,5120]{2,1,0:T(8,128)(2,1)S(1)}, bf16[1,216,5120]{2,1,0:T(8,128)(2,1)}, u32[]{:S(2)}) copy-start(bf16[1,216,5120]{2,1,0:T(8,128)(2,1)} %param.11) | copy-start | bytes 6635524
  69.2 7.2 %collective-permute-start.18 = (bf16[256,640]{1,0:T(8,128)(2,1)S(1)}, bf16[256,640]{1,0:T(8,128)(2,1)S(1)}, u32[]{:S(2)}, u32[]{:S(2)}) collective-permute-start(bf16[256,640]{1,0:T(8,128)(2,1)S(1)} %get-tuple-element.11), channel_id=1, source_target_pairs={{0,16},{16,32},{32,48},{48,0},{1,17},{17,33},{33,49},{49,1},{2,18}... | collective-permute-start | bytes 983048 | tf_op jit(solution)/shard_map/ppermute | solution.py:17
  69.4 7.2 %collective-permute-start.20 = (bf16[256,640]{1,0:T(8,128)(2,1)S(1)}, bf16[256,640]{1,0:T(8,128)(2,1)S(1)}, u32[]{:S(2)}, u32[]{:S(2)}) collective-permute-start(bf16[256,640]{1,0:T(8,128)(2,1)S(1)} %get-tuple-element.12), channel_id=1, source_target_pairs={{0,48},{16,0},{32,16},{48,32},{1,49},{17,1},{33,17},{49,33},{2,50}... | collective-permute-start | bytes 983048 | tf_op jit(solution)/shard_map/ppermute | solution.py:17
  76.5 14.3 %collective-permute-start.19 = (bf16[256,1280]{1,0:T(8,128)(2,1)S(1)}, bf16[256,1280]{1,0:T(8,128)(2,1)S(1)}, u32[]{:S(2)}, u32[]{:S(2)}) collective-permute-start(bf16[256,1280]{1,0:T(8,128)(2,1)S(1)} %pad_maximum_fusion.8), channel_id=1, source_target_pairs={{0,16},{16,32},{32,48},{48,0},{1,17},{17,33},{33,49},{49,1},{2,18}... | collective-permute-start | bytes 1966088 | tf_op jit(solution)/shard_map/ppermute | solution.py:17
  76.8 14.0 %collective-permute-start.21 = (bf16[256,1280]{1,0:T(8,128)(2,1)S(1)}, bf16[256,1280]{1,0:T(8,128)(2,1)S(1)}, u32[]{:S(2)}, u32[]{:S(2)}) collective-permute-start(bf16[256,1280]{1,0:T(8,128)(2,1)S(1)} %pad_maximum_fusion.9), channel_id=1, source_target_pairs={{0,48},{16,0},{32,16},{48,32},{1,49},{17,1},{33,17},{49,33},{2,50}... | collective-permute-start | bytes 1966088 | tf_op jit(solution)/shard_map/ppermute | solution.py:17
  79.5 11.1 %collective-permute-start.14 = (bf16[256,128]{1,0:T(8,128)(2,1)S(1)}, bf16[256,128]{1,0:T(8,128)(2,1)S(1)}, u32[]{:S(2)}, u32[]{:S(2)}) collective-permute-start(bf16[256,128]{1,0:T(8,128)(2,1)S(1)} %bitcast.27), channel_id=1, source_target_pairs={{0,1},{1,0},{2,3},{3,2},{4,5},{5,4},{6,7},{7,6},{8,9},{9,8},{10,11... | collective-permute-start | bytes 196616 | tf_op jit(solution)/shard_map/ppermute | solution.py:17
  90.1 29.1 %collective-permute-start.23 = (bf16[256,640]{1,0:T(8,128)(2,1)S(1)}, bf16[256,640]{1,0:T(8,128)(2,1)S(1)}, u32[]{:S(2)}, u32[]{:S(2)}) collective-permute-start(bf16[256,640]{1,0:T(8,128)(2,1)S(1)} %get-tuple-element.8), channel_id=1, source_target_pairs={{0,1},{1,0},{2,3},{3,2},{4,5},{5,4},{6,7},{7,6},{8,9},{9,8},{10,11... | collective-permute-start | bytes 983048 | tf_op jit(solution)/shard_map/ppermute | solution.py:17
  91.5 8.6 %collective-permute-start.22 = (bf16[256,640]{1,0:T(8,128)(2,1)S(1)}, bf16[256,640]{1,0:T(8,128)(2,1)S(1)}, u32[]{:S(2)}, u32[]{:S(2)}) collective-permute-start(bf16[256,640]{1,0:T(8,128)(2,1)S(1)} %get-tuple-element.10), channel_id=1, source_target_pairs={{0,1},{1,0},{2,3},{3,2},{4,5},{5,4},{6,7},{7,6},{8,9},{9,8},{10,11... | collective-permute-start | bytes 983048 | tf_op jit(solution)/shard_map/ppermute | solution.py:17
  100.4 6.7 %collective-permute-start.24 = (bf16[128,640]{1,0:T(8,128)(2,1)S(1)}, bf16[128,640]{1,0:T(8,128)(2,1)S(1)}, u32[]{:S(2)}, u32[]{:S(2)}) collective-permute-start(bf16[128,640]{1,0:T(8,128)(2,1)S(1)} %convolution_convert_fusion.2), channel_id=1, source_target_pairs={{0,2},{2,4},{4,6},{6,8},{8,10},{10,12},{12,14},{14,0},{1,3},{3,5},... | collective-permute-start | bytes 491528 | tf_op jit(solution)/shard_map/ppermute | solution.py:17
  100.8 6.7 %collective-permute-start.28 = (bf16[128,640]{1,0:T(8,128)(2,1)S(1)}, bf16[128,640]{1,0:T(8,128)(2,1)S(1)}, u32[]{:S(2)}, u32[]{:S(2)}) collective-permute-start(bf16[128,640]{1,0:T(8,128)(2,1)S(1)} %convolution_convert_fusion.1), channel_id=1, source_target_pairs={{0,14},{2,0},{4,2},{6,4},{8,6},{10,8},{12,10},{14,12},{1,15},{3,1}... | collective-permute-start | bytes 491528 | tf_op jit(solution)/shard_map/ppermute | solution.py:17
  107.4 5.8 %collective-permute-start.25 = (bf16[128,640]{1,0:T(8,128)(2,1)S(1)}, bf16[128,640]{1,0:T(8,128)(2,1)S(1)}, u32[]{:S(2)}, u32[]{:S(2)}) collective-permute-start(bf16[128,640]{1,0:T(8,128)(2,1)S(1)} %fusion.15), channel_id=1, source_target_pairs={{0,2},{2,4},{4,6},{6,8},{8,10},{10,12},{12,14},{14,0},{1,3},{3,5},... | collective-permute-start | bytes 491528 | tf_op jit(solution)/shard_map/ppermute | solution.py:17
  107.7 5.8 %collective-permute-start.29 = (bf16[128,640]{1,0:T(8,128)(2,1)S(1)}, bf16[128,640]{1,0:T(8,128)(2,1)S(1)}, u32[]{:S(2)}, u32[]{:S(2)}) collective-permute-start(bf16[128,640]{1,0:T(8,128)(2,1)S(1)} %fusion.17), channel_id=1, source_target_pairs={{0,14},{2,0},{4,2},{6,4},{8,6},{10,8},{12,10},{14,12},{1,15},{3,1}... | collective-permute-start | bytes 491528 | tf_op jit(solution)/shard_map/ppermute | solution.py:17
  113.4 5.5 %collective-permute-start.26 = (bf16[128,640]{1,0:T(8,128)(2,1)S(1)}, bf16[128,640]{1,0:T(8,128)(2,1)S(1)}, u32[]{:S(2)}, u32[]{:S(2)}) collective-permute-start(bf16[128,640]{1,0:T(8,128)(2,1)S(1)} %fusion.14), channel_id=1, source_target_pairs={{0,2},{2,4},{4,6},{6,8},{8,10},{10,12},{12,14},{14,0},{1,3},{3,5},... | collective-permute-start | bytes 491528 | tf_op jit(solution)/shard_map/ppermute | solution.py:17
  113.8 5.7 %collective-permute-start.30 = (bf16[128,640]{1,0:T(8,128)(2,1)S(1)}, bf16[128,640]{1,0:T(8,128)(2,1)S(1)}, u32[]{:S(2)}, u32[]{:S(2)}) collective-permute-start(bf16[128,640]{1,0:T(8,128)(2,1)S(1)} %fusion.16), channel_id=1, source_target_pairs={{0,14},{2,0},{4,2},{6,4},{8,6},{10,8},{12,10},{14,12},{1,15},{3,1}... | collective-permute-start | bytes 491528 | tf_op jit(solution)/shard_map/ppermute | solution.py:17
  119.2 5.5 %collective-permute-start.27 = (bf16[128,640]{1,0:T(8,128)(2,1)S(1)}, bf16[128,640]{1,0:T(8,128)(2,1)S(1)}, u32[]{:S(2)}, u32[]{:S(2)}) collective-permute-start(bf16[128,640]{1,0:T(8,128)(2,1)S(1)} %fusion.13), channel_id=1, source_target_pairs={{0,2},{2,4},{4,6},{6,8},{8,10},{10,12},{12,14},{14,0},{1,3},{3,5},... | collective-permute-start | bytes 491528 | tf_op jit(solution)/shard_map/ppermute | solution.py:17

commit v3 on v2

--- a/solution.py
+++ b/solution.py
@@ -9,7 +9,7 @@
 LANES = 128
 EPSILON = 1e-05
 BF, F32 = jnp.bfloat16, jnp.float32
-FIRST, LAST = (0, 1, 7, 2, 6), (3, 5, 4)
+ORDER = (0, 1, 7, 2, 6, 3, 5, 4)
 
 
 def shift(array, axis, by):
@@ -26,16 +26,18 @@
     return lax.ppermute(rows, ("section", "x"), pairs)
 
 
-def gather_z(block):
-    up = down = block
-    held = {0: block}
+def gather_z(blocks):
+    ups, downs = list(blocks), list(blocks)
+    held = {0: list(blocks)}
     for step in range(1, Z // 2 + 1):
-        up = shift(up, "z", 1)
-        held[step] = up
+        for i in range(len(blocks)):
+            ups[i] = shift(ups[i], "z", 1)
+            if step < Z // 2:
+                downs[i] = shift(downs[i], "z", -1)
+        held[step] = list(ups)
         if step < Z // 2:
-            down = shift(down, "z", -1)
-            held[Z - step] = down
-    return held
+            held[Z - step] = list(downs)
+    return [jnp.concatenate([held[k][i] for k in ORDER], 0) for i in range(len(blocks))]
 
 
 def add(a, b):
@@ -58,34 +60,31 @@
         for k in range(X)
     ]
 
-    line = jnp.zeros((X * rows_each, width + LANES), BF)
-    for k in range(X):
-        line = lax.dynamic_update_slice(
-            line, handoff(carried[0], k), (lax.rem(x + X - k, X) * rows_each, 0)
-        )
+    came = [handoff(carried[0], k) for k in range(X)]
+    line = [lax.select_n(lax.rem(x + X - j, X), *came) for j in range(X)]
     dest = jnp.broadcast_to(destination[0].astype(BF), (rows_each, LANES))
-    line = lax.dynamic_update_slice(line, dest, (0, width))
-    held = gather_z(line)
+    dest = jnp.concatenate([dest, jnp.zeros(((X - 1) * rows_each, LANES), BF)], 0)
+    line = jnp.concatenate(line, 0)
+    left = jnp.concatenate([line[:, : width // 2], dest], 1)
+    left, right = gather_z([left, line[:, width // 2 :]])
+    dest = left.reshape(Z, X * rows_each, -1)[:, :rows_each, width // 2 :]
+    rows = jnp.concatenate([left[:, : width // 2], right], 1)
 
     gain = norm_gain[0].astype(F32)
     contract = (((1,), (1,)), ((), ()))
-
-    def hidden_of(order):
-        floated = jnp.concatenate([held[k] for k in order], 0)[:, :width].astype(F32)
-        scale = lax.rsqrt(jnp.mean(floated * floated, axis=-1, keepdims=True) + EPSILON)
-        normed = (floated * scale * gain).astype(BF)
-        gate = lax.dot_general(normed, gate_mat, contract, preferred_element_type=F32)
-        up = lax.dot_general(normed, up_mat, contract, preferred_element_type=F32)
-        return (jax.nn.silu(gate) * up).astype(BF)
-
-    hidden = jnp.concatenate([hidden_of(FIRST), hidden_of(LAST)], 0)
-    order = FIRST + LAST
+    floated = rows.astype(F32)
+    scale = lax.rsqrt(jnp.mean(floated * floated, axis=-1, keepdims=True) + EPSILON)
+    normed = (floated * scale * gain).astype(BF)
+    gate = lax.dot_general(normed, gate_mat, contract, preferred_element_type=F32)
+    up = lax.dot_general(normed, up_mat, contract, preferred_element_type=F32)
+    hidden = (jax.nn.silu(gate) * up).astype(BF)
 
     def part(k):
         return jnp.dot(hidden, down_part[k], preferred_element_type=F32)
 
     half = quarter // 2
     far = part(2).astype(BF)
+    far, dest = lax.optimization_barrier((far, dest))
     up = shift(far[:, :half], "x", 1)
     down = shift(far[:, half:], "x", -1)
     near = part(1)
@@ -101,21 +100,21 @@
         theirs = lax.dynamic_slice_in_dim(array, (1 - core) * eighth, eighth, 1)
         return jnp.concatenate([mine, shift(theirs, "core", 1)], 0)
 
-    kept = jnp.concatenate([held[k][:, :width] for k in order], 0)
-    residual = swap(lax.dynamic_slice_in_dim(kept, x * quarter, quarter, 1))
+    residual = swap(lax.dynamic_slice_in_dim(rows, x * quarter, quarter, 1))
 
-    dest = jnp.concatenate([held[k][:rows_each, width:] for k in order], 0)
     dests = jnp.zeros((X,) + dest.shape, BF)
     for k in range(X):
         there = shift(dest, "x", k) if k else dest
-        dests = lax.dynamic_update_slice(dests, there[None], (lax.rem(x + X - k, X), 0, 0))
-    dests = dests.reshape(X, Z, rows_each, LANES).transpose(1, 0, 2, 3)
+        dests = lax.dynamic_update_slice(
+            dests, there[None], (lax.rem(x + X - k, X), 0, 0, 0)
+        )
+    dests = dests.transpose(1, 0, 2, 3)
     dests = dests.reshape(total // CORES, LANES)
     dest = jnp.concatenate([dests, shift(dests, "core", 1)], 0)[:, 0].astype(jnp.int32)
     index = jnp.arange(total, dtype=jnp.int32)
     block = (index // (X * rows_each)) % Z
     behind = jnp.zeros_like(block)
-    for i, k in enumerate(order):
+    for i, k in enumerate(ORDER):
         behind = jnp.where(block == i, k, behind)
     source_core = jnp.where(index < total // CORES, core, 1 - core)
     source = ((index // rows_each) % X) * Z + lax.rem(z + Z - behind, Z)
@@ -137,18 +136,24 @@
     def slotted(k):
         return jnp.dot(pick(k), summed, preferred_element_type=F32)
 
-    up = slotted(Z // 2)
-    for k in range(Z // 2 - 1, -1, -1):
-        up = shift(up.astype(BF), "z", 1)
-        if k:
-            up = add(slotted(k), up)
-    down = slotted(Z // 2 + 1)
-    for k in range(Z // 2 + 2, Z + 1):
-        down = shift(down.astype(BF), "z", -1)
-        if k < Z:
-            down = add(slotted(k), down)
+    def message(*steps):
+        return jnp.concatenate([slotted(k % Z).astype(BF) for k in steps], 0)
+
+    middle = slots // 2
+    up_near = shift(message(3, 1), "z", 1)
+    down_near = shift(message(-3, -1), "z", -1)
+    opposite = message(4)
+    up_far = shift(opposite[:middle], "z", 2)
+    down_far = shift(opposite[middle:], "z", -2)
+    up = add(slotted(2), up_near[:slots])
+    up = jnp.concatenate([add(up[:middle], up_far), up[middle:]], 0)
+    down = add(slotted(6), down_near[:slots])
+    down = jnp.concatenate([down[:middle], add(down[middle:], down_far)], 0)
+    up = shift(up.astype(BF), "z", 2)
+    down = shift(down.astype(BF), "z", -2)
     mine = slotted(0) + jnp.dot(pick(0), residual, preferred_element_type=F32)
-    mixed = (mine + up.astype(F32) + down.astype(F32)).astype(BF)
+    near = add(up_near[slots:], down_near[slots:])
+    mixed = (mine + near + add(up, down)).astype(BF)
 
     pieces = lax.all_to_all(
         mixed.reshape(X * CORES, SLOTS, eighth), ("x", "core"), 0, 0, tiled=True

time: 140 us -> 149 us (1.064)
  starting transfers between devices: 54 us -> 70.4 us
  waiting for transfers between devices: 55.3 us -> 52.2 us
  matrix products: 10.4 us -> 7.48 us
  blocking collectives: 14.3 us -> 12 us
    ppermute x27 -> x33, starting transfers between devices: 46.9 us -> 63.2 us  [shift(): return lax.ppermute(array, axis, [(i, (i + by) % n) for i in range(n)])]
    dot_general x4 -> x2, matrix products: 5.89 us -> 2.85 us  [the longest x1 1.43 us: body(): lax.dot_general(normed, gate_mat, contract, preferred_element_type=F32)]
    ppermute x4, waiting for transfers between devices: 5.22 us -> 2.49 us  [handoff(): return lax.ppermute(rows, ('section', 'x'), pairs)]
    all_to_all x1, blocking collectives: 14.3 us -> 12 us  [body(): lax.all_to_all(mixed.reshape(X * CORES, SLOTS, eighth), ('x', 'core'), 0,...]
    ppermute x27 -> x33, waiting for transfers between devices: 50.1 us -> 49.7 us  [shift(): return lax.ppermute(array, axis, [(i, (i + by) % n) for i in range(n)])]
  transfers between devices with their start and end apart: 31 -> 37, of which waited for: 13 -> 15; matrix products, arithmetic and copies ran while one was open for 10% -> 7% of each run, Pallas kernels for 0% -> 0%
where the time goes in v3:
time: 149 us
  starting transfers between devices  70.4 us (47%)
  waiting for transfers between devices  52.2 us (35%)
  blocking collectives  12 us (8%)
  matrix products  7.48 us (5%)
  other arithmetic  3.64 us (2%)
  local copies, waits for them, and re-layouts  2.73 us (2%)
    ppermute x33, starting transfers between devices, shift(): return lax.ppermute(array, axis, [(i, (i + by) % n) for i in range(n)])  63.2 us
    ppermute x33, waiting for transfers between devices, shift(): return lax.ppermute(array, axis, [(i, (i + by) % n) for i in range(n)])  49.7 us
    all_to_all x1, blocking collectives, body(): lax.all_to_all(mixed.reshape(X * CORES, SLOTS, eighth), ('x', 'core'), 0,...  12 us
    ppermute x4, starting transfers between devices, handoff(): return lax.ppermute(rows, ('section', 'x'), pairs)  7.18 us
  transfers between devices with their start and end apart: 37, of which 15 were waited for; matrix products, arithmetic and copies ran while one was open for 7% of the time, Pallas kernels for 0%

profile of v3, /device:TPU:1, one launch (start us, length us, event | category | flops | bytes accessed | tf_op | source)
XLA Modules:
  0.0 149.1 jit_solution(12318548991850482958)
XLA Ops:
  0.0 4.3 %collective-permute-start.3 = (bf16[8,5120]{1,0:T(8,128)(2,1)}, bf16[8,5120]{1,0:T(8,128)(2,1)S(1)}, u32[]{:S(2)}, u32[]{:S(2)}) collective-permute-start(bf16[8,5120]{1,0:T(8,128)(2,1)} %bitcast.47), channel_id=1, source_target_pairs={{0,112},{16,64},{32,80},{48,96},{64,176},{80,128},{96,144},{112,16... | collective-permute-start | bytes 245768 | tf_op jit(solution)/shard_map/ppermute | solution.py:26
  4.3 1.5 %collective-permute-start.2 = (bf16[8,5120]{1,0:T(8,128)(2,1)}, bf16[8,5120]{1,0:T(8,128)(2,1)S(1)}, u32[]{:S(2)}, u32[]{:S(2)}) collective-permute-start(bf16[8,5120]{1,0:T(8,128)(2,1)} %bitcast.48), channel_id=1, source_target_pairs={{0,96},{16,112},{32,64},{48,80},{64,160},{80,176},{96,128},{112,14... | collective-permute-start | bytes 245768 | tf_op jit(solution)/shard_map/ppermute | solution.py:26
  5.9 1.3 collective-permute-start.1
  7.2 1.7 %collective-permute-start.18 = (bf16[216,5120]{1,0:T(8,128)(2,1)}, bf16[216,5120]{1,0:T(8,128)(2,1)S(1)}, u32[]{:S(2)}, u32[]{:S(2)}) collective-permute-start(bf16[216,5120]{1,0:T(8,128)(2,1)} %bitcast.43), channel_id=1, source_target_pairs={{0,1},{1,0},{2,3},{3,2},{4,5},{5,4},{6,7},{7,6},{8,9},{9,8},{10,11... | collective-permute-start | bytes 6635528 | tf_op jit(solution)/shard_map/ppermute | solution.py:17
  8.9 0.7 convert_bitcast_fusion
  9.6 0.7 mul.123
  10.6 0.9 collective-permute-done.2
  11.5 2.6 %collective-permute-start.20 = (bf16[216,5120]{1,0:T(8,128)(2,1)}, bf16[216,5120]{1,0:T(8,128)(2,1)S(1)}, u32[]{:S(2)}, u32[]{:S(2)}) collective-permute-start(bf16[216,5120]{1,0:T(8,128)(2,1)} %bitcast.31), channel_id=1, source_target_pairs={{0,1},{1,0},{2,3},{3,2},{4,5},{5,4},{6,7},{7,6},{8,9},{9,8},{10,11... | collective-permute-start | bytes 6635528 | tf_op jit(solution)/shard_map/ppermute | solution.py:17
  14.0 1.6 %collective-permute-done = bf16[8,5120]{1,0:T(8,128)(2,1)S(1)} collective-permute-done((bf16[8,5120]{1,0:T(8,128)(2,1)}, bf16[8,5120]{1,0:T(8,128)(2,1)S(1)}, u32[]{:S(2)}, u32[]{:S(2)}) %collective-permute-start) | collective-permute-done | bytes 81952 | tf_op jit(solution)/shard_map/ppermute | solution.py:26
  15.8 5.7 %collective-permute-start.12 = (bf16[32,2560]{1,0:T(8,128)(2,1)S(1)}, bf16[32,2560]{1,0:T(8,128)(2,1)S(1)}, u32[]{:S(2)}, u32[]{:S(2)}) collective-permute-start(bf16[32,2560]{1,0:T(8,128)(2,1)S(1)} %get-tuple-element.17), channel_id=1, source_target_pairs={{0,14},{2,0},{4,2},{6,4},{8,6},{10,8},{12,10},{14,12},{1,15},{3,1}... | collective-permute-start | bytes 491528 | tf_op jit(solution)/shard_map/ppermute | solution.py:17
  21.5 5.6 %collective-permute-done.11 = bf16[32,2560]{1,0:T(8,128)(2,1)S(1)} collective-permute-done((bf16[32,2560]{1,0:T(8,128)(2,1)S(1)}, bf16[32,2560]{1,0:T(8,128)(2,1)S(1)}, u32[]{:S(2)}, u32[]{:S(2)}) %collective-permute-start.11) | collective-permute-done | bytes 163872 | tf_op jit(solution)/shard_map/ppermute | solution.py:17
  27.2 2.7 %collective-permute-start.5 = (bf16[32,2688]{1,0:T(8,128)(2,1)S(1)}, bf16[32,2688]{1,0:T(8,128)(2,1)S(1)}, u32[]{:S(2)}, u32[]{:S(2)}) collective-permute-start(bf16[32,2688]{1,0:T(8,128)(2,1)S(1)} %get-tuple-element.24), channel_id=1, source_target_pairs={{0,14},{2,0},{4,2},{6,4},{8,6},{10,8},{12,10},{14,12},{1,15},{3,1}... | collective-permute-start | bytes 516104 | tf_op jit(solution)/shard_map/ppermute | solution.py:17
  30.0 2.7 %collective-permute-done.4 = bf16[32,2688]{1,0:T(8,128)(2,1)S(1)} collective-permute-done((bf16[32,2688]{1,0:T(8,128)(2,1)S(1)}, bf16[32,2688]{1,0:T(8,128)(2,1)S(1)}, u32[]{:S(2)}, u32[]{:S(2)}) %collective-permute-start.4) | collective-permute-done | bytes 172064 | tf_op jit(solution)/shard_map/ppermute | solution.py:17
  32.7 1.5 %collective-permute-start.13 = (bf16[32,2560]{1,0:T(8,128)(2,1)S(1)}, bf16[32,2560]{1,0:T(8,128)(2,1)S(1)}, u32[]{:S(2)}, u32[]{:S(2)}) collective-permute-start(bf16[32,2560]{1,0:T(8,128)(2,1)S(1)} %collective-permute-done.11), channel_id=1, source_target_pairs={{0,2},{2,4},{4,6},{6,8},{8,10},{10,12},{12,14},{14,0},{1,3},{3,5},... | collective-permute-start | bytes 491528 | tf_op jit(solution)/shard_map/ppermute | solution.py:17
  34.2 3.9 %collective-permute-done.13 = bf16[32,2560]{1,0:T(8,128)(2,1)S(1)} collective-permute-done((bf16[32,2560]{1,0:T(8,128)(2,1)S(1)}, bf16[32,2560]{1,0:T(8,128)(2,1)S(1)}, u32[]{:S(2)}, u32[]{:S(2)}) %collective-permute-start.13) | collective-permute-done | bytes 163872 | tf_op jit(solution)/shard_map/ppermute | solution.py:17
  38.1 0.5 collective-permute-start.6
  38.7 2.2 %collective-permute-start.7 = (bf16[32,2688]{1,0:T(8,128)(2,1)S(1)}, bf16[32,2688]{1,0:T(8,128)(2,1)S(1)}, u32[]{:S(2)}, u32[]{:S(2)}) collective-permute-start(bf16[32,2688]{1,0:T(8,128)(2,1)S(1)} %collective-permute-done.5), channel_id=1, source_target_pairs={{0,14},{2,0},{4,2},{6,4},{8,6},{10,8},{12,10},{14,12},{1,15},{3,1}... | collective-permute-start | bytes 516104 | tf_op jit(solution)/shard_map/ppermute | solution.py:17
  40.9 4.5 %collective-permute-done.6 = bf16[32,2688]{1,0:T(8,128)(2,1)S(1)} collective-permute-done((bf16[32,2688]{1,0:T(8,128)(2,1)S(1)}, bf16[32,2688]{1,0:T(8,128)(2,1)S(1)}, u32[]{:S(2)}, u32[]{:S(2)}) %collective-permute-start.6) | collective-permute-done | bytes 172064 | tf_op jit(solution)/shard_map/ppermute | solution.py:17
  45.4 1.7 %collective-permute-start.15 = (bf16[32,2560]{1,0:T(8,128)(2,1)S(1)}, bf16[32,2560]{1,0:T(8,128)(2,1)S(1)}, u32[]{:S(2)}, u32[]{:S(2)}) collective-permute-start(bf16[32,2560]{1,0:T(8,128)(2,1)S(1)} %collective-permute-done.13), channel_id=1, source_target_pairs={{0,2},{2,4},{4,6},{6,8},{8,10},{10,12},{12,14},{14,0},{1,3},{3,5},... | collective-permute-start | bytes 491528 | tf_op jit(solution)/shard_map/ppermute | solution.py:17
  47.2 5.5 %collective-permute-done.15 = bf16[32,2560]{1,0:T(8,128)(2,1)S(1)} collective-permute-done((bf16[32,2560]{1,0:T(8,128)(2,1)S(1)}, bf16[32,2560]{1,0:T(8,128)(2,1)S(1)}, u32[]{:S(2)}, u32[]{:S(2)}) %collective-permute-start.15) | collective-permute-done | bytes 163872 | tf_op jit(solution)/shard_map/ppermute | solution.py:17
  52.7 2.7 %collective-permute-start.9 = (bf16[32,2688]{1,0:T(8,128)(2,1)S(1)}, bf16[32,2688]{1,0:T(8,128)(2,1)S(1)}, u32[]{:S(2)}, u32[]{:S(2)}) collective-permute-start(bf16[32,2688]{1,0:T(8,128)(2,1)S(1)} %collective-permute-done.7), channel_id=1, source_target_pairs={{0,14},{2,0},{4,2},{6,4},{8,6},{10,8},{12,10},{14,12},{1,15},{3,1}... | collective-permute-start | bytes 516104 | tf_op jit(solution)/shard_map/ppermute | solution.py:17
  55.5 3.0 %collective-permute-done.8 = bf16[32,2688]{1,0:T(8,128)(2,1)S(1)} collective-permute-done((bf16[32,2688]{1,0:T(8,128)(2,1)S(1)}, bf16[32,2688]{1,0:T(8,128)(2,1)S(1)}, u32[]{:S(2)}, u32[]{:S(2)}) %collective-permute-start.8) | collective-permute-done | bytes 172064 | tf_op jit(solution)/shard_map/ppermute | solution.py:17
  58.7 5.2 %collective-permute-done.17 = bf16[32,2560]{1,0:T(8,128)(2,1)S(1)} collective-permute-done((bf16[32,2560]{1,0:T(8,128)(2,1)S(1)}, bf16[32,2560]{1,0:T(8,128)(2,1)S(1)}, u32[]{:S(2)}, u32[]{:S(2)}) %collective-permute-start.17) | collective-permute-done | bytes 163872 | tf_op jit(solution)/shard_map/ppermute | solution.py:17
  63.9 3.1 %collective-permute-done.10 = bf16[32,2688]{1,0:T(8,128)(2,1)S(1)} collective-permute-done((bf16[32,2688]{1,0:T(8,128)(2,1)S(1)}, bf16[32,2688]{1,0:T(8,128)(2,1)S(1)}, u32[]{:S(2)}, u32[]{:S(2)}) %collective-permute-start.10) | collective-permute-done | bytes 172064 | tf_op jit(solution)/shard_map/ppermute | solution.py:17
  67.2 0.6 fusion
  67.8 1.0 copy-done.1
  68.8 1.4 fusion.3
  70.4 1.4 multiply_convert_fusion
  72.4 1.0 collective-permute-start.23
  73.4 0.6 collective-permute-start.22
  74.1 0.8 collective-permute-start.21
  74.9 1.3 collective-permute-start.25
  76.2 1.4 collective-permute-start.27
  78.2 0.5 fusion.16
  78.9 3.2 %collective-permute-done.25 = bf16[256,640]{1,0:T(8,128)(2,1)S(1)} collective-permute-done((bf16[256,640]{1,0:T(8,128)(2,1)S(1)}, bf16[256,640]{1,0:T(8,128)(2,1)S(1)}, u32[]{:S(2)}, u32[]{:S(2)}) %collective-permute-start.25) | collective-permute-done | bytes 327712 | tf_op jit(solution)/shard_map/ppermute | solution.py:17
  82.7 2.7 %collective-permute-start.28 = (bf16[256,1280]{1,0:T(8,128)(2,1)S(1)}, bf16[256,1280]{1,0:T(8,128)(2,1)S(1)}, u32[]{:S(2)}, u32[]{:S(2)}) collective-permute-start(bf16[256,1280]{1,0:T(8,128)(2,1)S(1)} %pad_maximum_fusion.2), channel_id=1, source_target_pairs={{0,48},{16,0},{32,16},{48,32},{1,49},{17,1},{33,17},{49,33},{2,50}... | collective-permute-start | bytes 1966088 | tf_op jit(solution)/shard_map/ppermute | solution.py:17
  85.4 15.8 %collective-permute-start.24 = (bf16[256,128]{1,0:T(8,128)(2,1)S(1)}, bf16[256,128]{1,0:T(8,128)(2,1)S(1)}, u32[]{:S(2)}, u32[]{:S(2)}) collective-permute-start(bf16[256,128]{1,0:T(8,128)(2,1)S(1)} %bitcast.38), channel_id=1, source_target_pairs={{0,1},{1,0},{2,3},{3,2},{4,5},{5,4},{6,7},{7,6},{8,9},{9,8},{10,11... | collective-permute-start | bytes 196616 | tf_op jit(solution)/shard_map/ppermute | solution.py:17
  101.2 0.6 fusion.31
  102.3 0.6 fusion.11
  103.0 7.2 %collective-permute-start.29 = (bf16[256,640]{1,0:T(8,128)(2,1)S(1)}, bf16[256,640]{1,0:T(8,128)(2,1)S(1)}, u32[]{:S(2)}, u32[]{:S(2)}) collective-permute-start(bf16[256,640]{1,0:T(8,128)(2,1)S(1)} %get-tuple-element.14), channel_id=1, source_target_pairs={{0,1},{1,0},{2,3},{3,2},{4,5},{5,4},{6,7},{7,6},{8,9},{9,8},{10,11... | collective-permute-start | bytes 983048 | tf_op jit(solution)/shard_map/ppermute | solution.py:17
  110.5 0.9 collective-permute-done.29
  111.8 3.6 %collective-permute-start.35 = (bf16[64,640]{1,0:T(8,128)(2,1)S(1)}, bf16[64,640]{1,0:T(8,128)(2,1)S(1)}, u32[]{:S(2)}, u32[]{:S(2)}) collective-permute-start(bf16[64,640]{1,0:T(8,128)(2,1)S(1)} %get-tuple-element.27), channel_id=1, source_target_pairs={{0,12},{2,14},{4,0},{6,2},{8,4},{10,6},{12,8},{14,10},{1,13},{3,15... | collective-permute-start | bytes 245768 | tf_op jit(solution)/shard_map/ppermute | solution.py:17
  116.7 2.7 %collective-permute-start.32 = (bf16[256,640]{1,0:T(8,128)(2,1)S(1)}, bf16[256,640]{1,0:T(8,128)(2,1)S(1)}, u32[]{:S(2)}, u32[]{:S(2)}) collective-permute-start(bf16[256,640]{1,0:T(8,128)(2,1)S(1)} %pad_maximum_fusion.6), channel_id=1, source_target_pairs={{0,14},{2,0},{4,2},{6,4},{8,6},{10,8},{12,10},{14,12},{1,15},{3,1}... | collective-permute-start | bytes 983048 | tf_op jit(solution)/shard_map/ppermute | solution.py:17
  119.4 6.1 %collective-permute-done.31 = bf16[256,640]{1,0:T(8,128)(2,1)S(1)} collective-permute-done((bf16[256,640]{1,0:T(8,128)(2,1)S(1)}, bf16[256,640]{1,0:T(8,128)(2,1)S(1)}, u32[]{:S(2)}, u32[]{:S(2)}) %collective-permute-start.31) | collective-permute-done | bytes 327712 | tf_op jit(solution)/shard_map/ppermute | solution.py:17
  126.4 3.6 %collective-permute-start.36 = (bf16[128,640]{1,0:T(8,128)(2,1)S(1)}, bf16[128,640]{1,0:T(8,128)(2,1)S(1)}, u32[]{:S(2)}, u32[]{:S(2)}) collective-permute-start(bf16[128,640]{1,0:T(8,128)(2,1)S(1)} %pad_maximum_fusion.9), channel_id=1, source_target_pairs={{0,12},{2,14},{4,0},{6,2},{8,4},{10,6},{12,8},{14,10},{1,13},{3,15... | collective-permute-start | bytes 491528 | tf_op jit(solution)/shard_map/ppermute | solution.py:17
  130.3 5.7 %collective-permute-done.34 = bf16[128,640]{1,0:T(8,128)(2,1)S(1)} collective-permute-done((bf16[128,640]{1,0:T(8,128)(2,1)S(1)}, bf16[128,640]{1,0:T(8,128)(2,1)S(1)}, u32[]{:S(2)}, u32[]{:S(2)}) %collective-permute-start.34) | collective-permute-done | bytes 163872 | tf_op jit(solution)/shard_map/ppermute | solution.py:17
  136.3 12.0 %all_to_all.5 = bf16[8,16,640]{2,1,0:T(8,128)(2,1)S(1)} all-to-all(bf16[8,16,640]{2,1,0:T(8,128)(2,1)S(1)} %bitcast.40), channel_id=1, replica_groups=mesh['section'=4,'x'=4,'z'=8,'core'=2] {'x','core'}, dimensions={0} | all-to-all | bytes 327680 | tf_op jit(solution)/shard_map/all_to_all | solution.py:158
  148.3 0.7 reshape.286
  (105 shorter events, 6.8 us)
Async XLA Ops:
  0.0 10.4 %collective-permute-start.3 = (bf16[8,5120]{1,0:T(8,128)(2,1)}, bf16[8,5120]{1,0:T(8,128)(2,1)S(1)}, u32[]{:S(2)}, u32[]{:S(2)}) collective-permute-start(bf16[8,5120]{1,0:T(8,128)(2,1)} %bitcast.47), channel_id=1, source_target_pairs={{0,112},{16,64},{32,80},{48,96},{64,176},{80,128},{96,144},{112,16... | collective-permute-start | bytes 245768 | tf_op jit(solution)/shard_map/ppermute | solution.py:26
  4.3 7.2 %collective-permute-start.2 = (bf16[8,5120]{1,0:T(8,128)(2,1)}, bf16[8,5120]{1,0:T(8,128)(2,1)S(1)}, u32[]{:S(2)}, u32[]{:S(2)}) collective-permute-start(bf16[8,5120]{1,0:T(8,128)(2,1)} %bitcast.48), channel_id=1, source_target_pairs={{0,96},{16,112},{32,64},{48,80},{64,160},{80,176},{96,128},{112,14... | collective-permute-start | bytes 245768 | tf_op jit(solution)/shard_map/ppermute | solution.py:26
  5.9 8.2 %collective-permute-start.1 = (bf16[8,5120]{1,0:T(8,128)(2,1)}, bf16[8,5120]{1,0:T(8,128)(2,1)S(1)}, u32[]{:S(2)}, u32[]{:S(2)}) collective-permute-start(bf16[8,5120]{1,0:T(8,128)(2,1)} %bitcast.49), channel_id=1, source_target_pairs={{0,80},{16,96},{32,112},{48,64},{64,144},{80,160},{96,176},{112,12... | collective-permute-start | bytes 245768 | tf_op jit(solution)/shard_map/ppermute | solution.py:26
  7.2 8.5 %collective-permute-start = (bf16[8,5120]{1,0:T(8,128)(2,1)}, bf16[8,5120]{1,0:T(8,128)(2,1)S(1)}, u32[]{:S(2)}, u32[]{:S(2)}) collective-permute-start(bf16[8,5120]{1,0:T(8,128)(2,1)} %bitcast.50), channel_id=1, source_target_pairs={{0,64},{16,80},{32,96},{48,112},{64,128},{80,144},{96,160},{112,17... | collective-permute-start | bytes 245768 | tf_op jit(solution)/shard_map/ppermute | solution.py:26
  7.2 60.6 %collective-permute-start.18 = (bf16[216,5120]{1,0:T(8,128)(2,1)}, bf16[216,5120]{1,0:T(8,128)(2,1)S(1)}, u32[]{:S(2)}, u32[]{:S(2)}) collective-permute-start(bf16[216,5120]{1,0:T(8,128)(2,1)} %bitcast.43), channel_id=1, source_target_pairs={{0,1},{1,0},{2,3},{3,2},{4,5},{5,4},{6,7},{7,6},{8,9},{9,8},{10,11... | collective-permute-start | bytes 6635528 | tf_op jit(solution)/shard_map/ppermute | solution.py:17
  10.4 59.8 %collective-permute-start.19 = (bf16[216,5120]{1,0:T(8,128)(2,1)}, bf16[216,5120]{1,0:T(8,128)(2,1)S(1)}, u32[]{:S(2)}, u32[]{:S(2)}) collective-permute-start(bf16[216,5120]{1,0:T(8,128)(2,1)} %bitcast.45), channel_id=1, source_target_pairs={{0,1},{1,0},{2,3},{3,2},{4,5},{5,4},{6,7},{7,6},{8,9},{9,8},{10,11... | collective-permute-start | bytes 6635528 | tf_op jit(solution)/shard_map/ppermute | solution.py:17
  11.5 60.3 %collective-permute-start.20 = (bf16[216,5120]{1,0:T(8,128)(2,1)}, bf16[216,5120]{1,0:T(8,128)(2,1)S(1)}, u32[]{:S(2)}, u32[]{:S(2)}) collective-permute-start(bf16[216,5120]{1,0:T(8,128)(2,1)} %bitcast.31), channel_id=1, source_target_pairs={{0,1},{1,0},{2,3},{3,2},{4,5},{5,4},{6,7},{7,6},{8,9},{9,8},{10,11... | collective-permute-start | bytes 6635528 | tf_op jit(solution)/shard_map/ppermute | solution.py:17
  15.8 11.4 %collective-permute-start.12 = (bf16[32,2560]{1,0:T(8,128)(2,1)S(1)}, bf16[32,2560]{1,0:T(8,128)(2,1)S(1)}, u32[]{:S(2)}, u32[]{:S(2)}) collective-permute-start(bf16[32,2560]{1,0:T(8,128)(2,1)S(1)} %get-tuple-element.17), channel_id=1, source_target_pairs={{0,14},{2,0},{4,2},{6,4},{8,6},{10,8},{12,10},{14,12},{1,15},{3,1}... | collective-permute-start | bytes 491528 | tf_op jit(solution)/shard_map/ppermute | solution.py:17
  21.4 5.7 %collective-permute-start.11 = (bf16[32,2560]{1,0:T(8,128)(2,1)S(1)}, bf16[32,2560]{1,0:T(8,128)(2,1)S(1)}, u32[]{:S(2)}, u32[]{:S(2)}) collective-permute-start(bf16[32,2560]{1,0:T(8,128)(2,1)S(1)} %get-tuple-element.17), channel_id=1, source_target_pairs={{0,2},{2,4},{4,6},{6,8},{8,10},{10,12},{12,14},{14,0},{1,3},{3,5},... | collective-permute-start | bytes 491528 | tf_op jit(solution)/shard_map/ppermute | solution.py:17
  27.2 5.5 %collective-permute-start.4 = (bf16[32,2688]{1,0:T(8,128)(2,1)S(1)}, bf16[32,2688]{1,0:T(8,128)(2,1)S(1)}, u32[]{:S(2)}, u32[]{:S(2)}) collective-permute-start(bf16[32,2688]{1,0:T(8,128)(2,1)S(1)} %get-tuple-element.24), channel_id=1, source_target_pairs={{0,2},{2,4},{4,6},{6,8},{8,10},{10,12},{12,14},{14,0},{1,3},{3,5},... | collective-permute-start | bytes 516104 | tf_op jit(solution)/shard_map/ppermute | solution.py:17
  27.2 5.5 %collective-permute-start.5 = (bf16[32,2688]{1,0:T(8,128)(2,1)S(1)}, bf16[32,2688]{1,0:T(8,128)(2,1)S(1)}, u32[]{:S(2)}, u32[]{:S(2)}) collective-permute-start(bf16[32,2688]{1,0:T(8,128)(2,1)S(1)} %get-tuple-element.24), channel_id=1, source_target_pairs={{0,14},{2,0},{4,2},{6,4},{8,6},{10,8},{12,10},{14,12},{1,15},{3,1}... | collective-permute-start | bytes 516104 | tf_op jit(solution)/shard_map/ppermute | solution.py:17
  32.6 6.1 %collective-permute-start.14 = (bf16[32,2560]{1,0:T(8,128)(2,1)S(1)}, bf16[32,2560]{1,0:T(8,128)(2,1)S(1)}, u32[]{:S(2)}, u32[]{:S(2)}) collective-permute-start(bf16[32,2560]{1,0:T(8,128)(2,1)S(1)} %collective-permute-done.12), channel_id=1, source_target_pairs={{0,14},{2,0},{4,2},{6,4},{8,6},{10,8},{12,10},{14,12},{1,15},{3,1}... | collective-permute-start | bytes 491528 | tf_op jit(solution)/shard_map/ppermute | solution.py:17
  32.7 5.5 %collective-permute-start.13 = (bf16[32,2560]{1,0:T(8,128)(2,1)S(1)}, bf16[32,2560]{1,0:T(8,128)(2,1)S(1)}, u32[]{:S(2)}, u32[]{:S(2)}) collective-permute-start(bf16[32,2560]{1,0:T(8,128)(2,1)S(1)} %collective-permute-done.11), channel_id=1, source_target_pairs={{0,2},{2,4},{4,6},{6,8},{8,10},{10,12},{12,14},{14,0},{1,3},{3,5},... | collective-permute-start | bytes 491528 | tf_op jit(solution)/shard_map/ppermute | solution.py:17
  38.1 7.3 %collective-permute-start.6 = (bf16[32,2688]{1,0:T(8,128)(2,1)S(1)}, bf16[32,2688]{1,0:T(8,128)(2,1)S(1)}, u32[]{:S(2)}, u32[]{:S(2)}) collective-permute-start(bf16[32,2688]{1,0:T(8,128)(2,1)S(1)} %collective-permute-done.4), channel_id=1, source_target_pairs={{0,2},{2,4},{4,6},{6,8},{8,10},{10,12},{12,14},{14,0},{1,3},{3,5},... | collective-permute-start | bytes 516104 | tf_op jit(solution)/shard_map/ppermute | solution.py:17
  38.7 6.7 %collective-permute-start.7 = (bf16[32,2688]{1,0:T(8,128)(2,1)S(1)}, bf16[32,2688]{1,0:T(8,128)(2,1)S(1)}, u32[]{:S(2)}, u32[]{:S(2)}) collective-permute-start(bf16[32,2688]{1,0:T(8,128)(2,1)S(1)} %collective-permute-done.5), channel_id=1, source_target_pairs={{0,14},{2,0},{4,2},{6,4},{8,6},{10,8},{12,10},{14,12},{1,15},{3,1}... | collective-permute-start | bytes 516104 | tf_op jit(solution)/shard_map/ppermute | solution.py:17
  45.4 7.3 %collective-permute-start.16 = (bf16[32,2560]{1,0:T(8,128)(2,1)S(1)}, bf16[32,2560]{1,0:T(8,128)(2,1)S(1)}, u32[]{:S(2)}, u32[]{:S(2)}) collective-permute-start(bf16[32,2560]{1,0:T(8,128)(2,1)S(1)} %collective-permute-done.14), channel_id=1, source_target_pairs={{0,14},{2,0},{4,2},{6,4},{8,6},{10,8},{12,10},{14,12},{1,15},{3,1}... | collective-permute-start | bytes 491528 | tf_op jit(solution)/shard_map/ppermute | solution.py:17
  45.4 7.2 %collective-permute-start.15 = (bf16[32,2560]{1,0:T(8,128)(2,1)S(1)}, bf16[32,2560]{1,0:T(8,128)(2,1)S(1)}, u32[]{:S(2)}, u32[]{:S(2)}) collective-permute-start(bf16[32,2560]{1,0:T(8,128)(2,1)S(1)} %collective-permute-done.13), channel_id=1, source_target_pairs={{0,2},{2,4},{4,6},{6,8},{8,10},{10,12},{12,14},{14,0},{1,3},{3,5},... | collective-permute-start | bytes 491528 | tf_op jit(solution)/shard_map/ppermute | solution.py:17
  52.7 5.8 %collective-permute-start.8 = (bf16[32,2688]{1,0:T(8,128)(2,1)S(1)}, bf16[32,2688]{1,0:T(8,128)(2,1)S(1)}, u32[]{:S(2)}, u32[]{:S(2)}) collective-permute-start(bf16[32,2688]{1,0:T(8,128)(2,1)S(1)} %collective-permute-done.6), channel_id=1, source_target_pairs={{0,2},{2,4},{4,6},{6,8},{8,10},{10,12},{12,14},{14,0},{1,3},{3,5},... | collective-permute-start | bytes 516104 | tf_op jit(solution)/shard_map/ppermute | solution.py:17
  52.7 5.8 %collective-permute-start.9 = (bf16[32,2688]{1,0:T(8,128)(2,1)S(1)}, bf16[32,2688]{1,0:T(8,128)(2,1)S(1)}, u32[]{:S(2)}, u32[]{:S(2)}) collective-permute-start(bf16[32,2688]{1,0:T(8,128)(2,1)S(1)} %collective-permute-done.7), channel_id=1, source_target_pairs={{0,14},{2,0},{4,2},{6,4},{8,6},{10,8},{12,10},{14,12},{1,15},{3,1}... | collective-permute-start | bytes 516104 | tf_op jit(solution)/shard_map/ppermute | solution.py:17
  58.5 5.4 %collective-permute-start.17 = (bf16[32,2560]{1,0:T(8,128)(2,1)S(1)}, bf16[32,2560]{1,0:T(8,128)(2,1)S(1)}, u32[]{:S(2)}, u32[]{:S(2)}) collective-permute-start(bf16[32,2560]{1,0:T(8,128)(2,1)S(1)} %collective-permute-done.15), channel_id=1, source_target_pairs={{0,2},{2,4},{4,6},{6,8},{8,10},{10,12},{12,14},{14,0},{1,3},{3,5},... | collective-permute-start | bytes 491528 | tf_op jit(solution)/shard_map/ppermute | solution.py:17
  58.5 8.5 %collective-permute-start.10 = (bf16[32,2688]{1,0:T(8,128)(2,1)S(1)}, bf16[32,2688]{1,0:T(8,128)(2,1)S(1)}, u32[]{:S(2)}, u32[]{:S(2)}) collective-permute-start(bf16[32,2688]{1,0:T(8,128)(2,1)S(1)} %collective-permute-done.8), channel_id=1, source_target_pairs={{0,2},{2,4},{4,6},{6,8},{8,10},{10,12},{12,14},{14,0},{1,3},{3,5},... | collective-permute-start | bytes 516104 | tf_op jit(solution)/shard_map/ppermute | solution.py:17
  67.1 1.6 %copy-start.1 = (bf16[1,216,5120]{2,1,0:T(8,128)(2,1)S(1)}, bf16[1,216,5120]{2,1,0:T(8,128)(2,1)}, u32[]{:S(2)}) copy-start(bf16[1,216,5120]{2,1,0:T(8,128)(2,1)} %param.9) | copy-start | bytes 6635524
  68.8 1.6 %copy-start.2 = (bf16[1,216,5120]{2,1,0:T(8,128)(2,1)S(1)}, bf16[1,216,5120]{2,1,0:T(8,128)(2,1)}, u32[]{:S(2)}) copy-start(bf16[1,216,5120]{2,1,0:T(8,128)(2,1)} %param.10) | copy-start | bytes 6635524
  70.2 1.7 %copy-start = (bf16[1,216,5120]{2,1,0:T(8,128)(2,1)S(1)}, bf16[1,216,5120]{2,1,0:T(8,128)(2,1)}, u32[]{:S(2)}) copy-start(bf16[1,216,5120]{2,1,0:T(8,128)(2,1)} %param.11) | copy-start | bytes 6635524
  72.4 13.0 %collective-permute-start.23 = (bf16[8,8,128]{2,1,0:T(8,128)(2,1)S(1)}, bf16[8,8,128]{2,1,0:T(8,128)(2,1)S(1)}, u32[]{:S(2)}, u32[]{:S(2)}) collective-permute-start(bf16[8,8,128]{2,1,0:T(8,128)(2,1)S(1)} %slice.91), channel_id=1, source_target_pairs={{0,48},{16,0},{32,16},{48,32},{1,49},{17,1},{33,17},{49,33},{2,50}... | collective-permute-start | bytes 49160 | tf_op jit(solution)/shard_map/ppermute | solution.py:17
  73.4 5.4 %collective-permute-start.22 = (bf16[8,8,128]{2,1,0:T(8,128)(2,1)S(1)}, bf16[8,8,128]{2,1,0:T(8,128)(2,1)S(1)}, u32[]{:S(2)}, u32[]{:S(2)}) collective-permute-start(bf16[8,8,128]{2,1,0:T(8,128)(2,1)S(1)} %slice.91), channel_id=1, source_target_pairs={{0,32},{16,48},{32,0},{48,16},{1,33},{17,49},{33,1},{49,17},{2,34}... | collective-permute-start | bytes 49160 | tf_op jit(solution)/shard_map/ppermute | solution.py:17
  74.1 4.8 %collective-permute-start.21 = (bf16[8,8,128]{2,1,0:T(8,128)(2,1)S(1)}, bf16[8,8,128]{2,1,0:T(8,128)(2,1)S(1)}, u32[]{:S(2)}, u32[]{:S(2)}) collective-permute-start(bf16[8,8,128]{2,1,0:T(8,128)(2,1)S(1)} %slice.91), channel_id=1, source_target_pairs={{0,16},{16,32},{32,48},{48,0},{1,17},{17,33},{33,49},{49,1},{2,18}... | collective-permute-start | bytes 49160 | tf_op jit(solution)/shard_map/ppermute | solution.py:17
  74.9 7.2 %collective-permute-start.25 = (bf16[256,640]{1,0:T(8,128)(2,1)S(1)}, bf16[256,640]{1,0:T(8,128)(2,1)S(1)}, u32[]{:S(2)}, u32[]{:S(2)}) collective-permute-start(bf16[256,640]{1,0:T(8,128)(2,1)S(1)} %get-tuple-element.15), channel_id=1, source_target_pairs={{0,16},{16,32},{32,48},{48,0},{1,17},{17,33},{33,49},{49,1},{2,18}... | collective-permute-start | bytes 983048 | tf_op jit(solution)/shard_map/ppermute | solution.py:17
  76.2 6.4 %collective-permute-start.27 = (bf16[256,640]{1,0:T(8,128)(2,1)S(1)}, bf16[256,640]{1,0:T(8,128)(2,1)S(1)}, u32[]{:S(2)}, u32[]{:S(2)}) collective-permute-start(bf16[256,640]{1,0:T(8,128)(2,1)S(1)} %get-tuple-element.16), channel_id=1, source_target_pairs={{0,48},{16,0},{32,16},{48,32},{1,49},{17,1},{33,17},{49,33},{2,50}... | collective-permute-start | bytes 983048 | tf_op jit(solution)/shard_map/ppermute | solution.py:17
  82.2 20.1 %collective-permute-start.26 = (bf16[256,1280]{1,0:T(8,128)(2,1)S(1)}, bf16[256,1280]{1,0:T(8,128)(2,1)S(1)}, u32[]{:S(2)}, u32[]{:S(2)}) collective-permute-start(bf16[256,1280]{1,0:T(8,128)(2,1)S(1)} %pad_maximum_fusion.1), channel_id=1, source_target_pairs={{0,16},{16,32},{32,48},{48,0},{1,17},{17,33},{33,49},{49,1},{2,18}... | collective-permute-start | bytes 1966088 | tf_op jit(solution)/shard_map/ppermute | solution.py:17
  82.7 19.6 %collective-permute-start.28 = (bf16[256,1280]{1,0:T(8,128)(2,1)S(1)}, bf16[256,1280]{1,0:T(8,128)(2,1)S(1)}, u32[]{:S(2)}, u32[]{:S(2)}) collective-permute-start(bf16[256,1280]{1,0:T(8,128)(2,1)S(1)} %pad_maximum_fusion.2), channel_id=1, source_target_pairs={{0,48},{16,0},{32,16},{48,32},{1,49},{17,1},{33,17},{49,33},{2,50}... | collective-permute-start | bytes 1966088 | tf_op jit(solution)/shard_map/ppermute | solution.py:17
  85.4 16.7 %collective-permute-start.24 = (bf16[256,128]{1,0:T(8,128)(2,1)S(1)}, bf16[256,128]{1,0:T(8,128)(2,1)S(1)}, u32[]{:S(2)}, u32[]{:S(2)}) collective-permute-start(bf16[256,128]{1,0:T(8,128)(2,1)S(1)} %bitcast.38), channel_id=1, source_target_pairs={{0,1},{1,0},{2,3},{3,2},{4,5},{5,4},{6,7},{7,6},{8,9},{9,8},{10,11... | collective-permute-start | bytes 196616 | tf_op jit(solution)/shard_map/ppermute | solution.py:17
  101.8 28.2 %collective-permute-start.30 = (bf16[256,640]{1,0:T(8,128)(2,1)S(1)}, bf16[256,640]{1,0:T(8,128)(2,1)S(1)}, u32[]{:S(2)}, u32[]{:S(2)}) collective-permute-start(bf16[256,640]{1,0:T(8,128)(2,1)S(1)} %get-tuple-element.12), channel_id=1, source_target_pairs={{0,1},{1,0},{2,3},{3,2},{4,5},{5,4},{6,7},{7,6},{8,9},{9,8},{10,11... | collective-permute-start | bytes 983048 | tf_op jit(solution)/shard_map/ppermute | solution.py:17
  103.0 8.5 %collective-permute-start.29 = (bf16[256,640]{1,0:T(8,128)(2,1)S(1)}, bf16[256,640]{1,0:T(8,128)(2,1)S(1)}, u32[]{:S(2)}, u32[]{:S(2)}) collective-permute-start(bf16[256,640]{1,0:T(8,128)(2,1)S(1)} %get-tuple-element.14), channel_id=1, source_target_pairs={{0,1},{1,0},{2,3},{3,2},{4,5},{5,4},{6,7},{7,6},{8,9},{9,8},{10,11... | collective-permute-start | bytes 983048 | tf_op jit(solution)/shard_map/ppermute | solution.py:17
  111.7 14.1 %collective-permute-start.33 = (bf16[64,640]{1,0:T(8,128)(2,1)S(1)}, bf16[64,640]{1,0:T(8,128)(2,1)S(1)}, u32[]{:S(2)}, u32[]{:S(2)}) collective-permute-start(bf16[64,640]{1,0:T(8,128)(2,1)S(1)} %get-tuple-element.26), channel_id=1, source_target_pairs={{0,4},{2,6},{4,8},{6,10},{8,12},{10,14},{12,0},{14,2},{1,5},{3,7},... | collective-permute-start | bytes 245768 | tf_op jit(solution)/shard_map/ppermute | solution.py:17
  111.8 14.5 %collective-permute-start.35 = (bf16[64,640]{1,0:T(8,128)(2,1)S(1)}, bf16[64,640]{1,0:T(8,128)(2,1)S(1)}, u32[]{:S(2)}, u32[]{:S(2)}) collective-permute-start(bf16[64,640]{1,0:T(8,128)(2,1)S(1)} %get-tuple-element.27), channel_id=1, source_target_pairs={{0,12},{2,14},{4,0},{6,2},{8,4},{10,6},{12,8},{14,10},{1,13},{3,15... | collective-permute-start | bytes 245768 | tf_op jit(solution)/shard_map/ppermute | solution.py:17
  116.0 9.6 %collective-permute-start.31 = (bf16[256,640]{1,0:T(8,128)(2,1)S(1)}, bf16[256,640]{1,0:T(8,128)(2,1)S(1)}, u32[]{:S(2)}, u32[]{:S(2)}) collective-permute-start(bf16[256,640]{1,0:T(8,128)(2,1)S(1)} %pad_maximum_fusion.5), channel_id=1, source_target_pairs={{0,2},{2,4},{4,6},{6,8},{8,10},{10,12},{12,14},{14,0},{1,3},{3,5},... | collective-permute-start | bytes 983048 | tf_op jit(solution)/shard_map/ppermute | solution.py:17
  116.7 9.3 %collective-permute-start.32 = (bf16[256,640]{1,0:T(8,128)(2,1)S(1)}, bf16[256,640]{1,0:T(8,128)(2,1)S(1)}, u32[]{:S(2)}, u32[]{:S(2)}) collective-permute-start(bf16[256,640]{1,0:T(8,128)(2,1)S(1)} %pad_maximum_fusion.6), channel_id=1, source_target_pairs={{0,14},{2,0},{4,2},{6,4},{8,6},{10,8},{12,10},{14,12},{1,15},{3,1}... | collective-permute-start | bytes 983048 | tf_op jit(solution)/shard_map/ppermute | solution.py:17
  125.9 10.1 %collective-permute-start.34 = (bf16[128,640]{1,0:T(8,128)(2,1)S(1)}, bf16[128,640]{1,0:T(8,128)(2,1)S(1)}, u32[]{:S(2)}, u32[]{:S(2)}) collective-permute-start(bf16[128,640]{1,0:T(8,128)(2,1)S(1)} %pad_maximum_fusion.8), channel_id=1, source_target_pairs={{0,4},{2,6},{4,8},{6,10},{8,12},{10,14},{12,0},{14,2},{1,5},{3,7},... | collective-permute-start | bytes 491528 | tf_op jit(solution)/shard_map/ppermute | solution.py:17
  126.4 9.6 %collective-permute-start.36 = (bf16[128,640]{1,0:T(8,128)(2,1)S(1)}, bf16[128,640]{1,0:T(8,128)(2,1)S(1)}, u32[]{:S(2)}, u32[]{:S(2)}) collective-permute-start(bf16[128,640]{1,0:T(8,128)(2,1)S(1)} %pad_maximum_fusion.9), channel_id=1, source_target_pairs={{0,12},{2,14},{4,0},{6,2},{8,4},{10,6},{12,8},{14,10},{1,13},{3,15... | collective-permute-start | bytes 491528 | tf_op jit(solution)/shard_map/ppermute | solution.py:17

commit v4 on v3

--- a/solution.py
+++ b/solution.py
@@ -9,7 +9,7 @@
 LANES = 128
 EPSILON = 1e-05
 BF, F32 = jnp.bfloat16, jnp.float32
-ORDER = (0, 1, 7, 2, 6, 3, 5, 4)
+ORDER = (0, 1, -1, 2, -2, 3, -3, 4)
 
 
 def shift(array, axis, by):
@@ -19,25 +19,37 @@
 
 def handoff(rows, by):
     pairs = [
-        (s * X + x, ((s + 1) % SECTIONS) * X + (x + by) % X)
+        (s * Z + z, ((s + 1) % SECTIONS) * Z + (z + by) % Z)
         for s in range(SECTIONS)
-        for x in range(X)
+        for z in range(Z)
     ]
-    return lax.ppermute(rows, ("section", "x"), pairs)
+    return lax.ppermute(rows, ("section", "z"), pairs)
 
 
-def gather_z(blocks):
-    ups, downs = list(blocks), list(blocks)
-    held = {0: list(blocks)}
-    for step in range(1, Z // 2 + 1):
-        for i in range(len(blocks)):
-            ups[i] = shift(ups[i], "z", 1)
-            if step < Z // 2:
-                downs[i] = shift(downs[i], "z", -1)
-        held[step] = list(ups)
-        if step < Z // 2:
-            held[Z - step] = list(downs)
-    return [jnp.concatenate([held[k][i] for k in ORDER], 0) for i in range(len(blocks))]
+def gather_z(rows):
+    came = {k: handoff(rows, k) for k in (0, 1, -1, 2, -2)}
+    came[3] = shift(came[2], "z", 1)
+    came[-3] = shift(came[-2], "z", -1)
+    came[4] = shift(came[2], "z", 2)
+    return jnp.concatenate([came[k] for k in ORDER], 0)
+
+
+def gather_x(block, x):
+    size = block.shape[0]
+    half = size // 2
+    up, down = shift(block, "x", 1), shift(block, "x", -1)
+    far_up, far_down = shift(up[:half], "x", 1), shift(down[half:], "x", -1)
+    rows = jnp.zeros((X * size, block.shape[1]), block.dtype)
+    for part, behind, offset in (
+        (block, 0, 0),
+        (up, 1, 0),
+        (down, 3, 0),
+        (far_up, 2, 0),
+        (far_down, 2, half),
+    ):
+        at = lax.rem(x + X - behind, X) * size + offset
+        rows = lax.dynamic_update_slice_in_dim(rows, part, at, 0)
+    return rows
 
 
 def add(a, b):
@@ -60,15 +72,15 @@
         for k in range(X)
     ]
 
-    came = [handoff(carried[0], k) for k in range(X)]
-    line = [lax.select_n(lax.rem(x + X - j, X), *came) for j in range(X)]
     dest = jnp.broadcast_to(destination[0].astype(BF), (rows_each, LANES))
-    dest = jnp.concatenate([dest, jnp.zeros(((X - 1) * rows_each, LANES), BF)], 0)
-    line = jnp.concatenate(line, 0)
-    left = jnp.concatenate([line[:, : width // 2], dest], 1)
-    left, right = gather_z([left, line[:, width // 2 :]])
-    dest = left.reshape(Z, X * rows_each, -1)[:, :rows_each, width // 2 :]
-    rows = jnp.concatenate([left[:, : width // 2], right], 1)
+    other_dest = shift(dest, "core", 1)
+    dest = [jnp.where(core == 0, dest, other_dest), jnp.where(core == 0, other_dest, dest)]
+    dest.append(jnp.zeros(((Z - CORES) * rows_each, LANES), BF))
+    block = jnp.concatenate([gather_z(carried[0]), jnp.concatenate(dest, 0)], 1)
+    rows = gather_x(block, x)
+    dest = rows.reshape(X, Z * rows_each, -1)[:, : CORES * rows_each, width:]
+    rows = rows[:, :width]
+    behind_1 = shift(dest, "z", 1)
 
     gain = norm_gain[0].astype(F32)
     contract = (((1,), (1,)), ((), ()))
@@ -83,17 +95,20 @@
         return jnp.dot(hidden, down_part[k], preferred_element_type=F32)
 
     half = quarter // 2
-    far = part(2).astype(BF)
-    far, dest = lax.optimization_barrier((far, dest))
+    far, dest, behind_1 = lax.optimization_barrier((part(2).astype(BF), dest, behind_1))
     up = shift(far[:, :half], "x", 1)
     down = shift(far[:, half:], "x", -1)
-    near = part(1)
-    up = jnp.concatenate([add(near[:, :half], up), near[:, half:]], 1).astype(BF)
+    dest = jnp.stack([dest, behind_1])
+    near_up, near_down, dest = lax.optimization_barrier((part(1), part(3), dest))
+    behind_2 = shift(dest, "z", 2)
+    up, down, dest, behind_2 = lax.optimization_barrier((up, down, dest, behind_2))
+    up = jnp.concatenate([add(near_up[:, :half], up), near_up[:, half:]], 1).astype(BF)
     up = shift(up, "x", 1)
-    near = part(3)
-    down = jnp.concatenate([near[:, :half], add(near[:, half:], down)], 1).astype(BF)
-    down = shift(down, "x", -1)
-    summed = part(0) + up.astype(F32) + down.astype(F32)
+    down = jnp.concatenate([near_down[:, :half], add(near_down[:, half:], down)], 1)
+    down = shift(down.astype(BF), "x", -1)
+    kept, dest = lax.optimization_barrier((part(0), jnp.concatenate([dest, behind_2], 0)))
+    dest = jnp.concatenate([dest, shift(dest, "z", 4)], 0)
+    summed = kept + up.astype(F32) + down.astype(F32)
 
     def swap(array):
         mine = lax.dynamic_slice_in_dim(array, core * eighth, eighth, 1)
@@ -102,22 +117,18 @@
 
     residual = swap(lax.dynamic_slice_in_dim(rows, x * quarter, quarter, 1))
 
-    dests = jnp.zeros((X,) + dest.shape, BF)
-    for k in range(X):
-        there = shift(dest, "x", k) if k else dest
-        dests = lax.dynamic_update_slice(
-            dests, there[None], (lax.rem(x + X - k, X), 0, 0, 0)
-        )
-    dests = dests.transpose(1, 0, 2, 3)
-    dests = dests.reshape(total // CORES, LANES)
-    dest = jnp.concatenate([dests, shift(dests, "core", 1)], 0)[:, 0].astype(jnp.int32)
+    dest = jnp.stack([dest[k % Z] for k in ORDER]).reshape(Z, X, CORES, rows_each, LANES)
+    dest = dest.transpose(2, 1, 0, 3, 4)
+    dest = jnp.where(core == 0, dest, dest[::-1])
+    dest = dest.reshape(total, LANES)[:, 0].astype(jnp.int32)
     index = jnp.arange(total, dtype=jnp.int32)
-    block = (index // (X * rows_each)) % Z
-    behind = jnp.zeros_like(block)
+    place_z = (index // rows_each) % Z
+    behind = jnp.zeros_like(index)
     for i, k in enumerate(ORDER):
-        behind = jnp.where(block == i, k, behind)
+        behind = jnp.where(place_z == i, k, behind)
     source_core = jnp.where(index < total // CORES, core, 1 - core)
-    source = ((index // rows_each) % X) * Z + lax.rem(z + Z - behind, Z)
+    source_x = (index // (rows_each * Z)) % X
+    source = source_x * Z + lax.rem(z + Z - behind, Z)
     key = (source * CORES + source_core) * rows_each + index % rows_each
     earlier = (dest[:, None] == dest[None, :]) & (key[None, :] < key[:, None])
     rank = jnp.sum(earlier.astype(jnp.int32), axis=1)

time: 149 us -> 144 us (0.966)
  starting transfers between devices: 70.4 us -> 50.9 us
  matrix products: 7.48 us -> 16.4 us
  local copies, waits for them, and re-layouts: 2.73 us -> 7.31 us
    ppermute x33 -> x26, starting transfers between devices: 63.2 us -> 40.8 us  [shift(): return lax.ppermute(array, axis, [(i, (i + by) % n) for i in range(n)])]
    ppermute x33 -> x26, waiting for transfers between devices: 49.7 us -> 45 us  [shift(): return lax.ppermute(array, axis, [(i, (i + by) % n) for i in range(n)])]
    dot_general x4, matrix products: 2.16 us -> 6.33 us  [part(): return jnp.dot(hidden, down_part[k], preferred_element_type=F32)]
    ppermute x4 -> x5, waiting for transfers between devices: 2.49 us -> 6.04 us  [handoff(): return lax.ppermute(rows, ('section', 'z'), pairs)]
    dynamic_update_slice x4, local copies, waits for them, and re-layouts: 0.06 us -> 3.31 us  [gather_x(): rows = lax.dynamic_update_slice_in_dim(rows, part, at, 0)]
    ppermute x4 -> x5, starting transfers between devices: 7.18 us -> 10.2 us  [handoff(): return lax.ppermute(rows, ('section', 'z'), pairs)]
    dot_general x1, matrix products: 1.43 us -> 3.79 us  [body(): up = lax.dot_general(normed, up_mat, contract, preferred_element_type=F32)]
    dot_general x1, matrix products: 1.43 us -> 3.79 us  [body(): lax.dot_general(normed, gate_mat, contract, preferred_element_type=F32)]
  transfers between devices with their start and end apart: 37 -> 31, of which waited for: 15 -> 14; matrix products, arithmetic and copies ran while one was open for 7% -> 18% of each run, Pallas kernels for 0% -> 0%
where the time goes in v4:
time: 144 us
  waiting for transfers between devices  51 us (35%)
  starting transfers between devices  50.9 us (35%)
  matrix products  16.4 us (11%)
  blocking collectives  12.9 us (9%)
  local copies, waits for them, and re-layouts  7.31 us (5%)
  other arithmetic  4.86 us (3%)
    ppermute x26, waiting for transfers between devices, shift(): return lax.ppermute(array, axis, [(i, (i + by) % n) for i in range(n)])  45 us
    ppermute x26, starting transfers between devices, shift(): return lax.ppermute(array, axis, [(i, (i + by) % n) for i in range(n)])  40.8 us
    all_to_all x1, blocking collectives, body(): lax.all_to_all(mixed.reshape(X * CORES, SLOTS, eighth), ('x', 'core'), 0,...  12.9 us
    ppermute x5, starting transfers between devices, handoff(): return lax.ppermute(rows, ('section', 'z'), pairs)  10.2 us
    dot_general x4, matrix products, part(): return jnp.dot(hidden, down_part[k], preferred_element_type=F32)  6.33 us
    ppermute x5, waiting for transfers between devices, handoff(): return lax.ppermute(rows, ('section', 'z'), pairs)  6.04 us
    dot_general x1, matrix products, body(): lax.dot_general(normed, gate_mat, contract, preferred_element_type=F32)  3.79 us
    dot_general x1, matrix products, body(): up = lax.dot_general(normed, up_mat, contract, preferred_element_type=F32)  3.79 us
  transfers between devices with their start and end apart: 31, of which 14 were waited for; matrix products, arithmetic and copies ran while one was open for 18% of the time, Pallas kernels for 0%

profile of v4, /device:TPU:1, one launch (start us, length us, event | category | flops | bytes accessed | tf_op | source)
XLA Modules:
  0.0 143.9 jit_solution(5593482775915400543)
XLA Ops:
  0.7 3.2 %collective-permute-start.8 = (bf16[8,128]{1,0:T(8,128)(2,1)S(1)}, bf16[8,128]{1,0:T(8,128)(2,1)S(1)}, u32[]{:S(2)}, u32[]{:S(2)}) collective-permute-start(bf16[8,128]{1,0:T(8,128)(2,1)S(1)} %broadcast_in_dim.28), channel_id=1, source_target_pairs={{0,1},{1,0},{2,3},{3,2},{4,5},{5,4},{6,7},{7,6},{8,9},{9,8},{10,11... | collective-permute-start | bytes 6152 | tf_op jit(solution)/shard_map/ppermute | solution.py:17
  4.0 2.2 %collective-permute-start.1 = (bf16[8,5120]{1,0:T(8,128)(2,1)}, bf16[8,5120]{1,0:T(8,128)(2,1)S(1)}, u32[]{:S(2)}, u32[]{:S(2)}) collective-permute-start(bf16[8,5120]{1,0:T(8,128)(2,1)} %bitcast.35), channel_id=1, source_target_pairs={{0,66},{2,68},{4,70},{6,72},{8,74},{10,76},{12,78},{14,64},{64,130... | collective-permute-start | bytes 245768 | tf_op jit(solution)/shard_map/ppermute | solution.py:26
  6.2 3.9 %collective-permute-start.2 = (bf16[8,5120]{1,0:T(8,128)(2,1)}, bf16[8,5120]{1,0:T(8,128)(2,1)S(1)}, u32[]{:S(2)}, u32[]{:S(2)}) collective-permute-start(bf16[8,5120]{1,0:T(8,128)(2,1)} %bitcast.36), channel_id=1, source_target_pairs={{0,78},{2,64},{4,66},{6,68},{8,70},{10,72},{12,74},{14,76},{64,142... | collective-permute-start | bytes 245768 | tf_op jit(solution)/shard_map/ppermute | solution.py:26
  10.1 4.0 %collective-permute-start.4 = (bf16[8,5120]{1,0:T(8,128)(2,1)}, bf16[8,5120]{1,0:T(8,128)(2,1)S(1)}, u32[]{:S(2)}, u32[]{:S(2)}) collective-permute-start(bf16[8,5120]{1,0:T(8,128)(2,1)} %bitcast.38), channel_id=1, source_target_pairs={{0,76},{2,78},{4,64},{6,66},{8,68},{10,70},{12,72},{14,74},{64,140... | collective-permute-start | bytes 245768 | tf_op jit(solution)/shard_map/ppermute | solution.py:26
  14.2 4.6 %collective-permute-done.3 = bf16[8,5120]{1,0:T(8,128)(2,1)S(1)} collective-permute-done((bf16[8,5120]{1,0:T(8,128)(2,1)}, bf16[8,5120]{1,0:T(8,128)(2,1)S(1)}, u32[]{:S(2)}, u32[]{:S(2)}) %collective-permute-start.3) | collective-permute-done | bytes 81952 | tf_op jit(solution)/shard_map/ppermute | solution.py:26
  18.8 1.1 collective-permute-start.7
  19.9 1.5 %collective-permute-done.4 = bf16[8,5120]{1,0:T(8,128)(2,1)S(1)} collective-permute-done((bf16[8,5120]{1,0:T(8,128)(2,1)}, bf16[8,5120]{1,0:T(8,128)(2,1)S(1)}, u32[]{:S(2)}, u32[]{:S(2)}) %collective-permute-start.4) | collective-permute-done | bytes 81952 | tf_op jit(solution)/shard_map/ppermute | solution.py:26
  21.6 1.6 %collective-permute-done.5 = bf16[8,5120]{1,0:T(8,128)(2,1)S(1)} collective-permute-done((bf16[8,5120]{1,0:T(8,128)(2,1)S(1)}, bf16[8,5120]{1,0:T(8,128)(2,1)S(1)}, u32[]{:S(2)}, u32[]{:S(2)}) %collective-permute-start.5) | collective-permute-done | bytes 81952 | tf_op jit(solution)/shard_map/ppermute | solution.py:17
  23.3 2.8 %collective-permute-done.6 = bf16[8,5120]{1,0:T(8,128)(2,1)S(1)} collective-permute-done((bf16[8,5120]{1,0:T(8,128)(2,1)S(1)}, bf16[8,5120]{1,0:T(8,128)(2,1)S(1)}, u32[]{:S(2)}, u32[]{:S(2)}) %collective-permute-start.6) | collective-permute-done | bytes 81952 | tf_op jit(solution)/shard_map/ppermute | solution.py:17
  26.3 0.9 maximum_maximum_fusion
  27.3 1.2 collective-permute-start.9
  28.5 1.5 %collective-permute-start.10 = (bf16[64,5248]{1,0:T(8,128)(2,1)}, bf16[64,5248]{1,0:T(8,128)(2,1)S(1)}, u32[]{:S(2)}, u32[]{:S(2)}) collective-permute-start(bf16[64,5248]{1,0:T(8,128)(2,1)} %get-tuple-element.33), channel_id=1, source_target_pairs={{0,48},{16,0},{32,16},{48,32},{1,49},{17,1},{33,17},{49,33},{2,50}... | collective-permute-start | bytes 2015240 | tf_op jit(solution)/shard_map/ppermute | solution.py:17
  30.0 4.1 %collective-permute-start.13 = (bf16[216,5120]{1,0:T(8,128)(2,1)}, bf16[216,5120]{1,0:T(8,128)(2,1)}, u32[]{:S(2)}, u32[]{:S(2)}) collective-permute-start(bf16[216,5120]{1,0:T(8,128)(2,1)} %bitcast.3), channel_id=1, source_target_pairs={{0,1},{1,0},{2,3},{3,2},{4,5},{5,4},{6,7},{7,6},{8,9},{9,8},{10,11... | collective-permute-start | bytes 6635528 | tf_op jit(solution)/shard_map/ppermute | solution.py:17
  34.6 1.4 mul.140
  36.0 5.8 %collective-permute-done.9 = bf16[64,5248]{1,0:T(8,128)(2,1)S(1)} collective-permute-done((bf16[64,5248]{1,0:T(8,128)(2,1)}, bf16[64,5248]{1,0:T(8,128)(2,1)S(1)}, u32[]{:S(2)}, u32[]{:S(2)}) %collective-permute-start.9) | collective-permute-done | bytes 671776 | tf_op jit(solution)/shard_map/ppermute | solution.py:17
  41.9 2.9 %collective-permute-start.12 = (bf16[32,5248]{1,0:T(8,128)(2,1)S(1)}, bf16[32,5248]{1,0:T(8,128)(2,1)S(1)}, u32[]{:S(2)}, u32[]{:S(2)}) collective-permute-start(bf16[32,5248]{1,0:T(8,128)(2,1)S(1)} %slice.119), channel_id=1, source_target_pairs={{0,48},{16,0},{32,16},{48,32},{1,49},{17,1},{33,17},{49,33},{2,50}... | collective-permute-start | bytes 1007624 | tf_op jit(solution)/shard_map/ppermute | solution.py:17
  44.8 0.9 constant_dynamic-update-slice_fusion.18
  45.7 0.9 constant_dynamic-update-slice_fusion.17
  46.6 2.5 %collective-permute-done.11 = bf16[32,5248]{1,0:T(8,128)(2,1)S(1)} collective-permute-done((bf16[32,5248]{1,0:T(8,128)(2,1)S(1)}, bf16[32,5248]{1,0:T(8,128)(2,1)S(1)}, u32[]{:S(2)}, u32[]{:S(2)}) %collective-permute-start.11) | collective-permute-done | bytes 335904 | tf_op jit(solution)/shard_map/ppermute | solution.py:17
  49.1 0.8 constant_dynamic-update-slice_fusion.16
  50.6 2.1 %slice.120 = bf16[256,5120]{1,0:T(8,128)(2,1)S(1)} slice(bf16[256,5248]{1,0:T(8,128)(2,1)} %constant_dynamic-update-slice_fusion.15), slice={[0:256], [0:5120]} | slice | bytes 5242880 | tf_op jit(solution)/shard_map/slice | solution.py:82
  53.1 5.7 %collective-permute-start.24 = (bf16[256,640]{1,0:T(8,128)(2,1)S(1)}, bf16[256,640]{1,0:T(8,128)(2,1)S(1)}, u32[]{:S(2)}, u32[]{:S(2)}) collective-permute-start(bf16[256,640]{1,0:T(8,128)(2,1)S(1)} %get-tuple-element.32), channel_id=1, source_target_pairs={{0,1},{1,0},{2,3},{3,2},{4,5},{5,4},{6,7},{7,6},{8,9},{9,8},{10,11... | collective-permute-start | bytes 983048 | tf_op jit(solution)/shard_map/ppermute | solution.py:17
  58.8 1.7 %collective-permute-start.16 = (bf16[4,16,128]{2,1,0:T(8,128)(2,1)S(1)}, bf16[4,16,128]{2,1,0:T(8,128)(2,1)S(1)}, u32[]{:S(2)}, u32[]{:S(2)}) collective-permute-start(bf16[4,16,128]{2,1,0:T(8,128)(2,1)S(1)} %slice.121), channel_id=1, source_target_pairs={{0,2},{2,4},{4,6},{6,8},{8,10},{10,12},{12,14},{14,0},{1,3},{3,5},... | collective-permute-start | bytes 49160 | tf_op jit(solution)/shard_map/ppermute | solution.py:17
  61.2 3.8 %fusion.3 = f32[256,432]{0,1:T(8,128)S(1)} fusion(bf16[216,5120]{1,0:T(8,128)(2,1)} %collective-permute-done.13, bf16[216,5120]{1,0:T(8,128)(2,1)} %bitcast.3, f32[5120]{0:T(1024)S(1)} %bitcast.31, f32[256]{0:T(256)S(1)} %add_rsqrt_fusion, bf16[256,5248]{1,0:T(8,128)(2,1)S(1)} %copy-done.2), kind=kOutput, calls=%fused_computation.13 | convolution fusion | flops 1146552320 | bytes 7508992 | tf_op jit(solution)/shard_map/dot_general | solution.py:90
  65.0 3.8 %multiply_convert_fusion = bf16[256,432]{0,1:T(8,128)(2,1)S(1)} fusion(f32[256,432]{0,1:T(8,128)S(1)} %fusion.3, bf16[216,5120]{1,0:T(8,128)(2,1)} %collective-permute-done.14, bf16[216,5120]{1,0:T(8,128)(2,1)} %bitcast.4, f32[5120]{0:T(1024)S(1)} %bitcast.32, f32[256]{0:T(256)S(1)} %add_rsqrt_fusion, bf16[256,5248]{1,0:T(8,128)(2,1)S(1)} %copy-done.2), kind=kOutput, calls=%fused_computation.55 | convolution fusion | flops 1147215872 | bytes 7730176 | tf_op jit(solution)/shard_map/dot_general | solution.py:91
  68.8 1.6 %convolution_convert_fusion = bf16[256,1280]{1,0:T(8,128)(2,1)S(1)} fusion(bf16[256,432]{0,1:T(8,128)(2,1)S(1)} %multiply_convert_fusion, s32[]{:T(128)S(6)} %select_n.300, bf16[216,5120]{1,0:T(8,128)(2,1)S(1)} %bitcast.21, bf16[216,5120]{1,0:T(8,128)(2,1)} %collective-permute-done.15), kind=kOutput, calls=%fused_computation.21 | convolution fusion | flops 285655040 | bytes 5300228 | tf_op jit(solution)/shard_map/dot_general | solution.py:95
  70.4 1.1 collective-permute-start.17
  71.6 1.6 %collective-permute-start.18 = (bf16[256,640]{1,0:T(8,128)(2,1)S(1)}, bf16[256,640]{1,0:T(8,128)(2,1)S(1)}, u32[]{:S(2)}, u32[]{:S(2)}) collective-permute-start(bf16[256,640]{1,0:T(8,128)(2,1)S(1)} %get-tuple-element.37), channel_id=1, source_target_pairs={{0,48},{16,0},{32,16},{48,32},{1,49},{17,1},{33,17},{49,33},{2,50}... | collective-permute-start | bytes 983048 | tf_op jit(solution)/shard_map/ppermute | solution.py:17
  73.2 1.6 %fusion.23 = f32[256,1280]{1,0:T(8,128)S(1)} fusion(bf16[256,432]{0,1:T(8,128)(2,1)S(1)} %multiply_convert_fusion, s32[]{:T(128)S(6)} %select_n.301, bf16[216,5120]{1,0:T(8,128)(2,1)S(1)} %bitcast.22, bf16[216,5120]{1,0:T(8,128)(2,1)} %collective-permute-done.15), kind=kOutput, calls=%fused_computation.40 | convolution fusion | flops 285327360 | bytes 5955588 | tf_op jit(solution)/shard_map/dot_general | solution.py:95
  74.8 1.6 %fusion.15 = f32[256,1280]{1,0:T(8,128)S(1)} fusion(bf16[256,432]{0,1:T(8,128)(2,1)S(1)} %multiply_convert_fusion, s32[]{:T(128)S(6)} %select_n.302, bf16[216,5120]{1,0:T(8,128)(2,1)S(1)} %bitcast.23, bf16[216,5120]{1,0:T(8,128)(2,1)} %collective-permute-done.15), kind=kOutput, calls=%fused_computation.35 | convolution fusion | flops 285327360 | bytes 5955588 | tf_op jit(solution)/shard_map/dot_general | solution.py:95
  76.4 1.1 collective-permute-start.19
  77.5 1.6 %fusion.18 = f32[256,1280]{1,0:T(8,128)S(1)} fusion(bf16[256,432]{0,1:T(8,128)(2,1)S(1)} %multiply_convert_fusion, s32[]{:T(128)S(6)} %select_n.299, bf16[216,5120]{1,0:T(8,128)(2,1)S(1)} %bitcast.24, bf16[216,5120]{1,0:T(8,128)(2,1)} %collective-permute-done.15), kind=kOutput, calls=%fused_computation.37 | convolution fusion | flops 285327360 | bytes 5955588 | tf_op jit(solution)/shard_map/dot_general | solution.py:95
  79.1 2.4 %collective-permute-done.19 = bf16[2,4,16,128]{3,2,1,0:T(8,128)(2,1)S(1)} collective-permute-done((bf16[2,4,16,128]{3,2,1,0:T(8,128)(2,1)S(1)}, bf16[2,4,16,128]{3,2,1,0:T(8,128)(2,1)S(1)}, u32[]{:S(2)}, u32[]{:S(2)}) %collective-permute-start.19) | collective-permute-done | bytes 32800 | tf_op jit(solution)/shard_map/ppermute | solution.py:17
  81.6 3.0 %collective-permute-start.20 = (bf16[4,4,16,128]{3,2,1,0:T(8,128)(2,1)S(1)}, bf16[4,4,16,128]{3,2,1,0:T(8,128)(2,1)S(1)}, u32[]{:S(2)}, u32[]{:S(2)}) collective-permute-start(bf16[4,4,16,128]{3,2,1,0:T(8,128)(2,1)S(1)} %pad_maximum_fusion.7), channel_id=1, source_target_pairs={{0,8},{2,10},{4,12},{6,14},{8,0},{10,2},{12,4},{14,6},{1,9},{3,11}... | collective-permute-start | bytes 196616 | tf_op jit(solution)/shard_map/ppermute | solution.py:17
  84.6 1.7 %collective-permute-start.22 = (bf16[256,1280]{1,0:T(8,128)(2,1)S(1)}, bf16[256,1280]{1,0:T(8,128)(2,1)S(1)}, u32[]{:S(2)}, u32[]{:S(2)}) collective-permute-start(bf16[256,1280]{1,0:T(8,128)(2,1)S(1)} %pad_maximum_fusion.1), channel_id=1, source_target_pairs={{0,48},{16,0},{32,16},{48,32},{1,49},{17,1},{33,17},{49,33},{2,50}... | collective-permute-start | bytes 1966088 | tf_op jit(solution)/shard_map/ppermute | solution.py:17
  86.5 2.9 %collective-permute-done.20 = bf16[4,4,16,128]{3,2,1,0:T(8,128)(2,1)S(1)} collective-permute-done((bf16[4,4,16,128]{3,2,1,0:T(8,128)(2,1)S(1)}, bf16[4,4,16,128]{3,2,1,0:T(8,128)(2,1)S(1)}, u32[]{:S(2)}, u32[]{:S(2)}) %collective-permute-start.20) | collective-permute-done | bytes 65568 | tf_op jit(solution)/shard_map/ppermute | solution.py:17
  89.7 9.0 %collective-permute-done.22 = bf16[256,1280]{1,0:T(8,128)(2,1)S(1)} collective-permute-done((bf16[256,1280]{1,0:T(8,128)(2,1)S(1)}, bf16[256,1280]{1,0:T(8,128)(2,1)S(1)}, u32[]{:S(2)}, u32[]{:S(2)}) %collective-permute-start.22) | collective-permute-done | bytes 655392 | tf_op jit(solution)/shard_map/ppermute | solution.py:17
  98.7 3.0 %collective-permute-done.21 = bf16[256,1280]{1,0:T(8,128)(2,1)S(1)} collective-permute-done((bf16[256,1280]{1,0:T(8,128)(2,1)S(1)}, bf16[256,1280]{1,0:T(8,128)(2,1)S(1)}, u32[]{:S(2)}, u32[]{:S(2)}) %collective-permute-start.21) | collective-permute-done | bytes 655392 | tf_op jit(solution)/shard_map/ppermute | solution.py:17
  102.1 3.4 %collective-permute-start.23 = (bf16[256,640]{1,0:T(8,128)(2,1)S(1)}, bf16[256,640]{1,0:T(8,128)(2,1)S(1)}, u32[]{:S(2)}, u32[]{:S(2)}) collective-permute-start(bf16[256,640]{1,0:T(8,128)(2,1)S(1)} %get-tuple-element.36), channel_id=1, source_target_pairs={{0,1},{1,0},{2,3},{3,2},{4,5},{5,4},{6,7},{7,6},{8,9},{9,8},{10,11... | collective-permute-start | bytes 983048 | tf_op jit(solution)/shard_map/ppermute | solution.py:17
  105.9 0.9 collective-permute-done.23
  108.4 1.1 collective-permute-start.29
  110.1 1.2 collective-permute-start.25
  111.3 1.0 collective-permute-start.27
  112.3 4.0 %collective-permute-done.26 = bf16[256,640]{1,0:T(8,128)(2,1)S(1)} collective-permute-done((bf16[256,640]{1,0:T(8,128)(2,1)S(1)}, bf16[256,640]{1,0:T(8,128)(2,1)S(1)}, u32[]{:S(2)}, u32[]{:S(2)}) %collective-permute-start.26) | collective-permute-done | bytes 327712 | tf_op jit(solution)/shard_map/ppermute | solution.py:17
  116.7 3.2 %collective-permute-done.29 = bf16[64,640]{1,0:T(8,128)(2,1)S(1)} collective-permute-done((bf16[64,640]{1,0:T(8,128)(2,1)S(1)}, bf16[64,640]{1,0:T(8,128)(2,1)S(1)}, u32[]{:S(2)}, u32[]{:S(2)}) %collective-permute-start.29) | collective-permute-done | bytes 81952 | tf_op jit(solution)/shard_map/ppermute | solution.py:17
  120.0 2.5 %collective-permute-start.30 = (bf16[128,640]{1,0:T(8,128)(2,1)S(1)}, bf16[128,640]{1,0:T(8,128)(2,1)S(1)}, u32[]{:S(2)}, u32[]{:S(2)}) collective-permute-start(bf16[128,640]{1,0:T(8,128)(2,1)S(1)} %pad_maximum_fusion.6), channel_id=1, source_target_pairs={{0,12},{2,14},{4,0},{6,2},{8,4},{10,6},{12,8},{14,10},{1,13},{3,15... | collective-permute-start | bytes 491528 | tf_op jit(solution)/shard_map/ppermute | solution.py:17
  123.2 6.8 %collective-permute-done.30 = bf16[128,640]{1,0:T(8,128)(2,1)S(1)} collective-permute-done((bf16[128,640]{1,0:T(8,128)(2,1)S(1)}, bf16[128,640]{1,0:T(8,128)(2,1)S(1)}, u32[]{:S(2)}, u32[]{:S(2)}) %collective-permute-start.30) | collective-permute-done | bytes 163872 | tf_op jit(solution)/shard_map/ppermute | solution.py:17
  130.2 12.9 %all_to_all.5 = bf16[8,16,640]{2,1,0:T(8,128)(2,1)S(1)} all-to-all(bf16[8,16,640]{2,1,0:T(8,128)(2,1)S(1)} %bitcast.29), channel_id=1, replica_groups=mesh['section'=4,'x'=4,'z'=8,'core'=2] {'x','core'}, dimensions={0} | all-to-all | bytes 327680 | tf_op jit(solution)/shard_map/all_to_all | solution.py:169
  (101 shorter events, 9.5 us)
Async XLA Ops:
  0.7 9.4 %collective-permute-start.8 = (bf16[8,128]{1,0:T(8,128)(2,1)S(1)}, bf16[8,128]{1,0:T(8,128)(2,1)S(1)}, u32[]{:S(2)}, u32[]{:S(2)}) collective-permute-start(bf16[8,128]{1,0:T(8,128)(2,1)S(1)} %broadcast_in_dim.28), channel_id=1, source_target_pairs={{0,1},{1,0},{2,3},{3,2},{4,5},{5,4},{6,7},{7,6},{8,9},{9,8},{10,11... | collective-permute-start | bytes 6152 | tf_op jit(solution)/shard_map/ppermute | solution.py:17
  4.0 14.8 %collective-permute-start = (bf16[8,5120]{1,0:T(8,128)(2,1)}, bf16[8,5120]{1,0:T(8,128)(2,1)S(1)}, u32[]{:S(2)}, u32[]{:S(2)}) collective-permute-start(bf16[8,5120]{1,0:T(8,128)(2,1)} %bitcast.34), channel_id=1, source_target_pairs={{0,64},{2,66},{4,68},{6,70},{8,72},{10,74},{12,76},{14,78},{64,128... | collective-permute-start | bytes 245768 | tf_op jit(solution)/shard_map/ppermute | solution.py:26
  4.0 15.9 %collective-permute-start.1 = (bf16[8,5120]{1,0:T(8,128)(2,1)}, bf16[8,5120]{1,0:T(8,128)(2,1)S(1)}, u32[]{:S(2)}, u32[]{:S(2)}) collective-permute-start(bf16[8,5120]{1,0:T(8,128)(2,1)} %bitcast.35), channel_id=1, source_target_pairs={{0,66},{2,68},{4,70},{6,72},{8,74},{10,76},{12,78},{14,64},{64,130... | collective-permute-start | bytes 245768 | tf_op jit(solution)/shard_map/ppermute | solution.py:26
  6.2 13.7 %collective-permute-start.2 = (bf16[8,5120]{1,0:T(8,128)(2,1)}, bf16[8,5120]{1,0:T(8,128)(2,1)S(1)}, u32[]{:S(2)}, u32[]{:S(2)}) collective-permute-start(bf16[8,5120]{1,0:T(8,128)(2,1)} %bitcast.36), channel_id=1, source_target_pairs={{0,78},{2,64},{4,66},{6,68},{8,70},{10,72},{12,74},{14,76},{64,142... | collective-permute-start | bytes 245768 | tf_op jit(solution)/shard_map/ppermute | solution.py:26
  10.1 8.6 %collective-permute-start.3 = (bf16[8,5120]{1,0:T(8,128)(2,1)}, bf16[8,5120]{1,0:T(8,128)(2,1)S(1)}, u32[]{:S(2)}, u32[]{:S(2)}) collective-permute-start(bf16[8,5120]{1,0:T(8,128)(2,1)} %bitcast.37), channel_id=1, source_target_pairs={{0,68},{2,70},{4,72},{6,74},{8,76},{10,78},{12,64},{14,66},{64,132... | collective-permute-start | bytes 245768 | tf_op jit(solution)/shard_map/ppermute | solution.py:26
  10.1 11.3 %collective-permute-start.4 = (bf16[8,5120]{1,0:T(8,128)(2,1)}, bf16[8,5120]{1,0:T(8,128)(2,1)S(1)}, u32[]{:S(2)}, u32[]{:S(2)}) collective-permute-start(bf16[8,5120]{1,0:T(8,128)(2,1)} %bitcast.38), channel_id=1, source_target_pairs={{0,76},{2,78},{4,64},{6,66},{8,68},{10,70},{12,72},{14,74},{64,140... | collective-permute-start | bytes 245768 | tf_op jit(solution)/shard_map/ppermute | solution.py:26
  18.8 4.5 %collective-permute-start.5 = (bf16[8,5120]{1,0:T(8,128)(2,1)S(1)}, bf16[8,5120]{1,0:T(8,128)(2,1)S(1)}, u32[]{:S(2)}, u32[]{:S(2)}) collective-permute-start(bf16[8,5120]{1,0:T(8,128)(2,1)S(1)} %collective-permute-done.3), channel_id=1, source_target_pairs={{0,2},{2,4},{4,6},{6,8},{8,10},{10,12},{12,14},{14,0},{1,3},{3,5},... | collective-permute-start | bytes 245768 | tf_op jit(solution)/shard_map/ppermute | solution.py:17
  18.8 7.3 %collective-permute-start.7 = (bf16[8,5120]{1,0:T(8,128)(2,1)S(1)}, bf16[8,5120]{1,0:T(8,128)(2,1)S(1)}, u32[]{:S(2)}, u32[]{:S(2)}) collective-permute-start(bf16[8,5120]{1,0:T(8,128)(2,1)S(1)} %collective-permute-done.3), channel_id=1, source_target_pairs={{0,4},{2,6},{4,8},{6,10},{8,12},{10,14},{12,0},{14,2},{1,5},{3,7},... | collective-permute-start | bytes 245768 | tf_op jit(solution)/shard_map/ppermute | solution.py:17
  21.4 4.7 %collective-permute-start.6 = (bf16[8,5120]{1,0:T(8,128)(2,1)S(1)}, bf16[8,5120]{1,0:T(8,128)(2,1)S(1)}, u32[]{:S(2)}, u32[]{:S(2)}) collective-permute-start(bf16[8,5120]{1,0:T(8,128)(2,1)S(1)} %collective-permute-done.4), channel_id=1, source_target_pairs={{0,14},{2,0},{4,2},{6,4},{8,6},{10,8},{12,10},{14,12},{1,15},{3,1}... | collective-permute-start | bytes 245768 | tf_op jit(solution)/shard_map/ppermute | solution.py:17
  26.1 7.9 %copy-start = (bf16[1,216,5120]{2,1,0:T(8,128)(2,1)S(1)}, bf16[1,216,5120]{2,1,0:T(8,128)(2,1)}, u32[]{:S(2)}) copy-start(bf16[1,216,5120]{2,1,0:T(8,128)(2,1)} %param.11) | copy-start | bytes 6635524
  27.3 6.8 %copy-start.1 = (bf16[256,5248]{1,0:T(8,128)(2,1)}, bf16[256,5248]{1,0:T(8,128)(2,1)S(1)}, u32[]{:S(2)}) copy-start(bf16[256,5248]{1,0:T(8,128)(2,1)S(1)} %get-tuple-element.34) | copy-start | bytes 8060932
  27.3 14.4 %collective-permute-start.9 = (bf16[64,5248]{1,0:T(8,128)(2,1)}, bf16[64,5248]{1,0:T(8,128)(2,1)S(1)}, u32[]{:S(2)}, u32[]{:S(2)}) collective-permute-start(bf16[64,5248]{1,0:T(8,128)(2,1)} %get-tuple-element.33), channel_id=1, source_target_pairs={{0,16},{16,32},{32,48},{48,0},{1,17},{17,33},{33,49},{49,1},{2,18}... | collective-permute-start | bytes 2015240 | tf_op jit(solution)/shard_map/ppermute | solution.py:17
  28.5 13.4 %collective-permute-start.10 = (bf16[64,5248]{1,0:T(8,128)(2,1)}, bf16[64,5248]{1,0:T(8,128)(2,1)S(1)}, u32[]{:S(2)}, u32[]{:S(2)}) collective-permute-start(bf16[64,5248]{1,0:T(8,128)(2,1)} %get-tuple-element.33), channel_id=1, source_target_pairs={{0,48},{16,0},{32,16},{48,32},{1,49},{17,1},{33,17},{49,33},{2,50}... | collective-permute-start | bytes 2015240 | tf_op jit(solution)/shard_map/ppermute | solution.py:17
  30.0 31.2 %collective-permute-start.13 = (bf16[216,5120]{1,0:T(8,128)(2,1)}, bf16[216,5120]{1,0:T(8,128)(2,1)}, u32[]{:S(2)}, u32[]{:S(2)}) collective-permute-start(bf16[216,5120]{1,0:T(8,128)(2,1)} %bitcast.3), channel_id=1, source_target_pairs={{0,1},{1,0},{2,3},{3,2},{4,5},{5,4},{6,7},{7,6},{8,9},{9,8},{10,11... | collective-permute-start | bytes 6635528 | tf_op jit(solution)/shard_map/ppermute | solution.py:17
  34.1 30.9 %collective-permute-start.14 = (bf16[216,5120]{1,0:T(8,128)(2,1)}, bf16[216,5120]{1,0:T(8,128)(2,1)}, u32[]{:S(2)}, u32[]{:S(2)}) collective-permute-start(bf16[216,5120]{1,0:T(8,128)(2,1)} %bitcast.4), channel_id=1, source_target_pairs={{0,1},{1,0},{2,3},{3,2},{4,5},{5,4},{6,7},{7,6},{8,9},{9,8},{10,11... | collective-permute-start | bytes 6635528 | tf_op jit(solution)/shard_map/ppermute | solution.py:17
  34.1 34.7 %collective-permute-start.15 = (bf16[216,5120]{1,0:T(8,128)(2,1)S(1)}, bf16[216,5120]{1,0:T(8,128)(2,1)}, u32[]{:S(2)}, u32[]{:S(2)}) collective-permute-start(bf16[216,5120]{1,0:T(8,128)(2,1)S(1)} %bitcast.20), channel_id=1, source_target_pairs={{0,1},{1,0},{2,3},{3,2},{4,5},{5,4},{6,7},{7,6},{8,9},{9,8},{10,11... | collective-permute-start | bytes 6635528 | tf_op jit(solution)/shard_map/ppermute | solution.py:17
  41.8 7.4 %collective-permute-start.11 = (bf16[32,5248]{1,0:T(8,128)(2,1)S(1)}, bf16[32,5248]{1,0:T(8,128)(2,1)S(1)}, u32[]{:S(2)}, u32[]{:S(2)}) collective-permute-start(bf16[32,5248]{1,0:T(8,128)(2,1)S(1)} %slice.118), channel_id=1, source_target_pairs={{0,16},{16,32},{32,48},{48,0},{1,17},{17,33},{33,49},{49,1},{2,18}... | collective-permute-start | bytes 1007624 | tf_op jit(solution)/shard_map/ppermute | solution.py:17
  41.9 8.0 %collective-permute-start.12 = (bf16[32,5248]{1,0:T(8,128)(2,1)S(1)}, bf16[32,5248]{1,0:T(8,128)(2,1)S(1)}, u32[]{:S(2)}, u32[]{:S(2)}) collective-permute-start(bf16[32,5248]{1,0:T(8,128)(2,1)S(1)} %slice.119), channel_id=1, source_target_pairs={{0,48},{16,0},{32,16},{48,32},{1,49},{17,1},{33,17},{49,33},{2,50}... | collective-permute-start | bytes 1007624 | tf_op jit(solution)/shard_map/ppermute | solution.py:17
  50.6 8.2 %copy-start.2 = (bf16[256,5248]{1,0:T(8,128)(2,1)S(1)}, bf16[256,5248]{1,0:T(8,128)(2,1)}, u32[]{:S(2)}) copy-start(bf16[256,5248]{1,0:T(8,128)(2,1)} %constant_dynamic-update-slice_fusion.15) | copy-start | bytes 8060932
  52.7 8.5 %copy-start.3 = (f32[1,5120]{1,0:T(1,128)S(1)}, f32[1,5120]{1,0:T(1,128)}, u32[]{:S(2)}) copy-start(f32[1,5120]{1,0:T(1,128)} %mul.140) | copy-start | bytes 61444
  53.1 69.8 %collective-permute-start.24 = (bf16[256,640]{1,0:T(8,128)(2,1)S(1)}, bf16[256,640]{1,0:T(8,128)(2,1)S(1)}, u32[]{:S(2)}, u32[]{:S(2)}) collective-permute-start(bf16[256,640]{1,0:T(8,128)(2,1)S(1)} %get-tuple-element.32), channel_id=1, source_target_pairs={{0,1},{1,0},{2,3},{3,2},{4,5},{5,4},{6,7},{7,6},{8,9},{9,8},{10,11... | collective-permute-start | bytes 983048 | tf_op jit(solution)/shard_map/ppermute | solution.py:17
  58.8 11.6 %collective-permute-start.16 = (bf16[4,16,128]{2,1,0:T(8,128)(2,1)S(1)}, bf16[4,16,128]{2,1,0:T(8,128)(2,1)S(1)}, u32[]{:S(2)}, u32[]{:S(2)}) collective-permute-start(bf16[4,16,128]{2,1,0:T(8,128)(2,1)S(1)} %slice.121), channel_id=1, source_target_pairs={{0,2},{2,4},{4,6},{6,8},{8,10},{10,12},{12,14},{14,0},{1,3},{3,5},... | collective-permute-start | bytes 49160 | tf_op jit(solution)/shard_map/ppermute | solution.py:17
  70.4 11.1 %collective-permute-start.17 = (bf16[256,640]{1,0:T(8,128)(2,1)S(1)}, bf16[256,640]{1,0:T(8,128)(2,1)S(1)}, u32[]{:S(2)}, u32[]{:S(2)}) collective-permute-start(bf16[256,640]{1,0:T(8,128)(2,1)S(1)} %get-tuple-element.38), channel_id=1, source_target_pairs={{0,16},{16,32},{32,48},{48,0},{1,17},{17,33},{33,49},{49,1},{2,18}... | collective-permute-start | bytes 983048 | tf_op jit(solution)/shard_map/ppermute | solution.py:17
  71.6 10.0 %collective-permute-start.18 = (bf16[256,640]{1,0:T(8,128)(2,1)S(1)}, bf16[256,640]{1,0:T(8,128)(2,1)S(1)}, u32[]{:S(2)}, u32[]{:S(2)}) collective-permute-start(bf16[256,640]{1,0:T(8,128)(2,1)S(1)} %get-tuple-element.37), channel_id=1, source_target_pairs={{0,48},{16,0},{32,16},{48,32},{1,49},{17,1},{33,17},{49,33},{2,50}... | collective-permute-start | bytes 983048 | tf_op jit(solution)/shard_map/ppermute | solution.py:17
  76.4 5.1 %collective-permute-start.19 = (bf16[2,4,16,128]{3,2,1,0:T(8,128)(2,1)S(1)}, bf16[2,4,16,128]{3,2,1,0:T(8,128)(2,1)S(1)}, u32[]{:S(2)}, u32[]{:S(2)}) collective-permute-start(bf16[2,4,16,128]{3,2,1,0:T(8,128)(2,1)S(1)} %pad_maximum_fusion.8), channel_id=1, source_target_pairs={{0,4},{2,6},{4,8},{6,10},{8,12},{10,14},{12,0},{14,2},{1,5},{3,7},... | collective-permute-start | bytes 98312 | tf_op jit(solution)/shard_map/ppermute | solution.py:17
  81.6 7.8 %collective-permute-start.20 = (bf16[4,4,16,128]{3,2,1,0:T(8,128)(2,1)S(1)}, bf16[4,4,16,128]{3,2,1,0:T(8,128)(2,1)S(1)}, u32[]{:S(2)}, u32[]{:S(2)}) collective-permute-start(bf16[4,4,16,128]{3,2,1,0:T(8,128)(2,1)S(1)} %pad_maximum_fusion.7), channel_id=1, source_target_pairs={{0,8},{2,10},{4,12},{6,14},{8,0},{10,2},{12,4},{14,6},{1,9},{3,11}... | collective-permute-start | bytes 196616 | tf_op jit(solution)/shard_map/ppermute | solution.py:17
  84.6 14.1 %collective-permute-start.22 = (bf16[256,1280]{1,0:T(8,128)(2,1)S(1)}, bf16[256,1280]{1,0:T(8,128)(2,1)S(1)}, u32[]{:S(2)}, u32[]{:S(2)}) collective-permute-start(bf16[256,1280]{1,0:T(8,128)(2,1)S(1)} %pad_maximum_fusion.1), channel_id=1, source_target_pairs={{0,48},{16,0},{32,16},{48,32},{1,49},{17,1},{33,17},{49,33},{2,50}... | collective-permute-start | bytes 1966088 | tf_op jit(solution)/shard_map/ppermute | solution.py:17
  86.4 15.3 %collective-permute-start.21 = (bf16[256,1280]{1,0:T(8,128)(2,1)S(1)}, bf16[256,1280]{1,0:T(8,128)(2,1)S(1)}, u32[]{:S(2)}, u32[]{:S(2)}) collective-permute-start(bf16[256,1280]{1,0:T(8,128)(2,1)S(1)} %pad_maximum_fusion), channel_id=1, source_target_pairs={{0,16},{16,32},{32,48},{48,0},{1,17},{17,33},{33,49},{49,1},{2,18}... | collective-permute-start | bytes 1966088 | tf_op jit(solution)/shard_map/ppermute | solution.py:17
  102.1 4.7 %collective-permute-start.23 = (bf16[256,640]{1,0:T(8,128)(2,1)S(1)}, bf16[256,640]{1,0:T(8,128)(2,1)S(1)}, u32[]{:S(2)}, u32[]{:S(2)}) collective-permute-start(bf16[256,640]{1,0:T(8,128)(2,1)S(1)} %get-tuple-element.36), channel_id=1, source_target_pairs={{0,1},{1,0},{2,3},{3,2},{4,5},{5,4},{6,7},{7,6},{8,9},{9,8},{10,11... | collective-permute-start | bytes 983048 | tf_op jit(solution)/shard_map/ppermute | solution.py:17
  107.4 9.0 %collective-permute-start.26 = (bf16[256,640]{1,0:T(8,128)(2,1)S(1)}, bf16[256,640]{1,0:T(8,128)(2,1)S(1)}, u32[]{:S(2)}, u32[]{:S(2)}) collective-permute-start(bf16[256,640]{1,0:T(8,128)(2,1)S(1)} %pad_maximum_fusion.4), channel_id=1, source_target_pairs={{0,14},{2,0},{4,2},{6,4},{8,6},{10,8},{12,10},{14,12},{1,15},{3,1}... | collective-permute-start | bytes 983048 | tf_op jit(solution)/shard_map/ppermute | solution.py:17
  108.4 11.5 %collective-permute-start.29 = (bf16[64,640]{1,0:T(8,128)(2,1)S(1)}, bf16[64,640]{1,0:T(8,128)(2,1)S(1)}, u32[]{:S(2)}, u32[]{:S(2)}) collective-permute-start(bf16[64,640]{1,0:T(8,128)(2,1)S(1)} %get-tuple-element.40), channel_id=1, source_target_pairs={{0,12},{2,14},{4,0},{6,2},{8,4},{10,6},{12,8},{14,10},{1,13},{3,15... | collective-permute-start | bytes 245768 | tf_op jit(solution)/shard_map/ppermute | solution.py:17
  110.1 12.3 %collective-permute-start.25 = (bf16[256,640]{1,0:T(8,128)(2,1)S(1)}, bf16[256,640]{1,0:T(8,128)(2,1)S(1)}, u32[]{:S(2)}, u32[]{:S(2)}) collective-permute-start(bf16[256,640]{1,0:T(8,128)(2,1)S(1)} %pad_maximum_fusion.3), channel_id=1, source_target_pairs={{0,2},{2,4},{4,6},{6,8},{8,10},{10,12},{12,14},{14,0},{1,3},{3,5},... | collective-permute-start | bytes 983048 | tf_op jit(solution)/shard_map/ppermute | solution.py:17
  111.3 11.4 %collective-permute-start.27 = (bf16[64,640]{1,0:T(8,128)(2,1)S(1)}, bf16[64,640]{1,0:T(8,128)(2,1)S(1)}, u32[]{:S(2)}, u32[]{:S(2)}) collective-permute-start(bf16[64,640]{1,0:T(8,128)(2,1)S(1)} %get-tuple-element.39), channel_id=1, source_target_pairs={{0,4},{2,6},{4,8},{6,10},{8,12},{10,14},{12,0},{14,2},{1,5},{3,7},... | collective-permute-start | bytes 245768 | tf_op jit(solution)/shard_map/ppermute | solution.py:17
  120.0 10.0 %collective-permute-start.30 = (bf16[128,640]{1,0:T(8,128)(2,1)S(1)}, bf16[128,640]{1,0:T(8,128)(2,1)S(1)}, u32[]{:S(2)}, u32[]{:S(2)}) collective-permute-start(bf16[128,640]{1,0:T(8,128)(2,1)S(1)} %pad_maximum_fusion.6), channel_id=1, source_target_pairs={{0,12},{2,14},{4,0},{6,2},{8,4},{10,6},{12,8},{14,10},{1,13},{3,15... | collective-permute-start | bytes 491528 | tf_op jit(solution)/shard_map/ppermute | solution.py:17
  122.8 7.1 %collective-permute-start.28 = (bf16[128,640]{1,0:T(8,128)(2,1)S(1)}, bf16[128,640]{1,0:T(8,128)(2,1)S(1)}, u32[]{:S(2)}, u32[]{:S(2)}) collective-permute-start(bf16[128,640]{1,0:T(8,128)(2,1)S(1)} %pad_maximum_fusion.5), channel_id=1, source_target_pairs={{0,4},{2,6},{4,8},{6,10},{8,12},{10,14},{12,0},{14,2},{1,5},{3,7},... | collective-permute-start | bytes 491528 | tf_op jit(solution)/shard_map/ppermute | solution.py:17

commit v5 on v4

v5 whole, which is shorter than its diff:
```python
import jax
import jax.numpy as jnp
from jax import lax
from jax.experimental import pallas as pl
from jax.experimental.pallas import tpu as pltpu
from jax.sharding import Mesh
from jax.sharding import PartitionSpec as P

SLOTS = 16
X, Z, CORES, SECTIONS = 4, 8, 2, 4
LANES = 128
VMEM = 32 * 1024 * 1024
EPSILON = 1e-05
BF, F32 = jnp.bfloat16, jnp.float32
ORDER = (0, 1, -1, 2, -2, 3, -3, 4)


def shift(array, axis, by):
    n = lax.axis_size(axis)
    return lax.ppermute(array, axis, [(i, (i + by) % n) for i in range(n)])


def handoff(rows, by):
    pairs = [
        (s * Z + z, ((s + 1) % SECTIONS) * Z + (z + by) % Z)
        for s in range(SECTIONS)
        for z in range(Z)
    ]
    return lax.ppermute(rows, ("section", "z"), pairs)


def gather_z(rows, dest):
    back = lax.ppermute(dest, "section", [(s, (s - 1) % SECTIONS) for s in range(SECTIONS)])
    first = handoff(rows, 0)
    rows = labelled(rows, back)
    came = {k: handoff(rows, k) for k in (2, -2, 1, -1)}
    came[0] = labelled(first, dest)
    came[3] = shift(came[2], "z", 1)
    came[-3] = shift(came[-2], "z", -1)
    came[4] = shift(came[2], "z", 2)
    return jnp.concatenate([came[k] for k in ORDER], 0)


def labelled(rows, dest):
    lanes = jnp.broadcast_to(dest.astype(BF), (rows.shape[0], LANES))
    return jnp.concatenate([rows, lanes], 1)


def norm_rows(rows, gain):
    floated = rows.astype(F32)
    scale = lax.rsqrt(jnp.mean(floated * floated, axis=-1, keepdims=True) + EPSILON)
    return (floated * scale * gain).astype(BF)


def norm_kernel(a_ref, b_ref, c_ref, gain_ref, out_ref):
    width = gain_ref.shape[1]
    gain = gain_ref[...].astype(F32)
    for i, ref in enumerate((a_ref, b_ref, c_ref)):
        size = ref.shape[0]
        out_ref[i * size : (i + 1) * size, :] = norm_rows(ref[:, :width], gain)


def normed_of(blocks, gain):
    size, width = blocks[0].shape[0], gain.shape[1]
    return pl.pallas_call(
        norm_kernel,
        out_shape=jax.ShapeDtypeStruct((len(blocks) * size, width), BF),
        compiler_params=pltpu.CompilerParams(vmem_limit_bytes=VMEM),
        cost_estimate=pl.CostEstimate(
            flops=15 * size * width, bytes_accessed=12 * size * width, transcendentals=0
        ),
    )(*blocks, gain)


def hidden_kernel(
    x_ref, normed_ref, far_up_ref, far_down_ref, gain_ref, gate_0, up_0, gate_1, up_1,
    down_0, down_1, hidden_0, hidden_1, far_ref, rows, far_rows, sums,
):
    step, steps = pl.program_id(0), pl.num_programs(0)
    width, part = gain_ref.shape[1], normed_ref.shape[1]
    size = far_rows.shape[0]
    half = size // 2

    @pl.when(step == 0)
    def _():
        gain = gain_ref[...].astype(F32)
        far_rows[:half, :] = norm_rows(far_up_ref[:, :width], gain)
        far_rows[half:, :] = norm_rows(far_down_ref[:, :width], gain)
        sums[...] = jnp.zeros_like(sums)

    rows[: 3 * size, :] = normed_ref[...]
    rows[3 * size :, :] = far_rows[:, pl.ds(pl.multiple_of(step * part, part), part)]
    contract = (((1,), (1,)), ((), ()))
    for i, weight in enumerate((gate_0, up_0, gate_1, up_1)):
        sums[i] += lax.dot_general(
            rows[...], weight[...], contract, preferred_element_type=F32
        )

    @pl.when(step == steps - 1)
    def _():
        for i, hidden in enumerate((hidden_0, hidden_1)):
            value = (jax.nn.silu(sums[2 * i]) * sums[2 * i + 1]).astype(BF)
            for j, behind in enumerate((0, 1, 3, 2)):
                at = lax.rem(x_ref[0] + X - behind, X) * size
                hidden[pl.ds(pl.multiple_of(at, size), size), :] = value[j * size : (j + 1) * size]
        far_ref[...] = (
            jnp.dot(hidden_0[...], down_0[...], preferred_element_type=F32)
            + jnp.dot(hidden_1[...], down_1[...], preferred_element_type=F32)
        ).astype(BF)


def hidden_of(x, normed, far_up, far_down, gain, gates, ups, downs):
    units, width = gates[0].shape
    size, part = 2 * far_up.shape[0], width // X
    total = X * size
    whole = lambda array: pl.BlockSpec(array.shape, lambda i, x: (0, 0))
    weight = pl.BlockSpec((units, part), lambda i, x: (0, i))
    down = pl.BlockSpec((units, part), lambda i, x: (0, lax.rem(x[0] + 2, X)))
    hidden = jax.ShapeDtypeStruct((total, units), BF)
    return pl.pallas_call(
        hidden_kernel,
        grid_spec=pltpu.PrefetchScalarGridSpec(
            num_scalar_prefetch=1,
            grid=(X,),
            in_specs=[
                pl.BlockSpec((3 * size, part), lambda i, x: (0, i)),
                whole(far_up), whole(far_down), whole(gain),
                weight, weight, weight, weight, down, down,
            ],
            out_specs=[
                pl.BlockSpec((total, units), lambda i, x: (0, 0)),
                pl.BlockSpec((total, units), lambda i, x: (0, 0)),
                pl.BlockSpec((total, part), lambda i, x: (0, 0)),
            ],
            scratch_shapes=[
                pltpu.VMEM((total, part), BF),
                pltpu.VMEM((size, width), BF),
                pltpu.VMEM((4, total, units), F32),
            ],
        ),
        out_shape=[hidden, hidden, jax.ShapeDtypeStruct((total, part), BF)],
        compiler_params=pltpu.CompilerParams(vmem_limit_bytes=VMEM),
        cost_estimate=pl.CostEstimate(
            flops=9 * total * units * width, bytes_accessed=10 * units * width, transcendentals=0
        ),
    )(x, normed, far_up, far_down, gain, gates[0], ups[0], gates[1], ups[1], *downs)


def part_kernel(x_ref, hidden_0, hidden_1, down_0, down_1, out_ref):
    out_ref[0] = jnp.dot(
        hidden_0[...], down_0[...], preferred_element_type=F32
    ) + jnp.dot(hidden_1[...], down_1[...], preferred_element_type=F32)


def parts_of(x, hiddens, downs):
    units, width = downs[0].shape
    total, part = hiddens[0].shape[0], width // X
    hidden = pl.BlockSpec((total, units), lambda i, x: (0, 0))
    quarter = lambda i, x: (0, lax.rem(x[0] + lax.rem(2 * i + 1, 5), X))
    down = pl.BlockSpec((units, part), quarter)
    return pl.pallas_call(
        part_kernel,
        grid_spec=pltpu.PrefetchScalarGridSpec(
            num_scalar_prefetch=1,
            grid=(3,),
            in_specs=[hidden, hidden, down, down],
            out_specs=pl.BlockSpec((1, total, part), lambda i, x: (i, 0, 0)),
        ),
        out_shape=jax.ShapeDtypeStruct((3, total, part), F32),
        compiler_params=pltpu.CompilerParams(vmem_limit_bytes=VMEM),
        cost_estimate=pl.CostEstimate(
            flops=3 * total * units * width, bytes_accessed=6 * units * width, transcendentals=0
        ),
    )(x, *hiddens, *downs)


def add(a, b):
    return a.astype(F32) + b.astype(F32)


def body(carried, destination, norm_gain, w_gate, w_up, w_down):
    width = carried.shape[2]
    x, z, core = lax.axis_index("x"), lax.axis_index("z"), lax.axis_index("core")
    rows_each = carried.shape[1]
    total = rows_each * X * Z * CORES
    quarter, eighth = width // X, width // (X * CORES)

    gates, ups, downs = (
        [w[0], shift(w[0], "core", 1)] for w in (w_gate, w_up, w_down)
    )
    at_x = x.astype(jnp.int32)[None]

    block = gather_z(carried[0], destination[0])
    size = block.shape[0]
    up, down = shift(block, "x", 1), shift(block, "x", -1)
    far_up, far_down = shift(up[: size // 2], "x", 1), shift(down[size // 2 :], "x", -1)
    normed = normed_of([block, up, down], norm_gain)
    *hiddens, far = hidden_of(
        at_x, normed, far_up, far_down, norm_gain, gates, ups, downs
    )

    rows = jnp.zeros((X * size, quarter + LANES), BF)
    for piece, behind, offset in (
        (block, 0, 0),
        (up, 1, 0),
        (down, 3, 0),
        (far_up, 2, 0),
        (far_down, 2, size // 2),
    ):
        at = lax.rem(x + X - behind, X) * size + offset
        kept = lax.dynamic_slice_in_dim(piece, x * quarter, quarter, 1)
        kept = jnp.concatenate([kept, piece[:, width:]], 1)
        rows = lax.dynamic_update_slice_in_dim(rows, kept, at, 0)

    half = quarter // 2
    up = shift(far[:, :half], "x", 1)
    down = shift(far[:, half:], "x", -1)
    near_up, near_down, own = parts_of(at_x, hiddens, downs)
    up = jnp.concatenate([add(near_up[:, :half], up), near_up[:, half:]], 1).astype(BF)
    up = shift(up, "x", 1)
    down = jnp.concatenate([near_down[:, :half], add(near_down[:, half:], down)], 1)
    down = shift(down.astype(BF), "x", -1)
    summed = own + up.astype(F32) + down.astype(F32)

    def swap(array, *more):
        mine = lax.dynamic_slice_in_dim(array, core * eighth, eighth, 1)
        theirs = lax.dynamic_slice_in_dim(array, (1 - core) * eighth, eighth, 1)
        mine, theirs = (jnp.concatenate([part, *more], 1) for part in (mine, theirs))
        return jnp.concatenate([mine, shift(theirs, "core", 1)], 0)

    residual = swap(rows[:, :quarter], rows[:, quarter:])
    dest = residual[:, eighth].astype(jnp.int32)
    residual = residual[:, :eighth]

    index = jnp.arange(total, dtype=jnp.int32)
    place_z = (index // rows_each) % Z
    behind = jnp.zeros_like(index)
    for i, k in enumerate(ORDER):
        behind = jnp.where(place_z == i, k, behind)
    source_core = jnp.where(index < total // CORES, core, 1 - core)
    source_x = (index // (rows_each * Z)) % X
    source = source_x * Z + lax.rem(z + Z - behind, Z)
    key = (source * CORES + source_core) * rows_each + index % rows_each
    earlier = (dest[:, None] == dest[None, :]) & (key[None, :] < key[:, None])
    rank = jnp.sum(earlier.astype(jnp.int32), axis=1)

    summed = swap(summed).astype(BF)

    slots = X * CORES * SLOTS
    dest_z = (dest // CORES) % Z
    slot_of = ((dest // (CORES * Z)) * CORES + dest % CORES) * SLOTS + rank
    slot = jnp.arange(slots, dtype=jnp.int32)

    def pick(k):
        at = lax.rem(z + k, Z)
        return ((slot_of[None, :] == slot[:, None]) & (dest_z == at)[None, :]).astype(BF)

    def slotted(k):
        return jnp.dot(pick(k), summed, preferred_element_type=F32)

    def message(*steps):
        return jnp.concatenate([slotted(k % Z).astype(BF) for k in steps], 0)

    middle = slots // 2
    up_near = shift(message(3, 1), "z", 1)
    down_near = shift(message(-3, -1), "z", -1)
    opposite = message(4)
    up_far = shift(opposite[:middle], "z", 2)
    down_far = shift(opposite[middle:], "z", -2)
    up = add(slotted(2), up_near[:slots])
    up = jnp.concatenate([add(up[:middle], up_far), up[middle:]], 0)
    down = add(slotted(6), down_near[:slots])
    down = jnp.concatenate([down[:middle], add(down[middle:], down_far)], 0)
    up = shift(up.astype(BF), "z", 2)
    down = shift(down.astype(BF), "z", -2)
    mine = slotted(0) + jnp.dot(pick(0), residual, preferred_element_type=F32)
    near = add(up_near[slots:], down_near[slots:])
    mixed = (mine + near + add(up, down)).astype(BF)

    pieces = lax.all_to_all(
        mixed.reshape(X * CORES, SLOTS, eighth), ("x", "core"), 0, 0, tiled=True
    )
    return pieces.transpose(1, 0, 2).reshape(1, SLOTS, width)


def solution(mesh):
    split = Mesh(
        mesh.devices.reshape(SECTIONS, X, Z, CORES), ("section", "x", "z", "core")
    )
    peers = ("x", "z", "core")
    return jax.shard_map(
        body,
        mesh=split,
        in_specs=(
            P("section", peers, None),
            P("section", peers, None),
            P("section", None),
            P("section", peers, None),
            P("section", peers, None),
            P("section", peers, None),
        ),
        out_specs=P("section", peers, None),
        check_vma=False,
    )
```

time: 144 us -> 167 us (1.16)
  local copies, waits for them, and re-layouts: 7.31 us -> 48.5 us
  waiting for transfers between devices: 51 us -> 34.5 us
  matrix products: 16.4 us -> 2.53 us
  Pallas kernels: 0 us -> 10.7 us
  blocking collectives: 12.9 us -> 10 us
  starting transfers between devices: 50.9 us -> 52.7 us
    dynamic_update_slice x4 -> x5, local copies, waits for them, and re-layouts: 3.31 us -> 21.9 us  [body(): rows = lax.dynamic_update_slice_in_dim(rows, kept, at, 0)]
    dot_general x6 -> x0, matrix products: 13.9 us -> none  [the longest x4 6.33 us: part(): return jnp.dot(hidden, down_part[k], preferred_element_type=F32)]
    ppermute x26 -> x22, waiting for transfers between devices: 45 us -> 31.8 us  [shift(): return lax.ppermute(array, axis, [(i, (i + by) % n) for i in range(n)])]
    pallas_call x0 -> x3, Pallas kernels: none -> 10.7 us  [the longest x1 6.67 us: hidden_of(): pl.pallas_call(hidden_kernel, grid_spec=pltpu.PrefetchScalarGridSpec(num_...]
    unnamed x21 -> x22, local copies, waits for them, and re-layouts: 0.11 us -> 10.7 us
    concatenate x0 -> x5, local copies, waits for them, and re-layouts: none -> 6.63 us  [body(): kept = jnp.concatenate([kept, piece[:, width:]], 1)]
    ppermute x26 -> x22, starting transfers between devices: 40.8 us -> 37.1 us  [shift(): return lax.ppermute(array, axis, [(i, (i + by) % n) for i in range(n)])]
    ppermute x0 -> x1, starting transfers between devices: none -> 3.56 us  [gather_z(): lax.ppermute(dest, 'section', [(s, (s - 1) % SECTIONS) for s in range(SEC...]
  transfers between devices with their start and end apart: 31 -> 28, of which waited for: 14 -> 10; matrix products, arithmetic and copies ran while one was open for 18% -> 29% of each run, Pallas kernels for 0% -> 6%
where the time goes in v5:
time: 167 us; the launch traced here: 166 us
  starting transfers between devices  52.7 us (32%)
  local copies, waits for them, and re-layouts  48.5 us (29%)
  waiting for transfers between devices  34.5 us (21%)
  Pallas kernels  10.7 us (6%)
  blocking collectives  10 us (6%)
  other arithmetic  6.25 us (4%)
  matrix products  2.53 us (2%)
    ppermute x22, starting transfers between devices, shift(): return lax.ppermute(array, axis, [(i, (i + by) % n) for i in range(n)])  37.1 us
    ppermute x22, waiting for transfers between devices, shift(): return lax.ppermute(array, axis, [(i, (i + by) % n) for i in range(n)])  31.8 us
    dynamic_update_slice x5, local copies, waits for them, and re-layouts, body(): rows = lax.dynamic_update_slice_in_dim(rows, kept, at, 0)  21.9 us
    ppermute x5, starting transfers between devices, handoff(): return lax.ppermute(rows, ('section', 'z'), pairs)  12 us
    unnamed x22, local copies, waits for them, and re-layouts  10.7 us
    all_to_all x1, blocking collectives, body(): lax.all_to_all(mixed.reshape(X * CORES, SLOTS, eighth), ('x', 'core'), 0,...  10 us
    pallas_call x1, Pallas kernels, hidden_of(): pl.pallas_call(hidden_kernel, grid_spec=pltpu.PrefetchScalarGridSpec(num_...  6.67 us
    concatenate x5, local copies, waits for them, and re-layouts, body(): kept = jnp.concatenate([kept, piece[:, width:]], 1)  6.63 us
  transfers between devices with their start and end apart: 28, of which 10 were waited for; matrix products, arithmetic and copies ran while one was open for 29% of the time, Pallas kernels for 6%

profile of v5, /device:TPU:1, one launch (start us, length us, event | category | flops | bytes accessed | tf_op | source)
XLA Modules:
  0.0 165.7 jit_solution(11072638691117016219)
XLA Ops:
  0.0 3.6 %collective-permute-start.1 = (s32[8,1]{0,1:T(1,128)}, s32[8,1]{0,1:T(1,128)S(1)}, u32[]{:S(2)}, u32[]{:S(2)}) collective-permute-start(s32[8,1]{0,1:T(1,128)} %bitcast.37), channel_id=1, source_target_pairs={{0,192},{64,0},{128,64},{192,128},{1,193},{65,1},{129,65},{193,129... | collective-permute-start | bytes 104 | tf_op jit(solution)/shard_map/ppermute | solution.py:33
  4.5 0.9 pad_maximum_fusion.17
  5.4 6.0 %collective-permute-start.5 = (bf16[8,5248]{1,0:T(8,128)(2,1)S(1)}, bf16[8,5248]{1,0:T(8,128)(2,1)S(1)}, u32[]{:S(2)}, u32[]{:S(2)}) collective-permute-start(bf16[8,5248]{1,0:T(8,128)(2,1)S(1)} %pad_maximum_fusion.17), channel_id=1, source_target_pairs={{0,76},{2,78},{4,64},{6,66},{8,68},{10,70},{12,72},{14,74},{64,140... | collective-permute-start | bytes 251912 | tf_op jit(solution)/shard_map/ppermute | solution.py:29
  11.4 6.1 %collective-permute-start.3 = (bf16[8,5248]{1,0:T(8,128)(2,1)S(1)}, bf16[8,5248]{1,0:T(8,128)(2,1)S(1)}, u32[]{:S(2)}, u32[]{:S(2)}) collective-permute-start(bf16[8,5248]{1,0:T(8,128)(2,1)S(1)} %pad_maximum_fusion.17), channel_id=1, source_target_pairs={{0,78},{2,64},{4,66},{6,68},{8,70},{10,72},{12,74},{14,76},{64,142... | collective-permute-start | bytes 251912 | tf_op jit(solution)/shard_map/ppermute | solution.py:29
  18.2 1.6 collective-permute-done.4
  19.8 1.0 collective-permute-start.6
  20.8 2.4 %collective-permute-start.7 = (bf16[8,5248]{1,0:T(8,128)(2,1)S(1)}, bf16[8,5248]{1,0:T(8,128)(2,1)S(1)}, u32[]{:S(2)}, u32[]{:S(2)}) collective-permute-start(bf16[8,5248]{1,0:T(8,128)(2,1)S(1)} %collective-permute-done.5), channel_id=1, source_target_pairs={{0,14},{2,0},{4,2},{6,4},{8,6},{10,8},{12,10},{14,12},{1,15},{3,1}... | collective-permute-start | bytes 251912 | tf_op jit(solution)/shard_map/ppermute | solution.py:20
  23.2 0.9 collective-permute-done.2
  29.2 2.5 %collective-permute-start.10 = (bf16[64,5248]{1,0:T(8,128)(2,1)}, bf16[64,5248]{1,0:T(8,128)(2,1)S(1)}, u32[]{:S(2)}, u32[]{:S(2)}) collective-permute-start(bf16[64,5248]{1,0:T(8,128)(2,1)} %constant_dynamic-update-slice_fusion.a_ref), channel_id=1, source_target_pairs={{0,48},{16,0},{32,16},{48,32},{1,49},{17,1},{33,17},{49,33},{2,50}... | collective-permute-start | bytes 2015240 | tf_op jit(solution)/shard_map/ppermute | solution.py:20
  31.7 4.3 %collective-permute-start.14 = (bf16[216,5120]{1,0:T(8,128)(2,1)}, bf16[216,5120]{1,0:T(8,128)(2,1)}, u32[]{:S(2)}, u32[]{:S(2)}) collective-permute-start(bf16[216,5120]{1,0:T(8,128)(2,1)} %bitcast.26), channel_id=1, source_target_pairs={{0,1},{1,0},{2,3},{3,2},{4,5},{5,4},{6,7},{7,6},{8,9},{9,8},{10,11... | collective-permute-start | bytes 6635528 | tf_op jit(solution)/shard_map/ppermute | solution.py:20
  37.3 0.9 constant_dynamic-slice_fusion.7
  38.9 1.8 %copy.14 = bf16[64,1408]{0,1:T(8,128)(2,1)} copy(bf16[64,1408]{1,0:T(8,128)(2,1)} %pad_maximum_fusion.10) | data formatting | bytes 360448 | tf_op jit(solution)/shard_map/concatenate | solution.py:212
  40.7 0.9 broadcast_in_dim.31
  41.6 4.7 %dynamic_update_slice.15 = bf16[256,1408]{0,1:T(8,128)(2,1)} dynamic-update-slice(bf16[256,1408]{0,1:T(8,128)(2,1)} %broadcast_in_dim.31, bf16[64,1408]{0,1:T(8,128)(2,1)} %copy.14, s32[]{:T(128)S(6)} %select_n.257, s32[]{:T(128)} %constant.162.clone.1) | dynamic-update-slice | bytes 360452 | tf_op jit(solution)/shard_map/dynamic_update_slice | solution.py:213
  46.3 0.7 slice.117
  47.1 2.9 %collective-permute-start.12 = (bf16[32,5248]{1,0:T(8,128)(2,1)}, bf16[32,5248]{1,0:T(8,128)(2,1)}, u32[]{:S(2)}, u32[]{:S(2)}) collective-permute-start(bf16[32,5248]{1,0:T(8,128)(2,1)} %slice.117), channel_id=1, source_target_pairs={{0,48},{16,0},{32,16},{48,32},{1,49},{17,1},{33,17},{49,33},{2,50}... | collective-permute-start | bytes 1007624 | tf_op jit(solution)/shard_map/ppermute | solution.py:20
  50.0 0.8 slice.115
  52.2 1.8 %copy.16 = bf16[64,1408]{0,1:T(8,128)(2,1)} copy(bf16[64,1408]{1,0:T(8,128)(2,1)} %pad_maximum_fusion.12) | data formatting | bytes 360448 | tf_op jit(solution)/shard_map/concatenate | solution.py:212
  54.0 1.6 pad_maximum_fusion.11
  55.6 1.8 %copy.15 = bf16[64,1408]{0,1:T(8,128)(2,1)} copy(bf16[64,1408]{1,0:T(8,128)(2,1)} %pad_maximum_fusion.11) | data formatting | bytes 360448 | tf_op jit(solution)/shard_map/concatenate | solution.py:212
  57.4 4.7 %dynamic_update_slice.16 = bf16[256,1408]{0,1:T(8,128)(2,1)} dynamic-update-slice(bf16[256,1408]{0,1:T(8,128)(2,1)} %dynamic_update_slice.15, bf16[64,1408]{0,1:T(8,128)(2,1)} %copy.15, s32[]{:T(128)S(6)} %select_n.258, s32[]{:T(128)} %constant.162.clone.1) | dynamic-update-slice | bytes 360452 | tf_op jit(solution)/shard_map/dynamic_update_slice | solution.py:213
  62.1 5.3 %dynamic_update_slice.17 = bf16[256,1408]{0,1:T(8,128)(2,1)} dynamic-update-slice(bf16[256,1408]{0,1:T(8,128)(2,1)} %dynamic_update_slice.16, bf16[64,1408]{0,1:T(8,128)(2,1)} %copy.16, s32[]{:T(128)S(6)} %select_n.259, s32[]{:T(128)} %constant.162.clone.1) | dynamic-update-slice | bytes 360452 | tf_op jit(solution)/shard_map/dynamic_update_slice | solution.py:213
  68.1 2.2 %shard_map.64.normed_ref = bf16[192,5120]{1,0:T(8,128)(2,1)S(1)} custom-call(bf16[64,5248]{1,0:T(8,128)(2,1)} %constant_dynamic-update-slice_fusion.a_ref, bf16[64,5248]{1,0:T(8,128)(2,1)S(1)} %collective-permute-done.9.b_ref, bf16[64,5248]{1,0:T(8,128)(2,1)S(1)} %collective-permute-done.10.c_ref, bf16[1,5120]{1,0:T(2,128)(2,1)S(1)} %copy-done.5), custom_call_target="tpu_custom_call" | custom-call | flops 4915200 | bytes 3932160 | tf_op jit(solution)/shard_map/pallas_call | solution.py:65
  70.3 1.3 copy-done.1
  71.6 0.8 slice.116
  72.4 0.9 constant_dynamic-slice_fusion.3
  74.3 0.9 copy.18
  75.2 2.4 %dynamic_update_slice.18 = bf16[256,1408]{0,1:T(8,128)(2,1)S(1)} dynamic-update-slice(bf16[256,1408]{0,1:T(8,128)(2,1)S(1)} %copy-done.7, bf16[32,1408]{0,1:T(8,128)(2,1)S(1)} %copy.17, s32[]{:T(128)S(6)} %select_n.260, s32[]{:T(128)} %constant.162.clone.1) | dynamic-update-slice | bytes 180228 | tf_op jit(solution)/shard_map/dynamic_update_slice | solution.py:213
  77.6 4.9 %dynamic_update_slice.19 = bf16[256,1408]{0,1:T(8,128)(2,1)S(1)} dynamic-update-slice(bf16[256,1408]{0,1:T(8,128)(2,1)S(1)} %dynamic_update_slice.18, bf16[32,1408]{0,1:T(8,128)(2,1)} %copy.18, s32[]{:T(128)S(6)} %select_n.261, s32[]{:T(128)} %constant.162.clone.1) | dynamic-update-slice | bytes 180228 | tf_op jit(solution)/shard_map/dynamic_update_slice | solution.py:213
  82.7 1.8 %collective-permute-start.13 = (bf16[256,768]{0,1:T(8,128)(2,1)S(1)}, bf16[256,768]{0,1:T(8,128)(2,1)S(1)}, u32[]{:S(2)}, u32[]{:S(2)}) collective-permute-start(bf16[256,768]{0,1:T(8,128)(2,1)S(1)} %pad_maximum_fusion.7), channel_id=1, source_target_pairs={{0,1},{1,0},{2,3},{3,2},{4,5},{5,4},{6,7},{7,6},{8,9},{9,8},{10,11... | collective-permute-start | bytes 1179656 | tf_op jit(solution)/shard_map/ppermute | solution.py:20
  84.5 1.5 copy-done.2
  86.0 1.6 copy-done.3
  87.7 1.6 copy-done.4
  89.3 6.7 %shard_map.65 = (bf16[256,216]{1,0:T(8,128)(2,1)S(1)}, bf16[256,216]{1,0:T(8,128)(2,1)S(1)}, bf16[256,1280]{1,0:T(8,128)(2,1)S(1)}) custom-call(s32[1]{0:T(128)} %bitcast.5.x_ref, bf16[192,5120]{1,0:T(8,128)(2,1)S(1)} %copy-done.2, bf16[32,5248]{1,0:T(8,128)(2,1)} %collective-permute-done.11.far_up_ref, ...), custom_call_target="tpu_custom_call" | custom-call | flops 2548039680 | bytes 11059200 | tf_op jit(solution)/shard_map/pallas_call | solution.py:120
  96.1 4.1 %collective-permute-start.19 = (bf16[256,640]{1,0:T(8,128)(2,1)S(1)}, bf16[256,640]{1,0:T(8,128)(2,1)S(1)}, u32[]{:S(2)}, u32[]{:S(2)}) collective-permute-start(bf16[256,640]{1,0:T(8,128)(2,1)S(1)} %get-tuple-element.18), channel_id=1, source_target_pairs={{0,48},{16,0},{32,16},{48,32},{1,49},{17,1},{33,17},{49,33},{2,50}... | collective-permute-start | bytes 983048 | tf_op jit(solution)/shard_map/ppermute | solution.py:20
  100.2 1.8 %shard_map.66 = f32[3,256,1280]{2,1,0:T(8,128)S(1)} custom-call(s32[1]{0:T(128)} %bitcast.5.x_ref, bf16[256,216]{1,0:T(8,128)(2,1)S(1)} %get-tuple-element.8.hidden_0, bf16[256,216]{1,0:T(8,128)(2,1)S(1)} %get-tuple-element.9.hidden_1, bf16[216,5120]{1,0:T(8,128)(2,1)S(1)} %bitcast.25, bf16[216,5120]{1,0:T(8,128)(2,1)S(1)} %collective-permute-done.16.down_1), custom_call_target="tpu_custom_call" | custom-call | flops 849346560 | bytes 6635520 | tf_op jit(solution)/shard_map/pallas_call | solution.py:161
  102.3 3.5 %collective-permute-done.19 = bf16[256,640]{1,0:T(8,128)(2,1)S(1)} collective-permute-done((bf16[256,640]{1,0:T(8,128)(2,1)S(1)}, bf16[256,640]{1,0:T(8,128)(2,1)S(1)}, u32[]{:S(2)}, u32[]{:S(2)}) %collective-permute-start.19) | collective-permute-done | bytes 327712 | tf_op jit(solution)/shard_map/ppermute | solution.py:20
  106.0 3.5 %collective-permute-start.20 = (bf16[256,1280]{1,0:T(8,128)(2,1)S(1)}, bf16[256,1280]{1,0:T(8,128)(2,1)S(1)}, u32[]{:S(2)}, u32[]{:S(2)}) collective-permute-start(bf16[256,1280]{1,0:T(8,128)(2,1)S(1)} %pad_maximum_fusion.5), channel_id=1, source_target_pairs={{0,48},{16,0},{32,16},{48,32},{1,49},{17,1},{33,17},{49,33},{2,50}... | collective-permute-start | bytes 1966088 | tf_op jit(solution)/shard_map/ppermute | solution.py:20
  109.8 11.4 %collective-permute-done.20 = bf16[256,1280]{1,0:T(8,128)(2,1)S(1)} collective-permute-done((bf16[256,1280]{1,0:T(8,128)(2,1)S(1)}, bf16[256,1280]{1,0:T(8,128)(2,1)S(1)}, u32[]{:S(2)}, u32[]{:S(2)}) %collective-permute-start.20) | collective-permute-done | bytes 655392 | tf_op jit(solution)/shard_map/ppermute | solution.py:20
  121.2 3.3 %collective-permute-done.18 = bf16[256,1280]{1,0:T(8,128)(2,1)S(1)} collective-permute-done((bf16[256,1280]{1,0:T(8,128)(2,1)S(1)}, bf16[256,1280]{1,0:T(8,128)(2,1)S(1)}, u32[]{:S(2)}, u32[]{:S(2)}) %collective-permute-start.18) | collective-permute-done | bytes 655392 | tf_op jit(solution)/shard_map/ppermute | solution.py:20
  124.9 3.5 %collective-permute-start.21 = (bf16[256,640]{1,0:T(8,128)(2,1)S(1)}, bf16[256,640]{1,0:T(8,128)(2,1)S(1)}, u32[]{:S(2)}, u32[]{:S(2)}) collective-permute-start(bf16[256,640]{1,0:T(8,128)(2,1)S(1)} %get-tuple-element.16), channel_id=1, source_target_pairs={{0,1},{1,0},{2,3},{3,2},{4,5},{5,4},{6,7},{7,6},{8,9},{9,8},{10,11... | collective-permute-start | bytes 983048 | tf_op jit(solution)/shard_map/ppermute | solution.py:20
  128.8 0.9 collective-permute-done.21
  130.3 3.6 %collective-permute-start.26 = (bf16[64,640]{1,0:T(8,128)(2,1)S(1)}, bf16[64,640]{1,0:T(8,128)(2,1)S(1)}, u32[]{:S(2)}, u32[]{:S(2)}) collective-permute-start(bf16[64,640]{1,0:T(8,128)(2,1)S(1)} %get-tuple-element.22), channel_id=1, source_target_pairs={{0,12},{2,14},{4,0},{6,2},{8,4},{10,6},{12,8},{14,10},{1,13},{3,15... | collective-permute-start | bytes 245768 | tf_op jit(solution)/shard_map/ppermute | solution.py:20
  135.1 2.7 %collective-permute-start.23 = (bf16[256,640]{1,0:T(8,128)(2,1)S(1)}, bf16[256,640]{1,0:T(8,128)(2,1)S(1)}, u32[]{:S(2)}, u32[]{:S(2)}) collective-permute-start(bf16[256,640]{1,0:T(8,128)(2,1)S(1)} %pad_maximum_fusion.9), channel_id=1, source_target_pairs={{0,14},{2,0},{4,2},{6,4},{8,6},{10,8},{12,10},{14,12},{1,15},{3,1}... | collective-permute-start | bytes 983048 | tf_op jit(solution)/shard_map/ppermute | solution.py:20
  137.9 6.4 %collective-permute-done.22 = bf16[256,640]{1,0:T(8,128)(2,1)S(1)} collective-permute-done((bf16[256,640]{1,0:T(8,128)(2,1)S(1)}, bf16[256,640]{1,0:T(8,128)(2,1)S(1)}, u32[]{:S(2)}, u32[]{:S(2)}) %collective-permute-start.22) | collective-permute-done | bytes 327712 | tf_op jit(solution)/shard_map/ppermute | solution.py:20
  145.1 3.6 %collective-permute-start.27 = (bf16[128,640]{1,0:T(8,128)(2,1)S(1)}, bf16[128,640]{1,0:T(8,128)(2,1)S(1)}, u32[]{:S(2)}, u32[]{:S(2)}) collective-permute-start(bf16[128,640]{1,0:T(8,128)(2,1)S(1)} %pad_maximum_fusion.14), channel_id=1, source_target_pairs={{0,12},{2,14},{4,0},{6,2},{8,4},{10,6},{12,8},{14,10},{1,13},{3,15... | collective-permute-start | bytes 491528 | tf_op jit(solution)/shard_map/ppermute | solution.py:20
  149.1 5.5 %collective-permute-done.25 = bf16[128,640]{1,0:T(8,128)(2,1)S(1)} collective-permute-done((bf16[128,640]{1,0:T(8,128)(2,1)S(1)}, bf16[128,640]{1,0:T(8,128)(2,1)S(1)}, u32[]{:S(2)}, u32[]{:S(2)}) %collective-permute-start.25) | collective-permute-done | bytes 163872 | tf_op jit(solution)/shard_map/ppermute | solution.py:20
  154.9 10.0 %all_to_all.5 = bf16[8,16,640]{2,1,0:T(8,128)(2,1)S(1)} all-to-all(bf16[8,16,640]{2,1,0:T(8,128)(2,1)S(1)} %bitcast.31), channel_id=1, replica_groups=mesh['section'=4,'x'=4,'z'=8,'core'=2] {'x','core'}, dimensions={0} | all-to-all | bytes 327680 | tf_op jit(solution)/shard_map/all_to_all | solution.py:280
  (108 shorter events, 17.4 us)
Async XLA Ops:
  0.0 4.4 %collective-permute-start.1 = (s32[8,1]{0,1:T(1,128)}, s32[8,1]{0,1:T(1,128)S(1)}, u32[]{:S(2)}, u32[]{:S(2)}) collective-permute-start(s32[8,1]{0,1:T(1,128)} %bitcast.37), channel_id=1, source_target_pairs={{0,192},{64,0},{128,64},{192,128},{1,193},{65,1},{129,65},{193,129... | collective-permute-start | bytes 104 | tf_op jit(solution)/shard_map/ppermute | solution.py:33
  3.6 13.9 %collective-permute-start = (bf16[8,5120]{1,0:T(8,128)(2,1)}, bf16[8,5120]{1,0:T(8,128)(2,1)S(1)}, u32[]{:S(2)}, u32[]{:S(2)}) collective-permute-start(bf16[8,5120]{1,0:T(8,128)(2,1)} %bitcast.32), channel_id=1, source_target_pairs={{0,64},{2,66},{4,68},{6,70},{8,72},{10,74},{12,76},{14,78},{64,128... | collective-permute-start | bytes 245768 | tf_op jit(solution)/shard_map/ppermute | solution.py:29
  5.4 15.4 %collective-permute-start.5 = (bf16[8,5248]{1,0:T(8,128)(2,1)S(1)}, bf16[8,5248]{1,0:T(8,128)(2,1)S(1)}, u32[]{:S(2)}, u32[]{:S(2)}) collective-permute-start(bf16[8,5248]{1,0:T(8,128)(2,1)S(1)} %pad_maximum_fusion.17), channel_id=1, source_target_pairs={{0,76},{2,78},{4,64},{6,66},{8,68},{10,70},{12,72},{14,74},{64,140... | collective-permute-start | bytes 251912 | tf_op jit(solution)/shard_map/ppermute | solution.py:29
  11.4 8.4 %collective-permute-start.4 = (bf16[8,5248]{1,0:T(8,128)(2,1)S(1)}, bf16[8,5248]{1,0:T(8,128)(2,1)S(1)}, u32[]{:S(2)}, u32[]{:S(2)}) collective-permute-start(bf16[8,5248]{1,0:T(8,128)(2,1)S(1)} %pad_maximum_fusion.17), channel_id=1, source_target_pairs={{0,68},{2,70},{4,72},{6,74},{8,76},{10,78},{12,64},{14,66},{64,132... | collective-permute-start | bytes 251912 | tf_op jit(solution)/shard_map/ppermute | solution.py:29
  11.4 13.3 %collective-permute-start.3 = (bf16[8,5248]{1,0:T(8,128)(2,1)S(1)}, bf16[8,5248]{1,0:T(8,128)(2,1)S(1)}, u32[]{:S(2)}, u32[]{:S(2)}) collective-permute-start(bf16[8,5248]{1,0:T(8,128)(2,1)S(1)} %pad_maximum_fusion.17), channel_id=1, source_target_pairs={{0,78},{2,64},{4,66},{6,68},{8,70},{10,72},{12,74},{14,76},{64,142... | collective-permute-start | bytes 251912 | tf_op jit(solution)/shard_map/ppermute | solution.py:29
  17.4 6.6 %collective-permute-start.2 = (bf16[8,5248]{1,0:T(8,128)(2,1)S(1)}, bf16[8,5248]{1,0:T(8,128)(2,1)S(1)}, u32[]{:S(2)}, u32[]{:S(2)}) collective-permute-start(bf16[8,5248]{1,0:T(8,128)(2,1)S(1)} %pad_maximum_fusion.17), channel_id=1, source_target_pairs={{0,66},{2,68},{4,70},{6,72},{8,74},{10,76},{12,78},{14,64},{64,130... | collective-permute-start | bytes 251912 | tf_op jit(solution)/shard_map/ppermute | solution.py:29
  19.8 8.8 %collective-permute-start.8 = (bf16[8,5248]{1,0:T(8,128)(2,1)S(1)}, bf16[8,5248]{1,0:T(8,128)(2,1)S(1)}, u32[]{:S(2)}, u32[]{:S(2)}) collective-permute-start(bf16[8,5248]{1,0:T(8,128)(2,1)S(1)} %collective-permute-done.4), channel_id=1, source_target_pairs={{0,4},{2,6},{4,8},{6,10},{8,12},{10,14},{12,0},{14,2},{1,5},{3,7},... | collective-permute-start | bytes 251912 | tf_op jit(solution)/shard_map/ppermute | solution.py:20
  19.8 7.5 %collective-permute-start.6 = (bf16[8,5248]{1,0:T(8,128)(2,1)S(1)}, bf16[8,5248]{1,0:T(8,128)(2,1)S(1)}, u32[]{:S(2)}, u32[]{:S(2)}) collective-permute-start(bf16[8,5248]{1,0:T(8,128)(2,1)S(1)} %collective-permute-done.4), channel_id=1, source_target_pairs={{0,2},{2,4},{4,6},{6,8},{8,10},{10,12},{12,14},{14,0},{1,3},{3,5},... | collective-permute-start | bytes 251912 | tf_op jit(solution)/shard_map/ppermute | solution.py:20
  20.8 7.2 %collective-permute-start.7 = (bf16[8,5248]{1,0:T(8,128)(2,1)S(1)}, bf16[8,5248]{1,0:T(8,128)(2,1)S(1)}, u32[]{:S(2)}, u32[]{:S(2)}) collective-permute-start(bf16[8,5248]{1,0:T(8,128)(2,1)S(1)} %collective-permute-done.5), channel_id=1, source_target_pairs={{0,14},{2,0},{4,2},{6,4},{8,6},{10,8},{12,10},{14,12},{1,15},{3,1}... | collective-permute-start | bytes 251912 | tf_op jit(solution)/shard_map/ppermute | solution.py:20
  29.2 17.1 %collective-permute-start.10 = (bf16[64,5248]{1,0:T(8,128)(2,1)}, bf16[64,5248]{1,0:T(8,128)(2,1)S(1)}, u32[]{:S(2)}, u32[]{:S(2)}) collective-permute-start(bf16[64,5248]{1,0:T(8,128)(2,1)} %constant_dynamic-update-slice_fusion.a_ref), channel_id=1, source_target_pairs={{0,48},{16,0},{32,16},{48,32},{1,49},{17,1},{33,17},{49,33},{2,50}... | collective-permute-start | bytes 2015240 | tf_op jit(solution)/shard_map/ppermute | solution.py:20
  31.7 18.3 %collective-permute-start.9 = (bf16[64,5248]{1,0:T(8,128)(2,1)}, bf16[64,5248]{1,0:T(8,128)(2,1)S(1)}, u32[]{:S(2)}, u32[]{:S(2)}) collective-permute-start(bf16[64,5248]{1,0:T(8,128)(2,1)} %constant_dynamic-update-slice_fusion.a_ref), channel_id=1, source_target_pairs={{0,16},{16,32},{32,48},{48,0},{1,17},{17,33},{33,49},{49,1},{2,18}... | collective-permute-start | bytes 2015240 | tf_op jit(solution)/shard_map/ppermute | solution.py:20
  31.7 52.7 %collective-permute-start.14 = (bf16[216,5120]{1,0:T(8,128)(2,1)}, bf16[216,5120]{1,0:T(8,128)(2,1)}, u32[]{:S(2)}, u32[]{:S(2)}) collective-permute-start(bf16[216,5120]{1,0:T(8,128)(2,1)} %bitcast.26), channel_id=1, source_target_pairs={{0,1},{1,0},{2,3},{3,2},{4,5},{5,4},{6,7},{7,6},{8,9},{9,8},{10,11... | collective-permute-start | bytes 6635528 | tf_op jit(solution)/shard_map/ppermute | solution.py:20
  36.0 48.4 %collective-permute-start.15 = (bf16[216,5120]{1,0:T(8,128)(2,1)}, bf16[216,5120]{1,0:T(8,128)(2,1)}, u32[]{:S(2)}, u32[]{:S(2)}) collective-permute-start(bf16[216,5120]{1,0:T(8,128)(2,1)} %bitcast.28), channel_id=1, source_target_pairs={{0,1},{1,0},{2,3},{3,2},{4,5},{5,4},{6,7},{7,6},{8,9},{9,8},{10,11... | collective-permute-start | bytes 6635528 | tf_op jit(solution)/shard_map/ppermute | solution.py:20
  36.0 48.4 %collective-permute-start.16 = (bf16[216,5120]{1,0:T(8,128)(2,1)}, bf16[216,5120]{1,0:T(8,128)(2,1)S(1)}, u32[]{:S(2)}, u32[]{:S(2)}) collective-permute-start(bf16[216,5120]{1,0:T(8,128)(2,1)} %bitcast.23), channel_id=1, source_target_pairs={{0,1},{1,0},{2,3},{3,2},{4,5},{5,4},{6,7},{7,6},{8,9},{9,8},{10,11... | collective-permute-start | bytes 6635528 | tf_op jit(solution)/shard_map/ppermute | solution.py:20
  47.1 25.4 %collective-permute-start.12 = (bf16[32,5248]{1,0:T(8,128)(2,1)}, bf16[32,5248]{1,0:T(8,128)(2,1)}, u32[]{:S(2)}, u32[]{:S(2)}) collective-permute-start(bf16[32,5248]{1,0:T(8,128)(2,1)} %slice.117), channel_id=1, source_target_pairs={{0,48},{16,0},{32,16},{48,32},{1,49},{17,1},{33,17},{49,33},{2,50}... | collective-permute-start | bytes 1007624 | tf_op jit(solution)/shard_map/ppermute | solution.py:20
  50.8 20.9 %collective-permute-start.11 = (bf16[32,5248]{1,0:T(8,128)(2,1)}, bf16[32,5248]{1,0:T(8,128)(2,1)}, u32[]{:S(2)}, u32[]{:S(2)}) collective-permute-start(bf16[32,5248]{1,0:T(8,128)(2,1)} %slice.115), channel_id=1, source_target_pairs={{0,16},{16,32},{32,48},{48,0},{1,17},{17,33},{33,49},{49,1},{2,18}... | collective-permute-start | bytes 1007624 | tf_op jit(solution)/shard_map/ppermute | solution.py:20
  67.4 0.7 copy-start.5
  70.3 1.3 copy-start.1
  71.6 3.6 %copy-start.7 = (bf16[256,1408]{0,1:T(8,128)(2,1)S(1)}, bf16[256,1408]{0,1:T(8,128)(2,1)}, u32[]{:S(2)}) copy-start(bf16[256,1408]{0,1:T(8,128)(2,1)} %dynamic_update_slice.17) | copy-start | bytes 2162692
  82.5 2.0 %copy-start = (bf16[1,216,5120]{2,1,0:T(8,128)(2,1)S(1)}, bf16[1,216,5120]{2,1,0:T(8,128)(2,1)}, u32[]{:S(2)}) copy-start(bf16[1,216,5120]{2,1,0:T(8,128)(2,1)} %param.11) | copy-start | bytes 6635524
  82.6 1.9 %copy-start.6 = (bf16[1,5120]{1,0:T(2,128)(2,1)S(1)}, bf16[1,5120]{1,0:T(2,128)(2,1)}, u32[]{:S(2)}) copy-start(bf16[1,5120]{1,0:T(2,128)(2,1)} %gain_ref.3) | copy-start | bytes 30724
  82.7 27.0 %collective-permute-start.13 = (bf16[256,768]{0,1:T(8,128)(2,1)S(1)}, bf16[256,768]{0,1:T(8,128)(2,1)S(1)}, u32[]{:S(2)}, u32[]{:S(2)}) collective-permute-start(bf16[256,768]{0,1:T(8,128)(2,1)S(1)} %pad_maximum_fusion.7), channel_id=1, source_target_pairs={{0,1},{1,0},{2,3},{3,2},{4,5},{5,4},{6,7},{7,6},{8,9},{9,8},{10,11... | collective-permute-start | bytes 1179656 | tf_op jit(solution)/shard_map/ppermute | solution.py:20
  84.5 1.5 copy-start.2
  86.0 1.6 copy-start.3
  87.7 1.6 copy-start.4
  96.0 13.5 %collective-permute-start.17 = (bf16[256,640]{1,0:T(8,128)(2,1)S(1)}, bf16[256,640]{1,0:T(8,128)(2,1)S(1)}, u32[]{:S(2)}, u32[]{:S(2)}) collective-permute-start(bf16[256,640]{1,0:T(8,128)(2,1)S(1)} %get-tuple-element.17), channel_id=1, source_target_pairs={{0,16},{16,32},{32,48},{48,0},{1,17},{17,33},{33,49},{49,1},{2,18}... | collective-permute-start | bytes 983048 | tf_op jit(solution)/shard_map/ppermute | solution.py:20
  96.1 9.7 %collective-permute-start.19 = (bf16[256,640]{1,0:T(8,128)(2,1)S(1)}, bf16[256,640]{1,0:T(8,128)(2,1)S(1)}, u32[]{:S(2)}, u32[]{:S(2)}) collective-permute-start(bf16[256,640]{1,0:T(8,128)(2,1)S(1)} %get-tuple-element.18), channel_id=1, source_target_pairs={{0,48},{16,0},{32,16},{48,32},{1,49},{17,1},{33,17},{49,33},{2,50}... | collective-permute-start | bytes 983048 | tf_op jit(solution)/shard_map/ppermute | solution.py:20
  106.0 15.2 %collective-permute-start.20 = (bf16[256,1280]{1,0:T(8,128)(2,1)S(1)}, bf16[256,1280]{1,0:T(8,128)(2,1)S(1)}, u32[]{:S(2)}, u32[]{:S(2)}) collective-permute-start(bf16[256,1280]{1,0:T(8,128)(2,1)S(1)} %pad_maximum_fusion.5), channel_id=1, source_target_pairs={{0,48},{16,0},{32,16},{48,32},{1,49},{17,1},{33,17},{49,33},{2,50}... | collective-permute-start | bytes 1966088 | tf_op jit(solution)/shard_map/ppermute | solution.py:20
  109.6 15.0 %collective-permute-start.18 = (bf16[256,1280]{1,0:T(8,128)(2,1)S(1)}, bf16[256,1280]{1,0:T(8,128)(2,1)S(1)}, u32[]{:S(2)}, u32[]{:S(2)}) collective-permute-start(bf16[256,1280]{1,0:T(8,128)(2,1)S(1)} %pad_maximum_fusion.4), channel_id=1, source_target_pairs={{0,16},{16,32},{32,48},{48,0},{1,17},{17,33},{33,49},{49,1},{2,18}... | collective-permute-start | bytes 1966088 | tf_op jit(solution)/shard_map/ppermute | solution.py:20
  124.9 4.8 %collective-permute-start.21 = (bf16[256,640]{1,0:T(8,128)(2,1)S(1)}, bf16[256,640]{1,0:T(8,128)(2,1)S(1)}, u32[]{:S(2)}, u32[]{:S(2)}) collective-permute-start(bf16[256,640]{1,0:T(8,128)(2,1)S(1)} %get-tuple-element.16), channel_id=1, source_target_pairs={{0,1},{1,0},{2,3},{3,2},{4,5},{5,4},{6,7},{7,6},{8,9},{9,8},{10,11... | collective-permute-start | bytes 983048 | tf_op jit(solution)/shard_map/ppermute | solution.py:20
  130.0 14.6 %collective-permute-start.24 = (bf16[64,640]{1,0:T(8,128)(2,1)S(1)}, bf16[64,640]{1,0:T(8,128)(2,1)S(1)}, u32[]{:S(2)}, u32[]{:S(2)}) collective-permute-start(bf16[64,640]{1,0:T(8,128)(2,1)S(1)} %get-tuple-element.21), channel_id=1, source_target_pairs={{0,4},{2,6},{4,8},{6,10},{8,12},{10,14},{12,0},{14,2},{1,5},{3,7},... | collective-permute-start | bytes 245768 | tf_op jit(solution)/shard_map/ppermute | solution.py:20
  130.3 14.8 %collective-permute-start.26 = (bf16[64,640]{1,0:T(8,128)(2,1)S(1)}, bf16[64,640]{1,0:T(8,128)(2,1)S(1)}, u32[]{:S(2)}, u32[]{:S(2)}) collective-permute-start(bf16[64,640]{1,0:T(8,128)(2,1)S(1)} %get-tuple-element.22), channel_id=1, source_target_pairs={{0,12},{2,14},{4,0},{6,2},{8,4},{10,6},{12,8},{14,10},{1,13},{3,15... | collective-permute-start | bytes 245768 | tf_op jit(solution)/shard_map/ppermute | solution.py:20
  134.4 9.9 %collective-permute-start.22 = (bf16[256,640]{1,0:T(8,128)(2,1)S(1)}, bf16[256,640]{1,0:T(8,128)(2,1)S(1)}, u32[]{:S(2)}, u32[]{:S(2)}) collective-permute-start(bf16[256,640]{1,0:T(8,128)(2,1)S(1)} %pad_maximum_fusion.8), channel_id=1, source_target_pairs={{0,2},{2,4},{4,6},{6,8},{8,10},{10,12},{12,14},{14,0},{1,3},{3,5},... | collective-permute-start | bytes 983048 | tf_op jit(solution)/shard_map/ppermute | solution.py:20
  135.1 9.6 %collective-permute-start.23 = (bf16[256,640]{1,0:T(8,128)(2,1)S(1)}, bf16[256,640]{1,0:T(8,128)(2,1)S(1)}, u32[]{:S(2)}, u32[]{:S(2)}) collective-permute-start(bf16[256,640]{1,0:T(8,128)(2,1)S(1)} %pad_maximum_fusion.9), channel_id=1, source_target_pairs={{0,14},{2,0},{4,2},{6,4},{8,6},{10,8},{12,10},{14,12},{1,15},{3,1}... | collective-permute-start | bytes 983048 | tf_op jit(solution)/shard_map/ppermute | solution.py:20
  144.7 9.9 %collective-permute-start.25 = (bf16[128,640]{1,0:T(8,128)(2,1)S(1)}, bf16[128,640]{1,0:T(8,128)(2,1)S(1)}, u32[]{:S(2)}, u32[]{:S(2)}) collective-permute-start(bf16[128,640]{1,0:T(8,128)(2,1)S(1)} %pad_maximum_fusion.13), channel_id=1, source_target_pairs={{0,4},{2,6},{4,8},{6,10},{8,12},{10,14},{12,0},{14,2},{1,5},{3,7},... | collective-permute-start | bytes 491528 | tf_op jit(solution)/shard_map/ppermute | solution.py:20
  145.1 9.5 %collective-permute-start.27 = (bf16[128,640]{1,0:T(8,128)(2,1)S(1)}, bf16[128,640]{1,0:T(8,128)(2,1)S(1)}, u32[]{:S(2)}, u32[]{:S(2)}) collective-permute-start(bf16[128,640]{1,0:T(8,128)(2,1)S(1)} %pad_maximum_fusion.14), channel_id=1, source_target_pairs={{0,12},{2,14},{4,0},{6,2},{8,4},{10,6},{12,8},{14,10},{1,13},{3,15... | collective-permute-start | bytes 491528 | tf_op jit(solution)/shard_map/ppermute | solution.py:20

commit v6 on v3

--- a/solution.py
+++ b/solution.py
@@ -26,18 +26,16 @@
     return lax.ppermute(rows, ("section", "x"), pairs)
 
 
-def gather_z(blocks):
-    ups, downs = list(blocks), list(blocks)
-    held = {0: list(blocks)}
+def gather_z(block):
+    up = down = block
+    held = {0: block}
     for step in range(1, Z // 2 + 1):
-        for i in range(len(blocks)):
-            ups[i] = shift(ups[i], "z", 1)
-            if step < Z // 2:
-                downs[i] = shift(downs[i], "z", -1)
-        held[step] = list(ups)
+        up = shift(up, "z", 1)
+        held[step] = up
         if step < Z // 2:
-            held[Z - step] = list(downs)
-    return [jnp.concatenate([held[k][i] for k in ORDER], 0) for i in range(len(blocks))]
+            down = shift(down, "z", -1)
+            held[Z - step] = down
+    return [held[k] for k in ORDER]
 
 
 def add(a, b):
@@ -64,11 +62,9 @@
     line = [lax.select_n(lax.rem(x + X - j, X), *came) for j in range(X)]
     dest = jnp.broadcast_to(destination[0].astype(BF), (rows_each, LANES))
     dest = jnp.concatenate([dest, jnp.zeros(((X - 1) * rows_each, LANES), BF)], 0)
-    line = jnp.concatenate(line, 0)
-    left = jnp.concatenate([line[:, : width // 2], dest], 1)
-    left, right = gather_z([left, line[:, width // 2 :]])
-    dest = left.reshape(Z, X * rows_each, -1)[:, :rows_each, width // 2 :]
-    rows = jnp.concatenate([left[:, : width // 2], right], 1)
+    held = gather_z(jnp.concatenate([jnp.concatenate(line, 0), dest], 1))
+    dest = jnp.stack([block[:rows_each, width:] for block in held])
+    rows = jnp.concatenate([block[:, :width] for block in held], 0)
 
     gain = norm_gain[0].astype(F32)
     contract = (((1,), (1,)), ((), ()))
@@ -84,10 +80,10 @@
 
     half = quarter // 2
     far = part(2).astype(BF)
-    far, dest = lax.optimization_barrier((far, dest))
     up = shift(far[:, :half], "x", 1)
     down = shift(far[:, half:], "x", -1)
     near = part(1)
+    up, dest = lax.optimization_barrier((up, dest))
     up = jnp.concatenate([add(near[:, :half], up), near[:, half:]], 1).astype(BF)
     up = shift(up, "x", 1)
     near = part(3)

time: 149 us -> 125 us (0.84)
  starting transfers between devices: 70.4 us -> 51.8 us
  waiting for transfers between devices: 52.2 us -> 48.2 us
    ppermute x33 -> x26, starting transfers between devices: 63.2 us -> 43.4 us  [shift(): return lax.ppermute(array, axis, [(i, (i + by) % n) for i in range(n)])]
    ppermute x33 -> x26, waiting for transfers between devices: 49.7 us -> 46.4 us  [shift(): return lax.ppermute(array, axis, [(i, (i + by) % n) for i in range(n)])]
  transfers between devices with their start and end apart: 37 -> 30, of which waited for: 15 -> 13; matrix products, arithmetic and copies ran while one was open for 7% -> 9% of each run, Pallas kernels for 0% -> 0%
where the time goes in v6:
time: 125 us
  starting transfers between devices  51.8 us (41%)
  waiting for transfers between devices  48.2 us (39%)
  blocking collectives  11.7 us (9%)
  matrix products  7.47 us (6%)
  other arithmetic  3.14 us (3%)
  local copies, waits for them, and re-layouts  2.12 us (2%)
    ppermute x26, waiting for transfers between devices, shift(): return lax.ppermute(array, axis, [(i, (i + by) % n) for i in range(n)])  46.4 us
    ppermute x26, starting transfers between devices, shift(): return lax.ppermute(array, axis, [(i, (i + by) % n) for i in range(n)])  43.4 us
    all_to_all x1, blocking collectives, body(): lax.all_to_all(mixed.reshape(X * CORES, SLOTS, eighth), ('x', 'core'), 0,...  11.7 us
    ppermute x4, starting transfers between devices, handoff(): return lax.ppermute(rows, ('section', 'x'), pairs)  8.39 us
  transfers between devices with their start and end apart: 30, of which 13 were waited for; matrix products, arithmetic and copies ran while one was open for 9% of the time, Pallas kernels for 0%

profile of v6, /device:TPU:1, one launch (start us, length us, event | category | flops | bytes accessed | tf_op | source)
XLA Modules:
  0.0 125.1 jit_solution(11908746202132996804)
XLA Ops:
  0.0 2.1 %collective-permute-start = (bf16[8,5120]{1,0:T(8,128)(2,1)}, bf16[8,5120]{1,0:T(8,128)(2,1)S(1)}, u32[]{:S(2)}, u32[]{:S(2)}) collective-permute-start(bf16[8,5120]{1,0:T(8,128)(2,1)} %bitcast.73), channel_id=1, source_target_pairs={{0,64},{16,80},{32,96},{48,112},{64,128},{80,144},{96,160},{112,17... | collective-permute-start | bytes 245768 | tf_op jit(solution)/shard_map/ppermute | solution.py:26
  2.1 2.2 %collective-permute-start.1 = (bf16[8,5120]{1,0:T(8,128)(2,1)}, bf16[8,5120]{1,0:T(8,128)(2,1)S(1)}, u32[]{:S(2)}, u32[]{:S(2)}) collective-permute-start(bf16[8,5120]{1,0:T(8,128)(2,1)} %bitcast.74), channel_id=1, source_target_pairs={{0,80},{16,96},{32,112},{48,64},{64,144},{80,160},{96,176},{112,12... | collective-permute-start | bytes 245768 | tf_op jit(solution)/shard_map/ppermute | solution.py:26
  4.4 3.2 %collective-permute-start.2 = (bf16[8,5120]{1,0:T(8,128)(2,1)}, bf16[8,5120]{1,0:T(8,128)(2,1)S(1)}, u32[]{:S(2)}, u32[]{:S(2)}) collective-permute-start(bf16[8,5120]{1,0:T(8,128)(2,1)} %bitcast.75), channel_id=1, source_target_pairs={{0,96},{16,112},{32,64},{48,80},{64,160},{80,176},{96,128},{112,14... | collective-permute-start | bytes 245768 | tf_op jit(solution)/shard_map/ppermute | solution.py:26
  7.5 0.9 collective-permute-start.3
  8.4 1.7 %collective-permute-start.11 = (bf16[216,5120]{1,0:T(8,128)(2,1)}, bf16[216,5120]{1,0:T(8,128)(2,1)S(1)}, u32[]{:S(2)}, u32[]{:S(2)}) collective-permute-start(bf16[216,5120]{1,0:T(8,128)(2,1)} %bitcast.69), channel_id=1, source_target_pairs={{0,1},{1,0},{2,3},{3,2},{4,5},{5,4},{6,7},{7,6},{8,9},{9,8},{10,11... | collective-permute-start | bytes 6635528 | tf_op jit(solution)/shard_map/ppermute | solution.py:17
  10.1 0.7 convert_bitcast_fusion
  10.8 0.7 mul.123
  11.8 0.5 collective-permute-start.13
  12.2 1.7 %collective-permute-done.3 = bf16[8,5120]{1,0:T(8,128)(2,1)S(1)} collective-permute-done((bf16[8,5120]{1,0:T(8,128)(2,1)}, bf16[8,5120]{1,0:T(8,128)(2,1)S(1)}, u32[]{:S(2)}, u32[]{:S(2)}) %collective-permute-start.3) | collective-permute-done | bytes 81952 | tf_op jit(solution)/shard_map/ppermute | solution.py:26
  14.3 1.7 %collective-permute-start.4 = (bf16[32,5248]{1,0:T(8,128)(2,1)S(1)}, bf16[32,5248]{1,0:T(8,128)(2,1)S(1)}, u32[]{:S(2)}, u32[]{:S(2)}) collective-permute-start(bf16[32,5248]{1,0:T(8,128)(2,1)S(1)} %pad_maximum_fusion.3), channel_id=1, source_target_pairs={{0,2},{2,4},{4,6},{6,8},{8,10},{10,12},{12,14},{14,0},{1,3},{3,5},... | collective-permute-start | bytes 1007624 | tf_op jit(solution)/shard_map/ppermute | solution.py:17
  16.0 4.0 %collective-permute-start.5 = (bf16[32,5248]{1,0:T(8,128)(2,1)S(1)}, bf16[32,5248]{1,0:T(8,128)(2,1)S(1)}, u32[]{:S(2)}, u32[]{:S(2)}) collective-permute-start(bf16[32,5248]{1,0:T(8,128)(2,1)S(1)} %pad_maximum_fusion.3), channel_id=1, source_target_pairs={{0,14},{2,0},{4,2},{6,4},{8,6},{10,8},{12,10},{14,12},{1,15},{3,1}... | collective-permute-start | bytes 1007624 | tf_op jit(solution)/shard_map/ppermute | solution.py:17
  20.1 6.2 %collective-permute-done.4 = bf16[32,5248]{1,0:T(8,128)(2,1)S(1)} collective-permute-done((bf16[32,5248]{1,0:T(8,128)(2,1)S(1)}, bf16[32,5248]{1,0:T(8,128)(2,1)S(1)}, u32[]{:S(2)}, u32[]{:S(2)}) %collective-permute-start.4) | collective-permute-done | bytes 335904 | tf_op jit(solution)/shard_map/ppermute | solution.py:17
  26.3 2.7 %collective-permute-start.7 = (bf16[32,5248]{1,0:T(8,128)(2,1)S(1)}, bf16[32,5248]{1,0:T(8,128)(2,1)S(1)}, u32[]{:S(2)}, u32[]{:S(2)}) collective-permute-start(bf16[32,5248]{1,0:T(8,128)(2,1)S(1)} %collective-permute-done.5), channel_id=1, source_target_pairs={{0,14},{2,0},{4,2},{6,4},{8,6},{10,8},{12,10},{14,12},{1,15},{3,1}... | collective-permute-start | bytes 1007624 | tf_op jit(solution)/shard_map/ppermute | solution.py:17
  29.1 5.4 %collective-permute-done.6 = bf16[32,5248]{1,0:T(8,128)(2,1)S(1)} collective-permute-done((bf16[32,5248]{1,0:T(8,128)(2,1)S(1)}, bf16[32,5248]{1,0:T(8,128)(2,1)S(1)}, u32[]{:S(2)}, u32[]{:S(2)}) %collective-permute-start.6) | collective-permute-done | bytes 335904 | tf_op jit(solution)/shard_map/ppermute | solution.py:17
  34.5 2.7 %collective-permute-start.9 = (bf16[32,5248]{1,0:T(8,128)(2,1)S(1)}, bf16[32,5248]{1,0:T(8,128)(2,1)S(1)}, u32[]{:S(2)}, u32[]{:S(2)}) collective-permute-start(bf16[32,5248]{1,0:T(8,128)(2,1)S(1)} %collective-permute-done.7), channel_id=1, source_target_pairs={{0,14},{2,0},{4,2},{6,4},{8,6},{10,8},{12,10},{14,12},{1,15},{3,1}... | collective-permute-start | bytes 1007624 | tf_op jit(solution)/shard_map/ppermute | solution.py:17
  37.2 4.4 %collective-permute-done.8 = bf16[32,5248]{1,0:T(8,128)(2,1)S(1)} collective-permute-done((bf16[32,5248]{1,0:T(8,128)(2,1)S(1)}, bf16[32,5248]{1,0:T(8,128)(2,1)S(1)}, u32[]{:S(2)}, u32[]{:S(2)}) %collective-permute-start.8) | collective-permute-done | bytes 335904 | tf_op jit(solution)/shard_map/ppermute | solution.py:17
  41.8 7.3 %collective-permute-done.10 = bf16[32,5248]{1,0:T(8,128)(2,1)S(1)} collective-permute-done((bf16[32,5248]{1,0:T(8,128)(2,1)S(1)}, bf16[32,5248]{1,0:T(8,128)(2,1)S(1)}, u32[]{:S(2)}, u32[]{:S(2)}) %collective-permute-start.10) | collective-permute-done | bytes 335904 | tf_op jit(solution)/shard_map/ppermute | solution.py:17
  49.1 0.6 fusion
  49.8 1.4 %fusion.3 = f32[256,432]{0,1:T(8,128)S(1)} fusion(bf16[216,5120]{1,0:T(8,128)(2,1)S(1)} %collective-permute-done.11, bf16[216,5120]{1,0:T(8,128)(2,1)S(1)} %bitcast.70, bf16[256,5120]{1,0:T(8,128)(2,1)S(1)} %slice_dynamic-update-slice_fusion, f32[5120]{0:T(1024)S(1)} %bitcast.67, f32[256]{0:T(256)S(1)} %add_rsqrt_fusion), kind=kOutput, calls=%fused_computation.13 | convolution fusion | flops 1146552320 | bytes 7508992 | tf_op jit(solution)/shard_map/dot_general | solution.py:74
  51.4 1.4 %multiply_convert_fusion = bf16[256,432]{0,1:T(8,128)(2,1)S(1)} fusion(f32[256,432]{0,1:T(8,128)S(1)} %fusion.3, bf16[216,5120]{1,0:T(8,128)(2,1)S(1)} %collective-permute-done.12, bf16[216,5120]{1,0:T(8,128)(2,1)S(1)} %bitcast.72, bf16[256,5120]{1,0:T(8,128)(2,1)S(1)} %slice_dynamic-update-slice_fusion, f32[5120]{0:T(1024)S(1)} %bitcast.68, ...), kind=kOutput, calls=%fused_computation.56 | convolution fusion | flops 1147215872 | bytes 7730176 | tf_op jit(solution)/shard_map/dot_general | solution.py:75
  52.9 0.5 convolution_convert_fusion
  53.6 0.5 fusion.23
  54.2 2.7 %collective-permute-start.20 = (bf16[256,640]{1,0:T(8,128)(2,1)S(1)}, bf16[256,640]{1,0:T(8,128)(2,1)S(1)}, u32[]{:S(2)}, u32[]{:S(2)}) collective-permute-start(bf16[256,640]{1,0:T(8,128)(2,1)S(1)} %get-tuple-element.23), channel_id=1, source_target_pairs={{0,48},{16,0},{32,16},{48,32},{1,49},{17,1},{33,17},{49,33},{2,50}... | collective-permute-start | bytes 983048 | tf_op jit(solution)/shard_map/ppermute | solution.py:17
  56.9 0.5 fusion.16
  57.5 3.2 %collective-permute-done.14 = bf16[256,640]{1,0:T(8,128)(2,1)S(1)} collective-permute-done((bf16[256,640]{1,0:T(8,128)(2,1)S(1)}, bf16[256,640]{1,0:T(8,128)(2,1)S(1)}, u32[]{:S(2)}, u32[]{:S(2)}) %collective-permute-start.14) | collective-permute-done | bytes 327712 | tf_op jit(solution)/shard_map/ppermute | solution.py:17
  60.7 0.9 collective-permute-start.16
  61.6 1.8 %collective-permute-start.17 = (bf16[8,8,128]{2,1,0:T(8,128)(2,1)S(1)}, bf16[8,8,128]{2,1,0:T(8,128)(2,1)S(1)}, u32[]{:S(2)}, u32[]{:S(2)}) collective-permute-start(bf16[8,8,128]{2,1,0:T(8,128)(2,1)S(1)} %constant_dynamic-update-slice_fusion.4), channel_id=1, source_target_pairs={{0,48},{16,0},{32,16},{48,32},{1,49},{17,1},{33,17},{49,33},{2,50}... | collective-permute-start | bytes 49160 | tf_op jit(solution)/shard_map/ppermute | solution.py:17
  63.5 0.7 collective-permute-start.19
  64.3 2.2 %collective-permute-start.21 = (bf16[256,1280]{1,0:T(8,128)(2,1)S(1)}, bf16[256,1280]{1,0:T(8,128)(2,1)S(1)}, u32[]{:S(2)}, u32[]{:S(2)}) collective-permute-start(bf16[256,1280]{1,0:T(8,128)(2,1)S(1)} %pad_maximum_fusion.1), channel_id=1, source_target_pairs={{0,48},{16,0},{32,16},{48,32},{1,49},{17,1},{33,17},{49,33},{2,50}... | collective-permute-start | bytes 1966088 | tf_op jit(solution)/shard_map/ppermute | solution.py:17
  66.6 8.3 %collective-permute-start.18 = (bf16[256,128]{1,0:T(8,128)(2,1)S(1)}, bf16[256,128]{1,0:T(8,128)(2,1)S(1)}, u32[]{:S(2)}, u32[]{:S(2)}) collective-permute-start(bf16[256,128]{1,0:T(8,128)(2,1)S(1)} %bitcast.64), channel_id=1, source_target_pairs={{0,1},{1,0},{2,3},{3,2},{4,5},{5,4},{6,7},{7,6},{8,9},{9,8},{10,11... | collective-permute-start | bytes 196616 | tf_op jit(solution)/shard_map/ppermute | solution.py:17
  74.9 0.4 constant_dynamic-slice_fusion.1
  75.3 0.3 collective-permute-start.23
  76.0 0.6 fusion.11
  76.7 7.5 %collective-permute-start.22 = (bf16[256,640]{1,0:T(8,128)(2,1)S(1)}, bf16[256,640]{1,0:T(8,128)(2,1)S(1)}, u32[]{:S(2)}, u32[]{:S(2)}) collective-permute-start(bf16[256,640]{1,0:T(8,128)(2,1)S(1)} %get-tuple-element.22), channel_id=1, source_target_pairs={{0,1},{1,0},{2,3},{3,2},{4,5},{5,4},{6,7},{7,6},{8,9},{9,8},{10,11... | collective-permute-start | bytes 983048 | tf_op jit(solution)/shard_map/ppermute | solution.py:17
  84.3 0.3 convert_reduce_fusion
  84.6 0.9 collective-permute-done.22
  85.8 0.3 convolution_convert_fusion.4
  86.5 2.3 %collective-permute-start.26 = (bf16[64,640]{1,0:T(8,128)(2,1)S(1)}, bf16[64,640]{1,0:T(8,128)(2,1)S(1)}, u32[]{:S(2)}, u32[]{:S(2)}) collective-permute-start(bf16[64,640]{1,0:T(8,128)(2,1)S(1)} %get-tuple-element.25), channel_id=1, source_target_pairs={{0,4},{2,6},{4,8},{6,10},{8,12},{10,14},{12,0},{14,2},{1,5},{3,7},... | collective-permute-start | bytes 245768 | tf_op jit(solution)/shard_map/ppermute | solution.py:17
  88.8 1.4 %collective-permute-start.28 = (bf16[64,640]{1,0:T(8,128)(2,1)S(1)}, bf16[64,640]{1,0:T(8,128)(2,1)S(1)}, u32[]{:S(2)}, u32[]{:S(2)}) collective-permute-start(bf16[64,640]{1,0:T(8,128)(2,1)S(1)} %get-tuple-element.26), channel_id=1, source_target_pairs={{0,12},{2,14},{4,0},{6,2},{8,4},{10,6},{12,8},{14,10},{1,13},{3,15... | collective-permute-start | bytes 245768 | tf_op jit(solution)/shard_map/ppermute | solution.py:17
  90.8 1.5 %collective-permute-start.25 = (bf16[256,640]{1,0:T(8,128)(2,1)S(1)}, bf16[256,640]{1,0:T(8,128)(2,1)S(1)}, u32[]{:S(2)}, u32[]{:S(2)}) collective-permute-start(bf16[256,640]{1,0:T(8,128)(2,1)S(1)} %pad_maximum_fusion.5), channel_id=1, source_target_pairs={{0,14},{2,0},{4,2},{6,4},{8,6},{10,8},{12,10},{14,12},{1,15},{3,1}... | collective-permute-start | bytes 983048 | tf_op jit(solution)/shard_map/ppermute | solution.py:17
  92.3 4.0 %collective-permute-done.24 = bf16[256,640]{1,0:T(8,128)(2,1)S(1)} collective-permute-done((bf16[256,640]{1,0:T(8,128)(2,1)S(1)}, bf16[256,640]{1,0:T(8,128)(2,1)S(1)}, u32[]{:S(2)}, u32[]{:S(2)}) %collective-permute-start.24) | collective-permute-done | bytes 327712 | tf_op jit(solution)/shard_map/ppermute | solution.py:17
  96.6 3.1 %collective-permute-done.26 = bf16[64,640]{1,0:T(8,128)(2,1)S(1)} collective-permute-done((bf16[64,640]{1,0:T(8,128)(2,1)S(1)}, bf16[64,640]{1,0:T(8,128)(2,1)S(1)}, u32[]{:S(2)}, u32[]{:S(2)}) %collective-permute-start.26) | collective-permute-done | bytes 81952 | tf_op jit(solution)/shard_map/ppermute | solution.py:17
  99.9 4.2 %collective-permute-done.25 = bf16[256,640]{1,0:T(8,128)(2,1)S(1)} collective-permute-done((bf16[256,640]{1,0:T(8,128)(2,1)S(1)}, bf16[256,640]{1,0:T(8,128)(2,1)S(1)}, u32[]{:S(2)}, u32[]{:S(2)}) %collective-permute-start.25) | collective-permute-done | bytes 327712 | tf_op jit(solution)/shard_map/ppermute | solution.py:17
  104.7 1.5 %collective-permute-done.27 = bf16[128,640]{1,0:T(8,128)(2,1)S(1)} collective-permute-done((bf16[128,640]{1,0:T(8,128)(2,1)S(1)}, bf16[128,640]{1,0:T(8,128)(2,1)S(1)}, u32[]{:S(2)}, u32[]{:S(2)}) %collective-permute-start.27) | collective-permute-done | bytes 163872 | tf_op jit(solution)/shard_map/ppermute | solution.py:17
  106.2 6.0 %collective-permute-done.29 = bf16[128,640]{1,0:T(8,128)(2,1)S(1)} collective-permute-done((bf16[128,640]{1,0:T(8,128)(2,1)S(1)}, bf16[128,640]{1,0:T(8,128)(2,1)S(1)}, u32[]{:S(2)}, u32[]{:S(2)}) %collective-permute-start.29) | collective-permute-done | bytes 163872 | tf_op jit(solution)/shard_map/ppermute | solution.py:17
  112.3 0.3 fusion.14
  112.5 11.7 %all_to_all.5 = bf16[8,16,640]{2,1,0:T(8,128)(2,1)S(1)} all-to-all(bf16[8,16,640]{2,1,0:T(8,128)(2,1)S(1)} %bitcast.66), channel_id=1, replica_groups=mesh['section'=4,'x'=4,'z'=8,'core'=2] {'x','core'}, dimensions={0} | all-to-all | bytes 327680 | tf_op jit(solution)/shard_map/all_to_all | solution.py:154
  124.3 0.7 reshape.282
  (91 shorter events, 4.3 us)
Async XLA Ops:
  0.0 11.6 %collective-permute-start = (bf16[8,5120]{1,0:T(8,128)(2,1)}, bf16[8,5120]{1,0:T(8,128)(2,1)S(1)}, u32[]{:S(2)}, u32[]{:S(2)}) collective-permute-start(bf16[8,5120]{1,0:T(8,128)(2,1)} %bitcast.73), channel_id=1, source_target_pairs={{0,64},{16,80},{32,96},{48,112},{64,128},{80,144},{96,160},{112,17... | collective-permute-start | bytes 245768 | tf_op jit(solution)/shard_map/ppermute | solution.py:26
  2.1 9.6 %collective-permute-start.1 = (bf16[8,5120]{1,0:T(8,128)(2,1)}, bf16[8,5120]{1,0:T(8,128)(2,1)S(1)}, u32[]{:S(2)}, u32[]{:S(2)}) collective-permute-start(bf16[8,5120]{1,0:T(8,128)(2,1)} %bitcast.74), channel_id=1, source_target_pairs={{0,80},{16,96},{32,112},{48,64},{64,144},{80,160},{96,176},{112,12... | collective-permute-start | bytes 245768 | tf_op jit(solution)/shard_map/ppermute | solution.py:26
  4.4 7.9 %collective-permute-start.2 = (bf16[8,5120]{1,0:T(8,128)(2,1)}, bf16[8,5120]{1,0:T(8,128)(2,1)S(1)}, u32[]{:S(2)}, u32[]{:S(2)}) collective-permute-start(bf16[8,5120]{1,0:T(8,128)(2,1)} %bitcast.75), channel_id=1, source_target_pairs={{0,96},{16,112},{32,64},{48,80},{64,160},{80,176},{96,128},{112,14... | collective-permute-start | bytes 245768 | tf_op jit(solution)/shard_map/ppermute | solution.py:26
  7.5 6.5 %collective-permute-start.3 = (bf16[8,5120]{1,0:T(8,128)(2,1)}, bf16[8,5120]{1,0:T(8,128)(2,1)S(1)}, u32[]{:S(2)}, u32[]{:S(2)}) collective-permute-start(bf16[8,5120]{1,0:T(8,128)(2,1)} %bitcast.76), channel_id=1, source_target_pairs={{0,112},{16,64},{32,80},{48,96},{64,176},{80,128},{96,144},{112,16... | collective-permute-start | bytes 245768 | tf_op jit(solution)/shard_map/ppermute | solution.py:26
  8.4 41.4 %collective-permute-start.11 = (bf16[216,5120]{1,0:T(8,128)(2,1)}, bf16[216,5120]{1,0:T(8,128)(2,1)S(1)}, u32[]{:S(2)}, u32[]{:S(2)}) collective-permute-start(bf16[216,5120]{1,0:T(8,128)(2,1)} %bitcast.69), channel_id=1, source_target_pairs={{0,1},{1,0},{2,3},{3,2},{4,5},{5,4},{6,7},{7,6},{8,9},{9,8},{10,11... | collective-permute-start | bytes 6635528 | tf_op jit(solution)/shard_map/ppermute | solution.py:17
  11.6 39.6 %collective-permute-start.12 = (bf16[216,5120]{1,0:T(8,128)(2,1)}, bf16[216,5120]{1,0:T(8,128)(2,1)S(1)}, u32[]{:S(2)}, u32[]{:S(2)}) collective-permute-start(bf16[216,5120]{1,0:T(8,128)(2,1)} %bitcast.71), channel_id=1, source_target_pairs={{0,1},{1,0},{2,3},{3,2},{4,5},{5,4},{6,7},{7,6},{8,9},{9,8},{10,11... | collective-permute-start | bytes 6635528 | tf_op jit(solution)/shard_map/ppermute | solution.py:17
  11.8 41.1 %collective-permute-start.13 = (bf16[216,5120]{1,0:T(8,128)(2,1)}, bf16[216,5120]{1,0:T(8,128)(2,1)S(1)}, u32[]{:S(2)}, u32[]{:S(2)}) collective-permute-start(bf16[216,5120]{1,0:T(8,128)(2,1)} %bitcast.58), channel_id=1, source_target_pairs={{0,1},{1,0},{2,3},{3,2},{4,5},{5,4},{6,7},{7,6},{8,9},{9,8},{10,11... | collective-permute-start | bytes 6635528 | tf_op jit(solution)/shard_map/ppermute | solution.py:17
  14.3 12.0 %collective-permute-start.4 = (bf16[32,5248]{1,0:T(8,128)(2,1)S(1)}, bf16[32,5248]{1,0:T(8,128)(2,1)S(1)}, u32[]{:S(2)}, u32[]{:S(2)}) collective-permute-start(bf16[32,5248]{1,0:T(8,128)(2,1)S(1)} %pad_maximum_fusion.3), channel_id=1, source_target_pairs={{0,2},{2,4},{4,6},{6,8},{8,10},{10,12},{12,14},{14,0},{1,3},{3,5},... | collective-permute-start | bytes 1007624 | tf_op jit(solution)/shard_map/ppermute | solution.py:17
  16.0 10.3 %collective-permute-start.5 = (bf16[32,5248]{1,0:T(8,128)(2,1)S(1)}, bf16[32,5248]{1,0:T(8,128)(2,1)S(1)}, u32[]{:S(2)}, u32[]{:S(2)}) collective-permute-start(bf16[32,5248]{1,0:T(8,128)(2,1)S(1)} %pad_maximum_fusion.3), channel_id=1, source_target_pairs={{0,14},{2,0},{4,2},{6,4},{8,6},{10,8},{12,10},{14,12},{1,15},{3,1}... | collective-permute-start | bytes 1007624 | tf_op jit(solution)/shard_map/ppermute | solution.py:17
  26.3 8.1 %collective-permute-start.6 = (bf16[32,5248]{1,0:T(8,128)(2,1)S(1)}, bf16[32,5248]{1,0:T(8,128)(2,1)S(1)}, u32[]{:S(2)}, u32[]{:S(2)}) collective-permute-start(bf16[32,5248]{1,0:T(8,128)(2,1)S(1)} %collective-permute-done.4), channel_id=1, source_target_pairs={{0,2},{2,4},{4,6},{6,8},{8,10},{10,12},{12,14},{14,0},{1,3},{3,5},... | collective-permute-start | bytes 1007624 | tf_op jit(solution)/shard_map/ppermute | solution.py:17
  26.3 8.1 %collective-permute-start.7 = (bf16[32,5248]{1,0:T(8,128)(2,1)S(1)}, bf16[32,5248]{1,0:T(8,128)(2,1)S(1)}, u32[]{:S(2)}, u32[]{:S(2)}) collective-permute-start(bf16[32,5248]{1,0:T(8,128)(2,1)S(1)} %collective-permute-done.5), channel_id=1, source_target_pairs={{0,14},{2,0},{4,2},{6,4},{8,6},{10,8},{12,10},{14,12},{1,15},{3,1}... | collective-permute-start | bytes 1007624 | tf_op jit(solution)/shard_map/ppermute | solution.py:17
  34.5 7.2 %collective-permute-start.8 = (bf16[32,5248]{1,0:T(8,128)(2,1)S(1)}, bf16[32,5248]{1,0:T(8,128)(2,1)S(1)}, u32[]{:S(2)}, u32[]{:S(2)}) collective-permute-start(bf16[32,5248]{1,0:T(8,128)(2,1)S(1)} %collective-permute-done.6), channel_id=1, source_target_pairs={{0,2},{2,4},{4,6},{6,8},{8,10},{10,12},{12,14},{14,0},{1,3},{3,5},... | collective-permute-start | bytes 1007624 | tf_op jit(solution)/shard_map/ppermute | solution.py:17
  34.5 7.2 %collective-permute-start.9 = (bf16[32,5248]{1,0:T(8,128)(2,1)S(1)}, bf16[32,5248]{1,0:T(8,128)(2,1)S(1)}, u32[]{:S(2)}, u32[]{:S(2)}) collective-permute-start(bf16[32,5248]{1,0:T(8,128)(2,1)S(1)} %collective-permute-done.7), channel_id=1, source_target_pairs={{0,14},{2,0},{4,2},{6,4},{8,6},{10,8},{12,10},{14,12},{1,15},{3,1}... | collective-permute-start | bytes 1007624 | tf_op jit(solution)/shard_map/ppermute | solution.py:17
  37.2 12.6 %copy-start.1 = (bf16[1,216,5120]{2,1,0:T(8,128)(2,1)S(1)}, bf16[1,216,5120]{2,1,0:T(8,128)(2,1)}, u32[]{:S(2)}) copy-start(bf16[1,216,5120]{2,1,0:T(8,128)(2,1)} %param.9) | copy-start | bytes 6635524
  41.7 7.4 %collective-permute-start.10 = (bf16[32,5248]{1,0:T(8,128)(2,1)S(1)}, bf16[32,5248]{1,0:T(8,128)(2,1)S(1)}, u32[]{:S(2)}, u32[]{:S(2)}) collective-permute-start(bf16[32,5248]{1,0:T(8,128)(2,1)S(1)} %collective-permute-done.8), channel_id=1, source_target_pairs={{0,2},{2,4},{4,6},{6,8},{8,10},{10,12},{12,14},{14,0},{1,3},{3,5},... | collective-permute-start | bytes 1007624 | tf_op jit(solution)/shard_map/ppermute | solution.py:17
  49.8 1.6 %copy-start.2 = (bf16[1,216,5120]{2,1,0:T(8,128)(2,1)S(1)}, bf16[1,216,5120]{2,1,0:T(8,128)(2,1)}, u32[]{:S(2)}) copy-start(bf16[1,216,5120]{2,1,0:T(8,128)(2,1)} %param.10) | copy-start | bytes 6635524
  51.2 1.7 %copy-start = (bf16[1,216,5120]{2,1,0:T(8,128)(2,1)S(1)}, bf16[1,216,5120]{2,1,0:T(8,128)(2,1)}, u32[]{:S(2)}) copy-start(bf16[1,216,5120]{2,1,0:T(8,128)(2,1)} %param.11) | copy-start | bytes 6635524
  53.5 7.2 %collective-permute-start.14 = (bf16[256,640]{1,0:T(8,128)(2,1)S(1)}, bf16[256,640]{1,0:T(8,128)(2,1)S(1)}, u32[]{:S(2)}, u32[]{:S(2)}) collective-permute-start(bf16[256,640]{1,0:T(8,128)(2,1)S(1)} %get-tuple-element.24), channel_id=1, source_target_pairs={{0,16},{16,32},{32,48},{48,0},{1,17},{17,33},{33,49},{49,1},{2,18}... | collective-permute-start | bytes 983048 | tf_op jit(solution)/shard_map/ppermute | solution.py:17
  54.2 10.0 %collective-permute-start.20 = (bf16[256,640]{1,0:T(8,128)(2,1)S(1)}, bf16[256,640]{1,0:T(8,128)(2,1)S(1)}, u32[]{:S(2)}, u32[]{:S(2)}) collective-permute-start(bf16[256,640]{1,0:T(8,128)(2,1)S(1)} %get-tuple-element.23), channel_id=1, source_target_pairs={{0,48},{16,0},{32,16},{48,32},{1,49},{17,1},{33,17},{49,33},{2,50}... | collective-permute-start | bytes 983048 | tf_op jit(solution)/shard_map/ppermute | solution.py:17
  60.7 5.8 %collective-permute-start.15 = (bf16[8,8,128]{2,1,0:T(8,128)(2,1)S(1)}, bf16[8,8,128]{2,1,0:T(8,128)(2,1)S(1)}, u32[]{:S(2)}, u32[]{:S(2)}) collective-permute-start(bf16[8,8,128]{2,1,0:T(8,128)(2,1)S(1)} %constant_dynamic-update-slice_fusion.4), channel_id=1, source_target_pairs={{0,16},{16,32},{32,48},{48,0},{1,17},{17,33},{33,49},{49,1},{2,18}... | collective-permute-start | bytes 49160 | tf_op jit(solution)/shard_map/ppermute | solution.py:17
  60.7 5.8 %collective-permute-start.16 = (bf16[8,8,128]{2,1,0:T(8,128)(2,1)S(1)}, bf16[8,8,128]{2,1,0:T(8,128)(2,1)S(1)}, u32[]{:S(2)}, u32[]{:S(2)}) collective-permute-start(bf16[8,8,128]{2,1,0:T(8,128)(2,1)S(1)} %constant_dynamic-update-slice_fusion.4), channel_id=1, source_target_pairs={{0,32},{16,48},{32,0},{48,16},{1,33},{17,49},{33,1},{49,17},{2,34}... | collective-permute-start | bytes 49160 | tf_op jit(solution)/shard_map/ppermute | solution.py:17
  61.6 5.0 %collective-permute-start.17 = (bf16[8,8,128]{2,1,0:T(8,128)(2,1)S(1)}, bf16[8,8,128]{2,1,0:T(8,128)(2,1)S(1)}, u32[]{:S(2)}, u32[]{:S(2)}) collective-permute-start(bf16[8,8,128]{2,1,0:T(8,128)(2,1)S(1)} %constant_dynamic-update-slice_fusion.4), channel_id=1, source_target_pairs={{0,48},{16,0},{32,16},{48,32},{1,49},{17,1},{33,17},{49,33},{2,50}... | collective-permute-start | bytes 49160 | tf_op jit(solution)/shard_map/ppermute | solution.py:17
  63.5 12.5 %collective-permute-start.19 = (bf16[256,1280]{1,0:T(8,128)(2,1)S(1)}, bf16[256,1280]{1,0:T(8,128)(2,1)S(1)}, u32[]{:S(2)}, u32[]{:S(2)}) collective-permute-start(bf16[256,1280]{1,0:T(8,128)(2,1)S(1)} %pad_maximum_fusion), channel_id=1, source_target_pairs={{0,16},{16,32},{32,48},{48,0},{1,17},{17,33},{33,49},{49,1},{2,18}... | collective-permute-start | bytes 1966088 | tf_op jit(solution)/shard_map/ppermute | solution.py:17
  64.3 11.7 %collective-permute-start.21 = (bf16[256,1280]{1,0:T(8,128)(2,1)S(1)}, bf16[256,1280]{1,0:T(8,128)(2,1)S(1)}, u32[]{:S(2)}, u32[]{:S(2)}) collective-permute-start(bf16[256,1280]{1,0:T(8,128)(2,1)S(1)} %pad_maximum_fusion.1), channel_id=1, source_target_pairs={{0,48},{16,0},{32,16},{48,32},{1,49},{17,1},{33,17},{49,33},{2,50}... | collective-permute-start | bytes 1966088 | tf_op jit(solution)/shard_map/ppermute | solution.py:17
  66.6 9.2 %collective-permute-start.18 = (bf16[256,128]{1,0:T(8,128)(2,1)S(1)}, bf16[256,128]{1,0:T(8,128)(2,1)S(1)}, u32[]{:S(2)}, u32[]{:S(2)}) collective-permute-start(bf16[256,128]{1,0:T(8,128)(2,1)S(1)} %bitcast.64), channel_id=1, source_target_pairs={{0,1},{1,0},{2,3},{3,2},{4,5},{5,4},{6,7},{7,6},{8,9},{9,8},{10,11... | collective-permute-start | bytes 196616 | tf_op jit(solution)/shard_map/ppermute | solution.py:17
  75.3 29.1 %collective-permute-start.23 = (bf16[256,640]{1,0:T(8,128)(2,1)S(1)}, bf16[256,640]{1,0:T(8,128)(2,1)S(1)}, u32[]{:S(2)}, u32[]{:S(2)}) collective-permute-start(bf16[256,640]{1,0:T(8,128)(2,1)S(1)} %get-tuple-element.20), channel_id=1, source_target_pairs={{0,1},{1,0},{2,3},{3,2},{4,5},{5,4},{6,7},{7,6},{8,9},{9,8},{10,11... | collective-permute-start | bytes 983048 | tf_op jit(solution)/shard_map/ppermute | solution.py:17
  76.7 8.8 %collective-permute-start.22 = (bf16[256,640]{1,0:T(8,128)(2,1)S(1)}, bf16[256,640]{1,0:T(8,128)(2,1)S(1)}, u32[]{:S(2)}, u32[]{:S(2)}) collective-permute-start(bf16[256,640]{1,0:T(8,128)(2,1)S(1)} %get-tuple-element.22), channel_id=1, source_target_pairs={{0,1},{1,0},{2,3},{3,2},{4,5},{5,4},{6,7},{7,6},{8,9},{9,8},{10,11... | collective-permute-start | bytes 983048 | tf_op jit(solution)/shard_map/ppermute | solution.py:17
  86.1 10.2 %collective-permute-start.24 = (bf16[256,640]{1,0:T(8,128)(2,1)S(1)}, bf16[256,640]{1,0:T(8,128)(2,1)S(1)}, u32[]{:S(2)}, u32[]{:S(2)}) collective-permute-start(bf16[256,640]{1,0:T(8,128)(2,1)S(1)} %pad_maximum_fusion.4), channel_id=1, source_target_pairs={{0,2},{2,4},{4,6},{6,8},{8,10},{10,12},{12,14},{14,0},{1,3},{3,5},... | collective-permute-start | bytes 983048 | tf_op jit(solution)/shard_map/ppermute | solution.py:17
  86.5 13.2 %collective-permute-start.26 = (bf16[64,640]{1,0:T(8,128)(2,1)S(1)}, bf16[64,640]{1,0:T(8,128)(2,1)S(1)}, u32[]{:S(2)}, u32[]{:S(2)}) collective-permute-start(bf16[64,640]{1,0:T(8,128)(2,1)S(1)} %get-tuple-element.25), channel_id=1, source_target_pairs={{0,4},{2,6},{4,8},{6,10},{8,12},{10,14},{12,0},{14,2},{1,5},{3,7},... | collective-permute-start | bytes 245768 | tf_op jit(solution)/shard_map/ppermute | solution.py:17
  88.8 15.5 %collective-permute-start.28 = (bf16[64,640]{1,0:T(8,128)(2,1)S(1)}, bf16[64,640]{1,0:T(8,128)(2,1)S(1)}, u32[]{:S(2)}, u32[]{:S(2)}) collective-permute-start(bf16[64,640]{1,0:T(8,128)(2,1)S(1)} %get-tuple-element.26), channel_id=1, source_target_pairs={{0,12},{2,14},{4,0},{6,2},{8,4},{10,6},{12,8},{14,10},{1,13},{3,15... | collective-permute-start | bytes 245768 | tf_op jit(solution)/shard_map/ppermute | solution.py:17
  90.8 13.2 %collective-permute-start.25 = (bf16[256,640]{1,0:T(8,128)(2,1)S(1)}, bf16[256,640]{1,0:T(8,128)(2,1)S(1)}, u32[]{:S(2)}, u32[]{:S(2)}) collective-permute-start(bf16[256,640]{1,0:T(8,128)(2,1)S(1)} %pad_maximum_fusion.5), channel_id=1, source_target_pairs={{0,14},{2,0},{4,2},{6,4},{8,6},{10,8},{12,10},{14,12},{1,15},{3,1}... | collective-permute-start | bytes 983048 | tf_op jit(solution)/shard_map/ppermute | solution.py:17
  99.8 6.5 %collective-permute-start.27 = (bf16[128,640]{1,0:T(8,128)(2,1)S(1)}, bf16[128,640]{1,0:T(8,128)(2,1)S(1)}, u32[]{:S(2)}, u32[]{:S(2)}) collective-permute-start(bf16[128,640]{1,0:T(8,128)(2,1)S(1)} %pad_maximum_fusion.6), channel_id=1, source_target_pairs={{0,4},{2,6},{4,8},{6,10},{8,12},{10,14},{12,0},{14,2},{1,5},{3,7},... | collective-permute-start | bytes 491528 | tf_op jit(solution)/shard_map/ppermute | solution.py:17
  104.4 7.9 %collective-permute-start.29 = (bf16[128,640]{1,0:T(8,128)(2,1)S(1)}, bf16[128,640]{1,0:T(8,128)(2,1)S(1)}, u32[]{:S(2)}, u32[]{:S(2)}) collective-permute-start(bf16[128,640]{1,0:T(8,128)(2,1)S(1)} %pad_maximum_fusion.7), channel_id=1, source_target_pairs={{0,12},{2,14},{4,0},{6,2},{8,4},{10,6},{12,8},{14,10},{1,13},{3,15... | collective-permute-start | bytes 491528 | tf_op jit(solution)/shard_map/ppermute | solution.py:17

commit v7 on v6

--- a/solution.py
+++ b/solution.py
@@ -9,7 +9,7 @@
 LANES = 128
 EPSILON = 1e-05
 BF, F32 = jnp.bfloat16, jnp.float32
-ORDER = (0, 1, 7, 2, 6, 3, 5, 4)
+ORDER = (0, 1, 7, 2, 6, 3, 5)
 
 
 def shift(array, axis, by):
@@ -29,13 +29,12 @@
 def gather_z(block):
     up = down = block
     held = {0: block}
-    for step in range(1, Z // 2 + 1):
-        up = shift(up, "z", 1)
-        held[step] = up
-        if step < Z // 2:
-            down = shift(down, "z", -1)
-            held[Z - step] = down
-    return [held[k] for k in ORDER]
+    for step in range(1, Z // 2):
+        up, down = shift(up, "z", 1), shift(down, "z", -1)
+        held[step], held[Z - step] = up, down
+    half = block.shape[0] // 2
+    far_up, far_down = shift(up[:half], "z", 1), shift(down[half:], "z", -1)
+    return [held[k] for k in ORDER] + [far_up, far_down]
 
 
 def add(a, b):
@@ -63,7 +62,7 @@
     dest = jnp.broadcast_to(destination[0].astype(BF), (rows_each, LANES))
     dest = jnp.concatenate([dest, jnp.zeros(((X - 1) * rows_each, LANES), BF)], 0)
     held = gather_z(jnp.concatenate([jnp.concatenate(line, 0), dest], 1))
-    dest = jnp.stack([block[:rows_each, width:] for block in held])
+    dest = jnp.stack([block[:rows_each, width:] for block in held[:-1]])
     rows = jnp.concatenate([block[:, :width] for block in held], 0)
 
     gain = norm_gain[0].astype(F32)
@@ -110,7 +109,7 @@
     index = jnp.arange(total, dtype=jnp.int32)
     block = (index // (X * rows_each)) % Z
     behind = jnp.zeros_like(block)
-    for i, k in enumerate(ORDER):
+    for i, k in enumerate(ORDER + (Z // 2,)):
         behind = jnp.where(block == i, k, behind)
     source_core = jnp.where(index < total // CORES, core, 1 - core)
     source = ((index // rows_each) % X) * Z + lax.rem(z + Z - behind, Z)
@@ -132,29 +131,33 @@
     def slotted(k):
         return jnp.dot(pick(k), summed, preferred_element_type=F32)
 
-    def message(*steps):
-        return jnp.concatenate([slotted(k % Z).astype(BF) for k in steps], 0)
+    middle = slots // 2
+    far = slotted(Z // 2).astype(BF)
+    up, down = shift(far[:middle], "z", 1), shift(far[middle:], "z", -1)
+    for k in range(Z // 2 - 1, 0, -1):
+        above, below = slotted(k), slotted(Z - k)
+        if k == Z // 2 - 1:
+            up = jnp.concatenate([add(above[:middle], up), above[middle:]], 0)
+            down = jnp.concatenate([below[:middle], add(below[middle:], down)], 0)
+        else:
+            up, down = add(above, up), add(below, down)
+        up, down = shift(up.astype(BF), "z", 1), shift(down.astype(BF), "z", -1)
+    mine = slotted(0) + jnp.dot(pick(0), residual, preferred_element_type=F32)
+    mixed = (mine + add(up, down)).astype(BF)
 
-    middle = slots // 2
-    up_near = shift(message(3, 1), "z", 1)
-    down_near = shift(message(-3, -1), "z", -1)
-    opposite = message(4)
-    up_far = shift(opposite[:middle], "z", 2)
-    down_far = shift(opposite[middle:], "z", -2)
-    up = add(slotted(2), up_near[:slots])
-    up = jnp.concatenate([add(up[:middle], up_far), up[middle:]], 0)
-    down = add(slotted(6), down_near[:slots])
-    down = jnp.concatenate([down[:middle], add(down[middle:], down_far)], 0)
-    up = shift(up.astype(BF), "z", 2)
-    down = shift(down.astype(BF), "z", -2)
-    mine = slotted(0) + jnp.dot(pick(0), residual, preferred_element_type=F32)
-    near = add(up_near[slots:], down_near[slots:])
-    mixed = (mine + near + add(up, down)).astype(BF)
-
-    pieces = lax.all_to_all(
-        mixed.reshape(X * CORES, SLOTS, eighth), ("x", "core"), 0, 0, tiled=True
-    )
-    return pieces.transpose(1, 0, 2).reshape(1, SLOTS, width)
+    mixed = mixed.reshape(X, CORES, SLOTS, eighth)
+    mine = lax.dynamic_index_in_dim(mixed, core, 1, keepdims=False)
+    theirs = lax.dynamic_index_in_dim(mixed, 1 - core, 1, keepdims=False)
+    theirs = shift(theirs, "core", 1)
+    pair = [jnp.where(core == 0, mine, theirs), jnp.where(core == 0, theirs, mine)]
+    pair = jnp.concatenate(pair, -1)
+    came = [
+        lax.dynamic_index_in_dim(pair, lax.rem(x + k, X), 0, keepdims=False) for k in range(X)
+    ]
+    came = [came[0]] + [shift(came[k], "x", k) for k in range(1, X)]
+    return jnp.concatenate(
+        [lax.select_n(lax.rem(x + X - j, X), *came) for j in range(X)], -1
+    )[None]
 
 
 def solution(mesh):

time: 125 us -> 123 us (0.984); the launches traced: 125 us -> 121 us
  starting transfers between devices: 51.8 us -> 69.5 us
  blocking collectives: 11.7 us -> 0 us
  waiting for transfers between devices: 48.2 us -> 38.2 us
    ppermute x26 -> x33, starting transfers between devices: 43.4 us -> 61.1 us  [shift(): return lax.ppermute(array, axis, [(i, (i + by) % n) for i in range(n)])]
    all_to_all x1 -> x0, blocking collectives: 11.7 us -> none  [body(): lax.all_to_all(mixed.reshape(X * CORES, SLOTS, eighth), ('x', 'core'), 0,...]
    ppermute x26 -> x33, waiting for transfers between devices: 46.4 us -> 36.4 us  [shift(): return lax.ppermute(array, axis, [(i, (i + by) % n) for i in range(n)])]
  transfers between devices with their start and end apart: 30 -> 37, of which waited for: 13 -> 17; matrix products, arithmetic and copies ran while one was open for 9% -> 9% of each run, Pallas kernels for 0% -> 0%
where the time goes in v7:
time: 123 us; the launch traced here: 121 us
  starting transfers between devices  69.5 us (57%)
  waiting for transfers between devices  38.2 us (31%)
  matrix products  7.47 us (6%)
  other arithmetic  3.85 us (3%)
  local copies, waits for them, and re-layouts  1.39 us (1%)
    ppermute x33, starting transfers between devices, shift(): return lax.ppermute(array, axis, [(i, (i + by) % n) for i in range(n)])  61.1 us
    ppermute x33, waiting for transfers between devices, shift(): return lax.ppermute(array, axis, [(i, (i + by) % n) for i in range(n)])  36.4 us
    ppermute x4, starting transfers between devices, handoff(): return lax.ppermute(rows, ('section', 'x'), pairs)  8.39 us
  transfers between devices with their start and end apart: 37, of which 17 were waited for; matrix products, arithmetic and copies ran while one was open for 9% of the time, Pallas kernels for 0%

profile of v7, /device:TPU:1, one launch (start us, length us, event | category | flops | bytes accessed | tf_op | source)
XLA Modules:
  0.0 121.1 jit_solution(1461029002381926746)
XLA Ops:
  0.0 2.1 %collective-permute-start = (bf16[8,5120]{1,0:T(8,128)(2,1)}, bf16[8,5120]{1,0:T(8,128)(2,1)S(1)}, u32[]{:S(2)}, u32[]{:S(2)}) collective-permute-start(bf16[8,5120]{1,0:T(8,128)(2,1)} %bitcast.88), channel_id=1, source_target_pairs={{0,64},{16,80},{32,96},{48,112},{64,128},{80,144},{96,160},{112,17... | collective-permute-start | bytes 245768 | tf_op jit(solution)/shard_map/ppermute | solution.py:26
  2.1 2.2 %collective-permute-start.1 = (bf16[8,5120]{1,0:T(8,128)(2,1)}, bf16[8,5120]{1,0:T(8,128)(2,1)S(1)}, u32[]{:S(2)}, u32[]{:S(2)}) collective-permute-start(bf16[8,5120]{1,0:T(8,128)(2,1)} %bitcast.89), channel_id=1, source_target_pairs={{0,80},{16,96},{32,112},{48,64},{64,144},{80,160},{96,176},{112,12... | collective-permute-start | bytes 245768 | tf_op jit(solution)/shard_map/ppermute | solution.py:26
  4.4 3.2 %collective-permute-start.2 = (bf16[8,5120]{1,0:T(8,128)(2,1)}, bf16[8,5120]{1,0:T(8,128)(2,1)S(1)}, u32[]{:S(2)}, u32[]{:S(2)}) collective-permute-start(bf16[8,5120]{1,0:T(8,128)(2,1)} %bitcast.90), channel_id=1, source_target_pairs={{0,96},{16,112},{32,64},{48,80},{64,160},{80,176},{96,128},{112,14... | collective-permute-start | bytes 245768 | tf_op jit(solution)/shard_map/ppermute | solution.py:26
  7.5 0.9 collective-permute-start.3
  8.4 1.7 %collective-permute-start.12 = (bf16[216,5120]{1,0:T(8,128)(2,1)}, bf16[216,5120]{1,0:T(8,128)(2,1)S(1)}, u32[]{:S(2)}, u32[]{:S(2)}) collective-permute-start(bf16[216,5120]{1,0:T(8,128)(2,1)} %bitcast.84), channel_id=1, source_target_pairs={{0,1},{1,0},{2,3},{3,2},{4,5},{5,4},{6,7},{7,6},{8,9},{9,8},{10,11... | collective-permute-start | bytes 6635528 | tf_op jit(solution)/shard_map/ppermute | solution.py:17
  10.1 0.7 convert_bitcast_fusion
  10.8 0.7 mul.123
  12.2 1.7 %collective-permute-done.3 = bf16[8,5120]{1,0:T(8,128)(2,1)S(1)} collective-permute-done((bf16[8,5120]{1,0:T(8,128)(2,1)}, bf16[8,5120]{1,0:T(8,128)(2,1)S(1)}, u32[]{:S(2)}, u32[]{:S(2)}) %collective-permute-start.3) | collective-permute-done | bytes 81952 | tf_op jit(solution)/shard_map/ppermute | solution.py:26
  14.3 1.7 %collective-permute-start.4 = (bf16[32,5248]{1,0:T(8,128)(2,1)S(1)}, bf16[32,5248]{1,0:T(8,128)(2,1)S(1)}, u32[]{:S(2)}, u32[]{:S(2)}) collective-permute-start(bf16[32,5248]{1,0:T(8,128)(2,1)S(1)} %pad_maximum_fusion.3), channel_id=1, source_target_pairs={{0,2},{2,4},{4,6},{6,8},{8,10},{10,12},{12,14},{14,0},{1,3},{3,5},... | collective-permute-start | bytes 1007624 | tf_op jit(solution)/shard_map/ppermute | solution.py:17
  16.0 4.0 %collective-permute-start.5 = (bf16[32,5248]{1,0:T(8,128)(2,1)S(1)}, bf16[32,5248]{1,0:T(8,128)(2,1)S(1)}, u32[]{:S(2)}, u32[]{:S(2)}) collective-permute-start(bf16[32,5248]{1,0:T(8,128)(2,1)S(1)} %pad_maximum_fusion.3), channel_id=1, source_target_pairs={{0,14},{2,0},{4,2},{6,4},{8,6},{10,8},{12,10},{14,12},{1,15},{3,1}... | collective-permute-start | bytes 1007624 | tf_op jit(solution)/shard_map/ppermute | solution.py:17
  20.1 6.2 %collective-permute-done.4 = bf16[32,5248]{1,0:T(8,128)(2,1)S(1)} collective-permute-done((bf16[32,5248]{1,0:T(8,128)(2,1)S(1)}, bf16[32,5248]{1,0:T(8,128)(2,1)S(1)}, u32[]{:S(2)}, u32[]{:S(2)}) %collective-permute-start.4) | collective-permute-done | bytes 335904 | tf_op jit(solution)/shard_map/ppermute | solution.py:17
  26.3 2.7 %collective-permute-start.7 = (bf16[32,5248]{1,0:T(8,128)(2,1)S(1)}, bf16[32,5248]{1,0:T(8,128)(2,1)S(1)}, u32[]{:S(2)}, u32[]{:S(2)}) collective-permute-start(bf16[32,5248]{1,0:T(8,128)(2,1)S(1)} %collective-permute-done.5), channel_id=1, source_target_pairs={{0,14},{2,0},{4,2},{6,4},{8,6},{10,8},{12,10},{14,12},{1,15},{3,1}... | collective-permute-start | bytes 1007624 | tf_op jit(solution)/shard_map/ppermute | solution.py:17
  29.1 5.4 %collective-permute-done.6 = bf16[32,5248]{1,0:T(8,128)(2,1)S(1)} collective-permute-done((bf16[32,5248]{1,0:T(8,128)(2,1)S(1)}, bf16[32,5248]{1,0:T(8,128)(2,1)S(1)}, u32[]{:S(2)}, u32[]{:S(2)}) %collective-permute-start.6) | collective-permute-done | bytes 335904 | tf_op jit(solution)/shard_map/ppermute | solution.py:17
  34.5 2.7 %collective-permute-start.9 = (bf16[32,5248]{1,0:T(8,128)(2,1)S(1)}, bf16[32,5248]{1,0:T(8,128)(2,1)S(1)}, u32[]{:S(2)}, u32[]{:S(2)}) collective-permute-start(bf16[32,5248]{1,0:T(8,128)(2,1)S(1)} %collective-permute-done.7), channel_id=1, source_target_pairs={{0,14},{2,0},{4,2},{6,4},{8,6},{10,8},{12,10},{14,12},{1,15},{3,1}... | collective-permute-start | bytes 1007624 | tf_op jit(solution)/shard_map/ppermute | solution.py:17
  37.2 4.5 %collective-permute-done.8 = bf16[32,5248]{1,0:T(8,128)(2,1)S(1)} collective-permute-done((bf16[32,5248]{1,0:T(8,128)(2,1)S(1)}, bf16[32,5248]{1,0:T(8,128)(2,1)S(1)}, u32[]{:S(2)}, u32[]{:S(2)}) %collective-permute-start.8) | collective-permute-done | bytes 335904 | tf_op jit(solution)/shard_map/ppermute | solution.py:17
  41.8 2.9 %collective-permute-start.11 = (bf16[16,5248]{1,0:T(8,128)(2,1)S(1)}, bf16[16,5248]{1,0:T(8,128)(2,1)S(1)}, u32[]{:S(2)}, u32[]{:S(2)}) collective-permute-start(bf16[16,5248]{1,0:T(8,128)(2,1)S(1)} %slice.132), channel_id=1, source_target_pairs={{0,14},{2,0},{4,2},{6,4},{8,6},{10,8},{12,10},{14,12},{1,15},{3,1}... | collective-permute-start | bytes 503816 | tf_op jit(solution)/shard_map/ppermute | solution.py:17
  44.8 2.5 %collective-permute-done.10 = bf16[16,5248]{1,0:T(8,128)(2,1)S(1)} collective-permute-done((bf16[16,5248]{1,0:T(8,128)(2,1)S(1)}, bf16[16,5248]{1,0:T(8,128)(2,1)S(1)}, u32[]{:S(2)}, u32[]{:S(2)}) %collective-permute-start.10) | collective-permute-done | bytes 167968 | tf_op jit(solution)/shard_map/ppermute | solution.py:17
  47.4 0.6 fusion
  48.0 1.4 %fusion.3 = f32[256,432]{0,1:T(8,128)S(1)} fusion(bf16[216,5120]{1,0:T(8,128)(2,1)S(1)} %collective-permute-done.12, bf16[216,5120]{1,0:T(8,128)(2,1)S(1)} %bitcast.85, bf16[256,5120]{1,0:T(8,128)(2,1)S(1)} %slice_dynamic-update-slice_fusion.6, f32[5120]{0:T(1024)S(1)} %bitcast.82, f32[256]{0:T(256)S(1)} %add_rsqrt_fusion), kind=kOutput, calls=%fused_computation.13 | convolution fusion | flops 1146552320 | bytes 7508992 | tf_op jit(solution)/shard_map/dot_general | solution.py:73
  49.6 1.4 %multiply_convert_fusion = bf16[256,432]{0,1:T(8,128)(2,1)S(1)} fusion(f32[256,432]{0,1:T(8,128)S(1)} %fusion.3, bf16[216,5120]{1,0:T(8,128)(2,1)S(1)} %collective-permute-done.13, bf16[216,5120]{1,0:T(8,128)(2,1)S(1)} %bitcast.87, bf16[256,5120]{1,0:T(8,128)(2,1)S(1)} %slice_dynamic-update-slice_fusion.6, f32[5120]{0:T(1024)S(1)} %bitcast.83, ...), kind=kOutput, calls=%fused_computation.57 | convolution fusion | flops 1147215872 | bytes 7730176 | tf_op jit(solution)/shard_map/dot_general | solution.py:74
  51.1 0.5 convolution_convert_fusion
  52.4 2.7 %collective-permute-start.21 = (bf16[256,640]{1,0:T(8,128)(2,1)S(1)}, bf16[256,640]{1,0:T(8,128)(2,1)S(1)}, u32[]{:S(2)}, u32[]{:S(2)}) collective-permute-start(bf16[256,640]{1,0:T(8,128)(2,1)S(1)} %get-tuple-element.25), channel_id=1, source_target_pairs={{0,48},{16,0},{32,16},{48,32},{1,49},{17,1},{33,17},{49,33},{2,50}... | collective-permute-start | bytes 983048 | tf_op jit(solution)/shard_map/ppermute | solution.py:17
  55.1 0.5 fusion.19
  55.7 3.2 %collective-permute-done.15 = bf16[256,640]{1,0:T(8,128)(2,1)S(1)} collective-permute-done((bf16[256,640]{1,0:T(8,128)(2,1)S(1)}, bf16[256,640]{1,0:T(8,128)(2,1)S(1)}, u32[]{:S(2)}, u32[]{:S(2)}) %collective-permute-start.15) | collective-permute-done | bytes 327712 | tf_op jit(solution)/shard_map/ppermute | solution.py:17
  58.9 1.0 collective-permute-start.17
  59.9 1.7 %collective-permute-start.18 = (bf16[8,8,128]{2,1,0:T(8,128)(2,1)S(1)}, bf16[8,8,128]{2,1,0:T(8,128)(2,1)S(1)}, u32[]{:S(2)}, u32[]{:S(2)}) collective-permute-start(bf16[8,8,128]{2,1,0:T(8,128)(2,1)S(1)} %constant_dynamic-update-slice_fusion.4), channel_id=1, source_target_pairs={{0,48},{16,0},{32,16},{48,32},{1,49},{17,1},{33,17},{49,33},{2,50}... | collective-permute-start | bytes 49160 | tf_op jit(solution)/shard_map/ppermute | solution.py:17
  61.7 0.7 collective-permute-start.20
  62.5 2.2 %collective-permute-start.22 = (bf16[256,1280]{1,0:T(8,128)(2,1)S(1)}, bf16[256,1280]{1,0:T(8,128)(2,1)S(1)}, u32[]{:S(2)}, u32[]{:S(2)}) collective-permute-start(bf16[256,1280]{1,0:T(8,128)(2,1)S(1)} %pad_maximum_fusion.1), channel_id=1, source_target_pairs={{0,48},{16,0},{32,16},{48,32},{1,49},{17,1},{33,17},{49,33},{2,50}... | collective-permute-start | bytes 1966088 | tf_op jit(solution)/shard_map/ppermute | solution.py:17
  64.8 8.3 %collective-permute-start.19 = (bf16[256,128]{1,0:T(8,128)(2,1)S(1)}, bf16[256,128]{1,0:T(8,128)(2,1)S(1)}, u32[]{:S(2)}, u32[]{:S(2)}) collective-permute-start(bf16[256,128]{1,0:T(8,128)(2,1)S(1)} %bitcast.78), channel_id=1, source_target_pairs={{0,1},{1,0},{2,3},{3,2},{4,5},{5,4},{6,7},{7,6},{8,9},{9,8},{10,11... | collective-permute-start | bytes 196616 | tf_op jit(solution)/shard_map/ppermute | solution.py:17
  74.3 0.6 fusion.11
  74.9 7.7 %collective-permute-start.23 = (bf16[256,640]{1,0:T(8,128)(2,1)S(1)}, bf16[256,640]{1,0:T(8,128)(2,1)S(1)}, u32[]{:S(2)}, u32[]{:S(2)}) collective-permute-start(bf16[256,640]{1,0:T(8,128)(2,1)S(1)} %get-tuple-element.24), channel_id=1, source_target_pairs={{0,1},{1,0},{2,3},{3,2},{4,5},{5,4},{6,7},{7,6},{8,9},{9,8},{10,11... | collective-permute-start | bytes 983048 | tf_op jit(solution)/shard_map/ppermute | solution.py:17
  83.0 0.9 collective-permute-done.23
  84.2 0.8 collective-permute-start.25
  85.3 3.2 %collective-permute-start.29 = (bf16[64,640]{1,0:T(8,128)(2,1)S(1)}, bf16[64,640]{1,0:T(8,128)(2,1)S(1)}, u32[]{:S(2)}, u32[]{:S(2)}) collective-permute-start(bf16[64,640]{1,0:T(8,128)(2,1)S(1)} %get-tuple-element.36), channel_id=1, source_target_pairs={{0,14},{2,0},{4,2},{6,4},{8,6},{10,8},{12,10},{14,12},{1,15},{3,1}... | collective-permute-start | bytes 245768 | tf_op jit(solution)/shard_map/ppermute | solution.py:17
  88.8 1.8 %collective-permute-done.25 = bf16[64,640]{1,0:T(8,128)(2,1)S(1)} collective-permute-done((bf16[64,640]{1,0:T(8,128)(2,1)S(1)}, bf16[64,640]{1,0:T(8,128)(2,1)S(1)}, u32[]{:S(2)}, u32[]{:S(2)}) %collective-permute-start.25) | collective-permute-done | bytes 81952 | tf_op jit(solution)/shard_map/ppermute | solution.py:17
  90.9 2.7 %collective-permute-start.30 = (bf16[128,640]{1,0:T(8,128)(2,1)S(1)}, bf16[128,640]{1,0:T(8,128)(2,1)S(1)}, u32[]{:S(2)}, u32[]{:S(2)}) collective-permute-start(bf16[128,640]{1,0:T(8,128)(2,1)S(1)} %pad_maximum_fusion.5), channel_id=1, source_target_pairs={{0,14},{2,0},{4,2},{6,4},{8,6},{10,8},{12,10},{14,12},{1,15},{3,1}... | collective-permute-start | bytes 491528 | tf_op jit(solution)/shard_map/ppermute | solution.py:17
  93.6 3.2 %collective-permute-done.26 = bf16[128,640]{1,0:T(8,128)(2,1)S(1)} collective-permute-done((bf16[128,640]{1,0:T(8,128)(2,1)S(1)}, bf16[128,640]{1,0:T(8,128)(2,1)S(1)}, u32[]{:S(2)}, u32[]{:S(2)}) %collective-permute-start.26) | collective-permute-done | bytes 163872 | tf_op jit(solution)/shard_map/ppermute | solution.py:17
  97.7 2.5 %collective-permute-start.31 = (bf16[128,640]{1,0:T(8,128)(2,1)S(1)}, bf16[128,640]{1,0:T(8,128)(2,1)S(1)}, u32[]{:S(2)}, u32[]{:S(2)}) collective-permute-start(bf16[128,640]{1,0:T(8,128)(2,1)S(1)} %fusion.16), channel_id=1, source_target_pairs={{0,14},{2,0},{4,2},{6,4},{8,6},{10,8},{12,10},{14,12},{1,15},{3,1}... | collective-permute-start | bytes 491528 | tf_op jit(solution)/shard_map/ppermute | solution.py:17
  100.2 2.3 %collective-permute-done.27 = bf16[128,640]{1,0:T(8,128)(2,1)S(1)} collective-permute-done((bf16[128,640]{1,0:T(8,128)(2,1)S(1)}, bf16[128,640]{1,0:T(8,128)(2,1)S(1)}, u32[]{:S(2)}, u32[]{:S(2)}) %collective-permute-start.27) | collective-permute-done | bytes 163872 | tf_op jit(solution)/shard_map/ppermute | solution.py:17
  103.2 2.7 %collective-permute-start.32 = (bf16[128,640]{1,0:T(8,128)(2,1)S(1)}, bf16[128,640]{1,0:T(8,128)(2,1)S(1)}, u32[]{:S(2)}, u32[]{:S(2)}) collective-permute-start(bf16[128,640]{1,0:T(8,128)(2,1)S(1)} %fusion.15), channel_id=1, source_target_pairs={{0,14},{2,0},{4,2},{6,4},{8,6},{10,8},{12,10},{14,12},{1,15},{3,1}... | collective-permute-start | bytes 491528 | tf_op jit(solution)/shard_map/ppermute | solution.py:17
  106.2 2.1 %collective-permute-done.28 = bf16[128,640]{1,0:T(8,128)(2,1)S(1)} collective-permute-done((bf16[128,640]{1,0:T(8,128)(2,1)S(1)}, bf16[128,640]{1,0:T(8,128)(2,1)S(1)}, u32[]{:S(2)}, u32[]{:S(2)}) %collective-permute-start.28) | collective-permute-done | bytes 163872 | tf_op jit(solution)/shard_map/ppermute | solution.py:17
  108.6 4.2 %collective-permute-start.33 = (bf16[4,16,640]{2,1,0:T(8,128)(2,1)S(1)}, bf16[4,16,640]{2,1,0:T(8,128)(2,1)S(1)}, u32[]{:S(2)}, u32[]{:S(2)}) collective-permute-start(bf16[4,16,640]{2,1,0:T(8,128)(2,1)S(1)} %dynamic-slice_bitcast_fusion), channel_id=1, source_target_pairs={{0,1},{1,0},{2,3},{3,2},{4,5},{5,4},{6,7},{7,6},{8,9},{9,8},{10,11... | collective-permute-start | bytes 245768 | tf_op jit(solution)/shard_map/ppermute | solution.py:17
  112.8 0.9 collective-permute-done.33
  114.3 3.1 %collective-permute-start.35 = (bf16[16,1280]{1,0:T(8,128)(2,1)S(1)}, bf16[16,1280]{1,0:T(8,128)(2,1)S(1)}, u32[]{:S(2)}, u32[]{:S(2)}) collective-permute-start(bf16[16,1280]{1,0:T(8,128)(2,1)S(1)} %get-tuple-element.33), channel_id=1, source_target_pairs={{0,32},{16,48},{32,0},{48,16},{1,33},{17,49},{33,1},{49,17},{2,34}... | collective-permute-start | bytes 122888 | tf_op jit(solution)/shard_map/ppermute | solution.py:17
  117.3 0.6 collective-permute-done.34
  117.9 1.3 %collective-permute-done.35 = bf16[16,1280]{1,0:T(8,128)(2,1)S(1)} collective-permute-done((bf16[16,1280]{1,0:T(8,128)(2,1)S(1)}, bf16[16,1280]{1,0:T(8,128)(2,1)S(1)}, u32[]{:S(2)}, u32[]{:S(2)}) %collective-permute-start.35) | collective-permute-done | bytes 40992 | tf_op jit(solution)/shard_map/ppermute | solution.py:17
  119.2 1.1 collective-permute-done.36
  120.4 0.7 maximum_bitcast_fusion
  (109 shorter events, 7.8 us)
Async XLA Ops:
  0.0 11.6 %collective-permute-start = (bf16[8,5120]{1,0:T(8,128)(2,1)}, bf16[8,5120]{1,0:T(8,128)(2,1)S(1)}, u32[]{:S(2)}, u32[]{:S(2)}) collective-permute-start(bf16[8,5120]{1,0:T(8,128)(2,1)} %bitcast.88), channel_id=1, source_target_pairs={{0,64},{16,80},{32,96},{48,112},{64,128},{80,144},{96,160},{112,17... | collective-permute-start | bytes 245768 | tf_op jit(solution)/shard_map/ppermute | solution.py:26
  2.1 9.6 %collective-permute-start.1 = (bf16[8,5120]{1,0:T(8,128)(2,1)}, bf16[8,5120]{1,0:T(8,128)(2,1)S(1)}, u32[]{:S(2)}, u32[]{:S(2)}) collective-permute-start(bf16[8,5120]{1,0:T(8,128)(2,1)} %bitcast.89), channel_id=1, source_target_pairs={{0,80},{16,96},{32,112},{48,64},{64,144},{80,160},{96,176},{112,12... | collective-permute-start | bytes 245768 | tf_op jit(solution)/shard_map/ppermute | solution.py:26
  4.4 7.9 %collective-permute-start.2 = (bf16[8,5120]{1,0:T(8,128)(2,1)}, bf16[8,5120]{1,0:T(8,128)(2,1)S(1)}, u32[]{:S(2)}, u32[]{:S(2)}) collective-permute-start(bf16[8,5120]{1,0:T(8,128)(2,1)} %bitcast.90), channel_id=1, source_target_pairs={{0,96},{16,112},{32,64},{48,80},{64,160},{80,176},{96,128},{112,14... | collective-permute-start | bytes 245768 | tf_op jit(solution)/shard_map/ppermute | solution.py:26
  7.5 6.5 %collective-permute-start.3 = (bf16[8,5120]{1,0:T(8,128)(2,1)}, bf16[8,5120]{1,0:T(8,128)(2,1)S(1)}, u32[]{:S(2)}, u32[]{:S(2)}) collective-permute-start(bf16[8,5120]{1,0:T(8,128)(2,1)} %bitcast.91), channel_id=1, source_target_pairs={{0,112},{16,64},{32,80},{48,96},{64,176},{80,128},{96,144},{112,16... | collective-permute-start | bytes 245768 | tf_op jit(solution)/shard_map/ppermute | solution.py:26
  8.4 39.6 %collective-permute-start.12 = (bf16[216,5120]{1,0:T(8,128)(2,1)}, bf16[216,5120]{1,0:T(8,128)(2,1)S(1)}, u32[]{:S(2)}, u32[]{:S(2)}) collective-permute-start(bf16[216,5120]{1,0:T(8,128)(2,1)} %bitcast.84), channel_id=1, source_target_pairs={{0,1},{1,0},{2,3},{3,2},{4,5},{5,4},{6,7},{7,6},{8,9},{9,8},{10,11... | collective-permute-start | bytes 6635528 | tf_op jit(solution)/shard_map/ppermute | solution.py:17
  11.6 37.8 %collective-permute-start.13 = (bf16[216,5120]{1,0:T(8,128)(2,1)}, bf16[216,5120]{1,0:T(8,128)(2,1)S(1)}, u32[]{:S(2)}, u32[]{:S(2)}) collective-permute-start(bf16[216,5120]{1,0:T(8,128)(2,1)} %bitcast.86), channel_id=1, source_target_pairs={{0,1},{1,0},{2,3},{3,2},{4,5},{5,4},{6,7},{7,6},{8,9},{9,8},{10,11... | collective-permute-start | bytes 6635528 | tf_op jit(solution)/shard_map/ppermute | solution.py:17
  11.8 39.3 %collective-permute-start.14 = (bf16[216,5120]{1,0:T(8,128)(2,1)}, bf16[216,5120]{1,0:T(8,128)(2,1)S(1)}, u32[]{:S(2)}, u32[]{:S(2)}) collective-permute-start(bf16[216,5120]{1,0:T(8,128)(2,1)} %bitcast.73), channel_id=1, source_target_pairs={{0,1},{1,0},{2,3},{3,2},{4,5},{5,4},{6,7},{7,6},{8,9},{9,8},{10,11... | collective-permute-start | bytes 6635528 | tf_op jit(solution)/shard_map/ppermute | solution.py:17
  14.3 12.0 %collective-permute-start.4 = (bf16[32,5248]{1,0:T(8,128)(2,1)S(1)}, bf16[32,5248]{1,0:T(8,128)(2,1)S(1)}, u32[]{:S(2)}, u32[]{:S(2)}) collective-permute-start(bf16[32,5248]{1,0:T(8,128)(2,1)S(1)} %pad_maximum_fusion.3), channel_id=1, source_target_pairs={{0,2},{2,4},{4,6},{6,8},{8,10},{10,12},{12,14},{14,0},{1,3},{3,5},... | collective-permute-start | bytes 1007624 | tf_op jit(solution)/shard_map/ppermute | solution.py:17
  16.0 10.3 %collective-permute-start.5 = (bf16[32,5248]{1,0:T(8,128)(2,1)S(1)}, bf16[32,5248]{1,0:T(8,128)(2,1)S(1)}, u32[]{:S(2)}, u32[]{:S(2)}) collective-permute-start(bf16[32,5248]{1,0:T(8,128)(2,1)S(1)} %pad_maximum_fusion.3), channel_id=1, source_target_pairs={{0,14},{2,0},{4,2},{6,4},{8,6},{10,8},{12,10},{14,12},{1,15},{3,1}... | collective-permute-start | bytes 1007624 | tf_op jit(solution)/shard_map/ppermute | solution.py:17
  26.3 8.1 %collective-permute-start.6 = (bf16[32,5248]{1,0:T(8,128)(2,1)S(1)}, bf16[32,5248]{1,0:T(8,128)(2,1)S(1)}, u32[]{:S(2)}, u32[]{:S(2)}) collective-permute-start(bf16[32,5248]{1,0:T(8,128)(2,1)S(1)} %collective-permute-done.4), channel_id=1, source_target_pairs={{0,2},{2,4},{4,6},{6,8},{8,10},{10,12},{12,14},{14,0},{1,3},{3,5},... | collective-permute-start | bytes 1007624 | tf_op jit(solution)/shard_map/ppermute | solution.py:17
  26.3 8.1 %collective-permute-start.7 = (bf16[32,5248]{1,0:T(8,128)(2,1)S(1)}, bf16[32,5248]{1,0:T(8,128)(2,1)S(1)}, u32[]{:S(2)}, u32[]{:S(2)}) collective-permute-start(bf16[32,5248]{1,0:T(8,128)(2,1)S(1)} %collective-permute-done.5), channel_id=1, source_target_pairs={{0,14},{2,0},{4,2},{6,4},{8,6},{10,8},{12,10},{14,12},{1,15},{3,1}... | collective-permute-start | bytes 1007624 | tf_op jit(solution)/shard_map/ppermute | solution.py:17
  34.5 7.2 %collective-permute-start.8 = (bf16[32,5248]{1,0:T(8,128)(2,1)S(1)}, bf16[32,5248]{1,0:T(8,128)(2,1)S(1)}, u32[]{:S(2)}, u32[]{:S(2)}) collective-permute-start(bf16[32,5248]{1,0:T(8,128)(2,1)S(1)} %collective-permute-done.6), channel_id=1, source_target_pairs={{0,2},{2,4},{4,6},{6,8},{8,10},{10,12},{12,14},{14,0},{1,3},{3,5},... | collective-permute-start | bytes 1007624 | tf_op jit(solution)/shard_map/ppermute | solution.py:17
  34.5 7.3 %collective-permute-start.9 = (bf16[32,5248]{1,0:T(8,128)(2,1)S(1)}, bf16[32,5248]{1,0:T(8,128)(2,1)S(1)}, u32[]{:S(2)}, u32[]{:S(2)}) collective-permute-start(bf16[32,5248]{1,0:T(8,128)(2,1)S(1)} %collective-permute-done.7), channel_id=1, source_target_pairs={{0,14},{2,0},{4,2},{6,4},{8,6},{10,8},{12,10},{14,12},{1,15},{3,1}... | collective-permute-start | bytes 1007624 | tf_op jit(solution)/shard_map/ppermute | solution.py:17
  41.7 5.6 %collective-permute-start.10 = (bf16[16,5248]{1,0:T(8,128)(2,1)S(1)}, bf16[16,5248]{1,0:T(8,128)(2,1)S(1)}, u32[]{:S(2)}, u32[]{:S(2)}) collective-permute-start(bf16[16,5248]{1,0:T(8,128)(2,1)S(1)} %slice.130), channel_id=1, source_target_pairs={{0,2},{2,4},{4,6},{6,8},{8,10},{10,12},{12,14},{14,0},{1,3},{3,5},... | collective-permute-start | bytes 503816 | tf_op jit(solution)/shard_map/ppermute | solution.py:17
  41.8 5.5 %collective-permute-start.11 = (bf16[16,5248]{1,0:T(8,128)(2,1)S(1)}, bf16[16,5248]{1,0:T(8,128)(2,1)S(1)}, u32[]{:S(2)}, u32[]{:S(2)}) collective-permute-start(bf16[16,5248]{1,0:T(8,128)(2,1)S(1)} %slice.132), channel_id=1, source_target_pairs={{0,14},{2,0},{4,2},{6,4},{8,6},{10,8},{12,10},{14,12},{1,15},{3,1}... | collective-permute-start | bytes 503816 | tf_op jit(solution)/shard_map/ppermute | solution.py:17
  44.7 3.3 %copy-start.1 = (bf16[1,216,5120]{2,1,0:T(8,128)(2,1)S(1)}, bf16[1,216,5120]{2,1,0:T(8,128)(2,1)}, u32[]{:S(2)}) copy-start(bf16[1,216,5120]{2,1,0:T(8,128)(2,1)} %param.9) | copy-start | bytes 6635524
  48.0 1.6 %copy-start.2 = (bf16[1,216,5120]{2,1,0:T(8,128)(2,1)S(1)}, bf16[1,216,5120]{2,1,0:T(8,128)(2,1)}, u32[]{:S(2)}) copy-start(bf16[1,216,5120]{2,1,0:T(8,128)(2,1)} %param.10) | copy-start | bytes 6635524
  49.5 1.7 %copy-start = (bf16[1,216,5120]{2,1,0:T(8,128)(2,1)S(1)}, bf16[1,216,5120]{2,1,0:T(8,128)(2,1)}, u32[]{:S(2)}) copy-start(bf16[1,216,5120]{2,1,0:T(8,128)(2,1)} %param.11) | copy-start | bytes 6635524
  51.7 7.2 %collective-permute-start.15 = (bf16[256,640]{1,0:T(8,128)(2,1)S(1)}, bf16[256,640]{1,0:T(8,128)(2,1)S(1)}, u32[]{:S(2)}, u32[]{:S(2)}) collective-permute-start(bf16[256,640]{1,0:T(8,128)(2,1)S(1)} %get-tuple-element.26), channel_id=1, source_target_pairs={{0,16},{16,32},{32,48},{48,0},{1,17},{17,33},{33,49},{49,1},{2,18}... | collective-permute-start | bytes 983048 | tf_op jit(solution)/shard_map/ppermute | solution.py:17
  52.4 10.0 %collective-permute-start.21 = (bf16[256,640]{1,0:T(8,128)(2,1)S(1)}, bf16[256,640]{1,0:T(8,128)(2,1)S(1)}, u32[]{:S(2)}, u32[]{:S(2)}) collective-permute-start(bf16[256,640]{1,0:T(8,128)(2,1)S(1)} %get-tuple-element.25), channel_id=1, source_target_pairs={{0,48},{16,0},{32,16},{48,32},{1,49},{17,1},{33,17},{49,33},{2,50}... | collective-permute-start | bytes 983048 | tf_op jit(solution)/shard_map/ppermute | solution.py:17
  58.9 5.8 %collective-permute-start.16 = (bf16[8,8,128]{2,1,0:T(8,128)(2,1)S(1)}, bf16[8,8,128]{2,1,0:T(8,128)(2,1)S(1)}, u32[]{:S(2)}, u32[]{:S(2)}) collective-permute-start(bf16[8,8,128]{2,1,0:T(8,128)(2,1)S(1)} %constant_dynamic-update-slice_fusion.4), channel_id=1, source_target_pairs={{0,16},{16,32},{32,48},{48,0},{1,17},{17,33},{33,49},{49,1},{2,18}... | collective-permute-start | bytes 49160 | tf_op jit(solution)/shard_map/ppermute | solution.py:17
  58.9 5.8 %collective-permute-start.17 = (bf16[8,8,128]{2,1,0:T(8,128)(2,1)S(1)}, bf16[8,8,128]{2,1,0:T(8,128)(2,1)S(1)}, u32[]{:S(2)}, u32[]{:S(2)}) collective-permute-start(bf16[8,8,128]{2,1,0:T(8,128)(2,1)S(1)} %constant_dynamic-update-slice_fusion.4), channel_id=1, source_target_pairs={{0,32},{16,48},{32,0},{48,16},{1,33},{17,49},{33,1},{49,17},{2,34}... | collective-permute-start | bytes 49160 | tf_op jit(solution)/shard_map/ppermute | solution.py:17
  59.9 4.9 %collective-permute-start.18 = (bf16[8,8,128]{2,1,0:T(8,128)(2,1)S(1)}, bf16[8,8,128]{2,1,0:T(8,128)(2,1)S(1)}, u32[]{:S(2)}, u32[]{:S(2)}) collective-permute-start(bf16[8,8,128]{2,1,0:T(8,128)(2,1)S(1)} %constant_dynamic-update-slice_fusion.4), channel_id=1, source_target_pairs={{0,48},{16,0},{32,16},{48,32},{1,49},{17,1},{33,17},{49,33},{2,50}... | collective-permute-start | bytes 49160 | tf_op jit(solution)/shard_map/ppermute | solution.py:17
  61.7 12.5 %collective-permute-start.20 = (bf16[256,1280]{1,0:T(8,128)(2,1)S(1)}, bf16[256,1280]{1,0:T(8,128)(2,1)S(1)}, u32[]{:S(2)}, u32[]{:S(2)}) collective-permute-start(bf16[256,1280]{1,0:T(8,128)(2,1)S(1)} %pad_maximum_fusion), channel_id=1, source_target_pairs={{0,16},{16,32},{32,48},{48,0},{1,17},{17,33},{33,49},{49,1},{2,18}... | collective-permute-start | bytes 1966088 | tf_op jit(solution)/shard_map/ppermute | solution.py:17
  62.5 11.7 %collective-permute-start.22 = (bf16[256,1280]{1,0:T(8,128)(2,1)S(1)}, bf16[256,1280]{1,0:T(8,128)(2,1)S(1)}, u32[]{:S(2)}, u32[]{:S(2)}) collective-permute-start(bf16[256,1280]{1,0:T(8,128)(2,1)S(1)} %pad_maximum_fusion.1), channel_id=1, source_target_pairs={{0,48},{16,0},{32,16},{48,32},{1,49},{17,1},{33,17},{49,33},{2,50}... | collective-permute-start | bytes 1966088 | tf_op jit(solution)/shard_map/ppermute | solution.py:17
  64.8 9.2 %collective-permute-start.19 = (bf16[256,128]{1,0:T(8,128)(2,1)S(1)}, bf16[256,128]{1,0:T(8,128)(2,1)S(1)}, u32[]{:S(2)}, u32[]{:S(2)}) collective-permute-start(bf16[256,128]{1,0:T(8,128)(2,1)S(1)} %bitcast.78), channel_id=1, source_target_pairs={{0,1},{1,0},{2,3},{3,2},{4,5},{5,4},{6,7},{7,6},{8,9},{9,8},{10,11... | collective-permute-start | bytes 196616 | tf_op jit(solution)/shard_map/ppermute | solution.py:17
  73.6 32.4 %collective-permute-start.24 = (bf16[256,640]{1,0:T(8,128)(2,1)S(1)}, bf16[256,640]{1,0:T(8,128)(2,1)S(1)}, u32[]{:S(2)}, u32[]{:S(2)}) collective-permute-start(bf16[256,640]{1,0:T(8,128)(2,1)S(1)} %get-tuple-element.22), channel_id=1, source_target_pairs={{0,1},{1,0},{2,3},{3,2},{4,5},{5,4},{6,7},{7,6},{8,9},{9,8},{10,11... | collective-permute-start | bytes 983048 | tf_op jit(solution)/shard_map/ppermute | solution.py:17
  74.9 8.9 %collective-permute-start.23 = (bf16[256,640]{1,0:T(8,128)(2,1)S(1)}, bf16[256,640]{1,0:T(8,128)(2,1)S(1)}, u32[]{:S(2)}, u32[]{:S(2)}) collective-permute-start(bf16[256,640]{1,0:T(8,128)(2,1)S(1)} %get-tuple-element.24), channel_id=1, source_target_pairs={{0,1},{1,0},{2,3},{3,2},{4,5},{5,4},{6,7},{7,6},{8,9},{9,8},{10,11... | collective-permute-start | bytes 983048 | tf_op jit(solution)/shard_map/ppermute | solution.py:17
  84.2 6.5 %collective-permute-start.25 = (bf16[64,640]{1,0:T(8,128)(2,1)S(1)}, bf16[64,640]{1,0:T(8,128)(2,1)S(1)}, u32[]{:S(2)}, u32[]{:S(2)}) collective-permute-start(bf16[64,640]{1,0:T(8,128)(2,1)S(1)} %get-tuple-element.35), channel_id=1, source_target_pairs={{0,2},{2,4},{4,6},{6,8},{8,10},{10,12},{12,14},{14,0},{1,3},{3,5},... | collective-permute-start | bytes 245768 | tf_op jit(solution)/shard_map/ppermute | solution.py:17
  85.3 5.5 %collective-permute-start.29 = (bf16[64,640]{1,0:T(8,128)(2,1)S(1)}, bf16[64,640]{1,0:T(8,128)(2,1)S(1)}, u32[]{:S(2)}, u32[]{:S(2)}) collective-permute-start(bf16[64,640]{1,0:T(8,128)(2,1)S(1)} %get-tuple-element.36), channel_id=1, source_target_pairs={{0,14},{2,0},{4,2},{6,4},{8,6},{10,8},{12,10},{14,12},{1,15},{3,1}... | collective-permute-start | bytes 245768 | tf_op jit(solution)/shard_map/ppermute | solution.py:17
  90.7 6.1 %collective-permute-start.26 = (bf16[128,640]{1,0:T(8,128)(2,1)S(1)}, bf16[128,640]{1,0:T(8,128)(2,1)S(1)}, u32[]{:S(2)}, u32[]{:S(2)}) collective-permute-start(bf16[128,640]{1,0:T(8,128)(2,1)S(1)} %pad_maximum_fusion.4), channel_id=1, source_target_pairs={{0,2},{2,4},{4,6},{6,8},{8,10},{10,12},{12,14},{14,0},{1,3},{3,5},... | collective-permute-start | bytes 491528 | tf_op jit(solution)/shard_map/ppermute | solution.py:17
  90.9 6.5 %collective-permute-start.30 = (bf16[128,640]{1,0:T(8,128)(2,1)S(1)}, bf16[128,640]{1,0:T(8,128)(2,1)S(1)}, u32[]{:S(2)}, u32[]{:S(2)}) collective-permute-start(bf16[128,640]{1,0:T(8,128)(2,1)S(1)} %pad_maximum_fusion.5), channel_id=1, source_target_pairs={{0,14},{2,0},{4,2},{6,4},{8,6},{10,8},{12,10},{14,12},{1,15},{3,1}... | collective-permute-start | bytes 491528 | tf_op jit(solution)/shard_map/ppermute | solution.py:17
  97.1 5.5 %collective-permute-start.27 = (bf16[128,640]{1,0:T(8,128)(2,1)S(1)}, bf16[128,640]{1,0:T(8,128)(2,1)S(1)}, u32[]{:S(2)}, u32[]{:S(2)}) collective-permute-start(bf16[128,640]{1,0:T(8,128)(2,1)S(1)} %fusion.14), channel_id=1, source_target_pairs={{0,2},{2,4},{4,6},{6,8},{8,10},{10,12},{12,14},{14,0},{1,3},{3,5},... | collective-permute-start | bytes 491528 | tf_op jit(solution)/shard_map/ppermute | solution.py:17
  97.7 5.3 %collective-permute-start.31 = (bf16[128,640]{1,0:T(8,128)(2,1)S(1)}, bf16[128,640]{1,0:T(8,128)(2,1)S(1)}, u32[]{:S(2)}, u32[]{:S(2)}) collective-permute-start(bf16[128,640]{1,0:T(8,128)(2,1)S(1)} %fusion.16), channel_id=1, source_target_pairs={{0,14},{2,0},{4,2},{6,4},{8,6},{10,8},{12,10},{14,12},{1,15},{3,1}... | collective-permute-start | bytes 491528 | tf_op jit(solution)/shard_map/ppermute | solution.py:17
  102.8 5.5 %collective-permute-start.28 = (bf16[128,640]{1,0:T(8,128)(2,1)S(1)}, bf16[128,640]{1,0:T(8,128)(2,1)S(1)}, u32[]{:S(2)}, u32[]{:S(2)}) collective-permute-start(bf16[128,640]{1,0:T(8,128)(2,1)S(1)} %fusion.13), channel_id=1, source_target_pairs={{0,2},{2,4},{4,6},{6,8},{8,10},{10,12},{12,14},{14,0},{1,3},{3,5},... | collective-permute-start | bytes 491528 | tf_op jit(solution)/shard_map/ppermute | solution.py:17
  103.2 5.1 %collective-permute-start.32 = (bf16[128,640]{1,0:T(8,128)(2,1)S(1)}, bf16[128,640]{1,0:T(8,128)(2,1)S(1)}, u32[]{:S(2)}, u32[]{:S(2)}) collective-permute-start(bf16[128,640]{1,0:T(8,128)(2,1)S(1)} %fusion.15), channel_id=1, source_target_pairs={{0,14},{2,0},{4,2},{6,4},{8,6},{10,8},{12,10},{14,12},{1,15},{3,1}... | collective-permute-start | bytes 491528 | tf_op jit(solution)/shard_map/ppermute | solution.py:17
  108.6 5.1 %collective-permute-start.33 = (bf16[4,16,640]{2,1,0:T(8,128)(2,1)S(1)}, bf16[4,16,640]{2,1,0:T(8,128)(2,1)S(1)}, u32[]{:S(2)}, u32[]{:S(2)}) collective-permute-start(bf16[4,16,640]{2,1,0:T(8,128)(2,1)S(1)} %dynamic-slice_bitcast_fusion), channel_id=1, source_target_pairs={{0,1},{1,0},{2,3},{3,2},{4,5},{5,4},{6,7},{7,6},{8,9},{9,8},{10,11... | collective-permute-start | bytes 245768 | tf_op jit(solution)/shard_map/ppermute | solution.py:17
  113.8 4.1 %collective-permute-start.34 = (bf16[16,1280]{1,0:T(8,128)(2,1)S(1)}, bf16[16,1280]{1,0:T(8,128)(2,1)S(1)}, u32[]{:S(2)}, u32[]{:S(2)}) collective-permute-start(bf16[16,1280]{1,0:T(8,128)(2,1)S(1)} %get-tuple-element.32), channel_id=1, source_target_pairs={{0,16},{16,32},{32,48},{48,0},{1,17},{17,33},{33,49},{49,1},{2,18}... | collective-permute-start | bytes 122888 | tf_op jit(solution)/shard_map/ppermute | solution.py:17
  114.3 5.0 %collective-permute-start.35 = (bf16[16,1280]{1,0:T(8,128)(2,1)S(1)}, bf16[16,1280]{1,0:T(8,128)(2,1)S(1)}, u32[]{:S(2)}, u32[]{:S(2)}) collective-permute-start(bf16[16,1280]{1,0:T(8,128)(2,1)S(1)} %get-tuple-element.33), channel_id=1, source_target_pairs={{0,32},{16,48},{32,0},{48,16},{1,33},{17,49},{33,1},{49,17},{2,34}... | collective-permute-start | bytes 122888 | tf_op jit(solution)/shard_map/ppermute | solution.py:17
  117.3 3.0 %collective-permute-start.36 = (bf16[16,1280]{1,0:T(8,128)(2,1)S(1)}, bf16[16,1280]{1,0:T(8,128)(2,1)S(1)}, u32[]{:S(2)}, u32[]{:S(2)}) collective-permute-start(bf16[16,1280]{1,0:T(8,128)(2,1)S(1)} %get-tuple-element.34), channel_id=1, source_target_pairs={{0,48},{16,0},{32,16},{48,32},{1,49},{17,1},{33,17},{49,33},{2,50}... | collective-permute-start | bytes 122888 | tf_op jit(solution)/shard_map/ppermute | solution.py:17

commit v8 on v7

--- a/solution.py
+++ b/solution.py
@@ -98,7 +98,7 @@
     residual = swap(lax.dynamic_slice_in_dim(rows, x * quarter, quarter, 1))
 
     dests = jnp.zeros((X,) + dest.shape, BF)
-    for k in range(X):
+    for k in (0, 1, 3, 2):
         there = shift(dest, "x", k) if k else dest
         dests = lax.dynamic_update_slice(
             dests, there[None], (lax.rem(x + X - k, X), 0, 0, 0)

time: 123 us -> 123 us (level)
  starting transfers between devices: 69.5 us -> 68.2 us
    ppermute x33, starting transfers between devices: 61.1 us -> 59.8 us  [shift(): return lax.ppermute(array, axis, [(i, (i + by) % n) for i in range(n)])]
where the time goes in v8:
time: 123 us; the launch traced here: 121 us
  starting transfers between devices  68.2 us (55%)
  waiting for transfers between devices  39 us (32%)
  matrix products  7.46 us (6%)
  other arithmetic  3.85 us (3%)
  local copies, waits for them, and re-layouts  1.38 us (1%)
    ppermute x33, starting transfers between devices, shift(): return lax.ppermute(array, axis, [(i, (i + by) % n) for i in range(n)])  59.8 us
    ppermute x33, waiting for transfers between devices, shift(): return lax.ppermute(array, axis, [(i, (i + by) % n) for i in range(n)])  37.3 us
    ppermute x4, starting transfers between devices, handoff(): return lax.ppermute(rows, ('section', 'x'), pairs)  8.39 us
  transfers between devices with their start and end apart: 37, of which 17 were waited for; matrix products, arithmetic and copies ran while one was open for 9% of the time, Pallas kernels for 0%

profile of v8, /device:TPU:1, one launch (start us, length us, event | category | flops | bytes accessed | tf_op | source)
XLA Modules:
  0.0 120.6 jit_solution(1611970368768972093)
XLA Ops:
  0.0 2.1 %collective-permute-start = (bf16[8,5120]{1,0:T(8,128)(2,1)}, bf16[8,5120]{1,0:T(8,128)(2,1)S(1)}, u32[]{:S(2)}, u32[]{:S(2)}) collective-permute-start(bf16[8,5120]{1,0:T(8,128)(2,1)} %bitcast.88), channel_id=1, source_target_pairs={{0,64},{16,80},{32,96},{48,112},{64,128},{80,144},{96,160},{112,17... | collective-permute-start | bytes 245768 | tf_op jit(solution)/shard_map/ppermute | solution.py:26
  2.1 2.2 %collective-permute-start.1 = (bf16[8,5120]{1,0:T(8,128)(2,1)}, bf16[8,5120]{1,0:T(8,128)(2,1)S(1)}, u32[]{:S(2)}, u32[]{:S(2)}) collective-permute-start(bf16[8,5120]{1,0:T(8,128)(2,1)} %bitcast.89), channel_id=1, source_target_pairs={{0,80},{16,96},{32,112},{48,64},{64,144},{80,160},{96,176},{112,12... | collective-permute-start | bytes 245768 | tf_op jit(solution)/shard_map/ppermute | solution.py:26
  4.4 3.2 %collective-permute-start.2 = (bf16[8,5120]{1,0:T(8,128)(2,1)}, bf16[8,5120]{1,0:T(8,128)(2,1)S(1)}, u32[]{:S(2)}, u32[]{:S(2)}) collective-permute-start(bf16[8,5120]{1,0:T(8,128)(2,1)} %bitcast.90), channel_id=1, source_target_pairs={{0,96},{16,112},{32,64},{48,80},{64,160},{80,176},{96,128},{112,14... | collective-permute-start | bytes 245768 | tf_op jit(solution)/shard_map/ppermute | solution.py:26
  7.5 0.9 collective-permute-start.3
  8.4 1.7 %collective-permute-start.12 = (bf16[216,5120]{1,0:T(8,128)(2,1)}, bf16[216,5120]{1,0:T(8,128)(2,1)S(1)}, u32[]{:S(2)}, u32[]{:S(2)}) collective-permute-start(bf16[216,5120]{1,0:T(8,128)(2,1)} %bitcast.84), channel_id=1, source_target_pairs={{0,1},{1,0},{2,3},{3,2},{4,5},{5,4},{6,7},{7,6},{8,9},{9,8},{10,11... | collective-permute-start | bytes 6635528 | tf_op jit(solution)/shard_map/ppermute | solution.py:17
  10.1 0.7 convert_bitcast_fusion
  10.8 0.7 mul.123
  12.2 1.7 %collective-permute-done.3 = bf16[8,5120]{1,0:T(8,128)(2,1)S(1)} collective-permute-done((bf16[8,5120]{1,0:T(8,128)(2,1)}, bf16[8,5120]{1,0:T(8,128)(2,1)S(1)}, u32[]{:S(2)}, u32[]{:S(2)}) %collective-permute-start.3) | collective-permute-done | bytes 81952 | tf_op jit(solution)/shard_map/ppermute | solution.py:26
  14.3 1.7 %collective-permute-start.4 = (bf16[32,5248]{1,0:T(8,128)(2,1)S(1)}, bf16[32,5248]{1,0:T(8,128)(2,1)S(1)}, u32[]{:S(2)}, u32[]{:S(2)}) collective-permute-start(bf16[32,5248]{1,0:T(8,128)(2,1)S(1)} %pad_maximum_fusion.3), channel_id=1, source_target_pairs={{0,2},{2,4},{4,6},{6,8},{8,10},{10,12},{12,14},{14,0},{1,3},{3,5},... | collective-permute-start | bytes 1007624 | tf_op jit(solution)/shard_map/ppermute | solution.py:17
  16.0 4.0 %collective-permute-start.5 = (bf16[32,5248]{1,0:T(8,128)(2,1)S(1)}, bf16[32,5248]{1,0:T(8,128)(2,1)S(1)}, u32[]{:S(2)}, u32[]{:S(2)}) collective-permute-start(bf16[32,5248]{1,0:T(8,128)(2,1)S(1)} %pad_maximum_fusion.3), channel_id=1, source_target_pairs={{0,14},{2,0},{4,2},{6,4},{8,6},{10,8},{12,10},{14,12},{1,15},{3,1}... | collective-permute-start | bytes 1007624 | tf_op jit(solution)/shard_map/ppermute | solution.py:17
  20.1 6.2 %collective-permute-done.4 = bf16[32,5248]{1,0:T(8,128)(2,1)S(1)} collective-permute-done((bf16[32,5248]{1,0:T(8,128)(2,1)S(1)}, bf16[32,5248]{1,0:T(8,128)(2,1)S(1)}, u32[]{:S(2)}, u32[]{:S(2)}) %collective-permute-start.4) | collective-permute-done | bytes 335904 | tf_op jit(solution)/shard_map/ppermute | solution.py:17
  26.3 2.7 %collective-permute-start.7 = (bf16[32,5248]{1,0:T(8,128)(2,1)S(1)}, bf16[32,5248]{1,0:T(8,128)(2,1)S(1)}, u32[]{:S(2)}, u32[]{:S(2)}) collective-permute-start(bf16[32,5248]{1,0:T(8,128)(2,1)S(1)} %collective-permute-done.5), channel_id=1, source_target_pairs={{0,14},{2,0},{4,2},{6,4},{8,6},{10,8},{12,10},{14,12},{1,15},{3,1}... | collective-permute-start | bytes 1007624 | tf_op jit(solution)/shard_map/ppermute | solution.py:17
  29.1 5.4 %collective-permute-done.6 = bf16[32,5248]{1,0:T(8,128)(2,1)S(1)} collective-permute-done((bf16[32,5248]{1,0:T(8,128)(2,1)S(1)}, bf16[32,5248]{1,0:T(8,128)(2,1)S(1)}, u32[]{:S(2)}, u32[]{:S(2)}) %collective-permute-start.6) | collective-permute-done | bytes 335904 | tf_op jit(solution)/shard_map/ppermute | solution.py:17
  34.5 2.7 %collective-permute-start.9 = (bf16[32,5248]{1,0:T(8,128)(2,1)S(1)}, bf16[32,5248]{1,0:T(8,128)(2,1)S(1)}, u32[]{:S(2)}, u32[]{:S(2)}) collective-permute-start(bf16[32,5248]{1,0:T(8,128)(2,1)S(1)} %collective-permute-done.7), channel_id=1, source_target_pairs={{0,14},{2,0},{4,2},{6,4},{8,6},{10,8},{12,10},{14,12},{1,15},{3,1}... | collective-permute-start | bytes 1007624 | tf_op jit(solution)/shard_map/ppermute | solution.py:17
  37.2 4.5 %collective-permute-done.8 = bf16[32,5248]{1,0:T(8,128)(2,1)S(1)} collective-permute-done((bf16[32,5248]{1,0:T(8,128)(2,1)S(1)}, bf16[32,5248]{1,0:T(8,128)(2,1)S(1)}, u32[]{:S(2)}, u32[]{:S(2)}) %collective-permute-start.8) | collective-permute-done | bytes 335904 | tf_op jit(solution)/shard_map/ppermute | solution.py:17
  41.8 2.9 %collective-permute-start.11 = (bf16[16,5248]{1,0:T(8,128)(2,1)S(1)}, bf16[16,5248]{1,0:T(8,128)(2,1)S(1)}, u32[]{:S(2)}, u32[]{:S(2)}) collective-permute-start(bf16[16,5248]{1,0:T(8,128)(2,1)S(1)} %slice.132), channel_id=1, source_target_pairs={{0,14},{2,0},{4,2},{6,4},{8,6},{10,8},{12,10},{14,12},{1,15},{3,1}... | collective-permute-start | bytes 503816 | tf_op jit(solution)/shard_map/ppermute | solution.py:17
  44.8 2.5 %collective-permute-done.10 = bf16[16,5248]{1,0:T(8,128)(2,1)S(1)} collective-permute-done((bf16[16,5248]{1,0:T(8,128)(2,1)S(1)}, bf16[16,5248]{1,0:T(8,128)(2,1)S(1)}, u32[]{:S(2)}, u32[]{:S(2)}) %collective-permute-start.10) | collective-permute-done | bytes 167968 | tf_op jit(solution)/shard_map/ppermute | solution.py:17
  47.4 0.6 fusion
  48.0 1.4 %fusion.3 = f32[256,432]{0,1:T(8,128)S(1)} fusion(bf16[216,5120]{1,0:T(8,128)(2,1)S(1)} %collective-permute-done.12, bf16[216,5120]{1,0:T(8,128)(2,1)S(1)} %bitcast.85, bf16[256,5120]{1,0:T(8,128)(2,1)S(1)} %slice_dynamic-update-slice_fusion.6, f32[5120]{0:T(1024)S(1)} %bitcast.82, f32[256]{0:T(256)S(1)} %add_rsqrt_fusion), kind=kOutput, calls=%fused_computation.13 | convolution fusion | flops 1146552320 | bytes 7508992 | tf_op jit(solution)/shard_map/dot_general | solution.py:73
  49.6 1.4 %multiply_convert_fusion = bf16[256,432]{0,1:T(8,128)(2,1)S(1)} fusion(f32[256,432]{0,1:T(8,128)S(1)} %fusion.3, bf16[216,5120]{1,0:T(8,128)(2,1)S(1)} %collective-permute-done.13, bf16[216,5120]{1,0:T(8,128)(2,1)S(1)} %bitcast.87, bf16[256,5120]{1,0:T(8,128)(2,1)S(1)} %slice_dynamic-update-slice_fusion.6, f32[5120]{0:T(1024)S(1)} %bitcast.83, ...), kind=kOutput, calls=%fused_computation.57 | convolution fusion | flops 1147215872 | bytes 7730176 | tf_op jit(solution)/shard_map/dot_general | solution.py:74
  51.1 0.5 convolution_convert_fusion
  51.8 0.5 fusion.26
  52.4 2.7 %collective-permute-start.21 = (bf16[256,640]{1,0:T(8,128)(2,1)S(1)}, bf16[256,640]{1,0:T(8,128)(2,1)S(1)}, u32[]{:S(2)}, u32[]{:S(2)}) collective-permute-start(bf16[256,640]{1,0:T(8,128)(2,1)S(1)} %get-tuple-element.25), channel_id=1, source_target_pairs={{0,48},{16,0},{32,16},{48,32},{1,49},{17,1},{33,17},{49,33},{2,50}... | collective-permute-start | bytes 983048 | tf_op jit(solution)/shard_map/ppermute | solution.py:17
  55.1 0.5 fusion.19
  55.7 3.2 %collective-permute-done.15 = bf16[256,640]{1,0:T(8,128)(2,1)S(1)} collective-permute-done((bf16[256,640]{1,0:T(8,128)(2,1)S(1)}, bf16[256,640]{1,0:T(8,128)(2,1)S(1)}, u32[]{:S(2)}, u32[]{:S(2)}) %collective-permute-start.15) | collective-permute-done | bytes 327712 | tf_op jit(solution)/shard_map/ppermute | solution.py:17
  58.9 2.7 %collective-permute-start.17 = (bf16[8,8,128]{2,1,0:T(8,128)(2,1)S(1)}, bf16[8,8,128]{2,1,0:T(8,128)(2,1)S(1)}, u32[]{:S(2)}, u32[]{:S(2)}) collective-permute-start(bf16[8,8,128]{2,1,0:T(8,128)(2,1)S(1)} %constant_dynamic-update-slice_fusion.4), channel_id=1, source_target_pairs={{0,48},{16,0},{32,16},{48,32},{1,49},{17,1},{33,17},{49,33},{2,50}... | collective-permute-start | bytes 49160 | tf_op jit(solution)/shard_map/ppermute | solution.py:17
  61.7 0.7 collective-permute-start.20
  62.5 2.2 %collective-permute-start.22 = (bf16[256,1280]{1,0:T(8,128)(2,1)S(1)}, bf16[256,1280]{1,0:T(8,128)(2,1)S(1)}, u32[]{:S(2)}, u32[]{:S(2)}) collective-permute-start(bf16[256,1280]{1,0:T(8,128)(2,1)S(1)} %pad_maximum_fusion.1), channel_id=1, source_target_pairs={{0,48},{16,0},{32,16},{48,32},{1,49},{17,1},{33,17},{49,33},{2,50}... | collective-permute-start | bytes 1966088 | tf_op jit(solution)/shard_map/ppermute | solution.py:17
  64.8 1.0 collective-permute-done.18
  65.8 8.7 %collective-permute-start.19 = (bf16[256,128]{1,0:T(8,128)(2,1)S(1)}, bf16[256,128]{1,0:T(8,128)(2,1)S(1)}, u32[]{:S(2)}, u32[]{:S(2)}) collective-permute-start(bf16[256,128]{1,0:T(8,128)(2,1)S(1)} %bitcast.78), channel_id=1, source_target_pairs={{0,1},{1,0},{2,3},{3,2},{4,5},{5,4},{6,7},{7,6},{8,9},{9,8},{10,11... | collective-permute-start | bytes 196616 | tf_op jit(solution)/shard_map/ppermute | solution.py:17
  75.6 0.6 fusion.11
  76.3 6.0 %collective-permute-start.23 = (bf16[256,640]{1,0:T(8,128)(2,1)S(1)}, bf16[256,640]{1,0:T(8,128)(2,1)S(1)}, u32[]{:S(2)}, u32[]{:S(2)}) collective-permute-start(bf16[256,640]{1,0:T(8,128)(2,1)S(1)} %get-tuple-element.24), channel_id=1, source_target_pairs={{0,1},{1,0},{2,3},{3,2},{4,5},{5,4},{6,7},{7,6},{8,9},{9,8},{10,11... | collective-permute-start | bytes 983048 | tf_op jit(solution)/shard_map/ppermute | solution.py:17
  82.7 0.9 collective-permute-done.23
  84.3 3.3 %collective-permute-start.29 = (bf16[64,640]{1,0:T(8,128)(2,1)S(1)}, bf16[64,640]{1,0:T(8,128)(2,1)S(1)}, u32[]{:S(2)}, u32[]{:S(2)}) collective-permute-start(bf16[64,640]{1,0:T(8,128)(2,1)S(1)} %get-tuple-element.36), channel_id=1, source_target_pairs={{0,14},{2,0},{4,2},{6,4},{8,6},{10,8},{12,10},{14,12},{1,15},{3,1}... | collective-permute-start | bytes 245768 | tf_op jit(solution)/shard_map/ppermute | solution.py:17
  87.8 1.8 %collective-permute-done.25 = bf16[64,640]{1,0:T(8,128)(2,1)S(1)} collective-permute-done((bf16[64,640]{1,0:T(8,128)(2,1)S(1)}, bf16[64,640]{1,0:T(8,128)(2,1)S(1)}, u32[]{:S(2)}, u32[]{:S(2)}) %collective-permute-start.25) | collective-permute-done | bytes 81952 | tf_op jit(solution)/shard_map/ppermute | solution.py:17
  89.9 2.7 %collective-permute-start.30 = (bf16[128,640]{1,0:T(8,128)(2,1)S(1)}, bf16[128,640]{1,0:T(8,128)(2,1)S(1)}, u32[]{:S(2)}, u32[]{:S(2)}) collective-permute-start(bf16[128,640]{1,0:T(8,128)(2,1)S(1)} %pad_maximum_fusion.5), channel_id=1, source_target_pairs={{0,14},{2,0},{4,2},{6,4},{8,6},{10,8},{12,10},{14,12},{1,15},{3,1}... | collective-permute-start | bytes 491528 | tf_op jit(solution)/shard_map/ppermute | solution.py:17
  92.6 3.2 %collective-permute-done.26 = bf16[128,640]{1,0:T(8,128)(2,1)S(1)} collective-permute-done((bf16[128,640]{1,0:T(8,128)(2,1)S(1)}, bf16[128,640]{1,0:T(8,128)(2,1)S(1)}, u32[]{:S(2)}, u32[]{:S(2)}) %collective-permute-start.26) | collective-permute-done | bytes 163872 | tf_op jit(solution)/shard_map/ppermute | solution.py:17
  96.7 2.5 %collective-permute-start.31 = (bf16[128,640]{1,0:T(8,128)(2,1)S(1)}, bf16[128,640]{1,0:T(8,128)(2,1)S(1)}, u32[]{:S(2)}, u32[]{:S(2)}) collective-permute-start(bf16[128,640]{1,0:T(8,128)(2,1)S(1)} %fusion.16), channel_id=1, source_target_pairs={{0,14},{2,0},{4,2},{6,4},{8,6},{10,8},{12,10},{14,12},{1,15},{3,1}... | collective-permute-start | bytes 491528 | tf_op jit(solution)/shard_map/ppermute | solution.py:17
  99.2 2.3 %collective-permute-done.27 = bf16[128,640]{1,0:T(8,128)(2,1)S(1)} collective-permute-done((bf16[128,640]{1,0:T(8,128)(2,1)S(1)}, bf16[128,640]{1,0:T(8,128)(2,1)S(1)}, u32[]{:S(2)}, u32[]{:S(2)}) %collective-permute-start.27) | collective-permute-done | bytes 163872 | tf_op jit(solution)/shard_map/ppermute | solution.py:17
  102.2 2.7 %collective-permute-start.32 = (bf16[128,640]{1,0:T(8,128)(2,1)S(1)}, bf16[128,640]{1,0:T(8,128)(2,1)S(1)}, u32[]{:S(2)}, u32[]{:S(2)}) collective-permute-start(bf16[128,640]{1,0:T(8,128)(2,1)S(1)} %fusion.15), channel_id=1, source_target_pairs={{0,14},{2,0},{4,2},{6,4},{8,6},{10,8},{12,10},{14,12},{1,15},{3,1}... | collective-permute-start | bytes 491528 | tf_op jit(solution)/shard_map/ppermute | solution.py:17
  105.2 2.1 %collective-permute-done.28 = bf16[128,640]{1,0:T(8,128)(2,1)S(1)} collective-permute-done((bf16[128,640]{1,0:T(8,128)(2,1)S(1)}, bf16[128,640]{1,0:T(8,128)(2,1)S(1)}, u32[]{:S(2)}, u32[]{:S(2)}) %collective-permute-start.28) | collective-permute-done | bytes 163872 | tf_op jit(solution)/shard_map/ppermute | solution.py:17
  107.6 4.2 %collective-permute-start.33 = (bf16[4,16,640]{2,1,0:T(8,128)(2,1)S(1)}, bf16[4,16,640]{2,1,0:T(8,128)(2,1)S(1)}, u32[]{:S(2)}, u32[]{:S(2)}) collective-permute-start(bf16[4,16,640]{2,1,0:T(8,128)(2,1)S(1)} %dynamic-slice_bitcast_fusion), channel_id=1, source_target_pairs={{0,1},{1,0},{2,3},{3,2},{4,5},{5,4},{6,7},{7,6},{8,9},{9,8},{10,11... | collective-permute-start | bytes 245768 | tf_op jit(solution)/shard_map/ppermute | solution.py:17
  111.8 0.9 collective-permute-done.33
  112.8 1.8 %collective-permute-start.34 = (bf16[16,1280]{1,0:T(8,128)(2,1)S(1)}, bf16[16,1280]{1,0:T(8,128)(2,1)S(1)}, u32[]{:S(2)}, u32[]{:S(2)}) collective-permute-start(bf16[16,1280]{1,0:T(8,128)(2,1)S(1)} %get-tuple-element.32), channel_id=1, source_target_pairs={{0,16},{16,32},{32,48},{48,0},{1,17},{17,33},{33,49},{49,1},{2,18}... | collective-permute-start | bytes 122888 | tf_op jit(solution)/shard_map/ppermute | solution.py:17
  114.6 2.2 %collective-permute-start.35 = (bf16[16,1280]{1,0:T(8,128)(2,1)S(1)}, bf16[16,1280]{1,0:T(8,128)(2,1)S(1)}, u32[]{:S(2)}, u32[]{:S(2)}) collective-permute-start(bf16[16,1280]{1,0:T(8,128)(2,1)S(1)} %get-tuple-element.33), channel_id=1, source_target_pairs={{0,32},{16,48},{32,0},{48,16},{1,33},{17,49},{33,1},{49,17},{2,34}... | collective-permute-start | bytes 122888 | tf_op jit(solution)/shard_map/ppermute | solution.py:17
  117.1 2.3 %collective-permute-done.35 = bf16[16,1280]{1,0:T(8,128)(2,1)S(1)} collective-permute-done((bf16[16,1280]{1,0:T(8,128)(2,1)S(1)}, bf16[16,1280]{1,0:T(8,128)(2,1)S(1)}, u32[]{:S(2)}, u32[]{:S(2)}) %collective-permute-start.35) | collective-permute-done | bytes 40992 | tf_op jit(solution)/shard_map/ppermute | solution.py:17
  119.4 0.5 collective-permute-done.36
  119.9 0.7 maximum_bitcast_fusion
  (109 shorter events, 7.2 us)
Async XLA Ops:
  0.0 11.6 %collective-permute-start = (bf16[8,5120]{1,0:T(8,128)(2,1)}, bf16[8,5120]{1,0:T(8,128)(2,1)S(1)}, u32[]{:S(2)}, u32[]{:S(2)}) collective-permute-start(bf16[8,5120]{1,0:T(8,128)(2,1)} %bitcast.88), channel_id=1, source_target_pairs={{0,64},{16,80},{32,96},{48,112},{64,128},{80,144},{96,160},{112,17... | collective-permute-start | bytes 245768 | tf_op jit(solution)/shard_map/ppermute | solution.py:26
  2.1 9.6 %collective-permute-start.1 = (bf16[8,5120]{1,0:T(8,128)(2,1)}, bf16[8,5120]{1,0:T(8,128)(2,1)S(1)}, u32[]{:S(2)}, u32[]{:S(2)}) collective-permute-start(bf16[8,5120]{1,0:T(8,128)(2,1)} %bitcast.89), channel_id=1, source_target_pairs={{0,80},{16,96},{32,112},{48,64},{64,144},{80,160},{96,176},{112,12... | collective-permute-start | bytes 245768 | tf_op jit(solution)/shard_map/ppermute | solution.py:26
  4.4 7.9 %collective-permute-start.2 = (bf16[8,5120]{1,0:T(8,128)(2,1)}, bf16[8,5120]{1,0:T(8,128)(2,1)S(1)}, u32[]{:S(2)}, u32[]{:S(2)}) collective-permute-start(bf16[8,5120]{1,0:T(8,128)(2,1)} %bitcast.90), channel_id=1, source_target_pairs={{0,96},{16,112},{32,64},{48,80},{64,160},{80,176},{96,128},{112,14... | collective-permute-start | bytes 245768 | tf_op jit(solution)/shard_map/ppermute | solution.py:26
  7.5 6.5 %collective-permute-start.3 = (bf16[8,5120]{1,0:T(8,128)(2,1)}, bf16[8,5120]{1,0:T(8,128)(2,1)S(1)}, u32[]{:S(2)}, u32[]{:S(2)}) collective-permute-start(bf16[8,5120]{1,0:T(8,128)(2,1)} %bitcast.91), channel_id=1, source_target_pairs={{0,112},{16,64},{32,80},{48,96},{64,176},{80,128},{96,144},{112,16... | collective-permute-start | bytes 245768 | tf_op jit(solution)/shard_map/ppermute | solution.py:26
  8.4 39.6 %collective-permute-start.12 = (bf16[216,5120]{1,0:T(8,128)(2,1)}, bf16[216,5120]{1,0:T(8,128)(2,1)S(1)}, u32[]{:S(2)}, u32[]{:S(2)}) collective-permute-start(bf16[216,5120]{1,0:T(8,128)(2,1)} %bitcast.84), channel_id=1, source_target_pairs={{0,1},{1,0},{2,3},{3,2},{4,5},{5,4},{6,7},{7,6},{8,9},{9,8},{10,11... | collective-permute-start | bytes 6635528 | tf_op jit(solution)/shard_map/ppermute | solution.py:17
  11.6 37.8 %collective-permute-start.13 = (bf16[216,5120]{1,0:T(8,128)(2,1)}, bf16[216,5120]{1,0:T(8,128)(2,1)S(1)}, u32[]{:S(2)}, u32[]{:S(2)}) collective-permute-start(bf16[216,5120]{1,0:T(8,128)(2,1)} %bitcast.86), channel_id=1, source_target_pairs={{0,1},{1,0},{2,3},{3,2},{4,5},{5,4},{6,7},{7,6},{8,9},{9,8},{10,11... | collective-permute-start | bytes 6635528 | tf_op jit(solution)/shard_map/ppermute | solution.py:17
  11.8 39.3 %collective-permute-start.14 = (bf16[216,5120]{1,0:T(8,128)(2,1)}, bf16[216,5120]{1,0:T(8,128)(2,1)S(1)}, u32[]{:S(2)}, u32[]{:S(2)}) collective-permute-start(bf16[216,5120]{1,0:T(8,128)(2,1)} %bitcast.73), channel_id=1, source_target_pairs={{0,1},{1,0},{2,3},{3,2},{4,5},{5,4},{6,7},{7,6},{8,9},{9,8},{10,11... | collective-permute-start | bytes 6635528 | tf_op jit(solution)/shard_map/ppermute | solution.py:17
  14.3 12.0 %collective-permute-start.4 = (bf16[32,5248]{1,0:T(8,128)(2,1)S(1)}, bf16[32,5248]{1,0:T(8,128)(2,1)S(1)}, u32[]{:S(2)}, u32[]{:S(2)}) collective-permute-start(bf16[32,5248]{1,0:T(8,128)(2,1)S(1)} %pad_maximum_fusion.3), channel_id=1, source_target_pairs={{0,2},{2,4},{4,6},{6,8},{8,10},{10,12},{12,14},{14,0},{1,3},{3,5},... | collective-permute-start | bytes 1007624 | tf_op jit(solution)/shard_map/ppermute | solution.py:17
  16.0 10.3 %collective-permute-start.5 = (bf16[32,5248]{1,0:T(8,128)(2,1)S(1)}, bf16[32,5248]{1,0:T(8,128)(2,1)S(1)}, u32[]{:S(2)}, u32[]{:S(2)}) collective-permute-start(bf16[32,5248]{1,0:T(8,128)(2,1)S(1)} %pad_maximum_fusion.3), channel_id=1, source_target_pairs={{0,14},{2,0},{4,2},{6,4},{8,6},{10,8},{12,10},{14,12},{1,15},{3,1}... | collective-permute-start | bytes 1007624 | tf_op jit(solution)/shard_map/ppermute | solution.py:17
  26.3 8.1 %collective-permute-start.6 = (bf16[32,5248]{1,0:T(8,128)(2,1)S(1)}, bf16[32,5248]{1,0:T(8,128)(2,1)S(1)}, u32[]{:S(2)}, u32[]{:S(2)}) collective-permute-start(bf16[32,5248]{1,0:T(8,128)(2,1)S(1)} %collective-permute-done.4), channel_id=1, source_target_pairs={{0,2},{2,4},{4,6},{6,8},{8,10},{10,12},{12,14},{14,0},{1,3},{3,5},... | collective-permute-start | bytes 1007624 | tf_op jit(solution)/shard_map/ppermute | solution.py:17
  26.3 8.1 %collective-permute-start.7 = (bf16[32,5248]{1,0:T(8,128)(2,1)S(1)}, bf16[32,5248]{1,0:T(8,128)(2,1)S(1)}, u32[]{:S(2)}, u32[]{:S(2)}) collective-permute-start(bf16[32,5248]{1,0:T(8,128)(2,1)S(1)} %collective-permute-done.5), channel_id=1, source_target_pairs={{0,14},{2,0},{4,2},{6,4},{8,6},{10,8},{12,10},{14,12},{1,15},{3,1}... | collective-permute-start | bytes 1007624 | tf_op jit(solution)/shard_map/ppermute | solution.py:17
  34.5 7.2 %collective-permute-start.8 = (bf16[32,5248]{1,0:T(8,128)(2,1)S(1)}, bf16[32,5248]{1,0:T(8,128)(2,1)S(1)}, u32[]{:S(2)}, u32[]{:S(2)}) collective-permute-start(bf16[32,5248]{1,0:T(8,128)(2,1)S(1)} %collective-permute-done.6), channel_id=1, source_target_pairs={{0,2},{2,4},{4,6},{6,8},{8,10},{10,12},{12,14},{14,0},{1,3},{3,5},... | collective-permute-start | bytes 1007624 | tf_op jit(solution)/shard_map/ppermute | solution.py:17
  34.5 7.3 %collective-permute-start.9 = (bf16[32,5248]{1,0:T(8,128)(2,1)S(1)}, bf16[32,5248]{1,0:T(8,128)(2,1)S(1)}, u32[]{:S(2)}, u32[]{:S(2)}) collective-permute-start(bf16[32,5248]{1,0:T(8,128)(2,1)S(1)} %collective-permute-done.7), channel_id=1, source_target_pairs={{0,14},{2,0},{4,2},{6,4},{8,6},{10,8},{12,10},{14,12},{1,15},{3,1}... | collective-permute-start | bytes 1007624 | tf_op jit(solution)/shard_map/ppermute | solution.py:17
  41.7 5.6 %collective-permute-start.10 = (bf16[16,5248]{1,0:T(8,128)(2,1)S(1)}, bf16[16,5248]{1,0:T(8,128)(2,1)S(1)}, u32[]{:S(2)}, u32[]{:S(2)}) collective-permute-start(bf16[16,5248]{1,0:T(8,128)(2,1)S(1)} %slice.130), channel_id=1, source_target_pairs={{0,2},{2,4},{4,6},{6,8},{8,10},{10,12},{12,14},{14,0},{1,3},{3,5},... | collective-permute-start | bytes 503816 | tf_op jit(solution)/shard_map/ppermute | solution.py:17
  41.8 5.5 %collective-permute-start.11 = (bf16[16,5248]{1,0:T(8,128)(2,1)S(1)}, bf16[16,5248]{1,0:T(8,128)(2,1)S(1)}, u32[]{:S(2)}, u32[]{:S(2)}) collective-permute-start(bf16[16,5248]{1,0:T(8,128)(2,1)S(1)} %slice.132), channel_id=1, source_target_pairs={{0,14},{2,0},{4,2},{6,4},{8,6},{10,8},{12,10},{14,12},{1,15},{3,1}... | collective-permute-start | bytes 503816 | tf_op jit(solution)/shard_map/ppermute | solution.py:17
  44.7 3.3 %copy-start.1 = (bf16[1,216,5120]{2,1,0:T(8,128)(2,1)S(1)}, bf16[1,216,5120]{2,1,0:T(8,128)(2,1)}, u32[]{:S(2)}) copy-start(bf16[1,216,5120]{2,1,0:T(8,128)(2,1)} %param.9) | copy-start | bytes 6635524
  48.0 1.6 %copy-start.2 = (bf16[1,216,5120]{2,1,0:T(8,128)(2,1)S(1)}, bf16[1,216,5120]{2,1,0:T(8,128)(2,1)}, u32[]{:S(2)}) copy-start(bf16[1,216,5120]{2,1,0:T(8,128)(2,1)} %param.10) | copy-start | bytes 6635524
  49.5 1.7 %copy-start = (bf16[1,216,5120]{2,1,0:T(8,128)(2,1)S(1)}, bf16[1,216,5120]{2,1,0:T(8,128)(2,1)}, u32[]{:S(2)}) copy-start(bf16[1,216,5120]{2,1,0:T(8,128)(2,1)} %param.11) | copy-start | bytes 6635524
  51.7 7.2 %collective-permute-start.15 = (bf16[256,640]{1,0:T(8,128)(2,1)S(1)}, bf16[256,640]{1,0:T(8,128)(2,1)S(1)}, u32[]{:S(2)}, u32[]{:S(2)}) collective-permute-start(bf16[256,640]{1,0:T(8,128)(2,1)S(1)} %get-tuple-element.26), channel_id=1, source_target_pairs={{0,16},{16,32},{32,48},{48,0},{1,17},{17,33},{33,49},{49,1},{2,18}... | collective-permute-start | bytes 983048 | tf_op jit(solution)/shard_map/ppermute | solution.py:17
  52.4 10.0 %collective-permute-start.21 = (bf16[256,640]{1,0:T(8,128)(2,1)S(1)}, bf16[256,640]{1,0:T(8,128)(2,1)S(1)}, u32[]{:S(2)}, u32[]{:S(2)}) collective-permute-start(bf16[256,640]{1,0:T(8,128)(2,1)S(1)} %get-tuple-element.25), channel_id=1, source_target_pairs={{0,48},{16,0},{32,16},{48,32},{1,49},{17,1},{33,17},{49,33},{2,50}... | collective-permute-start | bytes 983048 | tf_op jit(solution)/shard_map/ppermute | solution.py:17
  58.9 5.8 %collective-permute-start.16 = (bf16[8,8,128]{2,1,0:T(8,128)(2,1)S(1)}, bf16[8,8,128]{2,1,0:T(8,128)(2,1)S(1)}, u32[]{:S(2)}, u32[]{:S(2)}) collective-permute-start(bf16[8,8,128]{2,1,0:T(8,128)(2,1)S(1)} %constant_dynamic-update-slice_fusion.4), channel_id=1, source_target_pairs={{0,16},{16,32},{32,48},{48,0},{1,17},{17,33},{33,49},{49,1},{2,18}... | collective-permute-start | bytes 49160 | tf_op jit(solution)/shard_map/ppermute | solution.py:17
  58.9 5.8 %collective-permute-start.17 = (bf16[8,8,128]{2,1,0:T(8,128)(2,1)S(1)}, bf16[8,8,128]{2,1,0:T(8,128)(2,1)S(1)}, u32[]{:S(2)}, u32[]{:S(2)}) collective-permute-start(bf16[8,8,128]{2,1,0:T(8,128)(2,1)S(1)} %constant_dynamic-update-slice_fusion.4), channel_id=1, source_target_pairs={{0,48},{16,0},{32,16},{48,32},{1,49},{17,1},{33,17},{49,33},{2,50}... | collective-permute-start | bytes 49160 | tf_op jit(solution)/shard_map/ppermute | solution.py:17
  61.6 4.2 %collective-permute-start.18 = (bf16[8,8,128]{2,1,0:T(8,128)(2,1)S(1)}, bf16[8,8,128]{2,1,0:T(8,128)(2,1)S(1)}, u32[]{:S(2)}, u32[]{:S(2)}) collective-permute-start(bf16[8,8,128]{2,1,0:T(8,128)(2,1)S(1)} %constant_dynamic-update-slice_fusion.4), channel_id=1, source_target_pairs={{0,32},{16,48},{32,0},{48,16},{1,33},{17,49},{33,1},{49,17},{2,34}... | collective-permute-start | bytes 49160 | tf_op jit(solution)/shard_map/ppermute | solution.py:17
  61.7 13.8 %collective-permute-start.20 = (bf16[256,1280]{1,0:T(8,128)(2,1)S(1)}, bf16[256,1280]{1,0:T(8,128)(2,1)S(1)}, u32[]{:S(2)}, u32[]{:S(2)}) collective-permute-start(bf16[256,1280]{1,0:T(8,128)(2,1)S(1)} %pad_maximum_fusion), channel_id=1, source_target_pairs={{0,16},{16,32},{32,48},{48,0},{1,17},{17,33},{33,49},{49,1},{2,18}... | collective-permute-start | bytes 1966088 | tf_op jit(solution)/shard_map/ppermute | solution.py:17
  62.5 13.1 %collective-permute-start.22 = (bf16[256,1280]{1,0:T(8,128)(2,1)S(1)}, bf16[256,1280]{1,0:T(8,128)(2,1)S(1)}, u32[]{:S(2)}, u32[]{:S(2)}) collective-permute-start(bf16[256,1280]{1,0:T(8,128)(2,1)S(1)} %pad_maximum_fusion.1), channel_id=1, source_target_pairs={{0,48},{16,0},{32,16},{48,32},{1,49},{17,1},{33,17},{49,33},{2,50}... | collective-permute-start | bytes 1966088 | tf_op jit(solution)/shard_map/ppermute | solution.py:17
  65.8 9.6 %collective-permute-start.19 = (bf16[256,128]{1,0:T(8,128)(2,1)S(1)}, bf16[256,128]{1,0:T(8,128)(2,1)S(1)}, u32[]{:S(2)}, u32[]{:S(2)}) collective-permute-start(bf16[256,128]{1,0:T(8,128)(2,1)S(1)} %bitcast.78), channel_id=1, source_target_pairs={{0,1},{1,0},{2,3},{3,2},{4,5},{5,4},{6,7},{7,6},{8,9},{9,8},{10,11... | collective-permute-start | bytes 196616 | tf_op jit(solution)/shard_map/ppermute | solution.py:17
  74.9 30.1 %collective-permute-start.24 = (bf16[256,640]{1,0:T(8,128)(2,1)S(1)}, bf16[256,640]{1,0:T(8,128)(2,1)S(1)}, u32[]{:S(2)}, u32[]{:S(2)}) collective-permute-start(bf16[256,640]{1,0:T(8,128)(2,1)S(1)} %get-tuple-element.22), channel_id=1, source_target_pairs={{0,1},{1,0},{2,3},{3,2},{4,5},{5,4},{6,7},{7,6},{8,9},{9,8},{10,11... | collective-permute-start | bytes 983048 | tf_op jit(solution)/shard_map/ppermute | solution.py:17
  76.3 7.3 %collective-permute-start.23 = (bf16[256,640]{1,0:T(8,128)(2,1)S(1)}, bf16[256,640]{1,0:T(8,128)(2,1)S(1)}, u32[]{:S(2)}, u32[]{:S(2)}) collective-permute-start(bf16[256,640]{1,0:T(8,128)(2,1)S(1)} %get-tuple-element.24), channel_id=1, source_target_pairs={{0,1},{1,0},{2,3},{3,2},{4,5},{5,4},{6,7},{7,6},{8,9},{9,8},{10,11... | collective-permute-start | bytes 983048 | tf_op jit(solution)/shard_map/ppermute | solution.py:17
  83.9 5.8 %collective-permute-start.25 = (bf16[64,640]{1,0:T(8,128)(2,1)S(1)}, bf16[64,640]{1,0:T(8,128)(2,1)S(1)}, u32[]{:S(2)}, u32[]{:S(2)}) collective-permute-start(bf16[64,640]{1,0:T(8,128)(2,1)S(1)} %get-tuple-element.35), channel_id=1, source_target_pairs={{0,2},{2,4},{4,6},{6,8},{8,10},{10,12},{12,14},{14,0},{1,3},{3,5},... | collective-permute-start | bytes 245768 | tf_op jit(solution)/shard_map/ppermute | solution.py:17
  84.3 5.5 %collective-permute-start.29 = (bf16[64,640]{1,0:T(8,128)(2,1)S(1)}, bf16[64,640]{1,0:T(8,128)(2,1)S(1)}, u32[]{:S(2)}, u32[]{:S(2)}) collective-permute-start(bf16[64,640]{1,0:T(8,128)(2,1)S(1)} %get-tuple-element.36), channel_id=1, source_target_pairs={{0,14},{2,0},{4,2},{6,4},{8,6},{10,8},{12,10},{14,12},{1,15},{3,1}... | collective-permute-start | bytes 245768 | tf_op jit(solution)/shard_map/ppermute | solution.py:17
  89.7 6.1 %collective-permute-start.26 = (bf16[128,640]{1,0:T(8,128)(2,1)S(1)}, bf16[128,640]{1,0:T(8,128)(2,1)S(1)}, u32[]{:S(2)}, u32[]{:S(2)}) collective-permute-start(bf16[128,640]{1,0:T(8,128)(2,1)S(1)} %pad_maximum_fusion.4), channel_id=1, source_target_pairs={{0,2},{2,4},{4,6},{6,8},{8,10},{10,12},{12,14},{14,0},{1,3},{3,5},... | collective-permute-start | bytes 491528 | tf_op jit(solution)/shard_map/ppermute | solution.py:17
  89.9 6.5 %collective-permute-start.30 = (bf16[128,640]{1,0:T(8,128)(2,1)S(1)}, bf16[128,640]{1,0:T(8,128)(2,1)S(1)}, u32[]{:S(2)}, u32[]{:S(2)}) collective-permute-start(bf16[128,640]{1,0:T(8,128)(2,1)S(1)} %pad_maximum_fusion.5), channel_id=1, source_target_pairs={{0,14},{2,0},{4,2},{6,4},{8,6},{10,8},{12,10},{14,12},{1,15},{3,1}... | collective-permute-start | bytes 491528 | tf_op jit(solution)/shard_map/ppermute | solution.py:17
  96.1 5.5 %collective-permute-start.27 = (bf16[128,640]{1,0:T(8,128)(2,1)S(1)}, bf16[128,640]{1,0:T(8,128)(2,1)S(1)}, u32[]{:S(2)}, u32[]{:S(2)}) collective-permute-start(bf16[128,640]{1,0:T(8,128)(2,1)S(1)} %fusion.14), channel_id=1, source_target_pairs={{0,2},{2,4},{4,6},{6,8},{8,10},{10,12},{12,14},{14,0},{1,3},{3,5},... | collective-permute-start | bytes 491528 | tf_op jit(solution)/shard_map/ppermute | solution.py:17
  96.7 5.3 %collective-permute-start.31 = (bf16[128,640]{1,0:T(8,128)(2,1)S(1)}, bf16[128,640]{1,0:T(8,128)(2,1)S(1)}, u32[]{:S(2)}, u32[]{:S(2)}) collective-permute-start(bf16[128,640]{1,0:T(8,128)(2,1)S(1)} %fusion.16), channel_id=1, source_target_pairs={{0,14},{2,0},{4,2},{6,4},{8,6},{10,8},{12,10},{14,12},{1,15},{3,1}... | collective-permute-start | bytes 491528 | tf_op jit(solution)/shard_map/ppermute | solution.py:17
  101.8 5.5 %collective-permute-start.28 = (bf16[128,640]{1,0:T(8,128)(2,1)S(1)}, bf16[128,640]{1,0:T(8,128)(2,1)S(1)}, u32[]{:S(2)}, u32[]{:S(2)}) collective-permute-start(bf16[128,640]{1,0:T(8,128)(2,1)S(1)} %fusion.13), channel_id=1, source_target_pairs={{0,2},{2,4},{4,6},{6,8},{8,10},{10,12},{12,14},{14,0},{1,3},{3,5},... | collective-permute-start | bytes 491528 | tf_op jit(solution)/shard_map/ppermute | solution.py:17
  102.2 5.1 %collective-permute-start.32 = (bf16[128,640]{1,0:T(8,128)(2,1)S(1)}, bf16[128,640]{1,0:T(8,128)(2,1)S(1)}, u32[]{:S(2)}, u32[]{:S(2)}) collective-permute-start(bf16[128,640]{1,0:T(8,128)(2,1)S(1)} %fusion.15), channel_id=1, source_target_pairs={{0,14},{2,0},{4,2},{6,4},{8,6},{10,8},{12,10},{14,12},{1,15},{3,1}... | collective-permute-start | bytes 491528 | tf_op jit(solution)/shard_map/ppermute | solution.py:17
  107.6 5.1 %collective-permute-start.33 = (bf16[4,16,640]{2,1,0:T(8,128)(2,1)S(1)}, bf16[4,16,640]{2,1,0:T(8,128)(2,1)S(1)}, u32[]{:S(2)}, u32[]{:S(2)}) collective-permute-start(bf16[4,16,640]{2,1,0:T(8,128)(2,1)S(1)} %dynamic-slice_bitcast_fusion), channel_id=1, source_target_pairs={{0,1},{1,0},{2,3},{3,2},{4,5},{5,4},{6,7},{7,6},{8,9},{9,8},{10,11... | collective-permute-start | bytes 245768 | tf_op jit(solution)/shard_map/ppermute | solution.py:17
  112.8 4.3 %collective-permute-start.34 = (bf16[16,1280]{1,0:T(8,128)(2,1)S(1)}, bf16[16,1280]{1,0:T(8,128)(2,1)S(1)}, u32[]{:S(2)}, u32[]{:S(2)}) collective-permute-start(bf16[16,1280]{1,0:T(8,128)(2,1)S(1)} %get-tuple-element.32), channel_id=1, source_target_pairs={{0,16},{16,32},{32,48},{48,0},{1,17},{17,33},{33,49},{49,1},{2,18}... | collective-permute-start | bytes 122888 | tf_op jit(solution)/shard_map/ppermute | solution.py:17
  114.6 4.8 %collective-permute-start.35 = (bf16[16,1280]{1,0:T(8,128)(2,1)S(1)}, bf16[16,1280]{1,0:T(8,128)(2,1)S(1)}, u32[]{:S(2)}, u32[]{:S(2)}) collective-permute-start(bf16[16,1280]{1,0:T(8,128)(2,1)S(1)} %get-tuple-element.33), channel_id=1, source_target_pairs={{0,32},{16,48},{32,0},{48,16},{1,33},{17,49},{33,1},{49,17},{2,34}... | collective-permute-start | bytes 122888 | tf_op jit(solution)/shard_map/ppermute | solution.py:17
  116.7 3.1 %collective-permute-start.36 = (bf16[16,1280]{1,0:T(8,128)(2,1)S(1)}, bf16[16,1280]{1,0:T(8,128)(2,1)S(1)}, u32[]{:S(2)}, u32[]{:S(2)}) collective-permute-start(bf16[16,1280]{1,0:T(8,128)(2,1)S(1)} %get-tuple-element.34), channel_id=1, source_target_pairs={{0,48},{16,0},{32,16},{48,32},{1,49},{17,1},{33,17},{49,33},{2,50}... | collective-permute-start | bytes 122888 | tf_op jit(solution)/shard_map/ppermute | solution.py:17
